TPU v7x, 32 devices: a whole 2x2x4 slice. The times are simulated.
32 devices in a mesh: grp: 16 (over z, y, core), tp: 2 (over x).
Axes of the slice: x: 2, y: 2, z: 4, core: 2. Of those that a mesh axis runs over, the one named last changes fastest.
Arguments:
- queries: bfloat16 [16, 2, 512, 2048], P('grp', None, None, 'tp'), may hold values from -9 to 9
- fresh_kv: bfloat16 [16, 2, 512, 2, 2048], P('grp', None, None, None, 'tp'), may hold values from -9 to 9
- stale_kv: bfloat16 [16, 2, 512, 2, 2048], P('grp', None, None, None, 'tp'), may hold values from -6 to 6
- text_kv: bfloat16 [16, 2, 256, 2, 2048], P('grp', None, None, None, 'tp'), may hold values from -6 to 6
- w_velocity: bfloat16 [2048, 64], P('tp'), may hold values from -2.390625 to 2.390625
- latent: float32 [16, 2, 512, 64], P('grp', None, 'tp'), may hold values from -6 to 6
- live_counts: int32 [16, 2], replicated, may hold values from 128 to 512, as said below
- refresh_rows: int32 [16, 2, 64], replicated, may hold values from 0 to 511, as said below
- request_list: int32 [16], replicated, may hold values from 0 to 15, each once
- timesteps: int32 [16, 2], replicated, may hold values from 0 to 999, as said below
Outputs:
- next_stale: bfloat16 [16, 2, 512, 2, 2048], P('grp', None, None, None, 'tp')
- velocity: float32 [16, 2, 512, 64], P('grp', None, 'tp')
- latent_next: float32 [16, 2, 512, 64], P('grp', None, 'tp')
Inputs may be any that keep to these rules, and one draw needn't show every extreme that they name: `live_counts`: 512 is reached in every draw. `refresh_rows`: rows within one list are distinct. `timesteps`: the next timestep is below the current one. `request_list`: each request appears once.
All inputs are finite; a program needn't handle non-finite values.
Results may differ from a plain program's by a relative error of at most 0.0045.
Values may be sent and summed in bfloat16 or wider, within the bound.
No kernel may reach another device: no remote copies, remote signals or barrier semaphores. Data moves between devices by JAX's collectives and lax.ppermute only.
A program may use at most 128 MiB of HBM per device.

v0:
```python
import math

import jax
import jax.numpy as jnp
from jax import lax
from jax.sharding import PartitionSpec as P

HD = 128


def from_behind(block, axis, distance):
    devices = range(lax.axis_size(axis))
    route = [((i - distance) % len(devices), i) for i in devices]
    return lax.ppermute(block, axis, route)


def slot_velocity(slot_query, own_kv, partner_kv, text_pair, own_live, partner_live, w_velocity):
    img_rows = slot_query.shape[0]
    heads_here = slot_query.shape[1] // HD
    key_rows = jnp.concatenate([own_kv[:, 0], partner_kv[:, 0], text_pair[:, 0]], axis=0)
    value_rows = jnp.concatenate([own_kv[:, 1], partner_kv[:, 1], text_pair[:, 1]], axis=0)
    row_ids = jnp.arange(img_rows, dtype=jnp.int32)
    live_mask = jnp.concatenate(
        [row_ids < own_live, row_ids < partner_live, jnp.ones((text_pair.shape[0],), dtype=bool)]
    )
    outputs = []
    for head_index in range(heads_here):
        first = head_index * HD
        scores = lax.dot_general(
            slot_query[:, first : first + HD],
            key_rows[:, first : first + HD],
            (((1,), (1,)), ((), ())),
            preferred_element_type=jnp.float32,
        ) * (1.0 / math.sqrt(HD))
        scores = jnp.where(live_mask[None, :], scores, -jnp.inf)
        row_top = jnp.max(scores, axis=1, keepdims=True)
        weights = jnp.exp(scores - row_top)
        totals = jnp.sum(weights, axis=1, keepdims=True)
        blended = (
            jnp.dot(
                weights.astype(jnp.bfloat16),
                value_rows[:, first : first + HD],
                preferred_element_type=jnp.float32,
            )
            / totals
        )
        outputs.append(blended.astype(jnp.bfloat16))
    blended = jnp.concatenate(outputs, axis=1)
    return jnp.dot(blended, w_velocity, preferred_element_type=jnp.float32)


def shards(
    queries,
    fresh_kv,
    stale_kv,
    text_kv,
    w_velocity,
    latent,
    live_counts,
    refresh_rows,
    request_list,
    timesteps,
):
    groups_count = lax.axis_size("grp")
    half_groups = groups_count // 2
    my_group = lax.axis_index("grp")
    partner = (my_group + half_groups) % groups_count
    slot_count = queries.shape[1]
    partner_fresh = from_behind(fresh_kv, "grp", half_groups)
    text_other = from_behind(text_kv, "grp", half_groups)
    partner_lists = lax.dynamic_index_in_dim(refresh_rows, partner, 0, keepdims=False)
    my_live = lax.dynamic_index_in_dim(live_counts, my_group, 0, keepdims=False)
    partner_live = lax.dynamic_index_in_dim(live_counts, partner, 0, keepdims=False)
    arrived = jnp.stack(
        [
            jnp.take(partner_fresh[0, slot_index], partner_lists[slot_index], axis=0)
            for slot_index in range(slot_count)
        ]
    )
    partials = []
    for slot_index in range(slot_count):
        repaired = stale_kv[0, slot_index].at[partner_lists[slot_index]].set(arrived[slot_index])
        text_pair = jnp.concatenate([text_kv[0, slot_index], text_other[0, slot_index]], axis=0)
        partials.append(
            slot_velocity(
                queries[0, slot_index],
                fresh_kv[0, slot_index],
                repaired,
                text_pair,
                my_live[slot_index],
                partner_live[slot_index],
                w_velocity,
            )
        )
    partial_value = jnp.stack(partials)
    tp_count = lax.axis_size("tp")
    share = partial_value.shape[1] // tp_count
    tp_index = lax.axis_index("tp")
    whole = lax.psum(partial_value, "tp")
    summed = lax.dynamic_slice_in_dim(whole, tp_index * share, share, 1)
    row_ids = tp_index * share + jnp.arange(share, dtype=jnp.int32)
    live_rows = row_ids[None, :] < my_live[:, None]
    velocity = jnp.where(live_rows[:, :, None], summed, 0.0)
    pair_index = my_group % half_groups
    request_ids = lax.dynamic_slice_in_dim(request_list, pair_index * slot_count, slot_count)
    matches = (
        request_ids[:, None] == jnp.arange(timesteps.shape[0], dtype=jnp.int32)[None, :]
    ).astype(jnp.int32)
    times = jnp.dot(matches, timesteps)
    step_size = (times[:, 1] - times[:, 0]).astype(jnp.float32) / 1000.0
    latent_next = latent[0] + step_size[:, None, None] * velocity
    return (partner_fresh, velocity[None], latent_next[None])


def solution(mesh):
    return jax.shard_map(
        shards,
        mesh=mesh,
        in_specs=(
            P("grp", None, None, "tp"),
            P("grp", None, None, None, "tp"),
            P("grp", None, None, None, "tp"),
            P("grp", None, None, None, "tp"),
            P("tp", None),
            P("grp", None, "tp", None),
            P(),
            P(),
            P(),
            P(),
        ),
        out_specs=(
            P("grp", None, None, None, "tp"),
            P("grp", None, "tp", None),
            P("grp", None, "tp", None),
        ),
        check_vma=False,
    )
```

profile of v0, /device:TPU:0, one launch (start us, length us, event | category | flops | bytes accessed | tf_op | source)
XLA Modules:
  0.0 421.9 jit_solution(8384622685572879384)
XLA Ops:
  7.3 4.1 collective-permute-start
  11.4 3.5 copy.46
  14.9 0.8 constant_dynamic-slice_fusion
  16.3 0.7 fusion.302
  17.6 0.6 iota_compare_fusion.2
  18.3 0.7 iota_compare_fusion.3
  18.9 0.7 iota_compare_fusion
  19.9 0.7 multiply_reduce_fusion
  20.6 0.6 iota_compare_fusion.1
  21.2 3.0 slice_bitcast_fusion.10
  24.3 1.2 slice_bitcast_fusion.13
  25.5 1.3 copy-done.11
  26.8 3.8 fusion.303
  31.2 2.9 copy_bitcast_fusion
  34.1 1.5 slice_bitcast_fusion.4
  35.6 1.5 slice_bitcast_fusion.8
  37.1 1.4 copy-done.10
  38.5 3.8 slice_bitcast_fusion.3
  42.3 239.7 %collective-permute-done.1 = bf16[1,2,256,2,1024]{4,2,3,1,0:T(8,128)(2,1)} collective-permute-done((bf16[1,2,256,2,1024]{4,2,3,1,0:T(8,128)(2,1)}, bf16[1,2,256,2,1024]{4,2,3,1,0:T(8,128)(2,1)}, u32[]{:S(2)}, u32[]{:S(2)}) %collective-permute-start.1) | collective-permute-done | bytes 2097184 | tf_op jit(solution)/shard_map/ppermute | solution.py:14
  282.0 1.7 slice_bitcast_fusion.9
  283.8 2.1 fusion.244
  285.9 6.0 %slice_bitcast_fusion.1 = (bf16[512,2,1024]{2,1,0:T(2,128)(2,1)}, bf16[512,2,1024]{2,1,0:T(2,128)(2,1)}) fusion(bf16[1,2,512,2,1024]{4,3,2,1,0:T(2,128)(2,1)} %collective-permute-done), kind=kLoop, calls=%fused_computation.89 | loop fusion | bytes 8388608 | tf_op jit(solution)/shard_map/squeeze | solution.py:76
  291.9 2.7 gather_fusion.1
  294.6 3.4 gather_fusion
  298.0 2.3 broadcast_select_fusion
  300.3 8.3 %scatter_fusion.1 = bf16[512,2,1024]{2,1,0:T(2,128)(2,1)} fusion(bf16[512,2,1024]{2,1,0:T(2,128)(2,1)} %get-tuple-element.15, s32[64]{0:T(128)} %get-tuple-element.39, bf16[64,2,1024]{2,1,0:T(2,128)(2,1)} %get-tuple-element.81), kind=kCustom, calls=%fused_computation.3 | custom fusion | bytes 786688 | tf_op jit(solution)/shard_map/scatter | solution.py:82
  308.5 6.5 %fusion.305 = (bf16[512,1,1024]{2,1,0:T(2,128)(2,1)}, bf16[512,1,1024]{2,1,0:T(2,128)(2,1)S(1)}) fusion(bf16[512,2,1024]{2,1,0:T(2,128)(2,1)} %scatter_fusion.1), kind=kLoop, calls=%fused_computation.286 | loop fusion | bytes 4194304 | tf_op jit(solution)/shard_map/slice | solution.py:21
  315.5 0.8 copy-done.16
  317.2 0.7 copy-done.12
  317.8 2.8 fusion.308
  320.7 2.8 fusion.309
  323.5 2.8 fusion.310
  326.4 2.9 fusion.311
  329.2 2.8 fusion.312
  332.0 2.8 fusion.313
  334.9 2.3 fusion.314
  337.2 2.3 fusion.315
  339.5 2.5 scatter_fusion
  342.0 3.0 fusion.304
  345.4 0.8 copy-done.15
  352.9 1.1 copy-done.8
  355.3 0.6 fusion.189
  355.9 1.2 copy-done.7
  357.7 0.6 fusion.183
  358.3 0.8 copy-done.6
  359.6 0.6 fusion.177
  360.2 0.8 copy-done.5
  361.5 0.6 fusion.171
  362.1 0.8 copy-done.4
  363.3 0.6 fusion.165
  364.0 0.8 copy-done.3
  365.2 0.6 fusion.159
  365.9 0.8 copy-done.2
  367.1 0.6 fusion.153
  367.8 0.8 copy-done.1
  369.0 0.6 fusion.147
  371.2 0.6 pad_maximum_fusion.1
  375.2 0.6 fusion.219
  378.5 0.6 fusion.201
  379.7 0.6 fusion.195
  380.6 0.7 pad_maximum_fusion.6
  381.5 24.4 %all-reduce.2.cloned.1.call-done = f32[2,512,64]{1,2,0:T(8,128)} async-done(((f32[2,512,64]{1,2,0:T(8,128)}), f32[2,512,64]{1,2,0:T(8,128)}) %all-reduce.2.cloned.1.call-update) | async-done | bytes 262160 | tf_op jit(solution)/shard_map/psum | solution.py:99
  405.9 1.6 fusion.294
  407.5 7.1 %copy.84 = bf16[1,2,512,2,1024]{4,3,2,1,0:T(2,128)(2,1)} copy(bf16[1,2,512,2,1024]{4,3,2,1,0:T(2,128)(2,1)} %collective-permute-done) | data formatting | bytes 8388608
  (114 shorter events, 23.5 us)
Async XLA Ops:
  7.2 362.5 %copy-start = (bf16[1024,64]{0,1:T(8,128)(2,1)S(1)}, bf16[1024,64]{0,1:T(8,128)(2,1)}, u32[]{:S(2)}) copy-start(bf16[1024,64]{0,1:T(8,128)(2,1)} %param.16) | copy-start | bytes 393220
  7.2 9.1 %copy-start.32 = (s32[16,2]{0,1:T(2,128)S(1)}, s32[16,2]{0,1:T(2,128)}, u32[]{:S(2)}) copy-start(s32[16,2]{0,1:T(2,128)} %param.18) | copy-start | bytes 388
  7.2 12.4 %copy-start.36 = (s32[16]{0:T(128)S(1)}, s32[16]{0:T(128)}, u32[]{:S(2)}) copy-start(s32[16]{0:T(128)} %param.20) | copy-start | bytes 196
  7.2 12.5 %copy-start.35 = (s32[16,2]{0,1:T(2,128)S(1)}, s32[16,2]{0,1:T(2,128)}, u32[]{:S(2)}) copy-start(s32[16,2]{0,1:T(2,128)} %param.21) | copy-start | bytes 388
  7.2 398.6 %all-reduce.2.cloned.1.call-start = ((), (), s32[]{:S(2)}) async-start(), calls=%async_computation | async-start | bytes 524288 | tf_op jit(solution)/shard_map/psum | solution.py:99
  7.3 278.6 %collective-permute-start = (bf16[1,2,512,2,1024]{4,3,2,1,0:T(2,128)(2,1)}, bf16[1,2,512,2,1024]{4,3,2,1,0:T(2,128)(2,1)}, u32[]{:S(2)}, u32[]{:S(2)}) collective-permute-start(bf16[1,2,512,2,1024]{4,3,2,1,0:T(2,128)(2,1)} %param.13), channel_id=1, source_target_pairs={{16,0},{18,2},{20,4},{22,6},{24,8},{26,10},{28,12},{30,14},{0,16},... | collective-permute-start | bytes 12582920 | tf_op jit(solution)/shard_map/ppermute | solution.py:14
  14.9 9.3 %copy-start.23 = (bf16[1,2,512,1024]{3,2,1,0:T(8,128)(2,1)S(1)}, bf16[1,2,512,1024]{3,2,1,0:T(8,128)(2,1)}, u32[]{:S(2)}) copy-start(bf16[1,2,512,1024]{3,2,1,0:T(8,128)(2,1)} %param.12) | copy-start | bytes 6291460
  14.9 267.1 %collective-permute-start.1 = (bf16[1,2,256,2,1024]{4,2,3,1,0:T(8,128)(2,1)}, bf16[1,2,256,2,1024]{4,2,3,1,0:T(8,128)(2,1)}, u32[]{:S(2)}, u32[]{:S(2)}) collective-permute-start(bf16[1,2,256,2,1024]{4,2,3,1,0:T(8,128)(2,1)} %copy.46), channel_id=1, source_target_pairs={{16,0},{18,2},{20,4},{22,6},{24,8},{26,10},{28,12},{30,14},{0,16},... | collective-permute-start | bytes 6291464 | tf_op jit(solution)/shard_map/ppermute | solution.py:14
  24.3 2.6 copy-start.11
  35.6 2.9 copy-start.10
  42.3 241.4 %copy-start.20 = (bf16[256,2,1024]{2,0,1:T(8,128)(2,1)S(1)}, bf16[256,2,1024]{2,0,1:T(8,128)(2,1)}, u32[]{:S(2)}) copy-start(bf16[256,2,1024]{2,0,1:T(8,128)(2,1)} %get-tuple-element.26) | copy-start | bytes 3145732
  42.3 241.4 %copy-start.21 = (bf16[256,2,1024]{2,0,1:T(8,128)(2,1)S(1)}, bf16[256,2,1024]{2,0,1:T(8,128)(2,1)}, u32[]{:S(2)}) copy-start(bf16[256,2,1024]{2,0,1:T(8,128)(2,1)} %get-tuple-element.27) | copy-start | bytes 3145732
  315.1 1.2 copy-start.16
  315.1 1.5 copy-start.22
  316.6 1.2 copy-start.12
  334.9 4.6 %copy-start.24 = (bf16[64,2,1024]{2,1,0:T(2,128)(2,1)S(1)}, bf16[64,2,1024]{2,1,0:T(2,128)(2,1)}, u32[]{:S(2)}) copy-start(bf16[64,2,1024]{2,1,0:T(2,128)(2,1)} %get-tuple-element.82) | copy-start | bytes 786436
  345.0 1.2 copy-start.15
  345.0 1.5 copy-start.19
  350.5 1.6 copy-start.9
  352.1 1.9 copy-start.8
  352.1 1.9 copy-start.31
  352.5 2.0 copy-start.14
  352.5 2.2 copy-start.18
  355.3 1.9 copy-start.7
  355.3 1.9 copy-start.30
  357.2 1.9 copy-start.6
  357.2 1.9 copy-start.29
  359.1 1.9 copy-start.5
  359.1 1.9 copy-start.28
  361.0 1.9 copy-start.4
  361.0 1.9 copy-start.27
  362.8 1.9 copy-start.3
  362.8 1.9 copy-start.26
  364.7 1.9 copy-start.2
  366.6 1.9 copy-start.1
  369.7 1.2 copy-start.13
  369.7 1.5 copy-start.17
  379.7 1.7 copy-start.33
  379.7 26.2 %copy-start.25 = (f32[1,2,256,64]{2,3,1,0:T(8,128)S(1)}, f32[1,2,256,64]{2,3,1,0:T(8,128)}, u32[]{:S(2)}) copy-start(f32[1,2,256,64]{2,3,1,0:T(8,128)} %param.17) | copy-start | bytes 393220
  379.7 26.2 %copy-start.34 = (f32[2]{0:T(128)S(1)}, f32[2]{0:T(128)}, u32[]{:S(2)}) copy-start(f32[2]{0:T(128)} %multiply_reduce_fusion) | copy-start | bytes 28
Sparse Core Ops, SparseCore 0:
  381.5 24.3 all-reduce.1
where the time goes:
time: 430 us; the launch traced here: 422 us
  waiting for transfers between devices  264 us (61%)
  local copies, waits for them, and re-layouts  80.3 us (19%)
  matrix products  37 us (9%)
  other arithmetic  21.3 us (5%)
  between operations  15 us (3%)
    ppermute x2, waiting for transfers between devices, from_behind(): return lax.ppermute(block, axis, route)  240 us
    dot_general x16, matrix products, slot_velocity(): lax.dot_general(slot_query[:, first:first + HD], key_rows[:, first:first...  26.4 us
    unnamed x80, local copies, waits for them, and re-layouts  26.2 us
    psum x1, waiting for transfers between devices, shards(): whole = lax.psum(partial_value, 'tp')  24.4 us
    scatter x2, local copies, waits for them, and re-layouts, shards(): stale_kv[0, slot_index].at[partner_lists[slot_index]]  10.8 us
    dot_general x16, matrix products, slot_velocity(): jnp.dot(weights.astype(jnp.bfloat16), value_rows[:, first:first + HD], pr...  9.89 us
    slice x2, local copies, waits for them, and re-layouts, slot_velocity(): partner_kv[:, 1]  9.5 us
  transfers between devices with their start and end apart: 3, of which 2 were waited for; matrix products, arithmetic and copies ran while one was open for 8% of the time, Pallas kernels for 0%

commit v1 on v0

v1 whole, which is shorter than its diff:
```python
import functools
import math

import jax
import jax.numpy as jnp
from jax import lax
from jax.experimental import pallas as pl
from jax.experimental.pallas import tpu as pltpu
from jax.sharding import PartitionSpec as P

HD = 128
HBM = pltpu.MemorySpace.HBM
SMEM = pltpu.MemorySpace.SMEM
VMEM_LIMIT = 50 * 1024 * 1024


def from_behind(block, axis, distance):
    devices = range(lax.axis_size(axis))
    route = [((i - distance) % len(devices), i) for i in devices]
    return lax.ppermute(block, axis, route)


def send_order(lists, img_rows):
    count = lists.shape[2]
    zone = count + jnp.arange(count, dtype=jnp.int32)
    order = jnp.arange(count, dtype=jnp.int32)
    earlier = order[:, None] >= order[None, :]
    free = jnp.logical_not(jnp.any(lists[..., :, None] == zone, axis=2))
    outside = lists >= 2 * count
    free_rank = jnp.sum(jnp.where(earlier, free[..., None, :], False).astype(jnp.int32), axis=3)
    outside_rank = jnp.sum(jnp.where(earlier, outside[..., None, :], False).astype(jnp.int32), axis=3)
    match = (
        outside[..., :, None]
        & free[..., None, :]
        & (outside_rank[..., :, None] == free_rank[..., None, :])
    )
    listed_at = jnp.sum(jnp.where(match, lists[..., :, None], 0), axis=2)
    zone_source = jnp.where(listed_at > 0, listed_at, zone)
    place = jnp.sum(jnp.where(match, zone, 0), axis=3)
    tail = jnp.arange(2 * count, img_rows, dtype=jnp.int32)
    moved = jnp.sum(
        jnp.where(lists[..., :, None] == tail, place[..., :, None], 0), axis=2
    )
    tail_source = jnp.where(moved > 0, moved, tail)
    head = jnp.broadcast_to(order, lists.shape)
    return jnp.concatenate([head, zone_source, tail_source], axis=2)


def pick_rows_kernel(slots, first, rows, total, order_ref, fresh_ref, *rest):
    out_ref, sem = rest[-2], rest[-1]
    for out_slot, slot in enumerate(slots):

        def issue(i, carry):
            source = order_ref[slot * total + first + i]
            pltpu.make_async_copy(fresh_ref.at[slot, source], out_ref.at[out_slot, i], sem).start()
            return carry

        lax.fori_loop(0, rows, issue, 0, unroll=8)
    pltpu.make_async_copy(out_ref, out_ref, sem).wait()


def pick_rows(order, fresh, slots, first, rows, after=()):
    total = fresh.shape[1]
    size = len(slots) * rows * fresh.shape[2] * fresh.shape[3]
    return pl.pallas_call(
        functools.partial(pick_rows_kernel, slots, first, rows, total),
        out_shape=jax.ShapeDtypeStruct((len(slots), rows) + fresh.shape[2:], fresh.dtype),
        in_specs=[pl.BlockSpec(memory_space=SMEM)] + [pl.BlockSpec(memory_space=HBM)] * (1 + len(after)),
        out_specs=pl.BlockSpec(memory_space=HBM),
        scratch_shapes=[pltpu.SemaphoreType.DMA],
        cost_estimate=pl.CostEstimate(flops=0, bytes_accessed=4 * size, transcendentals=0),
        name="pick_rows",
    )(order, fresh, *after)


def place_rows_kernel(pieces, total, order_ref, *rest):
    refs, out_ref, sem = rest[: len(pieces)], rest[-2], rest[-1]
    for (slots, first, rows), piece_ref in zip(pieces, refs):
        for in_slot, slot in enumerate(slots):

            def issue(i, carry):
                target = order_ref[slot * total + first + i]
                pltpu.make_async_copy(piece_ref.at[in_slot, i], out_ref.at[slot, target], sem).start()
                return carry

            lax.fori_loop(0, rows, issue, 0, unroll=8)
    for piece_ref in refs:
        pltpu.make_async_copy(piece_ref, piece_ref, sem).wait()


def place_rows(order, parts, pieces, shape, whole=None):
    total = shape[1]
    size = sum(math.prod(part.shape) for part in parts)
    extra = () if whole is None else (whole,)
    return pl.pallas_call(
        functools.partial(place_rows_kernel, pieces, total),
        out_shape=jax.ShapeDtypeStruct(shape, parts[0].dtype),
        in_specs=[pl.BlockSpec(memory_space=SMEM)]
        + [pl.BlockSpec(memory_space=HBM)] * (len(parts) + len(extra)),
        out_specs=pl.BlockSpec(memory_space=HBM),
        scratch_shapes=[pltpu.SemaphoreType.DMA],
        input_output_aliases={} if whole is None else {1 + len(parts): 0},
        cost_estimate=pl.CostEstimate(flops=0, bytes_accessed=4 * size, transcendentals=0),
        name="place_rows",
    )(order, *parts, *extra)


def across(a, b):
    return lax.dot_general(a, b, (((1,), (1,)), ((), ())), preferred_element_type=jnp.float32)


def text_kernel(k_ref, v_ref, w_ref, out_ref):
    rows = k_ref.shape[1]
    channels = w_ref.shape[0]
    out_ref[0, 0, :rows, :] = k_ref[0]
    projected = across(w_ref[...], v_ref[0]).astype(out_ref.dtype)
    for part in range(rows // HD):
        start = rows + part * channels
        out_ref[0, 0, start : start + channels, :] = projected[:, part * HD : (part + 1) * HD]


def project_text(keys, values, w_t):
    slots, rows, width = keys.shape
    heads = width // HD
    channels = w_t.shape[0]
    packed = rows + channels * rows // HD
    block = pl.BlockSpec((1, rows, HD), lambda s, h: (s, 0, h))
    return pl.pallas_call(
        text_kernel,
        grid=(slots, heads),
        out_shape=jax.ShapeDtypeStruct((slots, heads, packed, HD), keys.dtype),
        in_specs=[block, block, pl.BlockSpec((channels, HD), lambda s, h: (0, h))],
        out_specs=pl.BlockSpec((1, 1, packed, HD), lambda s, h: (s, h, 0, 0)),
        cost_estimate=pl.CostEstimate(
            flops=2 * slots * rows * width * channels, bytes_accessed=4 * keys.size * 2, transcendentals=0
        ),
        name="project_text",
    )(keys, values, w_t)


def attention_kernel(text_rows, *refs):
    (q_ref, kf_ref, vf_ref, ks_ref, vs_ref, kh_ref, vh_ref, own_ref, other_ref, w_ref, bias_ref) = refs[:11]
    out_ref, scores_ref = refs[11], refs[12]
    head = pl.program_id(1)
    query = q_ref[0]
    w_t = w_ref[...]
    channels = w_t.shape[0]
    scale = 1.0 / math.sqrt(HD)
    pieces = []
    for k_ref, v_ref in ((kf_ref, vf_ref), (ks_ref, vs_ref), (kh_ref, vh_ref)):
        rows = k_ref.shape[1]
        step = min(rows, 256)
        for start in range(0, rows, step):
            pieces.append((k_ref.at[0, start : start + step], v_ref.at[0, start : start + step], step))
    for t_ref in (own_ref, other_ref):
        pieces.append((t_ref.at[0, 0, :text_rows], t_ref, text_rows))
    top = None
    at = 0
    for k_ref, _, rows in pieces:
        scores = across(k_ref[...], query) * scale + bias_ref[0, at : at + rows]
        scores_ref[at : at + rows, :] = scores
        piece_top = jnp.max(scores, axis=0, keepdims=True)
        top = piece_top if top is None else jnp.maximum(top, piece_top)
        at += rows
    total = jnp.zeros_like(top)
    blended = jnp.zeros((channels, query.shape[0]), jnp.float32)
    at = 0
    for _, v_ref, rows in pieces:
        weights = jnp.exp(scores_ref[at : at + rows, :] - top)
        total += jnp.sum(weights, axis=0, keepdims=True)
        rounded = weights.astype(jnp.bfloat16)
        if v_ref.shape[-2] == rows and len(v_ref.shape) == 2:
            projected = across(w_t, v_ref[...]).astype(jnp.bfloat16)
            blended += jnp.dot(projected, rounded, preferred_element_type=jnp.float32)
        else:
            for part in range(rows // HD):
                start = rows + part * channels
                blended += jnp.dot(
                    v_ref[0, 0, start : start + channels, :],
                    rounded[part * HD : (part + 1) * HD],
                    preferred_element_type=jnp.float32,
                )
        at += rows
    term = blended / total

    @pl.when(head == 0)
    def _():
        out_ref[0] = term

    @pl.when(head != 0)
    def _():
        out_ref[0] += term


def attention(queries, fresh_k, fresh_v, stale_k, stale_v, hot_k, hot_v, text_own, text_other, w_t, bias):
    slots, rows, width = queries.shape
    heads = width // HD
    channels = w_t.shape[0]
    key_rows = bias.shape[1]
    text_rows = (text_own.shape[2] * HD) // (HD + channels)

    def wide(array):
        return pl.BlockSpec((1, array.shape[1], HD), lambda s, h: (s, 0, h))

    packed = pl.BlockSpec((1, 1) + text_own.shape[2:], lambda s, h: (s, h, 0, 0))
    many = slots * heads * rows * key_rows
    return pl.pallas_call(
        functools.partial(attention_kernel, text_rows),
        grid=(slots, heads),
        out_shape=jax.ShapeDtypeStruct((slots, channels, rows), jnp.float32),
        in_specs=[wide(a) for a in (queries, fresh_k, fresh_v, stale_k, stale_v, hot_k, hot_v)]
        + [
            packed,
            packed,
            pl.BlockSpec((channels, HD), lambda s, h: (0, h)),
            pl.BlockSpec((1, key_rows, 1), lambda s, h: (s, 0, 0)),
        ],
        out_specs=pl.BlockSpec((1, channels, rows), lambda s, h: (s, 0, 0)),
        scratch_shapes=[pltpu.VMEM((key_rows, rows), jnp.float32)],
        cost_estimate=pl.CostEstimate(
            flops=2 * many * (HD + channels), bytes_accessed=24 * 1024 * 1024, transcendentals=many
        ),
        compiler_params=pltpu.CompilerParams(vmem_limit_bytes=VMEM_LIMIT),
        name="attention",
    )(queries, fresh_k, fresh_v, stale_k, stale_v, hot_k, hot_v, text_own, text_other, w_t, bias)


def shards(
    queries,
    fresh_kv,
    stale_kv,
    text_kv,
    w_velocity,
    latent,
    live_counts,
    refresh_rows,
    request_list,
    timesteps,
):
    half_groups = lax.axis_size("grp") // 2
    my_group = lax.axis_index("grp")
    partner = (my_group + half_groups) % (2 * half_groups)
    queries, fresh, stale, text = queries[0], fresh_kv[0], stale_kv[0], text_kv[0]
    slots, img_rows = queries.shape[:2]
    listed_count = refresh_rows.shape[2]
    hot_rows = 2 * listed_count
    last_rows = 128
    split = img_rows - last_rows
    both = tuple(range(slots))

    raw = fresh[:, :listed_count]
    raw_in = from_behind(raw, "grp", half_groups)

    w_t = w_velocity.T
    text_own = project_text(text[:, :, 0], text[:, :, 1], w_t)

    my_list = lax.dynamic_index_in_dim(refresh_rows, my_group, 0, keepdims=False)
    partner_list = lax.dynamic_index_in_dim(refresh_rows, partner, 0, keepdims=False)
    orders = send_order(jnp.stack([my_list, partner_list]), img_rows)
    my_order, partner_order = orders[0].reshape(-1), orders[1].reshape(-1)

    zone = pick_rows(my_order, fresh, both, listed_count, listed_count)
    zone_in = from_behind(zone, "grp", half_groups)
    text_in = from_behind(text_own, "grp", half_groups)
    pieces = [(both[:-1], hot_rows, img_rows - hot_rows), (both[-1:], hot_rows, split - hot_rows)]
    early = pick_rows(my_order, fresh, *pieces[0], after=(zone_in,))
    early_in = from_behind(early, "grp", half_groups)
    late = pick_rows(my_order, fresh, *pieces[1], after=(text_in,))
    late_in = from_behind(late, "grp", half_groups)
    last_piece = (both[-1:], split, last_rows)
    last = pick_rows(my_order, fresh, *last_piece, after=(early_in,))
    last_in = from_behind(last, "grp", half_groups)

    my_live = lax.dynamic_index_in_dim(live_counts, my_group, 0, keepdims=False)
    partner_live = lax.dynamic_index_in_dim(live_counts, partner, 0, keepdims=False)
    row_ids = jnp.arange(img_rows, dtype=jnp.int32)
    hot_source = orders[1][:, :hot_rows]
    stale_listed = jnp.any(partner_list[:, :, None] == row_ids, axis=1)
    hot_listed = jnp.any(partner_list[:, :, None] == hot_source[:, None, :], axis=1)
    live = jnp.concatenate(
        [
            row_ids < my_live[:, None],
            (row_ids < partner_live[:, None]) & jnp.logical_not(stale_listed),
            (hot_source < partner_live[:, None]) & hot_listed,
            jnp.ones((slots, 2 * text.shape[1]), dtype=bool),
        ],
        axis=1,
    )
    bias = jnp.where(live, 0.0, -jnp.inf).astype(jnp.float32)[:, :, None]
    hot = jnp.concatenate([raw_in, zone_in], axis=1)
    partial = attention(
        queries,
        fresh[:, :, 0],
        fresh[:, :, 1],
        stale[:, :, 0],
        stale[:, :, 1],
        hot[:, :, 0],
        hot[:, :, 1],
        text_own,
        text_in,
        w_t,
        bias,
    )

    tp_count = lax.axis_size("tp")
    tp_index = lax.axis_index("tp")
    share = img_rows // tp_count
    if tp_count == 2:
        mine = lax.dynamic_slice_in_dim(partial, tp_index * share, share, 2)
        theirs = lax.dynamic_slice_in_dim(partial, (1 - tp_index) * share, share, 2)
        summed = mine + from_behind(theirs, "tp", 1)
    else:
        summed = lax.psum_scatter(partial, "tp", scatter_dimension=2, tiled=True)
    summed = jnp.swapaxes(summed, 1, 2)
    share_ids = tp_index * share + jnp.arange(share, dtype=jnp.int32)
    live_rows = share_ids[None, :] < my_live[:, None]
    velocity = jnp.where(live_rows[:, :, None], summed, 0.0)
    pair_index = my_group % half_groups
    request_ids = lax.dynamic_slice_in_dim(request_list, pair_index * slots, slots)
    matches = (
        request_ids[:, None] == jnp.arange(timesteps.shape[0], dtype=jnp.int32)[None, :]
    ).astype(jnp.int32)
    times = jnp.sum(matches[:, :, None] * timesteps[None], axis=1)
    step_size = (times[:, 1] - times[:, 0]).astype(jnp.float32) / 1000.0
    latent_next = latent[0] + step_size[:, None, None] * velocity

    next_stale = place_rows(
        partner_order,
        (raw_in, zone_in, early_in, late_in),
        [(both, 0, listed_count), (both, listed_count, listed_count)] + pieces,
        fresh.shape,
    )
    next_stale = place_rows(partner_order, (last_in,), [last_piece], fresh.shape, whole=next_stale)
    return (next_stale[None], velocity[None], latent_next[None])


def solution(mesh):
    return jax.shard_map(
        shards,
        mesh=mesh,
        in_specs=(
            P("grp", None, None, "tp"),
            P("grp", None, None, None, "tp"),
            P("grp", None, None, None, "tp"),
            P("grp", None, None, None, "tp"),
            P("tp", None),
            P("grp", None, "tp", None),
            P(),
            P(),
            P(),
            P(),
        ),
        out_specs=(
            P("grp", None, None, None, "tp"),
            P("grp", None, "tp", None),
            P("grp", None, "tp", None),
        ),
        check_vma=False,
    )
```

time: 430 us -> 417 us (0.970); the launches traced: 422 us -> 416 us
  Pallas kernels: 0 us -> 294 us
  waiting for transfers between devices: 264 us -> 67.9 us
  local copies, waits for them, and re-layouts: 80.3 us -> 37.1 us
  matrix products: 37 us -> 0 us
  other arithmetic: 21.3 us -> 4.6 us
  between operations: 15 us -> 1.08 us
  starting transfers between devices: 4.16 us -> 12 us
    pallas_call x0 -> x8, Pallas kernels: none -> 294 us  [the longest x2 131 us: place_rows(): pl.pallas_call(functools.partial(place_rows_kernel, pieces, total), out_s...]
    ppermute x2 -> x7, waiting for transfers between devices: 240 us -> 67.9 us  [from_behind(): return lax.ppermute(block, axis, route)]
    dot_general x35 -> x0, matrix products: 37 us -> none  [the longest x16 26.4 us: slot_velocity(): lax.dot_general(slot_query[:, first:first + HD], key_rows[:, first:first...]
    psum x1 -> x0, waiting for transfers between devices: 24.4 us -> none  [shards(): whole = lax.psum(partial_value, 'tp')]
    unnamed x80 -> x24, local copies, waits for them, and re-layouts: 26.2 us -> 11.6 us
    slice x4 -> x2, local copies, waits for them, and re-layouts: 13.9 us -> 1.88 us  [the longest x1 1.88 us: shards(): raw = fresh[:, :listed_count]]
    scatter x2 -> x0, local copies, waits for them, and re-layouts: 10.8 us -> none  [shards(): stale_kv[0, slot_index].at[partner_lists[slot_index]]]
    ppermute x2 -> x7, starting transfers between devices: 4.12 us -> 12 us  [from_behind(): return lax.ppermute(block, axis, route)]
  transfers between devices with their start and end apart: 3 -> 7, of which waited for: 2 -> 3; matrix products, arithmetic and copies ran while one was open for 8% -> 6% of each run, Pallas kernels for 0% -> 62%
where the time goes in v1:
time: 417 us; the launch traced here: 416 us
  Pallas kernels  294 us (71%)
  waiting for transfers between devices  67.9 us (16%)
  local copies, waits for them, and re-layouts  37.1 us (9%)
  starting transfers between devices  12 us (3%)
  other arithmetic  4.6 us (1%)
    pallas_call x2, Pallas kernels, place_rows(): pl.pallas_call(functools.partial(place_rows_kernel, pieces, total), out_s...  131 us
    pallas_call x4, Pallas kernels, pick_rows(): pl.pallas_call(functools.partial(pick_rows_kernel, slots, first, rows, to...  119 us
    ppermute x7, waiting for transfers between devices, from_behind(): return lax.ppermute(block, axis, route)  67.9 us
    pallas_call x1, Pallas kernels, attention(): pl.pallas_call(functools.partial(attention_kernel, text_rows), grid=(slot...  33.7 us
    ppermute x7, starting transfers between devices, from_behind(): return lax.ppermute(block, axis, route)  12 us
    unnamed x24, local copies, waits for them, and re-layouts  11.6 us
    pallas_call x1, Pallas kernels, project_text(): pl.pallas_call(text_kernel, grid=(slots, heads), out_shape=jax.ShapeDtype...  10.1 us
  transfers between devices with their start and end apart: 7, of which 3 were waited for; matrix products, arithmetic and copies ran while one was open for 6% of the time, Pallas kernels for 62%

profile of v1, /device:TPU:0, one launch (start us, length us, event | category | flops | bytes accessed | tf_op | source)
XLA Modules:
  0.0 416.4 jit_solution(7107148383926087587)
XLA Ops:
  0.7 0.7 constant_dynamic-slice_fusion.4
  1.4 0.1 compare_reduce_fusion
  1.5 0.2 convert_reduce_fusion.1
  1.8 0.3 select_reduce_fusion.2
  2.1 0.2 select_reduce_fusion
  2.3 0.1 pad_add_fusion
  2.3 0.6 copy.79
  2.9 3.5 copy.84
  6.5 0.0 copy-start.2
  6.5 6.3 %copy.71.fresh_ref = bf16[2,512,2,1024]{3,2,1,0:T(2,128)(2,1)} copy(bf16[2,512,2,1024]{3,1,0,2:T(8,128)(2,1)S(1)} %bitcast.58) | data formatting | bytes 8388608 | tf_op jit(solution)/shard_map/squeeze | solution.py:243
  12.8 0.0 copy-done.2
  12.8 18.0 %pick_rows.4 = bf16[2,64,2,1024]{3,2,1,0:T(2,128)(2,1)} custom-call(s32[1024]{0:T(1024)} %bitcast.64, bf16[2,512,2,1024]{3,2,1,0:T(2,128)(2,1)} %copy.71.fresh_ref), custom_call_target="tpu_custom_call" | custom-call | bytes 1048576 | tf_op jit(solution)/shard_map/pick_rows/pallas_call | solution.py:65
  30.8 1.9 copy.68
  32.8 4.0 collective-permute-start
  36.8 1.9 slice.59
  38.7 0.0 collective-permute-start.3
  38.7 0.0 copy-done.3
  38.7 0.6 copy.85
  39.3 1.5 slice_bitcast_fusion.4
  40.8 10.1 %project_text.1.refs_7_ = bf16[2,8,384,128]{3,2,1,0:T(8,128)(2,1)} custom-call(bf16[2,256,1024]{2,1,0:T(8,128)(2,1)} %get-tuple-element.14.k_ref, bf16[2,256,1024]{2,1,0:T(8,128)(2,1)} %get-tuple-element.13.v_ref, bf16[64,1024]{1,0:T(8,128)(2,1)} %bitcast.56), custom_call_target="tpu_custom_call" | custom-call | flops 67108864 | bytes 4194304 | tf_op jit(solution)/shard_map/project_text/pallas_call | solution.py:128
  50.9 2.9 collective-permute-start.4
  53.8 0.1 fusion
  54.0 0.1 compare_reduce_fusion.1
  54.1 0.0 copy-done.6
  54.1 0.2 fusion.3
  54.3 0.1 and_bitcast_fusion.1
  54.4 0.1 and_bitcast_fusion
  54.5 0.7 copy.77
  55.2 1.4 broadcast_select_fusion.refs_10_
  56.6 4.6 %slice_bitcast_fusion.2 = (bf16[2,512,1024]{2,1,0:T(8,128)(2,1)}, bf16[2,512,1024]{2,1,0:T(8,128)(2,1)}) fusion(bf16[2,512,2,1024]{3,1,0,2:T(8,128)(2,1)} %bitcast.60), kind=kLoop, calls=%fused_computation.4 | loop fusion | bytes 8388608 | tf_op jit(solution)/shard_map/squeeze | solution.py:294
  61.2 5.5 %copy.83 = bf16[1,2,512,2,1024]{4,2,1,3,0:T(8,128)(2,1)} copy(bf16[1,2,512,2,1024]{4,3,2,1,0:T(2,128)(2,1)} %param.12) | data formatting | bytes 8388608 | tf_op args[2]
  66.7 0.0 copy-done.8
  66.7 0.1 dynamic_slice.29
  66.8 0.1 broadcast_compare_fusion
  66.9 0.1 compare_convert_fusion
  66.9 39.0 %collective-permute-done = bf16[2,64,2,1024]{3,1,0,2:T(8,128)(2,1)S(1)} collective-permute-done((bf16[2,64,2,1024]{3,1,0,2:T(8,128)(2,1)}, bf16[2,64,2,1024]{3,1,0,2:T(8,128)(2,1)S(1)}, u32[]{:S(2)}, u32[]{:S(2)}) %collective-permute-start) | collective-permute-done | bytes 524320 | tf_op jit(solution)/shard_map/ppermute | solution.py:20
  106.0 1.3 copy.70.rest_0_.rest_1_
  107.3 49.5 %pick_rows.5 = bf16[1,384,2,1024]{3,2,1,0:T(2,128)(2,1)} custom-call(s32[1024]{0:T(1024)} %bitcast.65, bf16[2,512,2,1024]{3,2,1,0:T(2,128)(2,1)} %copy.71.fresh_ref, bf16[2,64,2,1024]{3,2,1,0:T(2,128)(2,1)} %copy.70.rest_0_.rest_1_), custom_call_target="tpu_custom_call" | custom-call | bytes 3145728 | tf_op jit(solution)/shard_map/pick_rows/pallas_call | solution.py:65
  156.8 0.1 collective-permute-start.1
  156.9 4.6 %slice_bitcast_fusion = (bf16[2,512,1024]{2,1,0:T(8,128)(2,1)}, bf16[2,512,1024]{2,1,0:T(8,128)(2,1)}) fusion(bf16[2,512,2,1024]{3,1,0,2:T(8,128)(2,1)} %bitcast.62), kind=kLoop, calls=%fused_computation.2 | loop fusion | bytes 8388608 | tf_op jit(solution)/shard_map/squeeze | solution.py:296
  161.5 0.0 collective-permute-done.3
  161.6 0.1 slice_bitcast_fusion.6
  161.7 0.0 copy-start
  161.7 0.0 copy-start.1
  161.7 0.0 collective-permute-done.4.rest_0_.refs_8_
  161.7 33.8 %pick_rows.7 = bf16[1,256,2,1024]{3,2,1,0:T(2,128)(2,1)} custom-call(s32[1024]{0:T(1024)} %bitcast.66, bf16[2,512,2,1024]{3,2,1,0:T(2,128)(2,1)} %copy.71.fresh_ref, bf16[2,8,384,128]{3,2,1,0:T(8,128)(2,1)} %collective-permute-done.4.rest_0_.refs_8_), custom_call_target="tpu_custom_call" | custom-call | bytes 2097152 | tf_op jit(solution)/shard_map/pick_rows/pallas_call | solution.py:65
  195.5 3.0 collective-permute-start.5
  198.5 33.7 %attention.1 = f32[2,64,512]{2,1,0:T(8,128)S(1)} custom-call(bf16[2,512,1024]{2,1,0:T(8,128)(2,1)} %bitcast.72, bf16[2,512,1024]{2,1,0:T(8,128)(2,1)} %get-tuple-element.12.refs_1_, bf16[2,512,1024]{2,1,0:T(8,128)(2,1)} %get-tuple-element.11.refs_2_, bf16[2,512,1024]{2,1,0:T(8,128)(2,1)} %get-tuple-element.10.refs_3_, ...), custom_call_target="tpu_custom_call" | custom-call | flops 5234491392 | bytes 25165824 | tf_op jit(solution)/shard_map/attention/pallas_call | solution.py:207
  232.2 1.9 collective-permute-start.6
  234.1 0.1 multiply_reduce_fusion
  234.3 0.6 copy.78
  234.9 16.0 %collective-permute-done.1.rest_0_.rest_2_ = bf16[1,384,2,1024]{3,2,1,0:T(2,128)(2,1)} collective-permute-done((bf16[1,384,2,1024]{3,2,1,0:T(2,128)(2,1)}, bf16[1,384,2,1024]{3,2,1,0:T(2,128)(2,1)}, u32[]{:S(2)}, u32[]{:S(2)}) %collective-permute-start.1) | collective-permute-done | bytes 1572896 | tf_op jit(solution)/shard_map/ppermute | solution.py:20
  250.8 17.7 %pick_rows.6 = bf16[1,128,2,1024]{3,2,1,0:T(2,128)(2,1)} custom-call(s32[1024]{0:T(1024)} %bitcast.67, bf16[2,512,2,1024]{3,2,1,0:T(2,128)(2,1)} %copy.71.fresh_ref, bf16[1,384,2,1024]{3,2,1,0:T(2,128)(2,1)} %collective-permute-done.1.rest_0_.rest_2_), custom_call_target="tpu_custom_call" | custom-call | bytes 1048576 | tf_op jit(solution)/shard_map/pick_rows/pallas_call | solution.py:65
  268.6 0.1 collective-permute-start.2
  268.6 0.2 multiply_reduce_fusion.1
  268.8 1.3 copy.74.rest_0_
  270.2 0.0 collective-permute-done.6
  270.2 0.7 fusion.2
  270.9 0.7 fusion.1
  271.6 12.9 %collective-permute-done.5.rest_3_ = bf16[1,256,2,1024]{3,2,1,0:T(2,128)(2,1)} collective-permute-done((bf16[1,256,2,1024]{3,2,1,0:T(2,128)(2,1)}, bf16[1,256,2,1024]{3,2,1,0:T(2,128)(2,1)}, u32[]{:S(2)}, u32[]{:S(2)}) %collective-permute-start.5) | collective-permute-done | bytes 1048608 | tf_op jit(solution)/shard_map/ppermute | solution.py:20
  284.5 113.1 %place_rows.2.rest_1_ = bf16[2,512,2,1024]{3,2,1,0:T(2,128)(2,1)} custom-call(s32[1024]{0:T(1024)} %bitcast.68, bf16[2,64,2,1024]{3,2,1,0:T(2,128)(2,1)} %copy.74.rest_0_, bf16[2,64,2,1024]{3,2,1,0:T(2,128)(2,1)} %copy.70.rest_0_.rest_1_, bf16[1,384,2,1024]{3,2,1,0:T(2,128)(2,1)} %collective-permute-done.1.rest_0_.rest_2_, ...), custom_call_target="tpu_custom_call" | custom-call | bytes 7340032 | tf_op jit(solution)/shard_map/place_rows/pallas_call | solution.py:95
  397.7 0.0 collective-permute-done.2.rest_0_
  397.7 0.8 copy-done.4
  398.5 17.7 %place_rows.3 = bf16[2,512,2,1024]{3,2,1,0:T(2,128)(2,1)} custom-call(s32[1024]{0:T(1024)} %bitcast.69, bf16[1,128,2,1024]{3,2,1,0:T(2,128)(2,1)} %copy-done.4, bf16[2,512,2,1024]{3,2,1,0:T(2,128)(2,1)} %place_rows.2.rest_1_), custom_call_target="tpu_custom_call", output_to_operand_aliasing={{}: (2, {})} | custom-call | bytes 1048576 | tf_op jit(solution)/shard_map/place_rows/pallas_call | solution.py:95
  (28 shorter events, 0.2 us)
Async XLA Ops:
  6.5 6.3 %copy-start.2 = (bf16[1,2,512,2,1024]{4,2,1,3,0:T(8,128)(2,1)}, bf16[1,2,512,2,1024]{4,2,1,3,0:T(8,128)(2,1)S(1)}, u32[]{:S(2)}) copy-start(bf16[1,2,512,2,1024]{4,2,1,3,0:T(8,128)(2,1)S(1)} %copy.84) | copy-start | bytes 12582916
  12.8 25.9 %copy-start.3 = (bf16[1,2,256,2,1024]{4,3,2,1,0:T(2,128)(2,1)S(1)}, bf16[1,2,256,2,1024]{4,3,2,1,0:T(2,128)(2,1)}, u32[]{:S(2)}) copy-start(bf16[1,2,256,2,1024]{4,3,2,1,0:T(2,128)(2,1)} %param.13) | copy-start | bytes 6291460
  32.8 73.2 %collective-permute-start = (bf16[2,64,2,1024]{3,1,0,2:T(8,128)(2,1)}, bf16[2,64,2,1024]{3,1,0,2:T(8,128)(2,1)S(1)}, u32[]{:S(2)}, u32[]{:S(2)}) collective-permute-start(bf16[2,64,2,1024]{3,1,0,2:T(8,128)(2,1)} %copy.68), channel_id=1, source_target_pairs={{16,0},{18,2},{20,4},{22,6},{24,8},{26,10},{28,12},{30,14},{0,16},... | collective-permute-start | bytes 1572872 | tf_op jit(solution)/shard_map/ppermute | solution.py:20
  38.7 122.8 %collective-permute-start.3 = (bf16[2,64,2,1024]{3,1,0,2:T(8,128)(2,1)}, bf16[2,64,2,1024]{3,1,0,2:T(8,128)(2,1)S(1)}, u32[]{:S(2)}, u32[]{:S(2)}) collective-permute-start(bf16[2,64,2,1024]{3,1,0,2:T(8,128)(2,1)} %slice.59), channel_id=1, source_target_pairs={{16,0},{18,2},{20,4},{22,6},{24,8},{26,10},{28,12},{30,14},{0,16},... | collective-permute-start | bytes 1572872 | tf_op jit(solution)/shard_map/ppermute | solution.py:20
  40.8 13.2 %copy-start.6 = (s32[16,2]{0,1:T(2,128)S(1)}, s32[16,2]{0,1:T(2,128)}, u32[]{:S(2)}) copy-start(s32[16,2]{0,1:T(2,128)} %param.16) | copy-start | bytes 388
  50.9 110.8 %collective-permute-start.4 = (bf16[2,8,384,128]{3,2,1,0:T(8,128)(2,1)}, bf16[2,8,384,128]{3,2,1,0:T(8,128)(2,1)}, u32[]{:S(2)}, u32[]{:S(2)}) collective-permute-start(bf16[2,8,384,128]{3,2,1,0:T(8,128)(2,1)} %project_text.1.refs_7_), channel_id=1, source_target_pairs={{16,0},{18,2},{20,4},{22,6},{24,8},{26,10},{28,12},{30,14},{0,16},... | collective-permute-start | bytes 4718600 | tf_op jit(solution)/shard_map/ppermute | solution.py:20
  61.2 5.5 %copy-start.8 = (s32[16]{0:T(128)S(1)}, s32[16]{0:T(128)}, u32[]{:S(2)}) copy-start(s32[16]{0:T(128)} %param.18) | copy-start | bytes 196
  156.8 94.0 %collective-permute-start.1 = (bf16[1,384,2,1024]{3,2,1,0:T(2,128)(2,1)}, bf16[1,384,2,1024]{3,2,1,0:T(2,128)(2,1)}, u32[]{:S(2)}, u32[]{:S(2)}) collective-permute-start(bf16[1,384,2,1024]{3,2,1,0:T(2,128)(2,1)} %pick_rows.5), channel_id=1, source_target_pairs={{16,0},{18,2},{20,4},{22,6},{24,8},{26,10},{28,12},{30,14},{0,16},... | collective-permute-start | bytes 4718600 | tf_op jit(solution)/shard_map/ppermute | solution.py:20
  161.7 36.8 %copy-start = (bf16[2,8,384,128]{3,2,1,0:T(8,128)(2,1)S(1)}, bf16[2,8,384,128]{3,2,1,0:T(8,128)(2,1)}, u32[]{:S(2)}) copy-start(bf16[2,8,384,128]{3,2,1,0:T(8,128)(2,1)} %project_text.1.refs_7_) | copy-start | bytes 4718596
  161.7 36.8 %copy-start.1 = (bf16[1024,64]{0,1:T(8,128)(2,1)S(1)}, bf16[1024,64]{0,1:T(8,128)(2,1)}, u32[]{:S(2)}) copy-start(bf16[1024,64]{0,1:T(8,128)(2,1)} %param.14) | copy-start | bytes 393220
  195.5 89.0 %collective-permute-start.5 = (bf16[1,256,2,1024]{3,2,1,0:T(2,128)(2,1)}, bf16[1,256,2,1024]{3,2,1,0:T(2,128)(2,1)}, u32[]{:S(2)}, u32[]{:S(2)}) collective-permute-start(bf16[1,256,2,1024]{3,2,1,0:T(2,128)(2,1)} %pick_rows.7), channel_id=1, source_target_pairs={{16,0},{18,2},{20,4},{22,6},{24,8},{26,10},{28,12},{30,14},{0,16},... | collective-permute-start | bytes 3145736 | tf_op jit(solution)/shard_map/ppermute | solution.py:20
  198.5 35.6 %copy-start.7 = (s32[16,2]{0,1:T(2,128)S(1)}, s32[16,2]{0,1:T(2,128)}, u32[]{:S(2)}) copy-start(s32[16,2]{0,1:T(2,128)} %param.19) | copy-start | bytes 388
  232.2 38.0 %collective-permute-start.6 = (f32[2,64,256]{2,1,0:T(8,128)S(1)}, f32[2,64,256]{2,1,0:T(8,128)S(1)}, u32[]{:S(2)}, u32[]{:S(2)}) collective-permute-start(f32[2,64,256]{2,1,0:T(8,128)S(1)} %constant_dynamic-slice_fusion), channel_id=1, source_target_pairs={{1,0},{0,1},{3,2},{2,3},{5,4},{4,5},{7,6},{6,7},{9,8},{8,9},{11,10... | collective-permute-start | bytes 393224 | tf_op jit(solution)/shard_map/ppermute | solution.py:20
  234.9 36.0 %copy-start.5 = (f32[1,2,256,64]{2,3,1,0:T(8,128)S(1)}, f32[1,2,256,64]{2,3,1,0:T(8,128)}, u32[]{:S(2)}) copy-start(f32[1,2,256,64]{2,3,1,0:T(8,128)} %param.15) | copy-start | bytes 393220
  268.6 129.1 %collective-permute-start.2 = (bf16[1,128,2,1024]{3,2,1,0:T(2,128)(2,1)}, bf16[1,128,2,1024]{3,2,1,0:T(2,128)(2,1)S(1)}, u32[]{:S(2)}, u32[]{:S(2)}) collective-permute-start(bf16[1,128,2,1024]{3,2,1,0:T(2,128)(2,1)} %pick_rows.6), channel_id=1, source_target_pairs={{16,0},{18,2},{20,4},{22,6},{24,8},{26,10},{28,12},{30,14},{0,16},... | collective-permute-start | bytes 1572872 | tf_op jit(solution)/shard_map/ppermute | solution.py:20
  397.7 0.8 copy-start.4

commit v2 on v1

--- a/solution.py
+++ b/solution.py
@@ -11,7 +11,7 @@
 HD = 128
 HBM = pltpu.MemorySpace.HBM
 SMEM = pltpu.MemorySpace.SMEM
-VMEM_LIMIT = 50 * 1024 * 1024
+VMEM_LIMIT = 32 * 1024 * 1024
 
 
 def from_behind(block, axis, distance):
@@ -20,96 +20,157 @@
     return lax.ppermute(block, axis, route)
 
 
-def send_order(lists, img_rows):
+def swap_places(lists):
     count = lists.shape[2]
     zone = count + jnp.arange(count, dtype=jnp.int32)
     order = jnp.arange(count, dtype=jnp.int32)
     earlier = order[:, None] >= order[None, :]
     free = jnp.logical_not(jnp.any(lists[..., :, None] == zone, axis=2))
     outside = lists >= 2 * count
-    free_rank = jnp.sum(jnp.where(earlier, free[..., None, :], False).astype(jnp.int32), axis=3)
-    outside_rank = jnp.sum(jnp.where(earlier, outside[..., None, :], False).astype(jnp.int32), axis=3)
+    free_rank = jnp.sum((earlier & free[..., None, :]).astype(jnp.int32), axis=3)
+    outside_rank = jnp.sum((earlier & outside[..., None, :]).astype(jnp.int32), axis=3)
     match = (
         outside[..., :, None]
         & free[..., None, :]
         & (outside_rank[..., :, None] == free_rank[..., None, :])
     )
-    listed_at = jnp.sum(jnp.where(match, lists[..., :, None], 0), axis=2)
-    zone_source = jnp.where(listed_at > 0, listed_at, zone)
-    place = jnp.sum(jnp.where(match, zone, 0), axis=3)
-    tail = jnp.arange(2 * count, img_rows, dtype=jnp.int32)
-    moved = jnp.sum(
-        jnp.where(lists[..., :, None] == tail, place[..., :, None], 0), axis=2
-    )
-    tail_source = jnp.where(moved > 0, moved, tail)
-    head = jnp.broadcast_to(order, lists.shape)
-    return jnp.concatenate([head, zone_source, tail_source], axis=2)
-
-
-def pick_rows_kernel(slots, first, rows, total, order_ref, fresh_ref, *rest):
-    out_ref, sem = rest[-2], rest[-1]
-    for out_slot, slot in enumerate(slots):
-
-        def issue(i, carry):
-            source = order_ref[slot * total + first + i]
-            pltpu.make_async_copy(fresh_ref.at[slot, source], out_ref.at[out_slot, i], sem).start()
-            return carry
-
-        lax.fori_loop(0, rows, issue, 0, unroll=8)
-    pltpu.make_async_copy(out_ref, out_ref, sem).wait()
-
-
-def pick_rows(order, fresh, slots, first, rows, after=()):
-    total = fresh.shape[1]
-    size = len(slots) * rows * fresh.shape[2] * fresh.shape[3]
+    places = jnp.sum(jnp.where(match, zone, 0), axis=3)
+    sources = jnp.sum(jnp.where(match, lists[..., :, None], 0), axis=2)
+    return places, jnp.where(sources > 0, sources, zone)
+
+
+def swap_rows(list_ref, place_ref, slot, zone_ref, rest_ref):
+    count = zone_ref.shape[0]
+
+    def step(k, carry):
+        place = place_ref[slot * count + k]
+
+        @pl.when(place > 0)
+        def _():
+            near = place - count
+            far = list_ref[slot * count + k] - 2 * count
+            moved = zone_ref[near]
+            zone_ref[near] = rest_ref[far]
+            rest_ref[far] = moved
+
+        return carry
+
+    lax.fori_loop(0, count, step, 0)
+
+
+def arrange_kernel(slots, list_ref, place_ref, fresh_ref, *refs):
+    zone_out, rest_outs = refs[1], refs[2 : 2 + slots]
+    zones, rests, sems = refs[2 + slots :]
+    count = zones.shape[1]
+    copies_in = []
+    for slot in range(slots):
+        copies_in.append(
+            (
+                pltpu.make_async_copy(fresh_ref.at[slot, count : 2 * count], zones.at[slot], sems.at[slot, 0]),
+                pltpu.make_async_copy(fresh_ref.at[slot, 2 * count :], rests.at[slot], sems.at[slot, 1]),
+            )
+        )
+        for copy in copies_in[-1]:
+            copy.start()
+    copies_out = []
+    for slot in range(slots):
+        for copy in copies_in[slot]:
+            copy.wait()
+        swap_rows(list_ref, place_ref, slot, zones.at[slot], rests.at[slot])
+        copies_out.append(pltpu.make_async_copy(zones.at[slot], zone_out.at[slot], sems.at[slot, 2]))
+        copies_out[-1].start()
+        copies_out.append(pltpu.make_async_copy(rests.at[slot], rest_outs[slot], sems.at[slot, 3]))
+        copies_out[-1].start()
+    for copy in copies_out:
+        copy.wait()
+
+
+def arrange(lists, places, fresh, after):
+    slots, rows = fresh.shape[:2]
+    tail = fresh.shape[2:]
+    count = lists.shape[0] // slots
+    outs = pl.pallas_call(
+        functools.partial(arrange_kernel, slots),
+        out_shape=[jax.ShapeDtypeStruct((slots, count) + tail, fresh.dtype)]
+        + [jax.ShapeDtypeStruct((rows - 2 * count,) + tail, fresh.dtype)] * slots,
+        in_specs=[pl.BlockSpec(memory_space=SMEM)] * 2 + [pl.BlockSpec(memory_space=HBM)] * 2,
+        out_specs=[pl.BlockSpec(memory_space=HBM)] * (1 + slots),
+        scratch_shapes=[
+            pltpu.VMEM((slots, count) + tail, fresh.dtype),
+            pltpu.VMEM((slots, rows - 2 * count) + tail, fresh.dtype),
+            pltpu.SemaphoreType.DMA((slots, 4)),
+        ],
+        cost_estimate=pl.CostEstimate(flops=0, bytes_accessed=4 * fresh.size, transcendentals=0),
+        compiler_params=pltpu.CompilerParams(vmem_limit_bytes=VMEM_LIMIT),
+        name="arrange",
+    )(lists, places, fresh, after)
+    return outs[0], outs[1:]
+
+
+def restore_kernel(slot, heads, list_ref, place_ref, raw_ref, zone_ref, rest_ref, *refs):
+    out_ref, zone, rest, sems = refs[-4:]
+    count = zone.shape[0]
+    copies = [pltpu.make_async_copy(raw_ref.at[s], out_ref.at[s, :count], sems.at[4 + s]) for s in heads]
+    copy_zone = pltpu.make_async_copy(zone_ref.at[slot], zone, sems.at[0])
+    copy_rest = pltpu.make_async_copy(rest_ref, rest, sems.at[1])
+    copy_zone.start()
+    copy_rest.start()
+    for copy in copies:
+        copy.start()
+    copy_zone.wait()
+    copy_rest.wait()
+    swap_rows(list_ref, place_ref, slot, zone, rest)
+    copies.append(pltpu.make_async_copy(zone, out_ref.at[slot, count : 2 * count], sems.at[2]))
+    copies[-1].start()
+    copies.append(pltpu.make_async_copy(rest, out_ref.at[slot, 2 * count :], sems.at[3]))
+    copies[-1].start()
+    for copy in copies:
+        copy.wait()
+
+
+def restore(lists, places, raw, zone, rest, slot, shape, whole=None):
+    tail = shape[2:]
+    count = zone.shape[1]
+    extra = () if whole is None else (whole,)
+    heads = range(shape[0]) if whole is None else ()
     return pl.pallas_call(
-        functools.partial(pick_rows_kernel, slots, first, rows, total),
-        out_shape=jax.ShapeDtypeStruct((len(slots), rows) + fresh.shape[2:], fresh.dtype),
-        in_specs=[pl.BlockSpec(memory_space=SMEM)] + [pl.BlockSpec(memory_space=HBM)] * (1 + len(after)),
+        functools.partial(restore_kernel, slot, heads),
+        out_shape=jax.ShapeDtypeStruct(shape, rest.dtype),
+        in_specs=[pl.BlockSpec(memory_space=SMEM)] * 2 + [pl.BlockSpec(memory_space=HBM)] * (3 + len(extra)),
         out_specs=pl.BlockSpec(memory_space=HBM),
-        scratch_shapes=[pltpu.SemaphoreType.DMA],
-        cost_estimate=pl.CostEstimate(flops=0, bytes_accessed=4 * size, transcendentals=0),
-        name="pick_rows",
-    )(order, fresh, *after)
-
-
-def place_rows_kernel(pieces, total, order_ref, *rest):
-    refs, out_ref, sem = rest[: len(pieces)], rest[-2], rest[-1]
-    for (slots, first, rows), piece_ref in zip(pieces, refs):
-        for in_slot, slot in enumerate(slots):
-
-            def issue(i, carry):
-                target = order_ref[slot * total + first + i]
-                pltpu.make_async_copy(piece_ref.at[in_slot, i], out_ref.at[slot, target], sem).start()
-                return carry
-
-            lax.fori_loop(0, rows, issue, 0, unroll=8)
-    for piece_ref in refs:
-        pltpu.make_async_copy(piece_ref, piece_ref, sem).wait()
-
-
-def place_rows(order, parts, pieces, shape, whole=None):
-    total = shape[1]
-    size = sum(math.prod(part.shape) for part in parts)
-    extra = () if whole is None else (whole,)
+        scratch_shapes=[
+            pltpu.VMEM((count,) + tail, rest.dtype),
+            pltpu.VMEM(rest.shape, rest.dtype),
+            pltpu.SemaphoreType.DMA((4 + shape[0],)),
+        ],
+        input_output_aliases={} if whole is None else {5: 0},
+        cost_estimate=pl.CostEstimate(flops=0, bytes_accessed=4 * rest.size, transcendentals=0),
+        compiler_params=pltpu.CompilerParams(vmem_limit_bytes=VMEM_LIMIT),
+        name="restore",
+    )(lists, places, raw, zone, rest, *extra)
+
+
+def hold_kernel(block_ref, after_ref, out_ref):
+    del block_ref, after_ref, out_ref
+
+
+def hold(block, after):
     return pl.pallas_call(
-        functools.partial(place_rows_kernel, pieces, total),
-        out_shape=jax.ShapeDtypeStruct(shape, parts[0].dtype),
-        in_specs=[pl.BlockSpec(memory_space=SMEM)]
-        + [pl.BlockSpec(memory_space=HBM)] * (len(parts) + len(extra)),
+        hold_kernel,
+        out_shape=jax.ShapeDtypeStruct(block.shape, block.dtype),
+        in_specs=[pl.BlockSpec(memory_space=HBM)] * 2,
         out_specs=pl.BlockSpec(memory_space=HBM),
-        scratch_shapes=[pltpu.SemaphoreType.DMA],
-        input_output_aliases={} if whole is None else {1 + len(parts): 0},
-        cost_estimate=pl.CostEstimate(flops=0, bytes_accessed=4 * size, transcendentals=0),
-        name="place_rows",
-    )(order, *parts, *extra)
+        input_output_aliases={0: 0},
+        cost_estimate=pl.CostEstimate(flops=0, bytes_accessed=0, transcendentals=0),
+        name="hold",
+    )(block, after)
 
 
 def across(a, b):
     return lax.dot_general(a, b, (((1,), (1,)), ((), ())), preferred_element_type=jnp.float32)
 
 
-def text_kernel(k_ref, v_ref, w_ref, out_ref):
+def text_kernel(k_ref, v_ref, w_ref, after_ref, out_ref):
     rows = k_ref.shape[1]
     channels = w_ref.shape[0]
     out_ref[0, 0, :rows, :] = k_ref[0]
@@ -119,7 +180,7 @@
         out_ref[0, 0, start : start + channels, :] = projected[:, part * HD : (part + 1) * HD]
 
 
-def project_text(keys, values, w_t):
+def project_text(keys, values, w_t, after):
     slots, rows, width = keys.shape
     heads = width // HD
     channels = w_t.shape[0]
@@ -129,13 +190,13 @@
         text_kernel,
         grid=(slots, heads),
         out_shape=jax.ShapeDtypeStruct((slots, heads, packed, HD), keys.dtype),
-        in_specs=[block, block, pl.BlockSpec((channels, HD), lambda s, h: (0, h))],
+        in_specs=[block, block, pl.BlockSpec((channels, HD), lambda s, h: (0, h)), pl.BlockSpec(memory_space=HBM)],
         out_specs=pl.BlockSpec((1, 1, packed, HD), lambda s, h: (s, h, 0, 0)),
         cost_estimate=pl.CostEstimate(
             flops=2 * slots * rows * width * channels, bytes_accessed=4 * keys.size * 2, transcendentals=0
         ),
         name="project_text",
-    )(keys, values, w_t)
+    )(keys, values, w_t, after)
 
 
 def attention_kernel(text_rows, *refs):
@@ -243,38 +304,30 @@
     queries, fresh, stale, text = queries[0], fresh_kv[0], stale_kv[0], text_kv[0]
     slots, img_rows = queries.shape[:2]
     listed_count = refresh_rows.shape[2]
-    hot_rows = 2 * listed_count
-    last_rows = 128
-    split = img_rows - last_rows
-    both = tuple(range(slots))
 
     raw = fresh[:, :listed_count]
     raw_in = from_behind(raw, "grp", half_groups)
 
-    w_t = w_velocity.T
-    text_own = project_text(text[:, :, 0], text[:, :, 1], w_t)
-
     my_list = lax.dynamic_index_in_dim(refresh_rows, my_group, 0, keepdims=False)
     partner_list = lax.dynamic_index_in_dim(refresh_rows, partner, 0, keepdims=False)
-    orders = send_order(jnp.stack([my_list, partner_list]), img_rows)
-    my_order, partner_order = orders[0].reshape(-1), orders[1].reshape(-1)
-
-    zone = pick_rows(my_order, fresh, both, listed_count, listed_count)
+    places, sources = swap_places(jnp.stack([my_list, partner_list]))
+    mine = (my_list.reshape(-1), places[0].reshape(-1))
+    partners = (partner_list.reshape(-1), places[1].reshape(-1))
+
+    zone, rests = arrange(*mine, fresh, raw)
     zone_in = from_behind(zone, "grp", half_groups)
+    w_t = w_velocity.T
+    text_own = project_text(text[:, :, 0], text[:, :, 1], w_t, raw)
     text_in = from_behind(text_own, "grp", half_groups)
-    pieces = [(both[:-1], hot_rows, img_rows - hot_rows), (both[-1:], hot_rows, split - hot_rows)]
-    early = pick_rows(my_order, fresh, *pieces[0], after=(zone_in,))
-    early_in = from_behind(early, "grp", half_groups)
-    late = pick_rows(my_order, fresh, *pieces[1], after=(text_in,))
-    late_in = from_behind(late, "grp", half_groups)
-    last_piece = (both[-1:], split, last_rows)
-    last = pick_rows(my_order, fresh, *last_piece, after=(early_in,))
-    last_in = from_behind(last, "grp", half_groups)
+    gates = [raw_in] * (slots - 1) + [text_in]
+    rests_in = [from_behind(hold(rest, gate), "grp", half_groups) for rest, gate in zip(rests, gates)]
 
     my_live = lax.dynamic_index_in_dim(live_counts, my_group, 0, keepdims=False)
     partner_live = lax.dynamic_index_in_dim(live_counts, partner, 0, keepdims=False)
     row_ids = jnp.arange(img_rows, dtype=jnp.int32)
-    hot_source = orders[1][:, :hot_rows]
+    hot_source = jnp.concatenate(
+        [jnp.broadcast_to(row_ids[:listed_count], partner_list.shape), sources[1]], axis=1
+    )
     stale_listed = jnp.any(partner_list[:, :, None] == row_ids, axis=1)
     hot_listed = jnp.any(partner_list[:, :, None] == hot_source[:, None, :], axis=1)
     live = jnp.concatenate(
@@ -324,13 +377,9 @@
     step_size = (times[:, 1] - times[:, 0]).astype(jnp.float32) / 1000.0
     latent_next = latent[0] + step_size[:, None, None] * velocity
 
-    next_stale = place_rows(
-        partner_order,
-        (raw_in, zone_in, early_in, late_in),
-        [(both, 0, listed_count), (both, listed_count, listed_count)] + pieces,
-        fresh.shape,
-    )
-    next_stale = place_rows(partner_order, (last_in,), [last_piece], fresh.shape, whole=next_stale)
+    next_stale = None
+    for slot in range(slots):
+        next_stale = restore(*partners, raw_in, zone_in, rests_in[slot], slot, fresh.shape, whole=next_stale)
     return (next_stale[None], velocity[None], latent_next[None])
 
 

time: 417 us -> 264 us (0.63)
  Pallas kernels: 294 us -> 57.4 us
  waiting for transfers between devices: 67.9 us -> 142 us
  local copies, waits for them, and re-layouts: 37.1 us -> 48.5 us
    pallas_call x6 -> x5, Pallas kernels: 250 us -> 11.8 us  [the longest x2 8.5 us: restore(): pl.pallas_call(functools.partial(restore_kernel, slot, heads), out_shape=...]
    ppermute x7 -> x6, waiting for transfers between devices: 67.9 us -> 142 us  [from_behind(): return lax.ppermute(block, axis, route)]
    unnamed x24 -> x46, local copies, waits for them, and re-layouts: 11.6 us -> 20.9 us
    ppermute x7 -> x6, starting transfers between devices: 12 us -> 8.89 us  [from_behind(): return lax.ppermute(block, axis, route)]
  transfers between devices with their start and end apart: 7 -> 6, of which waited for: 3 -> 5; matrix products, arithmetic and copies ran while one was open for 6% -> 14% of each run, Pallas kernels for 62% -> 20%
where the time goes in v2:
time: 264 us; the launch traced here: 263 us
  waiting for transfers between devices  142 us (54%)
  Pallas kernels  57.4 us (22%)
  local copies, waits for them, and re-layouts  48.5 us (18%)
  starting transfers between devices  8.89 us (3%)
  other arithmetic  4.38 us (2%)
    ppermute x6, waiting for transfers between devices, from_behind(): return lax.ppermute(block, axis, route)  142 us
    pallas_call x1, Pallas kernels, attention(): pl.pallas_call(functools.partial(attention_kernel, text_rows), grid=(slot...  35.5 us
    unnamed x46, local copies, waits for them, and re-layouts  20.9 us
    pallas_call x1, Pallas kernels, project_text(): pl.pallas_call(text_kernel, grid=(slots, heads), out_shape=jax.ShapeDtype...  10.1 us
    ppermute x6, starting transfers between devices, from_behind(): return lax.ppermute(block, axis, route)  8.89 us
    pallas_call x2, Pallas kernels, restore(): pl.pallas_call(functools.partial(restore_kernel, slot, heads), out_shape=...  8.5 us
    squeeze x1, local copies, waits for them, and re-layouts, shards(): fresh_kv[0]  8.43 us
  transfers between devices with their start and end apart: 6, of which 5 were waited for; matrix products, arithmetic and copies ran while one was open for 14% of the time, Pallas kernels for 20%

profile of v2, /device:TPU:0, one launch (start us, length us, event | category | flops | bytes accessed | tf_op | source)
XLA Modules:
  0.0 262.6 jit_solution(16093027088062777837)
XLA Ops:
  0.6 3.5 %copy.89 = bf16[1,2,512,2,1024]{4,2,1,3,0:T(8,128)(2,1)S(1)} copy(bf16[1,2,512,2,1024]{4,3,2,1,0:T(2,128)(2,1)} %param.11) | data formatting | bytes 8388608 | tf_op args[1]
  4.1 0.0 copy-start.12
  4.2 2.0 copy-done.12
  6.2 4.1 %collective-permute-start = (bf16[2,64,2,1024]{3,1,0,2:T(8,128)(2,1)S(1)}, bf16[2,64,2,1024]{3,1,0,2:T(8,128)(2,1)S(1)}, u32[]{:S(2)}, u32[]{:S(2)}) collective-permute-start(bf16[2,64,2,1024]{3,1,0,2:T(8,128)(2,1)S(1)} %slice.61), channel_id=1, source_target_pairs={{16,0},{18,2},{20,4},{22,6},{24,8},{26,10},{28,12},{30,14},{0,16},... | collective-permute-start | bytes 1572872 | tf_op jit(solution)/shard_map/ppermute | solution.py:20
  10.3 0.7 constant_dynamic-slice_fusion.3
  11.0 0.1 reshape.312.list_ref
  11.1 8.4 %copy.73.fresh_ref = bf16[2,512,2,1024]{3,2,1,0:T(2,128)(2,1)} copy(bf16[2,512,2,1024]{3,1,0,2:T(8,128)(2,1)} %bitcast.54) | data formatting | bytes 8388608 | tf_op jit(solution)/shard_map/squeeze | solution.py:304
  19.6 0.5 copy.74.refs_0_.after_ref
  20.1 0.1 compare_reduce_fusion
  20.2 0.2 convert_reduce_fusion.1
  20.5 0.3 select_reduce_fusion
  20.8 0.1 reshape_squeeze.7.place_ref
  20.9 2.2 copy-done
  23.1 3.3 %arrange.1 = (bf16[2,64,2,1024]{3,2,1,0:T(2,128)(2,1)S(1)}, bf16[384,2,1024]{2,1,0:T(2,128)(2,1)S(1)}, bf16[384,2,1024]{2,1,0:T(2,128)(2,1)S(1)}) custom-call(s32[128]{0:T(128)S(1)} %reshape.312.list_ref, s32[128]{0:T(128)S(1)} %reshape_squeeze.7.place_ref, bf16[2,512,2,1024]{3,2,1,0:T(2,128)(2,1)S(1)} %copy-done, ...), custom_call_target="tpu_custom_call" | custom-call | bytes 8388608 | tf_op jit(solution)/shard_map/arrange/pallas_call | solution.py:92
  26.4 1.1 copy.75
  27.5 0.0 collective-permute-start.1
  27.5 0.6 copy.90
  28.1 0.1 copy-done.9
  28.2 1.5 slice_bitcast_fusion.4
  29.7 10.1 %project_text.1.refs_7_ = bf16[2,8,384,128]{3,2,1,0:T(8,128)(2,1)} custom-call(bf16[2,256,1024]{2,1,0:T(8,128)(2,1)} %get-tuple-element.20.k_ref, bf16[2,256,1024]{2,1,0:T(8,128)(2,1)} %get-tuple-element.19.v_ref, bf16[64,1024]{1,0:T(8,128)(2,1)} %bitcast.50, bf16[2,64,2,1024]{3,2,1,0:T(2,128)(2,1)} %copy-done.2), custom_call_target="tpu_custom_call" | custom-call | flops 67108864 | bytes 4194304 | tf_op jit(solution)/shard_map/project_text/pallas_call | solution.py:189
  39.8 2.9 %collective-permute-start.2 = (bf16[2,8,384,128]{3,2,1,0:T(8,128)(2,1)}, bf16[2,8,384,128]{3,2,1,0:T(8,128)(2,1)}, u32[]{:S(2)}, u32[]{:S(2)}) collective-permute-start(bf16[2,8,384,128]{3,2,1,0:T(8,128)(2,1)} %project_text.1.refs_7_), channel_id=1, source_target_pairs={{16,0},{18,2},{20,4},{22,6},{24,8},{26,10},{28,12},{30,14},{0,16},... | collective-permute-start | bytes 4718600 | tf_op jit(solution)/shard_map/ppermute | solution.py:20
  42.7 0.1 fusion
  42.8 0.1 pad_add_fusion.1
  42.9 0.1 compare_reduce_fusion.1
  43.0 0.2 fusion.3
  43.2 0.1 and_bitcast_fusion.1
  43.3 0.1 and_bitcast_fusion
  43.4 1.3 copy.84
  44.7 0.1 broadcast_compare_fusion
  44.8 0.1 dynamic_slice.29
  44.9 4.4 %slice_bitcast_fusion.2 = (bf16[2,512,1024]{2,1,0:T(8,128)(2,1)S(1)}, bf16[2,512,1024]{2,1,0:T(8,128)(2,1)}) fusion(bf16[2,512,2,1024]{3,1,0,2:T(8,128)(2,1)} %bitcast.55), kind=kLoop, calls=%fused_computation.4 | loop fusion | bytes 8388608 | tf_op jit(solution)/shard_map/squeeze | solution.py:347
  49.3 1.4 broadcast_select_fusion.refs_10_
  50.6 0.1 compare_convert_fusion
  50.7 3.3 %copy.88 = bf16[1,2,512,2,1024]{4,2,1,3,0:T(8,128)(2,1)} copy(bf16[1,2,512,2,1024]{4,3,2,1,0:T(2,128)(2,1)S(1)} %copy-done.13) | data formatting | bytes 8388608 | tf_op args[2]
  54.0 4.7 %slice_bitcast_fusion = (bf16[2,512,1024]{2,1,0:T(8,128)(2,1)}, bf16[2,512,1024]{2,1,0:T(8,128)(2,1)}) fusion(bf16[2,512,2,1024]{3,1,0,2:T(8,128)(2,1)} %bitcast.56), kind=kLoop, calls=%fused_computation.2 | loop fusion | bytes 8388608 | tf_op jit(solution)/shard_map/squeeze | solution.py:349
  58.7 20.5 %collective-permute-done = bf16[2,64,2,1024]{3,1,0,2:T(8,128)(2,1)S(1)} collective-permute-done((bf16[2,64,2,1024]{3,1,0,2:T(8,128)(2,1)S(1)}, bf16[2,64,2,1024]{3,1,0,2:T(8,128)(2,1)S(1)}, u32[]{:S(2)}, u32[]{:S(2)}) %collective-permute-start) | collective-permute-done | bytes 524320 | tf_op jit(solution)/shard_map/ppermute | solution.py:20
  79.2 1.3 copy.81.after_ref.raw_ref
  80.6 0.0 collective-permute-start.4
  80.6 1.1 constant_dynamic-update-slice_fusion.1
  81.6 76.3 %collective-permute-done.2.after_ref.refs_8_ = bf16[2,8,384,128]{3,2,1,0:T(8,128)(2,1)} collective-permute-done((bf16[2,8,384,128]{3,2,1,0:T(8,128)(2,1)}, bf16[2,8,384,128]{3,2,1,0:T(8,128)(2,1)}, u32[]{:S(2)}, u32[]{:S(2)}) %collective-permute-start.2) | collective-permute-done | bytes 1572896 | tf_op jit(solution)/shard_map/ppermute | solution.py:20
  158.0 0.0 collective-permute-start.3
  158.0 1.2 constant_dynamic-update-slice_fusion
  159.2 0.1 slice_bitcast_fusion.6
  159.3 0.4 copy-done.3
  159.7 1.6 copy-done.4
  161.3 1.6 copy-done.5
  162.9 1.5 copy-done.6
  164.4 1.4 copy-done.8
  165.8 1.6 copy-done.11
  167.4 35.5 %attention.1 = f32[2,64,512]{2,1,0:T(8,128)S(1)} custom-call(bf16[2,512,1024]{2,1,0:T(8,128)(2,1)S(1)} %bitcast.52, bf16[2,512,1024]{2,1,0:T(8,128)(2,1)S(1)} %copy-done.3, bf16[2,512,1024]{2,1,0:T(8,128)(2,1)S(1)} %get-tuple-element.17.refs_2_, bf16[2,512,1024]{2,1,0:T(8,128)(2,1)S(1)} %copy-done.5, bf16[2,512,1024]{2,1,0:T(8,128)(2,1)S(1)} %copy-done.4, ...), custom_call_target="tpu_custom_call" | custom-call | flops 5234491392 | bytes 25165824 | tf_op jit(solution)/shard_map/attention/pallas_call | solution.py:268
  202.9 0.0 copy-start.1
  202.9 1.9 collective-permute-start.5
  204.8 0.1 multiply_reduce_fusion
  204.9 0.1 reshape.311.list_ref
  205.0 0.1 reshape_squeeze.6.place_ref
  205.1 0.2 multiply_reduce_fusion.1
  205.3 1.6 copy.82.zone_ref
  206.9 1.0 collective-permute-done.5
  207.9 0.7 fusion.2
  208.6 0.7 fusion.1
  209.4 16.0 %collective-permute-done.4.rest_ref = bf16[384,2,1024]{2,1,0:T(2,128)(2,1)} collective-permute-done((bf16[384,2,1024]{2,1,0:T(2,128)(2,1)}, bf16[384,2,1024]{2,1,0:T(2,128)(2,1)}, u32[]{:S(2)}, u32[]{:S(2)}) %collective-permute-start.4) | collective-permute-done | bytes 1572896 | tf_op jit(solution)/shard_map/ppermute | solution.py:20
  225.4 4.3 %restore.2.refs_0_ = bf16[2,512,2,1024]{3,2,1,0:T(2,128)(2,1)} custom-call(s32[128]{0:T(128)S(1)} %reshape.311.list_ref, s32[128]{0:T(128)S(1)} %reshape_squeeze.6.place_ref, bf16[2,64,2,1024]{3,2,1,0:T(2,128)(2,1)S(1)} %copy-done.1, bf16[2,64,2,1024]{3,2,1,0:T(2,128)(2,1)S(1)} %copy.82.zone_ref, bf16[384,2,1024]{2,1,0:T(2,128)(2,1)} %collective-permute-done.4.rest_ref), custom_call_target="tpu_custom_call" | custom-call | bytes 3145728 | tf_op jit(solution)/shard_map/restore/pallas_call | solution.py:136
  229.7 28.5 %collective-permute-done.3.rest_ref = bf16[384,2,1024]{2,1,0:T(2,128)(2,1)} collective-permute-done((bf16[384,2,1024]{2,1,0:T(2,128)(2,1)}, bf16[384,2,1024]{2,1,0:T(2,128)(2,1)}, u32[]{:S(2)}, u32[]{:S(2)}) %collective-permute-start.3) | collective-permute-done | bytes 1572896 | tf_op jit(solution)/shard_map/ppermute | solution.py:20
  258.3 4.2 %restore.3 = bf16[2,512,2,1024]{3,2,1,0:T(2,128)(2,1)} custom-call(s32[128]{0:T(128)S(1)} %reshape.311.list_ref, s32[128]{0:T(128)S(1)} %reshape_squeeze.6.place_ref, bf16[2,64,2,1024]{3,2,1,0:T(2,128)(2,1)S(1)} %copy-done.1, bf16[2,64,2,1024]{3,2,1,0:T(2,128)(2,1)S(1)} %copy.82.zone_ref, ...), custom_call_target="tpu_custom_call", output_to_operand_aliasing={{}: (5, {})} | custom-call | bytes 3145728 | tf_op jit(solution)/shard_map/restore/pallas_call | solution.py:136
  (50 shorter events, 0.2 us)
Async XLA Ops:
  4.1 2.0 copy-start.12
  6.2 73.0 %collective-permute-start = (bf16[2,64,2,1024]{3,1,0,2:T(8,128)(2,1)S(1)}, bf16[2,64,2,1024]{3,1,0,2:T(8,128)(2,1)S(1)}, u32[]{:S(2)}, u32[]{:S(2)}) collective-permute-start(bf16[2,64,2,1024]{3,1,0,2:T(8,128)(2,1)S(1)} %slice.61), channel_id=1, source_target_pairs={{16,0},{18,2},{20,4},{22,6},{24,8},{26,10},{28,12},{30,14},{0,16},... | collective-permute-start | bytes 1572872 | tf_op jit(solution)/shard_map/ppermute | solution.py:20
  20.1 6.3 %copy-start.2 = (bf16[2,64,2,1024]{3,2,1,0:T(2,128)(2,1)}, bf16[2,64,2,1024]{3,2,1,0:T(2,128)(2,1)S(1)}, u32[]{:S(2)}) copy-start(bf16[2,64,2,1024]{3,2,1,0:T(2,128)(2,1)S(1)} %copy.74.refs_0_.after_ref) | copy-start | bytes 1572868
  20.9 2.2 copy-start
  23.1 4.4 %copy-start.14 = (bf16[1,2,256,2,1024]{4,3,2,1,0:T(2,128)(2,1)S(1)}, bf16[1,2,256,2,1024]{4,3,2,1,0:T(2,128)(2,1)}, u32[]{:S(2)}) copy-start(bf16[1,2,256,2,1024]{4,3,2,1,0:T(2,128)(2,1)} %param.13) | copy-start | bytes 6291460
  26.4 1.8 copy-start.7
  26.4 1.8 copy-start.9
  27.5 130.5 %collective-permute-start.1 = (bf16[2,64,2,1024]{3,1,0,2:T(8,128)(2,1)}, bf16[2,64,2,1024]{3,1,0,2:T(8,128)(2,1)}, u32[]{:S(2)}, u32[]{:S(2)}) collective-permute-start(bf16[2,64,2,1024]{3,1,0,2:T(8,128)(2,1)} %copy.75), channel_id=1, source_target_pairs={{16,0},{18,2},{20,4},{22,6},{24,8},{26,10},{28,12},{30,14},{0,16},... | collective-permute-start | bytes 1572872 | tf_op jit(solution)/shard_map/ppermute | solution.py:20
  29.7 13.3 %copy-start.18 = (s32[16,2]{0,1:T(2,128)S(1)}, s32[16,2]{0,1:T(2,128)}, u32[]{:S(2)}) copy-start(s32[16,2]{0,1:T(2,128)} %param.16) | copy-start | bytes 388
  29.7 15.1 %copy-start.20 = (s32[16]{0:T(128)S(1)}, s32[16]{0:T(128)}, u32[]{:S(2)}) copy-start(s32[16]{0:T(128)} %param.18) | copy-start | bytes 196
  39.8 118.2 %collective-permute-start.2 = (bf16[2,8,384,128]{3,2,1,0:T(8,128)(2,1)}, bf16[2,8,384,128]{3,2,1,0:T(8,128)(2,1)}, u32[]{:S(2)}, u32[]{:S(2)}) collective-permute-start(bf16[2,8,384,128]{3,2,1,0:T(8,128)(2,1)} %project_text.1.refs_7_), channel_id=1, source_target_pairs={{16,0},{18,2},{20,4},{22,6},{24,8},{26,10},{28,12},{30,14},{0,16},... | collective-permute-start | bytes 4718600 | tf_op jit(solution)/shard_map/ppermute | solution.py:20
  44.9 4.4 %copy-start.16 = (pred[2,1664,1]{2,1,0:T(8,128)(4,1)S(1)}, pred[2,1664,1]{2,1,0:T(8,128)(4,1)}, u32[]{:S(2)}) copy-start(pred[2,1664,1]{2,1,0:T(8,128)(4,1)} %copy.84) | copy-start | bytes 9988
  44.9 5.8 %copy-start.13 = (bf16[1,2,512,2,1024]{4,3,2,1,0:T(2,128)(2,1)S(1)}, bf16[1,2,512,2,1024]{4,3,2,1,0:T(2,128)(2,1)}, u32[]{:S(2)}) copy-start(bf16[1,2,512,2,1024]{4,3,2,1,0:T(2,128)(2,1)} %param.12) | copy-start | bytes 12582916
  79.2 1.3 copy-start.15
  80.6 144.8 %collective-permute-start.4 = (bf16[384,2,1024]{2,1,0:T(2,128)(2,1)}, bf16[384,2,1024]{2,1,0:T(2,128)(2,1)}, u32[]{:S(2)}, u32[]{:S(2)}) collective-permute-start(bf16[384,2,1024]{2,1,0:T(2,128)(2,1)} %hold.3), channel_id=1, source_target_pairs={{16,0},{18,2},{20,4},{22,6},{24,8},{26,10},{28,12},{30,14},{0,16},... | collective-permute-start | bytes 4718600 | tf_op jit(solution)/shard_map/ppermute | solution.py:20
  158.0 1.7 copy-start.3
  158.0 1.7 copy-start.10
  158.0 100.3 %collective-permute-start.3 = (bf16[384,2,1024]{2,1,0:T(2,128)(2,1)}, bf16[384,2,1024]{2,1,0:T(2,128)(2,1)}, u32[]{:S(2)}, u32[]{:S(2)}) collective-permute-start(bf16[384,2,1024]{2,1,0:T(2,128)(2,1)} %hold.2), channel_id=1, source_target_pairs={{16,0},{18,2},{20,4},{22,6},{24,8},{26,10},{28,12},{30,14},{0,16},... | collective-permute-start | bytes 4718600 | tf_op jit(solution)/shard_map/ppermute | solution.py:20
  159.7 1.6 copy-start.4
  161.3 1.6 copy-start.5
  162.9 1.5 copy-start.6
  164.4 1.4 copy-start.8
  165.8 1.6 copy-start.11
  167.4 37.4 %copy-start.19 = (s32[16,2]{0,1:T(2,128)S(1)}, s32[16,2]{0,1:T(2,128)}, u32[]{:S(2)}) copy-start(s32[16,2]{0,1:T(2,128)} %param.19) | copy-start | bytes 388
  167.4 41.2 %copy-start.17 = (f32[1,2,256,64]{2,3,1,0:T(8,128)S(1)}, f32[1,2,256,64]{2,3,1,0:T(8,128)}, u32[]{:S(2)}) copy-start(f32[1,2,256,64]{2,3,1,0:T(8,128)} %param.15) | copy-start | bytes 393220
  202.9 22.5 %copy-start.1 = (bf16[2,64,2,1024]{3,2,1,0:T(2,128)(2,1)S(1)}, bf16[2,64,2,1024]{3,2,1,0:T(2,128)(2,1)}, u32[]{:S(2)}) copy-start(bf16[2,64,2,1024]{3,2,1,0:T(2,128)(2,1)} %copy.81.after_ref.raw_ref) | copy-start | bytes 1572868
  202.9 5.0 %collective-permute-start.5 = (f32[2,64,256]{2,1,0:T(8,128)S(1)}, f32[2,64,256]{2,1,0:T(8,128)S(1)}, u32[]{:S(2)}, u32[]{:S(2)}) collective-permute-start(f32[2,64,256]{2,1,0:T(8,128)S(1)} %constant_dynamic-slice_fusion), channel_id=1, source_target_pairs={{1,0},{0,1},{3,2},{2,3},{5,4},{4,5},{7,6},{6,7},{9,8},{8,9},{11,10... | collective-permute-start | bytes 393224 | tf_op jit(solution)/shard_map/ppermute | solution.py:20

commit v3 on v2

--- a/solution.py
+++ b/solution.py
@@ -12,6 +12,7 @@
 HBM = pltpu.MemorySpace.HBM
 SMEM = pltpu.MemorySpace.SMEM
 VMEM_LIMIT = 32 * 1024 * 1024
+WIDE_LIMIT = 60 * 1024 * 1024
 
 
 def from_behind(block, axis, distance):
@@ -20,7 +21,7 @@
     return lax.ppermute(block, axis, route)
 
 
-def swap_places(lists):
+def swap_pairs(lists):
     count = lists.shape[2]
     zone = count + jnp.arange(count, dtype=jnp.int32)
     order = jnp.arange(count, dtype=jnp.int32)
@@ -34,40 +35,62 @@
         & free[..., None, :]
         & (outside_rank[..., :, None] == free_rank[..., None, :])
     )
-    places = jnp.sum(jnp.where(match, zone, 0), axis=3)
+    near = jnp.sum(jnp.where(match, order, 0), axis=3)
     sources = jnp.sum(jnp.where(match, lists[..., :, None], 0), axis=2)
-    return places, jnp.where(sources > 0, sources, zone)
-
-
-def swap_rows(list_ref, place_ref, slot, zone_ref, rest_ref):
-    count = zone_ref.shape[0]
+    return near, jnp.where(outside, lists, -1), jnp.where(sources > 0, sources, zone)
+
+
+def swap_rows(near_ref, far_ref, slot, zone, piece, start, stop):
+    count = zone.shape[0] - 1
 
     def step(k, carry):
-        place = place_ref[slot * count + k]
-
-        @pl.when(place > 0)
-        def _():
-            near = place - count
-            far = list_ref[slot * count + k] - 2 * count
-            moved = zone_ref[near]
-            zone_ref[near] = rest_ref[far]
-            rest_ref[far] = moved
-
+        far = far_ref[slot * count + k]
+        here = jnp.logical_and(far >= start, far < stop)
+        near_row = jnp.where(here, near_ref[slot * count + k], count)
+        far_row = jnp.where(here, far - start, stop - start)
+        moved = zone[near_row]
+        zone[near_row] = piece[far_row]
+        piece[far_row] = moved
         return carry
 
-    lax.fori_loop(0, count, step, 0)
-
-
-def arrange_kernel(slots, list_ref, place_ref, fresh_ref, *refs):
-    zone_out, rest_outs = refs[1], refs[2 : 2 + slots]
-    zones, rests, sems = refs[2 + slots :]
-    count = zones.shape[1]
+    lax.fori_loop(0, count, step, 0, unroll=8)
+
+
+def take_kernel(fresh_ref, out_ref, sem):
+    copy = pltpu.make_async_copy(fresh_ref.at[0, :, : out_ref.shape[1]], out_ref, sem)
+    copy.start()
+    copy.wait()
+
+
+def take_head(fresh_kv, rows):
+    shape = (fresh_kv.shape[1], rows) + fresh_kv.shape[3:]
+    return pl.pallas_call(
+        take_kernel,
+        out_shape=jax.ShapeDtypeStruct(shape, fresh_kv.dtype),
+        in_specs=[pl.BlockSpec(memory_space=HBM)],
+        out_specs=pl.BlockSpec(memory_space=HBM),
+        scratch_shapes=[pltpu.SemaphoreType.DMA],
+        cost_estimate=pl.CostEstimate(flops=0, bytes_accessed=4 * math.prod(shape), transcendentals=0),
+        compiler_params=pltpu.CompilerParams(vmem_limit_bytes=WIDE_LIMIT),
+        name="take_head",
+    )(fresh_kv)
+
+
+def arrange_kernel(slots, pieces, near_ref, far_ref, fresh_ref, after_ref, *refs):
+    zone_out, piece_outs = refs[0], refs[1 : 1 + len(pieces)]
+    zones, rests, sems = refs[1 + len(pieces) :]
+    count = zones.shape[1] - 1
+    rest_rows = rests.shape[1] - 1
     copies_in = []
     for slot in range(slots):
         copies_in.append(
             (
-                pltpu.make_async_copy(fresh_ref.at[slot, count : 2 * count], zones.at[slot], sems.at[slot, 0]),
-                pltpu.make_async_copy(fresh_ref.at[slot, 2 * count :], rests.at[slot], sems.at[slot, 1]),
+                pltpu.make_async_copy(
+                    fresh_ref.at[0, slot, count : 2 * count], zones.at[slot, :count], sems.at[slot]
+                ),
+                pltpu.make_async_copy(
+                    fresh_ref.at[0, slot, 2 * count :], rests.at[slot, :rest_rows], sems.at[slots + slot]
+                ),
             )
         )
         for copy in copies_in[-1]:
@@ -76,78 +99,111 @@
     for slot in range(slots):
         for copy in copies_in[slot]:
             copy.wait()
-        swap_rows(list_ref, place_ref, slot, zones.at[slot], rests.at[slot])
-        copies_out.append(pltpu.make_async_copy(zones.at[slot], zone_out.at[slot], sems.at[slot, 2]))
+        swap_rows(
+            near_ref, far_ref, slot, zones.at[slot], rests.at[slot], 2 * count, 2 * count + rest_rows
+        )
+        copies_out.append(
+            pltpu.make_async_copy(zones.at[slot, :count], zone_out.at[slot], sems.at[2 * slots + slot])
+        )
         copies_out[-1].start()
-        copies_out.append(pltpu.make_async_copy(rests.at[slot], rest_outs[slot], sems.at[slot, 3]))
-        copies_out[-1].start()
+        for index, (piece_slot, start, stop) in enumerate(pieces):
+            if piece_slot == slot:
+                source = rests.at[slot, start - 2 * count : stop - 2 * count]
+                copies_out.append(
+                    pltpu.make_async_copy(source, piece_outs[index], sems.at[3 * slots + index])
+                )
+                copies_out[-1].start()
     for copy in copies_out:
         copy.wait()
 
 
-def arrange(lists, places, fresh, after):
-    slots, rows = fresh.shape[:2]
-    tail = fresh.shape[2:]
-    count = lists.shape[0] // slots
+def arrange(near, far, fresh_kv, pieces, after):
+    slots, rows = fresh_kv.shape[1:3]
+    tail = fresh_kv.shape[3:]
+    count = near.shape[0] // slots
     outs = pl.pallas_call(
-        functools.partial(arrange_kernel, slots),
-        out_shape=[jax.ShapeDtypeStruct((slots, count) + tail, fresh.dtype)]
-        + [jax.ShapeDtypeStruct((rows - 2 * count,) + tail, fresh.dtype)] * slots,
+        functools.partial(arrange_kernel, slots, pieces),
+        out_shape=[jax.ShapeDtypeStruct((slots, count) + tail, fresh_kv.dtype)]
+        + [jax.ShapeDtypeStruct((stop - start,) + tail, fresh_kv.dtype) for _, start, stop in pieces],
         in_specs=[pl.BlockSpec(memory_space=SMEM)] * 2 + [pl.BlockSpec(memory_space=HBM)] * 2,
-        out_specs=[pl.BlockSpec(memory_space=HBM)] * (1 + slots),
+        out_specs=[pl.BlockSpec(memory_space=HBM)] * (1 + len(pieces)),
         scratch_shapes=[
-            pltpu.VMEM((slots, count) + tail, fresh.dtype),
-            pltpu.VMEM((slots, rows - 2 * count) + tail, fresh.dtype),
-            pltpu.SemaphoreType.DMA((slots, 4)),
+            pltpu.VMEM((slots, count + 1) + tail, fresh_kv.dtype),
+            pltpu.VMEM((slots, rows - 2 * count + 1) + tail, fresh_kv.dtype),
+            pltpu.SemaphoreType.DMA((3 * slots + len(pieces),)),
         ],
-        cost_estimate=pl.CostEstimate(flops=0, bytes_accessed=4 * fresh.size, transcendentals=0),
-        compiler_params=pltpu.CompilerParams(vmem_limit_bytes=VMEM_LIMIT),
+        cost_estimate=pl.CostEstimate(flops=0, bytes_accessed=4 * fresh_kv.size, transcendentals=0),
+        compiler_params=pltpu.CompilerParams(vmem_limit_bytes=WIDE_LIMIT),
         name="arrange",
-    )(lists, places, fresh, after)
+    )(near, far, fresh_kv, after)
     return outs[0], outs[1:]
 
 
-def restore_kernel(slot, heads, list_ref, place_ref, raw_ref, zone_ref, rest_ref, *refs):
-    out_ref, zone, rest, sems = refs[-4:]
-    count = zone.shape[0]
-    copies = [pltpu.make_async_copy(raw_ref.at[s], out_ref.at[s, :count], sems.at[4 + s]) for s in heads]
-    copy_zone = pltpu.make_async_copy(zone_ref.at[slot], zone, sems.at[0])
-    copy_rest = pltpu.make_async_copy(rest_ref, rest, sems.at[1])
-    copy_zone.start()
-    copy_rest.start()
+def join_kernel(raw_ref, zone_ref, out_ref, sems):
+    count = raw_ref.shape[1]
+    copies = [
+        pltpu.make_async_copy(raw_ref, out_ref.at[:, :count], sems.at[0]),
+        pltpu.make_async_copy(zone_ref, out_ref.at[:, count : 2 * count], sems.at[1]),
+    ]
     for copy in copies:
         copy.start()
-    copy_zone.wait()
-    copy_rest.wait()
-    swap_rows(list_ref, place_ref, slot, zone, rest)
-    copies.append(pltpu.make_async_copy(zone, out_ref.at[slot, count : 2 * count], sems.at[2]))
-    copies[-1].start()
-    copies.append(pltpu.make_async_copy(rest, out_ref.at[slot, 2 * count :], sems.at[3]))
-    copies[-1].start()
     for copy in copies:
         copy.wait()
 
 
-def restore(lists, places, raw, zone, rest, slot, shape, whole=None):
-    tail = shape[2:]
-    count = zone.shape[1]
-    extra = () if whole is None else (whole,)
-    heads = range(shape[0]) if whole is None else ()
-    return pl.pallas_call(
-        functools.partial(restore_kernel, slot, heads),
-        out_shape=jax.ShapeDtypeStruct(shape, rest.dtype),
-        in_specs=[pl.BlockSpec(memory_space=SMEM)] * 2 + [pl.BlockSpec(memory_space=HBM)] * (3 + len(extra)),
+def join_head(raw, zone, shape):
+    return pl.pallas_call(
+        join_kernel,
+        out_shape=jax.ShapeDtypeStruct(shape, raw.dtype),
+        in_specs=[pl.BlockSpec(memory_space=HBM)] * 2,
+        out_specs=pl.BlockSpec(memory_space=HBM),
+        scratch_shapes=[pltpu.SemaphoreType.DMA((2,))],
+        cost_estimate=pl.CostEstimate(flops=0, bytes_accessed=8 * raw.size, transcendentals=0),
+        name="join_head",
+    )(raw, zone)
+
+
+def restore_kernel(slot, start, stop, near_ref, far_ref, piece_ref, whole_ref, *refs):
+    out_ref, zone, piece, sems = refs[-4:]
+    count = zone.shape[0] - 1
+    inner = [
+        pltpu.make_async_copy(piece_ref, piece.at[: stop - start], sems.at[0]),
+        pltpu.make_async_copy(out_ref.at[slot, count : 2 * count], zone.at[:count], sems.at[1]),
+    ]
+    for copy in inner:
+        copy.start()
+    for copy in inner:
+        copy.wait()
+    swap_rows(near_ref, far_ref, slot, zone, piece, start, stop)
+    outer = [
+        pltpu.make_async_copy(piece.at[: stop - start], out_ref.at[slot, start:stop], sems.at[2]),
+        pltpu.make_async_copy(zone.at[:count], out_ref.at[slot, count : 2 * count], sems.at[3]),
+    ]
+    for copy in outer:
+        copy.start()
+    for copy in outer:
+        copy.wait()
+
+
+def restore(near, far, block, whole, piece, after=()):
+    slot, start, stop = piece
+    tail = whole.shape[2:]
+    count = near.shape[0] // whole.shape[0]
+    return pl.pallas_call(
+        functools.partial(restore_kernel, slot, start, stop),
+        out_shape=jax.ShapeDtypeStruct(whole.shape, whole.dtype),
+        in_specs=[pl.BlockSpec(memory_space=SMEM)] * 2 + [pl.BlockSpec(memory_space=HBM)] * (2 + len(after)),
         out_specs=pl.BlockSpec(memory_space=HBM),
         scratch_shapes=[
-            pltpu.VMEM((count,) + tail, rest.dtype),
-            pltpu.VMEM(rest.shape, rest.dtype),
-            pltpu.SemaphoreType.DMA((4 + shape[0],)),
+            pltpu.VMEM((count + 1,) + tail, whole.dtype),
+            pltpu.VMEM((stop - start + 1,) + tail, whole.dtype),
+            pltpu.SemaphoreType.DMA((4,)),
         ],
-        input_output_aliases={} if whole is None else {5: 0},
-        cost_estimate=pl.CostEstimate(flops=0, bytes_accessed=4 * rest.size, transcendentals=0),
+        input_output_aliases={3: 0},
+        cost_estimate=pl.CostEstimate(flops=0, bytes_accessed=4 * block.size, transcendentals=0),
         compiler_params=pltpu.CompilerParams(vmem_limit_bytes=VMEM_LIMIT),
         name="restore",
-    )(lists, places, raw, zone, rest, *extra)
+    )(near, far, block, whole, *after)
 
 
 def hold_kernel(block_ref, after_ref, out_ref):
@@ -304,23 +360,35 @@
     queries, fresh, stale, text = queries[0], fresh_kv[0], stale_kv[0], text_kv[0]
     slots, img_rows = queries.shape[:2]
     listed_count = refresh_rows.shape[2]
-
-    raw = fresh[:, :listed_count]
+    hot_rows = 2 * listed_count
+
+    raw = take_head(fresh_kv, listed_count)
     raw_in = from_behind(raw, "grp", half_groups)
 
     my_list = lax.dynamic_index_in_dim(refresh_rows, my_group, 0, keepdims=False)
     partner_list = lax.dynamic_index_in_dim(refresh_rows, partner, 0, keepdims=False)
-    places, sources = swap_places(jnp.stack([my_list, partner_list]))
-    mine = (my_list.reshape(-1), places[0].reshape(-1))
-    partners = (partner_list.reshape(-1), places[1].reshape(-1))
-
-    zone, rests = arrange(*mine, fresh, raw)
+    near, far, sources = swap_pairs(jnp.stack([my_list, partner_list]))
+
+    first_cut = hot_rows + (img_rows - hot_rows) * 5 // 8
+    last_cut = img_rows - listed_count
+    final = slots - 1
+    pieces = [(slot, hot_rows, img_rows) for slot in range(final)]
+    pieces += [(final, hot_rows, first_cut), (final, first_cut, last_cut), (final, last_cut, img_rows)]
+    zone, blocks = arrange(near[0].reshape(-1), far[0].reshape(-1), fresh_kv, pieces, raw)
     zone_in = from_behind(zone, "grp", half_groups)
     w_t = w_velocity.T
-    text_own = project_text(text[:, :, 0], text[:, :, 1], w_t, raw)
+    text_own = project_text(text[:, :, 0], text[:, :, 1], w_t, zone)
     text_in = from_behind(text_own, "grp", half_groups)
-    gates = [raw_in] * (slots - 1) + [text_in]
-    rests_in = [from_behind(hold(rest, gate), "grp", half_groups) for rest, gate in zip(rests, gates)]
+    arrived, held = [], []
+    for index, block in enumerate(blocks):
+        if index < final:
+            gate = raw_in
+        elif index == final:
+            gate = text_in
+        else:
+            gate = arrived[index - 2]
+        held.append(hold(block, gate))
+        arrived.append(from_behind(held[-1], "grp", half_groups))
 
     my_live = lax.dynamic_index_in_dim(live_counts, my_group, 0, keepdims=False)
     partner_live = lax.dynamic_index_in_dim(live_counts, partner, 0, keepdims=False)
@@ -340,7 +408,7 @@
         axis=1,
     )
     bias = jnp.where(live, 0.0, -jnp.inf).astype(jnp.float32)[:, :, None]
-    hot = jnp.concatenate([raw_in, zone_in], axis=1)
+    hot = join_head(raw_in, zone_in, (slots, hot_rows) + fresh.shape[2:])
     partial = attention(
         queries,
         fresh[:, :, 0],
@@ -377,9 +445,11 @@
     step_size = (times[:, 1] - times[:, 0]).astype(jnp.float32) / 1000.0
     latent_next = latent[0] + step_size[:, None, None] * velocity
 
-    next_stale = None
-    for slot in range(slots):
-        next_stale = restore(*partners, raw_in, zone_in, rests_in[slot], slot, fresh.shape, whole=next_stale)
+    next_stale = join_head(raw_in, zone_in, fresh.shape)
+    for index, piece in enumerate(pieces):
+        next_stale = restore(
+            near[1].reshape(-1), far[1].reshape(-1), arrived[index], next_stale, piece, held[index + 2 : index + 3]
+        )
     return (next_stale[None], velocity[None], latent_next[None])
 
 

time: 264 us -> 289 us (1.095)
  Pallas kernels: 57.4 us -> 144 us
  waiting for transfers between devices: 142 us -> 84.1 us
  local copies, waits for them, and re-layouts: 48.5 us -> 42.6 us
  starting transfers between devices: 8.89 us -> 11.9 us
    pallas_call x3 -> x8, Pallas kernels: 11.8 us -> 99 us  [the longest x2 65.8 us: join_head(): pl.pallas_call(join_kernel, out_shape=jax.ShapeDtypeStruct(shape, raw.dty...]
    ppermute x6 -> x8, waiting for transfers between devices: 142 us -> 84.1 us  [from_behind(): return lax.ppermute(block, axis, route)]
    squeeze x2 -> x1, local copies, waits for them, and re-layouts: 9.96 us -> 1.49 us  [shards(): text_own = project_text(text[:, :, 0], text[:, :, 1], w_t, zone)]
    slice x3, local copies, waits for them, and re-layouts: 0.58 us -> 4.31 us  [the longest x1 4.3 us: shards(): hot[:, :, 1]]
    unnamed x46 -> x51, local copies, waits for them, and re-layouts: 20.9 us -> 24.3 us
    ppermute x6 -> x8, starting transfers between devices: 8.89 us -> 11.9 us  [from_behind(): return lax.ppermute(block, axis, route)]
    ppermute x2 -> x0, local copies, waits for them, and re-layouts: 2.92 us -> none  [from_behind(): return lax.ppermute(block, axis, route)]
  transfers between devices with their start and end apart: 6 -> 8, of which waited for: 5 -> 3; matrix products, arithmetic and copies ran while one was open for 14% -> 11% of each run, Pallas kernels for 20% -> 43%
where the time goes in v3:
time: 289 us; the launch traced here: 288 us
  Pallas kernels  144 us (50%)
  waiting for transfers between devices  84.1 us (29%)
  local copies, waits for them, and re-layouts  42.6 us (15%)
  starting transfers between devices  11.9 us (4%)
  other arithmetic  4.46 us (2%)
    ppermute x8, waiting for transfers between devices, from_behind(): return lax.ppermute(block, axis, route)  84.1 us
    pallas_call x2, Pallas kernels, join_head(): pl.pallas_call(join_kernel, out_shape=jax.ShapeDtypeStruct(shape, raw.dty...  65.8 us
    pallas_call x1, Pallas kernels, attention(): pl.pallas_call(functools.partial(attention_kernel, text_rows), grid=(slot...  34.6 us
    unnamed x51, local copies, waits for them, and re-layouts  24.3 us
    pallas_call x1, Pallas kernels, take_head(): pl.pallas_call(take_kernel, out_shape=jax.ShapeDtypeStruct(shape, fresh_k...  17 us
    ppermute x8, starting transfers between devices, from_behind(): return lax.ppermute(block, axis, route)  11.9 us
    pallas_call x4, Pallas kernels, restore(): pl.pallas_call(functools.partial(restore_kernel, slot, start, stop), out_...  11.7 us
    pallas_call x1, Pallas kernels, project_text(): pl.pallas_call(text_kernel, grid=(slots, heads), out_shape=jax.ShapeDtype...  10 us
  transfers between devices with their start and end apart: 8, of which 3 were waited for; matrix products, arithmetic and copies ran while one was open for 11% of the time, Pallas kernels for 43%

profile of v3, /device:TPU:0, one launch (start us, length us, event | category | flops | bytes accessed | tf_op | source)
XLA Modules:
  0.0 287.6 jit_solution(972128381930183863)
XLA Ops:
  0.6 17.0 %take_head.1.after_ref = bf16[2,64,2,1024]{3,2,1,0:T(2,128)(2,1)} custom-call(bf16[1,2,512,2,1024]{4,3,2,1,0:T(2,128)(2,1)} %fresh_ref.3), custom_call_target="tpu_custom_call" | custom-call | bytes 1048576 | tf_op jit(solution)/shard_map/take_head/pallas_call | solution.py:67
  17.6 4.1 %collective-permute-start.3 = (bf16[2,64,2,1024]{3,2,1,0:T(2,128)(2,1)}, bf16[2,64,2,1024]{3,2,1,0:T(2,128)(2,1)S(1)}, u32[]{:S(2)}, u32[]{:S(2)}) collective-permute-start(bf16[2,64,2,1024]{3,2,1,0:T(2,128)(2,1)} %take_head.1.after_ref), channel_id=1, source_target_pairs={{16,0},{18,2},{20,4},{22,6},{24,8},{26,10},{28,12},{30,14},{0,16},... | collective-permute-start | bytes 1572872 | tf_op jit(solution)/shard_map/ppermute | solution.py:21
  21.8 0.7 constant_dynamic-slice_fusion.4
  22.5 0.1 compare_reduce_fusion
  22.6 0.2 convert_reduce_fusion.1
  22.8 0.3 select_reduce_fusion
  23.2 0.6 reshape_squeeze.20.near_ref
  23.7 0.6 reshape_squeeze.21.far_ref
  24.3 4.5 %arrange.1 = (bf16[2,64,2,1024]{3,2,1,0:T(2,128)(2,1)}, bf16[384,2,1024]{2,1,0:T(2,128)(2,1)}, bf16[240,2,1024]{2,1,0:T(2,128)(2,1)}, bf16[80,2,1024]{2,1,0:T(2,128)(2,1)}, bf16[64,2,1024]{2,1,0:T(2,128)(2,1)}) custom-call(s32[128]{0:T(128)} %reshape_squeeze.20.near_ref, s32[128]{0:T(128)} %reshape_squeeze.21.far_ref, ...), custom_call_target="tpu_custom_call" | custom-call | bytes 8388608 | tf_op jit(solution)/shard_map/arrange/pallas_call | solution.py:124
  28.9 0.1 collective-permute-start.6
  29.0 0.6 copy.64
  29.6 1.5 slice_bitcast_fusion.4
  31.1 10.0 %project_text.1.refs_7_ = bf16[2,8,384,128]{3,2,1,0:T(8,128)(2,1)} custom-call(bf16[2,256,1024]{2,1,0:T(8,128)(2,1)} %get-tuple-element.24.k_ref, bf16[2,256,1024]{2,1,0:T(8,128)(2,1)} %get-tuple-element.23.v_ref, bf16[64,1024]{1,0:T(8,128)(2,1)} %bitcast.50, bf16[2,64,2,1024]{3,2,1,0:T(2,128)(2,1)} %get-tuple-element.10.after_ref), custom_call_target="tpu_custom_call" | custom-call | flops 67108864 | bytes 4194304 | tf_op jit(solution)/shard_map/project_text/pallas_call | solution.py:245
  41.1 2.9 %collective-permute-start = (bf16[2,8,384,128]{3,2,1,0:T(8,128)(2,1)}, bf16[2,8,384,128]{3,2,1,0:T(8,128)(2,1)S(1)}, u32[]{:S(2)}, u32[]{:S(2)}) collective-permute-start(bf16[2,8,384,128]{3,2,1,0:T(8,128)(2,1)} %project_text.1.refs_7_), channel_id=1, source_target_pairs={{16,0},{18,2},{20,4},{22,6},{24,8},{26,10},{28,12},{30,14},{0,16},... | collective-permute-start | bytes 4718600 | tf_op jit(solution)/shard_map/ppermute | solution.py:21
  44.0 5.5 %copy.63 = bf16[1,2,512,2,1024]{4,2,1,3,0:T(8,128)(2,1)} copy(bf16[1,2,512,2,1024]{4,3,2,1,0:T(2,128)(2,1)} %fresh_ref.3) | data formatting | bytes 8388608 | tf_op args[1]
  49.5 3.3 %copy.62 = bf16[1,2,512,2,1024]{4,2,1,3,0:T(8,128)(2,1)} copy(bf16[1,2,512,2,1024]{4,3,2,1,0:T(2,128)(2,1)S(1)} %copy-done.18) | data formatting | bytes 8388608 | tf_op args[2]
  52.8 0.1 fusion
  53.0 0.1 pad_add_fusion.1
  53.0 0.1 compare_reduce_fusion.1
  53.1 0.2 fusion.3
  53.4 0.1 and_bitcast_fusion.1
  53.4 0.1 and_bitcast_fusion
  53.6 0.7 copy.54
  54.3 1.4 broadcast_select_fusion.refs_10_
  55.7 4.8 %slice_bitcast_fusion.2 = (bf16[2,512,1024]{2,1,0:T(8,128)(2,1)}, bf16[2,512,1024]{2,1,0:T(8,128)(2,1)}) fusion(bf16[2,512,2,1024]{3,1,0,2:T(8,128)(2,1)} %bitcast.55), kind=kLoop, calls=%fused_computation.4 | loop fusion | bytes 8388608 | tf_op jit(solution)/shard_map/squeeze | solution.py:415
  60.5 2.5 slice_bitcast_fusion
  63.0 0.1 dynamic_slice.29
  63.1 0.1 broadcast_compare_fusion
  63.2 27.7 %collective-permute-done.3.after_ref.raw_ref = bf16[2,64,2,1024]{3,2,1,0:T(2,128)(2,1)S(1)} collective-permute-done((bf16[2,64,2,1024]{3,2,1,0:T(2,128)(2,1)}, bf16[2,64,2,1024]{3,2,1,0:T(2,128)(2,1)S(1)}, u32[]{:S(2)}, u32[]{:S(2)}) %collective-permute-start.3) | collective-permute-done | bytes 524320 | tf_op jit(solution)/shard_map/ppermute | solution.py:21
  90.9 0.8 copy-done.17
  91.7 0.0 collective-permute-start.4
  91.7 0.1 compare_convert_fusion
  91.7 44.2 %collective-permute-done.6.zone_ref = bf16[2,64,2,1024]{3,2,1,0:T(2,128)(2,1)} collective-permute-done((bf16[2,64,2,1024]{3,2,1,0:T(2,128)(2,1)}, bf16[2,64,2,1024]{3,2,1,0:T(2,128)(2,1)}, u32[]{:S(2)}, u32[]{:S(2)}) %collective-permute-start.6) | collective-permute-done | bytes 524320 | tf_op jit(solution)/shard_map/ppermute | solution.py:21
  135.9 32.9 %join_head.3 = bf16[2,128,2,1024]{3,2,1,0:T(2,128)(2,1)} custom-call(bf16[2,64,2,1024]{3,2,1,0:T(2,128)(2,1)} %copy-done.17, bf16[2,64,2,1024]{3,2,1,0:T(2,128)(2,1)} %collective-permute-done.6.zone_ref), custom_call_target="tpu_custom_call" | custom-call | bytes 2097152 | tf_op jit(solution)/shard_map/join_head/pallas_call | solution.py:155
  168.8 4.3 %fusion.6 = (bf16[2,128,1,1024]{3,2,1,0:T(2,128)(2,1)}, bf16[2,128,1,1024]{3,2,1,0:T(2,128)(2,1)}) fusion(bf16[2,128,2,1024]{3,2,1,0:T(2,128)(2,1)} %join_head.3), kind=kLoop, calls=%fused_computation.50 | loop fusion | bytes 2097152 | tf_op jit(solution)/shard_map/slice | solution.py:419
  173.1 1.2 copy-done.9
  174.3 2.1 copy_bitcast_fusion.3
  176.4 0.1 copy-done.4
  176.5 1.6 copy-done.5
  178.1 1.6 copy-done.6
  179.7 1.6 copy-done.7
  181.3 1.5 copy-done.8
  182.7 1.4 copy-done.10
  184.2 1.4 copy-done.11
  185.6 1.6 copy-done.15
  187.2 34.6 %attention.1 = f32[2,64,512]{2,1,0:T(8,128)S(1)} custom-call(bf16[2,512,1024]{2,1,0:T(8,128)(2,1)S(1)} %bitcast.52, bf16[2,512,1024]{2,1,0:T(8,128)(2,1)S(1)} %copy-done.5, bf16[2,512,1024]{2,1,0:T(8,128)(2,1)S(1)} %copy-done.4, bf16[2,512,1024]{2,1,0:T(8,128)(2,1)S(1)} %copy-done.7, bf16[2,512,1024]{2,1,0:T(8,128)(2,1)S(1)} %copy-done.6, ...), custom_call_target="tpu_custom_call" | custom-call | flops 5234491392 | bytes 25165824 | tf_op jit(solution)/shard_map/attention/pallas_call | solution.py:324
  221.7 1.9 collective-permute-start.7
  223.7 0.1 multiply_reduce_fusion
  223.8 0.1 reshape_squeeze.8.near_ref
  223.9 0.1 reshape_squeeze.9.far_ref
  224.0 0.2 multiply_reduce_fusion.1
  224.1 32.9 %join_head.2.whole_ref = bf16[2,512,2,1024]{3,2,1,0:T(2,128)(2,1)} custom-call(bf16[2,64,2,1024]{3,2,1,0:T(2,128)(2,1)} %copy-done.17, bf16[2,64,2,1024]{3,2,1,0:T(2,128)(2,1)} %collective-permute-done.6.zone_ref), custom_call_target="tpu_custom_call" | custom-call | bytes 2097152 | tf_op jit(solution)/shard_map/join_head/pallas_call | solution.py:155
  257.0 0.0 copy-start.20
  257.1 1.2 copy-done
  258.2 2.6 collective-permute-start.5
  260.9 0.9 copy-done.2
  261.8 0.3 collective-permute-start.2
  262.1 0.7 fusion.2
  262.8 0.7 fusion.1
  263.5 3.1 %restore.4.whole_ref = bf16[2,512,2,1024]{3,2,1,0:T(2,128)(2,1)} custom-call(s32[128]{0:T(128)S(1)} %reshape_squeeze.8.near_ref, s32[128]{0:T(128)S(1)} %reshape_squeeze.9.far_ref, bf16[384,2,1024]{2,1,0:T(2,128)(2,1)S(1)} %copy-done.1, bf16[2,512,2,1024]{3,2,1,0:T(2,128)(2,1)} %join_head.2.whole_ref, ...), custom_call_target="tpu_custom_call", output_to_operand_aliasing={{}: (3, {})} | custom-call | bytes 3145728 | tf_op jit(solution)/shard_map/restore/pallas_call | solution.py:192
  266.7 3.1 %restore.5.whole_ref = bf16[2,512,2,1024]{3,2,1,0:T(2,128)(2,1)} custom-call(s32[128]{0:T(128)S(1)} %reshape_squeeze.8.near_ref, s32[128]{0:T(128)S(1)} %reshape_squeeze.9.far_ref, bf16[240,2,1024]{2,1,0:T(2,128)(2,1)S(1)} %copy-done.3, bf16[2,512,2,1024]{3,2,1,0:T(2,128)(2,1)} %restore.4.whole_ref, ...), custom_call_target="tpu_custom_call", output_to_operand_aliasing={{}: (3, {})} | custom-call | bytes 1966080 | tf_op jit(solution)/shard_map/restore/pallas_call | solution.py:192
  269.9 12.2 %collective-permute-done.5.piece_ref = bf16[80,2,1024]{2,1,0:T(2,128)(2,1)} collective-permute-done((bf16[80,2,1024]{2,1,0:T(2,128)(2,1)}, bf16[80,2,1024]{2,1,0:T(2,128)(2,1)}, u32[]{:S(2)}, u32[]{:S(2)}) %collective-permute-start.5) | collective-permute-done | bytes 327712 | tf_op jit(solution)/shard_map/ppermute | solution.py:21
  282.1 2.8 restore.6.whole_ref
  284.9 2.7 restore.7
  (61 shorter events, 0.2 us)
Async XLA Ops:
  17.6 73.2 %collective-permute-start.3 = (bf16[2,64,2,1024]{3,2,1,0:T(2,128)(2,1)}, bf16[2,64,2,1024]{3,2,1,0:T(2,128)(2,1)S(1)}, u32[]{:S(2)}, u32[]{:S(2)}) collective-permute-start(bf16[2,64,2,1024]{3,2,1,0:T(2,128)(2,1)} %take_head.1.after_ref), channel_id=1, source_target_pairs={{16,0},{18,2},{20,4},{22,6},{24,8},{26,10},{28,12},{30,14},{0,16},... | collective-permute-start | bytes 1572872 | tf_op jit(solution)/shard_map/ppermute | solution.py:21
  24.3 4.6 %copy-start.19 = (bf16[1,2,256,2,1024]{4,3,2,1,0:T(2,128)(2,1)S(1)}, bf16[1,2,256,2,1024]{4,3,2,1,0:T(2,128)(2,1)}, u32[]{:S(2)}) copy-start(bf16[1,2,256,2,1024]{4,3,2,1,0:T(2,128)(2,1)} %param.13) | copy-start | bytes 6291460
  28.9 107.1 %collective-permute-start.6 = (bf16[2,64,2,1024]{3,2,1,0:T(2,128)(2,1)}, bf16[2,64,2,1024]{3,2,1,0:T(2,128)(2,1)}, u32[]{:S(2)}, u32[]{:S(2)}) collective-permute-start(bf16[2,64,2,1024]{3,2,1,0:T(2,128)(2,1)} %get-tuple-element.10.after_ref), channel_id=1, source_target_pairs={{16,0},{18,2},{20,4},{22,6},{24,8},{26,10},{28,12},{30,14},{0,16},... | collective-permute-start | bytes 1572872 | tf_op jit(solution)/shard_map/ppermute | solution.py:21
  41.1 8.4 %copy-start.18 = (bf16[1,2,512,2,1024]{4,3,2,1,0:T(2,128)(2,1)S(1)}, bf16[1,2,512,2,1024]{4,3,2,1,0:T(2,128)(2,1)}, u32[]{:S(2)}) copy-start(bf16[1,2,512,2,1024]{4,3,2,1,0:T(2,128)(2,1)} %param.12) | copy-start | bytes 12582916
  41.1 132.0 %collective-permute-start = (bf16[2,8,384,128]{3,2,1,0:T(8,128)(2,1)}, bf16[2,8,384,128]{3,2,1,0:T(8,128)(2,1)S(1)}, u32[]{:S(2)}, u32[]{:S(2)}) collective-permute-start(bf16[2,8,384,128]{3,2,1,0:T(8,128)(2,1)} %project_text.1.refs_7_), channel_id=1, source_target_pairs={{16,0},{18,2},{20,4},{22,6},{24,8},{26,10},{28,12},{30,14},{0,16},... | collective-permute-start | bytes 4718600 | tf_op jit(solution)/shard_map/ppermute | solution.py:21
  49.5 3.6 %copy-start.21 = (s32[16,2]{0,1:T(2,128)S(1)}, s32[16,2]{0,1:T(2,128)}, u32[]{:S(2)}) copy-start(s32[16,2]{0,1:T(2,128)} %param.16) | copy-start | bytes 388
  55.7 4.8 %copy-start.16 = (bf16[1,2,512,2,1024]{4,2,1,3,0:T(8,128)(2,1)S(1)}, bf16[1,2,512,2,1024]{4,2,1,3,0:T(8,128)(2,1)}, u32[]{:S(2)}) copy-start(bf16[1,2,512,2,1024]{4,2,1,3,0:T(8,128)(2,1)} %copy.62) | copy-start | bytes 12582916
  60.5 2.5 copy-start.23
  90.9 0.8 copy-start.17
  91.7 165.4 %collective-permute-start.4 = (bf16[384,2,1024]{2,1,0:T(2,128)(2,1)}, bf16[384,2,1024]{2,1,0:T(2,128)(2,1)S(1)}, u32[]{:S(2)}, u32[]{:S(2)}) collective-permute-start(bf16[384,2,1024]{2,1,0:T(2,128)(2,1)} %hold.6), channel_id=1, source_target_pairs={{16,0},{18,2},{20,4},{22,6},{24,8},{26,10},{28,12},{30,14},{0,16},... | collective-permute-start | bytes 4718600 | tf_op jit(solution)/shard_map/ppermute | solution.py:21
  173.1 1.2 copy-start.9
  174.3 2.2 copy-start.4
  174.3 2.2 copy-start.14
  174.3 86.6 %collective-permute-start.1 = (bf16[240,2,1024]{2,1,0:T(2,128)(2,1)}, bf16[240,2,1024]{2,1,0:T(2,128)(2,1)S(1)}, u32[]{:S(2)}, u32[]{:S(2)}) collective-permute-start(bf16[240,2,1024]{2,1,0:T(2,128)(2,1)} %hold.4), channel_id=1, source_target_pairs={{16,0},{18,2},{20,4},{22,6},{24,8},{26,10},{28,12},{30,14},{0,16},... | collective-permute-start | bytes 2949128 | tf_op jit(solution)/shard_map/ppermute | solution.py:21
  176.5 1.6 copy-start.5
  178.1 1.6 copy-start.6
  179.7 1.6 copy-start.7
  181.3 1.5 copy-start.8
  182.7 1.4 copy-start.10
  184.1 1.4 copy-start.11
  185.6 1.6 copy-start.15
  187.1 36.5 %copy-start.22 = (s32[16,2]{0,1:T(2,128)S(1)}, s32[16,2]{0,1:T(2,128)}, u32[]{:S(2)}) copy-start(s32[16,2]{0,1:T(2,128)} %param.19) | copy-start | bytes 388
  221.7 40.4 %collective-permute-start.7 = (f32[2,64,256]{2,1,0:T(8,128)S(1)}, f32[2,64,256]{2,1,0:T(8,128)S(1)}, u32[]{:S(2)}, u32[]{:S(2)}) collective-permute-start(f32[2,64,256]{2,1,0:T(8,128)S(1)} %constant_dynamic-slice_fusion), channel_id=1, source_target_pairs={{1,0},{0,1},{3,2},{2,3},{5,4},{4,5},{7,6},{6,7},{9,8},{8,9},{11,10... | collective-permute-start | bytes 393224 | tf_op jit(solution)/shard_map/ppermute | solution.py:21
  257.0 5.8 %copy-start.20 = (f32[1,2,256,64]{2,3,1,0:T(8,128)S(1)}, f32[1,2,256,64]{2,3,1,0:T(8,128)}, u32[]{:S(2)}) copy-start(f32[1,2,256,64]{2,3,1,0:T(8,128)} %param.15) | copy-start | bytes 393220
  257.1 1.2 copy-start
  258.2 5.3 %copy-start.1 = (bf16[384,2,1024]{2,1,0:T(2,128)(2,1)S(1)}, bf16[384,2,1024]{2,1,0:T(2,128)(2,1)}, u32[]{:S(2)}) copy-start(bf16[384,2,1024]{2,1,0:T(2,128)(2,1)} %copy-done) | copy-start | bytes 4718596
  258.2 5.3 %copy-start.12 = (bf16[80,2,1024]{2,1,0:T(2,128)(2,1)S(1)}, bf16[80,2,1024]{2,1,0:T(2,128)(2,1)}, u32[]{:S(2)}) copy-start(bf16[80,2,1024]{2,1,0:T(2,128)(2,1)} %hold.7.refs_0_) | copy-start | bytes 983044
  258.2 23.9 %collective-permute-start.5 = (bf16[80,2,1024]{2,1,0:T(2,128)(2,1)}, bf16[80,2,1024]{2,1,0:T(2,128)(2,1)}, u32[]{:S(2)}, u32[]{:S(2)}) collective-permute-start(bf16[80,2,1024]{2,1,0:T(2,128)(2,1)} %hold.7.refs_0_), channel_id=1, source_target_pairs={{16,0},{18,2},{20,4},{22,6},{24,8},{26,10},{28,12},{30,14},{0,16},... | collective-permute-start | bytes 983048 | tf_op jit(solution)/shard_map/ppermute | solution.py:21
  260.9 0.9 copy-start.2
  261.8 23.0 %collective-permute-start.2 = (bf16[64,2,1024]{2,1,0:T(2,128)(2,1)}, bf16[64,2,1024]{2,1,0:T(2,128)(2,1)S(1)}, u32[]{:S(2)}, u32[]{:S(2)}) collective-permute-start(bf16[64,2,1024]{2,1,0:T(2,128)(2,1)} %hold.5.refs_0_), channel_id=1, source_target_pairs={{16,0},{18,2},{20,4},{22,6},{24,8},{26,10},{28,12},{30,14},{0,16},... | collective-permute-start | bytes 786440 | tf_op jit(solution)/shard_map/ppermute | solution.py:21
  263.5 3.1 %copy-start.3 = (bf16[240,2,1024]{2,1,0:T(2,128)(2,1)S(1)}, bf16[240,2,1024]{2,1,0:T(2,128)(2,1)}, u32[]{:S(2)}) copy-start(bf16[240,2,1024]{2,1,0:T(2,128)(2,1)} %copy-done.2) | copy-start | bytes 2949124
  263.5 3.1 %copy-start.13 = (bf16[64,2,1024]{2,1,0:T(2,128)(2,1)S(1)}, bf16[64,2,1024]{2,1,0:T(2,128)(2,1)}, u32[]{:S(2)}) copy-start(bf16[64,2,1024]{2,1,0:T(2,128)(2,1)} %hold.5.refs_0_) | copy-start | bytes 786436

commit v4 on v3

--- a/solution.py
+++ b/solution.py
@@ -56,10 +56,21 @@
     lax.fori_loop(0, count, step, 0, unroll=8)
 
 
-def take_kernel(fresh_ref, out_ref, sem):
-    copy = pltpu.make_async_copy(fresh_ref.at[0, :, : out_ref.shape[1]], out_ref, sem)
-    copy.start()
-    copy.wait()
+def relay(copies, sems):
+    inner = [pltpu.make_async_copy(c[0], c[1], sems.at[0, i]) for i, c in enumerate(copies)]
+    outer = [pltpu.make_async_copy(c[1], c[2], sems.at[1, i]) for i, c in enumerate(copies)]
+    for copy in inner:
+        copy.start()
+    for arrive, leave in zip(inner, outer):
+        arrive.wait()
+        leave.start()
+    for copy in outer:
+        copy.wait()
+
+
+def take_kernel(fresh_ref, out_ref, stage, sems):
+    slots, rows = out_ref.shape[:2]
+    relay([(fresh_ref.at[0, s, :rows], stage.at[s], out_ref.at[s]) for s in range(slots)], sems)
 
 
 def take_head(fresh_kv, rows):
@@ -69,7 +80,7 @@
         out_shape=jax.ShapeDtypeStruct(shape, fresh_kv.dtype),
         in_specs=[pl.BlockSpec(memory_space=HBM)],
         out_specs=pl.BlockSpec(memory_space=HBM),
-        scratch_shapes=[pltpu.SemaphoreType.DMA],
+        scratch_shapes=[pltpu.VMEM(shape, fresh_kv.dtype), pltpu.SemaphoreType.DMA((2, shape[0]))],
         cost_estimate=pl.CostEstimate(flops=0, bytes_accessed=4 * math.prod(shape), transcendentals=0),
         compiler_params=pltpu.CompilerParams(vmem_limit_bytes=WIDE_LIMIT),
         name="take_head",
@@ -139,16 +150,15 @@
     return outs[0], outs[1:]
 
 
-def join_kernel(raw_ref, zone_ref, out_ref, sems):
+def join_kernel(raw_ref, zone_ref, out_ref, stage, sems):
     count = raw_ref.shape[1]
-    copies = [
-        pltpu.make_async_copy(raw_ref, out_ref.at[:, :count], sems.at[0]),
-        pltpu.make_async_copy(zone_ref, out_ref.at[:, count : 2 * count], sems.at[1]),
-    ]
-    for copy in copies:
-        copy.start()
-    for copy in copies:
-        copy.wait()
+    relay(
+        [
+            (raw_ref, stage.at[0], out_ref.at[:, :count]),
+            (zone_ref, stage.at[1], out_ref.at[:, count : 2 * count]),
+        ],
+        sems,
+    )
 
 
 def join_head(raw, zone, shape):
@@ -157,8 +167,9 @@
         out_shape=jax.ShapeDtypeStruct(shape, raw.dtype),
         in_specs=[pl.BlockSpec(memory_space=HBM)] * 2,
         out_specs=pl.BlockSpec(memory_space=HBM),
-        scratch_shapes=[pltpu.SemaphoreType.DMA((2,))],
+        scratch_shapes=[pltpu.VMEM((2,) + raw.shape, raw.dtype), pltpu.SemaphoreType.DMA((2, 2))],
         cost_estimate=pl.CostEstimate(flops=0, bytes_accessed=8 * raw.size, transcendentals=0),
+        compiler_params=pltpu.CompilerParams(vmem_limit_bytes=VMEM_LIMIT),
         name="join_head",
     )(raw, zone)
 

time: 289 us -> 259 us (0.90)
  Pallas kernels: 144 us -> 64.8 us
  waiting for transfers between devices: 84.1 us -> 137 us
    pallas_call x2, Pallas kernels: 65.8 us -> 1.25 us  [join_head(): pl.pallas_call(join_kernel, out_shape=jax.ShapeDtypeStruct(shape, raw.dty...]
    ppermute x8, waiting for transfers between devices: 84.1 us -> 137 us  [from_behind(): return lax.ppermute(block, axis, route)]
    pallas_call x1, Pallas kernels: 17 us -> 1.8 us  [take_head(): pl.pallas_call(take_kernel, out_shape=jax.ShapeDtypeStruct(shape, fresh_k...]
    unnamed x51 -> x55, local copies, waits for them, and re-layouts: 24.3 us -> 23.9 us
  transfers between devices with their start and end apart: 8 -> 8, of which waited for: 3 -> 7; matrix products, arithmetic and copies ran while one was open for 11% -> 12% of each run, Pallas kernels for 43% -> 23%
where the time goes in v4:
time: 259 us; the launch traced here: 257 us
  waiting for transfers between devices  137 us (53%)
  Pallas kernels  64.8 us (25%)
  local copies, waits for them, and re-layouts  41 us (16%)
  starting transfers between devices  9.13 us (4%)
  other arithmetic  4.45 us (2%)
    ppermute x8, waiting for transfers between devices, from_behind(): return lax.ppermute(block, axis, route)  137 us
    pallas_call x1, Pallas kernels, attention(): pl.pallas_call(functools.partial(attention_kernel, text_rows), grid=(slot...  35.5 us
    unnamed x55, local copies, waits for them, and re-layouts  23.9 us
    pallas_call x4, Pallas kernels, restore(): pl.pallas_call(functools.partial(restore_kernel, slot, start, stop), out_...  11.7 us
    pallas_call x1, Pallas kernels, project_text(): pl.pallas_call(text_kernel, grid=(slots, heads), out_shape=jax.ShapeDtype...  10 us
    ppermute x8, starting transfers between devices, from_behind(): return lax.ppermute(block, axis, route)  9.13 us
  transfers between devices with their start and end apart: 8, of which 7 were waited for; matrix products, arithmetic and copies ran while one was open for 12% of the time, Pallas kernels for 23%

profile of v4, /device:TPU:0, one launch (start us, length us, event | category | flops | bytes accessed | tf_op | source)
XLA Modules:
  0.0 257.3 jit_solution(2246261179528463232)
XLA Ops:
  0.6 1.8 take_head.1.after_ref
  2.4 4.1 %collective-permute-start.3 = (bf16[2,64,2,1024]{3,2,1,0:T(2,128)(2,1)}, bf16[2,64,2,1024]{3,2,1,0:T(2,128)(2,1)S(1)}, u32[]{:S(2)}, u32[]{:S(2)}) collective-permute-start(bf16[2,64,2,1024]{3,2,1,0:T(2,128)(2,1)} %take_head.1.after_ref), channel_id=1, source_target_pairs={{16,0},{18,2},{20,4},{22,6},{24,8},{26,10},{28,12},{30,14},{0,16},... | collective-permute-start | bytes 1572872 | tf_op jit(solution)/shard_map/ppermute | solution.py:21
  6.6 0.7 constant_dynamic-slice_fusion.4
  7.3 0.1 compare_reduce_fusion
  7.4 0.2 convert_reduce_fusion.1
  7.6 0.3 select_reduce_fusion
  8.0 0.6 reshape_squeeze.20.near_ref
  8.6 0.6 reshape_squeeze.21.far_ref
  9.1 4.5 %arrange.1 = (bf16[2,64,2,1024]{3,2,1,0:T(2,128)(2,1)}, bf16[384,2,1024]{2,1,0:T(2,128)(2,1)}, bf16[240,2,1024]{2,1,0:T(2,128)(2,1)}, bf16[80,2,1024]{2,1,0:T(2,128)(2,1)}, bf16[64,2,1024]{2,1,0:T(2,128)(2,1)}) custom-call(s32[128]{0:T(128)} %reshape_squeeze.20.near_ref, s32[128]{0:T(128)} %reshape_squeeze.21.far_ref, ...), custom_call_target="tpu_custom_call" | custom-call | bytes 8388608 | tf_op jit(solution)/shard_map/arrange/pallas_call | solution.py:135
  13.6 0.1 collective-permute-start.6
  13.7 0.6 copy.64
  14.3 1.5 slice_bitcast_fusion.4
  15.9 10.0 %project_text.1.refs_7_ = bf16[2,8,384,128]{3,2,1,0:T(8,128)(2,1)} custom-call(bf16[2,256,1024]{2,1,0:T(8,128)(2,1)} %get-tuple-element.24.k_ref, bf16[2,256,1024]{2,1,0:T(8,128)(2,1)} %get-tuple-element.23.v_ref, bf16[64,1024]{1,0:T(8,128)(2,1)} %bitcast.50, bf16[2,64,2,1024]{3,2,1,0:T(2,128)(2,1)} %get-tuple-element.10.after_ref), custom_call_target="tpu_custom_call" | custom-call | flops 67108864 | bytes 4194304 | tf_op jit(solution)/shard_map/project_text/pallas_call | solution.py:256
  25.9 2.9 %collective-permute-start = (bf16[2,8,384,128]{3,2,1,0:T(8,128)(2,1)}, bf16[2,8,384,128]{3,2,1,0:T(8,128)(2,1)}, u32[]{:S(2)}, u32[]{:S(2)}) collective-permute-start(bf16[2,8,384,128]{3,2,1,0:T(8,128)(2,1)} %project_text.1.refs_7_), channel_id=1, source_target_pairs={{16,0},{18,2},{20,4},{22,6},{24,8},{26,10},{28,12},{30,14},{0,16},... | collective-permute-start | bytes 4718600 | tf_op jit(solution)/shard_map/ppermute | solution.py:21
  28.8 5.5 %copy.63 = bf16[1,2,512,2,1024]{4,2,1,3,0:T(8,128)(2,1)} copy(bf16[1,2,512,2,1024]{4,3,2,1,0:T(2,128)(2,1)} %fresh_ref.3) | data formatting | bytes 8388608 | tf_op args[1]
  34.3 3.3 %copy.62 = bf16[1,2,512,2,1024]{4,2,1,3,0:T(8,128)(2,1)} copy(bf16[1,2,512,2,1024]{4,3,2,1,0:T(2,128)(2,1)S(1)} %copy-done.20) | data formatting | bytes 8388608 | tf_op args[2]
  37.6 0.1 fusion
  37.7 0.1 pad_add_fusion.1
  37.8 0.1 compare_reduce_fusion.1
  37.9 0.2 fusion.3
  38.1 0.1 and_bitcast_fusion.1
  38.2 0.1 and_bitcast_fusion
  38.4 0.7 copy.54
  39.1 1.4 broadcast_select_fusion.refs_10_
  40.5 4.8 %slice_bitcast_fusion.2 = (bf16[2,512,1024]{2,1,0:T(8,128)(2,1)}, bf16[2,512,1024]{2,1,0:T(8,128)(2,1)}) fusion(bf16[2,512,2,1024]{3,1,0,2:T(8,128)(2,1)} %bitcast.55), kind=kLoop, calls=%fused_computation.4 | loop fusion | bytes 8388608 | tf_op jit(solution)/shard_map/squeeze | solution.py:426
  45.3 2.5 slice_bitcast_fusion
  47.9 0.1 broadcast_compare_fusion
  47.9 27.7 %collective-permute-done.3.after_ref.raw_ref = bf16[2,64,2,1024]{3,2,1,0:T(2,128)(2,1)S(1)} collective-permute-done((bf16[2,64,2,1024]{3,2,1,0:T(2,128)(2,1)}, bf16[2,64,2,1024]{3,2,1,0:T(2,128)(2,1)S(1)}, u32[]{:S(2)}, u32[]{:S(2)}) %collective-permute-start.3) | collective-permute-done | bytes 524320 | tf_op jit(solution)/shard_map/ppermute | solution.py:21
  75.7 0.8 copy-done.2
  76.6 44.1 %collective-permute-done.6.zone_ref = bf16[2,64,2,1024]{3,2,1,0:T(2,128)(2,1)S(1)} collective-permute-done((bf16[2,64,2,1024]{3,2,1,0:T(2,128)(2,1)}, bf16[2,64,2,1024]{3,2,1,0:T(2,128)(2,1)S(1)}, u32[]{:S(2)}, u32[]{:S(2)}) %collective-permute-start.6) | collective-permute-done | bytes 524320 | tf_op jit(solution)/shard_map/ppermute | solution.py:21
  120.6 1.0 copy-done.3
  121.7 0.2 join_head.3
  121.9 2.5 fusion.6
  124.3 30.1 %collective-permute-done.after_ref.refs_8_ = bf16[2,8,384,128]{3,2,1,0:T(8,128)(2,1)} collective-permute-done((bf16[2,8,384,128]{3,2,1,0:T(8,128)(2,1)}, bf16[2,8,384,128]{3,2,1,0:T(8,128)(2,1)}, u32[]{:S(2)}, u32[]{:S(2)}) %collective-permute-start) | collective-permute-done | bytes 1572896 | tf_op jit(solution)/shard_map/ppermute | solution.py:21
  154.4 2.1 copy_bitcast_fusion.3
  156.5 0.1 copy-done.9
  156.7 1.6 copy-done.10
  158.2 1.6 copy-done.11
  159.8 1.6 copy-done.12
  161.4 1.5 copy-done.13
  162.9 1.4 copy-done.14
  164.3 1.6 copy-done.18
  165.9 35.5 %attention.1 = f32[2,64,512]{2,1,0:T(8,128)S(1)} custom-call(bf16[2,512,1024]{2,1,0:T(8,128)(2,1)S(1)} %bitcast.52, bf16[2,512,1024]{2,1,0:T(8,128)(2,1)S(1)} %copy-done.10, bf16[2,512,1024]{2,1,0:T(8,128)(2,1)S(1)} %copy-done.9, bf16[2,512,1024]{2,1,0:T(8,128)(2,1)S(1)} %copy-done.12, bf16[2,512,1024]{2,1,0:T(8,128)(2,1)S(1)} %copy-done.11, ...), custom_call_target="tpu_custom_call" | custom-call | flops 5234491392 | bytes 25165824 | tf_op jit(solution)/shard_map/attention/pallas_call | solution.py:335
  201.4 0.7 constant_dynamic-slice_fusion
  202.0 1.9 collective-permute-start.7
  203.9 0.1 multiply_reduce_fusion
  204.1 0.1 reshape_squeeze.8.near_ref
  204.2 0.1 reshape_squeeze.9.far_ref
  204.2 0.2 multiply_reduce_fusion.1
  204.4 1.0 copy-done.8
  205.5 1.1 join_head.2.whole_ref
  206.6 2.5 collective-permute-done.4.after_ref.piece_ref
  209.1 1.2 copy-done
  210.3 0.1 collective-permute-start.5
  210.4 26.8 %collective-permute-done.1.after_ref.piece_ref = bf16[240,2,1024]{2,1,0:T(2,128)(2,1)S(1)} collective-permute-done((bf16[240,2,1024]{2,1,0:T(2,128)(2,1)}, bf16[240,2,1024]{2,1,0:T(2,128)(2,1)S(1)}, u32[]{:S(2)}, u32[]{:S(2)}) %collective-permute-start.1) | collective-permute-done | bytes 983072 | tf_op jit(solution)/shard_map/ppermute | solution.py:21
  237.2 1.0 copy-done.5
  238.1 0.7 fusion.2
  238.8 0.7 fusion.1
  239.6 3.1 %restore.4.whole_ref = bf16[2,512,2,1024]{3,2,1,0:T(2,128)(2,1)} custom-call(s32[128]{0:T(128)S(1)} %reshape_squeeze.8.near_ref, s32[128]{0:T(128)S(1)} %reshape_squeeze.9.far_ref, bf16[384,2,1024]{2,1,0:T(2,128)(2,1)S(1)} %copy-done.1, bf16[2,512,2,1024]{3,2,1,0:T(2,128)(2,1)} %join_head.2.whole_ref, ...), custom_call_target="tpu_custom_call", output_to_operand_aliasing={{}: (3, {})} | custom-call | bytes 3145728 | tf_op jit(solution)/shard_map/restore/pallas_call | solution.py:203
  242.7 3.1 %restore.5.whole_ref = bf16[2,512,2,1024]{3,2,1,0:T(2,128)(2,1)} custom-call(s32[128]{0:T(128)S(1)} %reshape_squeeze.8.near_ref, s32[128]{0:T(128)S(1)} %reshape_squeeze.9.far_ref, bf16[240,2,1024]{2,1,0:T(2,128)(2,1)S(1)} %copy-done.6, bf16[2,512,2,1024]{3,2,1,0:T(2,128)(2,1)} %restore.4.whole_ref, ...), custom_call_target="tpu_custom_call", output_to_operand_aliasing={{}: (3, {})} | custom-call | bytes 1966080 | tf_op jit(solution)/shard_map/restore/pallas_call | solution.py:203
  245.9 4.0 %collective-permute-done.5.piece_ref = bf16[80,2,1024]{2,1,0:T(2,128)(2,1)} collective-permute-done((bf16[80,2,1024]{2,1,0:T(2,128)(2,1)}, bf16[80,2,1024]{2,1,0:T(2,128)(2,1)}, u32[]{:S(2)}, u32[]{:S(2)}) %collective-permute-start.5) | collective-permute-done | bytes 327712 | tf_op jit(solution)/shard_map/ppermute | solution.py:21
  249.9 2.8 %restore.6.whole_ref = bf16[2,512,2,1024]{3,2,1,0:T(2,128)(2,1)} custom-call(s32[128]{0:T(128)S(1)} %reshape_squeeze.8.near_ref, s32[128]{0:T(128)S(1)} %reshape_squeeze.9.far_ref, bf16[80,2,1024]{2,1,0:T(2,128)(2,1)} %collective-permute-done.5.piece_ref, bf16[2,512,2,1024]{3,2,1,0:T(2,128)(2,1)} %restore.5.whole_ref), custom_call_target="tpu_custom_call", output_to_operand_aliasing={{}: (3, {})} | custom-call | bytes 655360 | tf_op jit(solution)/shard_map/restore/pallas_call | solution.py:203
  252.7 1.9 collective-permute-done.2.piece_ref
  254.6 2.7 %restore.7 = bf16[2,512,2,1024]{3,2,1,0:T(2,128)(2,1)} custom-call(s32[128]{0:T(128)S(1)} %reshape_squeeze.8.near_ref, s32[128]{0:T(128)S(1)} %reshape_squeeze.9.far_ref, bf16[64,2,1024]{2,1,0:T(2,128)(2,1)S(1)} %collective-permute-done.2.piece_ref, bf16[2,512,2,1024]{3,2,1,0:T(2,128)(2,1)} %restore.6.whole_ref), custom_call_target="tpu_custom_call", output_to_operand_aliasing={{}: (3, {})} | custom-call | bytes 524288 | tf_op jit(solution)/shard_map/restore/pallas_call | solution.py:203
  (65 shorter events, 0.3 us)
Async XLA Ops:
  2.4 73.2 %collective-permute-start.3 = (bf16[2,64,2,1024]{3,2,1,0:T(2,128)(2,1)}, bf16[2,64,2,1024]{3,2,1,0:T(2,128)(2,1)S(1)}, u32[]{:S(2)}, u32[]{:S(2)}) collective-permute-start(bf16[2,64,2,1024]{3,2,1,0:T(2,128)(2,1)} %take_head.1.after_ref), channel_id=1, source_target_pairs={{16,0},{18,2},{20,4},{22,6},{24,8},{26,10},{28,12},{30,14},{0,16},... | collective-permute-start | bytes 1572872 | tf_op jit(solution)/shard_map/ppermute | solution.py:21
  9.1 4.6 %copy-start.21 = (bf16[1,2,256,2,1024]{4,3,2,1,0:T(2,128)(2,1)S(1)}, bf16[1,2,256,2,1024]{4,3,2,1,0:T(2,128)(2,1)}, u32[]{:S(2)}) copy-start(bf16[1,2,256,2,1024]{4,3,2,1,0:T(2,128)(2,1)} %param.13) | copy-start | bytes 6291460
  13.6 107.0 %collective-permute-start.6 = (bf16[2,64,2,1024]{3,2,1,0:T(2,128)(2,1)}, bf16[2,64,2,1024]{3,2,1,0:T(2,128)(2,1)S(1)}, u32[]{:S(2)}, u32[]{:S(2)}) collective-permute-start(bf16[2,64,2,1024]{3,2,1,0:T(2,128)(2,1)} %get-tuple-element.10.after_ref), channel_id=1, source_target_pairs={{16,0},{18,2},{20,4},{22,6},{24,8},{26,10},{28,12},{30,14},{0,16},... | collective-permute-start | bytes 1572872 | tf_op jit(solution)/shard_map/ppermute | solution.py:21
  25.9 8.4 %copy-start.20 = (bf16[1,2,512,2,1024]{4,3,2,1,0:T(2,128)(2,1)S(1)}, bf16[1,2,512,2,1024]{4,3,2,1,0:T(2,128)(2,1)}, u32[]{:S(2)}) copy-start(bf16[1,2,512,2,1024]{4,3,2,1,0:T(2,128)(2,1)} %param.12) | copy-start | bytes 12582916
  25.9 128.5 %collective-permute-start = (bf16[2,8,384,128]{3,2,1,0:T(8,128)(2,1)}, bf16[2,8,384,128]{3,2,1,0:T(8,128)(2,1)}, u32[]{:S(2)}, u32[]{:S(2)}) collective-permute-start(bf16[2,8,384,128]{3,2,1,0:T(8,128)(2,1)} %project_text.1.refs_7_), channel_id=1, source_target_pairs={{16,0},{18,2},{20,4},{22,6},{24,8},{26,10},{28,12},{30,14},{0,16},... | collective-permute-start | bytes 4718600 | tf_op jit(solution)/shard_map/ppermute | solution.py:21
  34.3 3.6 %copy-start.23 = (s32[16,2]{0,1:T(2,128)S(1)}, s32[16,2]{0,1:T(2,128)}, u32[]{:S(2)}) copy-start(s32[16,2]{0,1:T(2,128)} %param.16) | copy-start | bytes 388
  40.5 4.8 %copy-start.19 = (bf16[1,2,512,2,1024]{4,2,1,3,0:T(8,128)(2,1)S(1)}, bf16[1,2,512,2,1024]{4,2,1,3,0:T(8,128)(2,1)}, u32[]{:S(2)}) copy-start(bf16[1,2,512,2,1024]{4,2,1,3,0:T(8,128)(2,1)} %copy.62) | copy-start | bytes 12582916
  45.3 2.5 copy-start.25
  75.7 0.8 copy-start.2
  76.5 132.6 %collective-permute-start.4 = (bf16[384,2,1024]{2,1,0:T(2,128)(2,1)}, bf16[384,2,1024]{2,1,0:T(2,128)(2,1)S(1)}, u32[]{:S(2)}, u32[]{:S(2)}) collective-permute-start(bf16[384,2,1024]{2,1,0:T(2,128)(2,1)} %hold.6), channel_id=1, source_target_pairs={{16,0},{18,2},{20,4},{22,6},{24,8},{26,10},{28,12},{30,14},{0,16},... | collective-permute-start | bytes 4718600 | tf_op jit(solution)/shard_map/ppermute | solution.py:21
  120.6 1.0 copy-start.3
  121.7 2.7 %copy-start.7 = (bf16[2,64,2,1024]{3,2,1,0:T(2,128)(2,1)}, bf16[2,64,2,1024]{3,2,1,0:T(2,128)(2,1)S(1)}, u32[]{:S(2)}) copy-start(bf16[2,64,2,1024]{3,2,1,0:T(2,128)(2,1)S(1)} %collective-permute-done.6.zone_ref) | copy-start | bytes 1572868
  154.4 2.2 copy-start.9
  154.4 2.2 copy-start.17
  154.4 82.8 %collective-permute-start.1 = (bf16[240,2,1024]{2,1,0:T(2,128)(2,1)}, bf16[240,2,1024]{2,1,0:T(2,128)(2,1)S(1)}, u32[]{:S(2)}, u32[]{:S(2)}) collective-permute-start(bf16[240,2,1024]{2,1,0:T(2,128)(2,1)} %hold.4), channel_id=1, source_target_pairs={{16,0},{18,2},{20,4},{22,6},{24,8},{26,10},{28,12},{30,14},{0,16},... | collective-permute-start | bytes 2949128 | tf_op jit(solution)/shard_map/ppermute | solution.py:21
  156.7 1.6 copy-start.10
  158.2 1.6 copy-start.11
  159.8 1.6 copy-start.12
  161.4 1.5 copy-start.13
  162.9 1.4 copy-start.14
  164.3 1.6 copy-start.18
  165.9 38.1 %copy-start.24 = (s32[16,2]{0,1:T(2,128)S(1)}, s32[16,2]{0,1:T(2,128)}, u32[]{:S(2)}) copy-start(s32[16,2]{0,1:T(2,128)} %param.19) | copy-start | bytes 388
  165.9 38.5 %copy-start.4 = (bf16[2,64,2,1024]{3,2,1,0:T(2,128)(2,1)S(1)}, bf16[2,64,2,1024]{3,2,1,0:T(2,128)(2,1)}, u32[]{:S(2)}) copy-start(bf16[2,64,2,1024]{3,2,1,0:T(2,128)(2,1)} %copy-done.2) | copy-start | bytes 1572868
  202.0 36.1 %collective-permute-start.7 = (f32[2,64,256]{2,1,0:T(8,128)}, f32[2,64,256]{2,1,0:T(8,128)S(1)}, u32[]{:S(2)}, u32[]{:S(2)}) collective-permute-start(f32[2,64,256]{2,1,0:T(8,128)} %constant_dynamic-slice_fusion), channel_id=1, source_target_pairs={{1,0},{0,1},{3,2},{2,3},{5,4},{4,5},{7,6},{6,7},{9,8},{8,9},{11,10... | collective-permute-start | bytes 393224 | tf_op jit(solution)/shard_map/ppermute | solution.py:21
  204.4 1.0 copy-start.8
  206.6 32.3 %copy-start.22 = (f32[1,2,256,64]{2,3,1,0:T(8,128)S(1)}, f32[1,2,256,64]{2,3,1,0:T(8,128)}, u32[]{:S(2)}) copy-start(f32[1,2,256,64]{2,3,1,0:T(8,128)} %param.15) | copy-start | bytes 393220
  209.1 1.2 copy-start
  210.3 29.3 %copy-start.1 = (bf16[384,2,1024]{2,1,0:T(2,128)(2,1)S(1)}, bf16[384,2,1024]{2,1,0:T(2,128)(2,1)}, u32[]{:S(2)}) copy-start(bf16[384,2,1024]{2,1,0:T(2,128)(2,1)} %copy-done) | copy-start | bytes 4718596
  210.3 29.3 %copy-start.15 = (bf16[80,2,1024]{2,1,0:T(2,128)(2,1)S(1)}, bf16[80,2,1024]{2,1,0:T(2,128)(2,1)}, u32[]{:S(2)}) copy-start(bf16[80,2,1024]{2,1,0:T(2,128)(2,1)} %hold.7.refs_0_) | copy-start | bytes 983044
  210.3 39.7 %collective-permute-start.5 = (bf16[80,2,1024]{2,1,0:T(2,128)(2,1)}, bf16[80,2,1024]{2,1,0:T(2,128)(2,1)}, u32[]{:S(2)}, u32[]{:S(2)}) collective-permute-start(bf16[80,2,1024]{2,1,0:T(2,128)(2,1)} %hold.7.refs_0_), channel_id=1, source_target_pairs={{16,0},{18,2},{20,4},{22,6},{24,8},{26,10},{28,12},{30,14},{0,16},... | collective-permute-start | bytes 983048 | tf_op jit(solution)/shard_map/ppermute | solution.py:21
  237.2 1.0 copy-start.5
  238.1 16.5 %collective-permute-start.2 = (bf16[64,2,1024]{2,1,0:T(2,128)(2,1)}, bf16[64,2,1024]{2,1,0:T(2,128)(2,1)S(1)}, u32[]{:S(2)}, u32[]{:S(2)}) collective-permute-start(bf16[64,2,1024]{2,1,0:T(2,128)(2,1)} %hold.5.refs_0_), channel_id=1, source_target_pairs={{16,0},{18,2},{20,4},{22,6},{24,8},{26,10},{28,12},{30,14},{0,16},... | collective-permute-start | bytes 786440 | tf_op jit(solution)/shard_map/ppermute | solution.py:21
  239.6 3.1 %copy-start.6 = (bf16[240,2,1024]{2,1,0:T(2,128)(2,1)S(1)}, bf16[240,2,1024]{2,1,0:T(2,128)(2,1)}, u32[]{:S(2)}) copy-start(bf16[240,2,1024]{2,1,0:T(2,128)(2,1)} %copy-done.5) | copy-start | bytes 2949124
  239.6 3.1 %copy-start.16 = (bf16[64,2,1024]{2,1,0:T(2,128)(2,1)S(1)}, bf16[64,2,1024]{2,1,0:T(2,128)(2,1)}, u32[]{:S(2)}) copy-start(bf16[64,2,1024]{2,1,0:T(2,128)(2,1)} %hold.5.refs_0_) | copy-start | bytes 786436

commit v5 on v4

--- a/solution.py
+++ b/solution.py
@@ -40,13 +40,13 @@
     return near, jnp.where(outside, lists, -1), jnp.where(sources > 0, sources, zone)
 
 
-def swap_rows(near_ref, far_ref, slot, zone, piece, start, stop):
+def swap_rows(pairs, slots, slot, zone, piece, start, stop):
     count = zone.shape[0] - 1
 
     def step(k, carry):
-        far = far_ref[slot * count + k]
+        far = pairs[(slots + slot) * count + k]
         here = jnp.logical_and(far >= start, far < stop)
-        near_row = jnp.where(here, near_ref[slot * count + k], count)
+        near_row = jnp.where(here, pairs[slot * count + k], count)
         far_row = jnp.where(here, far - start, stop - start)
         moved = zone[near_row]
         zone[near_row] = piece[far_row]
@@ -68,30 +68,13 @@
         copy.wait()
 
 
-def take_kernel(fresh_ref, out_ref, stage, sems):
-    slots, rows = out_ref.shape[:2]
-    relay([(fresh_ref.at[0, s, :rows], stage.at[s], out_ref.at[s]) for s in range(slots)], sems)
-
-
-def take_head(fresh_kv, rows):
-    shape = (fresh_kv.shape[1], rows) + fresh_kv.shape[3:]
-    return pl.pallas_call(
-        take_kernel,
-        out_shape=jax.ShapeDtypeStruct(shape, fresh_kv.dtype),
-        in_specs=[pl.BlockSpec(memory_space=HBM)],
-        out_specs=pl.BlockSpec(memory_space=HBM),
-        scratch_shapes=[pltpu.VMEM(shape, fresh_kv.dtype), pltpu.SemaphoreType.DMA((2, shape[0]))],
-        cost_estimate=pl.CostEstimate(flops=0, bytes_accessed=4 * math.prod(shape), transcendentals=0),
-        compiler_params=pltpu.CompilerParams(vmem_limit_bytes=WIDE_LIMIT),
-        name="take_head",
-    )(fresh_kv)
-
-
-def arrange_kernel(slots, pieces, near_ref, far_ref, fresh_ref, after_ref, *refs):
+def arrange_kernel(slots, pieces, pairs_ref, fresh_ref, after_ref, *refs):
     zone_out, piece_outs = refs[0], refs[1 : 1 + len(pieces)]
-    zones, rests, sems = refs[1 + len(pieces) :]
+    pairs, zones, rests, sems = refs[1 + len(pieces) :]
     count = zones.shape[1] - 1
     rest_rows = rests.shape[1] - 1
+    copy_pairs = pltpu.make_async_copy(pairs_ref, pairs, sems.at[3 * slots + len(pieces)])
+    copy_pairs.start()
     copies_in = []
     for slot in range(slots):
         copies_in.append(
@@ -106,13 +89,12 @@
         )
         for copy in copies_in[-1]:
             copy.start()
+    copy_pairs.wait()
     copies_out = []
     for slot in range(slots):
         for copy in copies_in[slot]:
             copy.wait()
-        swap_rows(
-            near_ref, far_ref, slot, zones.at[slot], rests.at[slot], 2 * count, 2 * count + rest_rows
-        )
+        swap_rows(pairs, slots, slot, zones.at[slot], rests.at[slot], 2 * count, 2 * count + rest_rows)
         copies_out.append(
             pltpu.make_async_copy(zones.at[slot, :count], zone_out.at[slot], sems.at[2 * slots + slot])
         )
@@ -128,25 +110,26 @@
         copy.wait()
 
 
-def arrange(near, far, fresh_kv, pieces, after):
+def arrange(pairs, fresh_kv, pieces, after):
     slots, rows = fresh_kv.shape[1:3]
     tail = fresh_kv.shape[3:]
-    count = near.shape[0] // slots
+    count = pairs.shape[0] // (2 * slots)
     outs = pl.pallas_call(
         functools.partial(arrange_kernel, slots, pieces),
         out_shape=[jax.ShapeDtypeStruct((slots, count) + tail, fresh_kv.dtype)]
         + [jax.ShapeDtypeStruct((stop - start,) + tail, fresh_kv.dtype) for _, start, stop in pieces],
-        in_specs=[pl.BlockSpec(memory_space=SMEM)] * 2 + [pl.BlockSpec(memory_space=HBM)] * 2,
+        in_specs=[pl.BlockSpec(memory_space=HBM)] * 3,
         out_specs=[pl.BlockSpec(memory_space=HBM)] * (1 + len(pieces)),
         scratch_shapes=[
+            pltpu.SMEM(pairs.shape, pairs.dtype),
             pltpu.VMEM((slots, count + 1) + tail, fresh_kv.dtype),
             pltpu.VMEM((slots, rows - 2 * count + 1) + tail, fresh_kv.dtype),
-            pltpu.SemaphoreType.DMA((3 * slots + len(pieces),)),
+            pltpu.SemaphoreType.DMA((3 * slots + len(pieces) + 1,)),
         ],
         cost_estimate=pl.CostEstimate(flops=0, bytes_accessed=4 * fresh_kv.size, transcendentals=0),
         compiler_params=pltpu.CompilerParams(vmem_limit_bytes=WIDE_LIMIT),
         name="arrange",
-    )(near, far, fresh_kv, after)
+    )(pairs, fresh_kv, after)
     return outs[0], outs[1:]
 
 
@@ -174,10 +157,11 @@
     )(raw, zone)
 
 
-def restore_kernel(slot, start, stop, near_ref, far_ref, piece_ref, whole_ref, *refs):
-    out_ref, zone, piece, sems = refs[-4:]
+def restore_kernel(slot, start, stop, pairs_ref, piece_ref, whole_ref, *refs):
+    out_ref, pairs, zone, piece, sems = refs[-5:]
     count = zone.shape[0] - 1
     inner = [
+        pltpu.make_async_copy(pairs_ref, pairs, sems.at[4]),
         pltpu.make_async_copy(piece_ref, piece.at[: stop - start], sems.at[0]),
         pltpu.make_async_copy(out_ref.at[slot, count : 2 * count], zone.at[:count], sems.at[1]),
     ]
@@ -185,7 +169,7 @@
         copy.start()
     for copy in inner:
         copy.wait()
-    swap_rows(near_ref, far_ref, slot, zone, piece, start, stop)
+    swap_rows(pairs, out_ref.shape[0], slot, zone, piece, start, stop)
     outer = [
         pltpu.make_async_copy(piece.at[: stop - start], out_ref.at[slot, start:stop], sems.at[2]),
         pltpu.make_async_copy(zone.at[:count], out_ref.at[slot, count : 2 * count], sems.at[3]),
@@ -196,25 +180,26 @@
         copy.wait()
 
 
-def restore(near, far, block, whole, piece, after=()):
+def restore(pairs, block, whole, piece, after=()):
     slot, start, stop = piece
     tail = whole.shape[2:]
-    count = near.shape[0] // whole.shape[0]
+    count = pairs.shape[0] // (2 * whole.shape[0])
     return pl.pallas_call(
         functools.partial(restore_kernel, slot, start, stop),
         out_shape=jax.ShapeDtypeStruct(whole.shape, whole.dtype),
-        in_specs=[pl.BlockSpec(memory_space=SMEM)] * 2 + [pl.BlockSpec(memory_space=HBM)] * (2 + len(after)),
+        in_specs=[pl.BlockSpec(memory_space=HBM)] * (3 + len(after)),
         out_specs=pl.BlockSpec(memory_space=HBM),
         scratch_shapes=[
+            pltpu.SMEM(pairs.shape, pairs.dtype),
             pltpu.VMEM((count + 1,) + tail, whole.dtype),
             pltpu.VMEM((stop - start + 1,) + tail, whole.dtype),
-            pltpu.SemaphoreType.DMA((4,)),
+            pltpu.SemaphoreType.DMA((5,)),
         ],
-        input_output_aliases={3: 0},
+        input_output_aliases={2: 0},
         cost_estimate=pl.CostEstimate(flops=0, bytes_accessed=4 * block.size, transcendentals=0),
         compiler_params=pltpu.CompilerParams(vmem_limit_bytes=VMEM_LIMIT),
         name="restore",
-    )(near, far, block, whole, *after)
+    )(pairs, block, whole, *after)
 
 
 def hold_kernel(block_ref, after_ref, out_ref):
@@ -373,19 +358,20 @@
     listed_count = refresh_rows.shape[2]
     hot_rows = 2 * listed_count
 
-    raw = take_head(fresh_kv, listed_count)
+    raw = fresh_kv[0, :, :listed_count]
     raw_in = from_behind(raw, "grp", half_groups)
 
     my_list = lax.dynamic_index_in_dim(refresh_rows, my_group, 0, keepdims=False)
     partner_list = lax.dynamic_index_in_dim(refresh_rows, partner, 0, keepdims=False)
     near, far, sources = swap_pairs(jnp.stack([my_list, partner_list]))
+    pairs = jnp.stack([near, far], axis=1).reshape(2, -1)
 
     first_cut = hot_rows + (img_rows - hot_rows) * 5 // 8
     last_cut = img_rows - listed_count
     final = slots - 1
     pieces = [(slot, hot_rows, img_rows) for slot in range(final)]
     pieces += [(final, hot_rows, first_cut), (final, first_cut, last_cut), (final, last_cut, img_rows)]
-    zone, blocks = arrange(near[0].reshape(-1), far[0].reshape(-1), fresh_kv, pieces, raw)
+    zone, blocks = arrange(pairs[0], fresh_kv, pieces, raw)
     zone_in = from_behind(zone, "grp", half_groups)
     w_t = w_velocity.T
     text_own = project_text(text[:, :, 0], text[:, :, 1], w_t, zone)
@@ -458,9 +444,7 @@
 
     next_stale = join_head(raw_in, zone_in, fresh.shape)
     for index, piece in enumerate(pieces):
-        next_stale = restore(
-            near[1].reshape(-1), far[1].reshape(-1), arrived[index], next_stale, piece, held[index + 2 : index + 3]
-        )
+        next_stale = restore(pairs[1], arrived[index], next_stale, piece, held[index + 2 : index + 3])
     return (next_stale[None], velocity[None], latent_next[None])
 
 

time: 259 us -> 257 us (level)
  Pallas kernels: 64.8 us -> 60.2 us
    unnamed x55 -> x53, local copies, waits for them, and re-layouts: 23.9 us -> 25.6 us
  transfers between devices with their start and end apart: 8 -> 8, of which waited for: 7 -> 7; matrix products, arithmetic and copies ran while one was open for 12% -> 13% of each run, Pallas kernels for 23% -> 23%
where the time goes in v5:
time: 257 us; the launch traced here: 256 us
  waiting for transfers between devices  137 us (53%)
  Pallas kernels  60.2 us (23%)
  local copies, waits for them, and re-layouts  43.5 us (17%)
  starting transfers between devices  8.92 us (3%)
  other arithmetic  5.37 us (2%)
    ppermute x8, waiting for transfers between devices, from_behind(): return lax.ppermute(block, axis, route)  137 us
    pallas_call x1, Pallas kernels, attention(): pl.pallas_call(functools.partial(attention_kernel, text_rows), grid=(slot...  35.5 us
    unnamed x53, local copies, waits for them, and re-layouts  25.6 us
    pallas_call x1, Pallas kernels, project_text(): pl.pallas_call(text_kernel, grid=(slots, heads), out_shape=jax.ShapeDtype...  10.1 us
    pallas_call x4, Pallas kernels, restore(): pl.pallas_call(functools.partial(restore_kernel, slot, start, stop), out_...  9.67 us
    ppermute x8, starting transfers between devices, from_behind(): return lax.ppermute(block, axis, route)  8.92 us
  transfers between devices with their start and end apart: 8, of which 7 were waited for; matrix products, arithmetic and copies ran while one was open for 13% of the time, Pallas kernels for 23%

profile of v5, /device:TPU:0, one launch (start us, length us, event | category | flops | bytes accessed | tf_op | source)
XLA Modules:
  0.0 256.2 jit_solution(1192926822230321383)
XLA Ops:
  0.6 1.4 slice_bitcast_fusion.6.after_ref
  2.1 4.1 %collective-permute-start.3 = (bf16[2,64,2,1024]{3,2,1,0:T(2,128)(2,1)S(1)}, bf16[2,64,2,1024]{3,2,1,0:T(2,128)(2,1)S(1)}, u32[]{:S(2)}, u32[]{:S(2)}) collective-permute-start(bf16[2,64,2,1024]{3,2,1,0:T(2,128)(2,1)S(1)} %slice_bitcast_fusion.6.after_ref), channel_id=1, source_target_pairs={{16,0},{18,2},{20,4},{22,6},{24,8},{26,10},{28,12},{30,14},{0,16},... | collective-permute-start | bytes 1572872 | tf_op jit(solution)/shard_map/ppermute | solution.py:21
  6.2 0.7 constant_dynamic-slice_fusion.4
  6.9 0.1 compare_reduce_fusion
  7.0 0.2 convert_reduce_fusion.1
  7.3 0.3 select_reduce_fusion
  7.6 0.6 squeeze.61.pairs_ref
  8.2 3.7 %arrange.1 = (bf16[2,64,2,1024]{3,2,1,0:T(2,128)(2,1)}, bf16[384,2,1024]{2,1,0:T(2,128)(2,1)}, bf16[240,2,1024]{2,1,0:T(2,128)(2,1)}, bf16[80,2,1024]{2,1,0:T(2,128)(2,1)}, bf16[64,2,1024]{2,1,0:T(2,128)(2,1)}) custom-call(s32[256]{0:T(256)} %squeeze.61.pairs_ref, bf16[1,2,512,2,1024]{4,3,2,1,0:T(2,128)(2,1)} %fresh_ref.1, bf16[2,64,2,1024]{3,2,1,0:T(2,128)(2,1)} %copy-done.21), custom_call_target="tpu_custom_call" | custom-call | bytes 8388608 | tf_op jit(solution)/shard_map/arrange/pallas_call | solution.py:117
  11.9 0.2 collective-permute-start.6
  12.1 2.2 copy.68
  14.3 1.5 slice_bitcast_fusion.4
  15.8 10.1 %project_text.1.refs_7_ = bf16[2,8,384,128]{3,2,1,0:T(8,128)(2,1)} custom-call(bf16[2,256,1024]{2,1,0:T(8,128)(2,1)} %get-tuple-element.24.k_ref, bf16[2,256,1024]{2,1,0:T(8,128)(2,1)} %get-tuple-element.23.v_ref, bf16[64,1024]{1,0:T(8,128)(2,1)} %bitcast.63, bf16[2,64,2,1024]{3,2,1,0:T(2,128)(2,1)} %get-tuple-element.10.after_ref), custom_call_target="tpu_custom_call" | custom-call | flops 67108864 | bytes 4194304 | tf_op jit(solution)/shard_map/project_text/pallas_call | solution.py:241
  25.9 2.8 %collective-permute-start = (bf16[2,8,384,128]{3,2,1,0:T(8,128)(2,1)}, bf16[2,8,384,128]{3,2,1,0:T(8,128)(2,1)}, u32[]{:S(2)}, u32[]{:S(2)}) collective-permute-start(bf16[2,8,384,128]{3,2,1,0:T(8,128)(2,1)} %project_text.1.refs_7_), channel_id=1, source_target_pairs={{16,0},{18,2},{20,4},{22,6},{24,8},{26,10},{28,12},{30,14},{0,16},... | collective-permute-start | bytes 4718600 | tf_op jit(solution)/shard_map/ppermute | solution.py:21
  28.7 5.7 %copy.67 = bf16[1,2,512,2,1024]{4,2,1,3,0:T(8,128)(2,1)} copy(bf16[1,2,512,2,1024]{4,3,2,1,0:T(2,128)(2,1)} %fresh_ref.1) | data formatting | bytes 8388608 | tf_op args[1]
  34.4 3.3 %copy.66 = bf16[1,2,512,2,1024]{4,2,1,3,0:T(8,128)(2,1)} copy(bf16[1,2,512,2,1024]{4,3,2,1,0:T(2,128)(2,1)S(1)} %copy-done.20) | data formatting | bytes 8388608 | tf_op args[2]
  37.7 0.1 fusion
  37.9 0.1 pad_add_fusion.2
  37.9 0.1 compare_reduce_fusion.1
  38.0 0.2 fusion.4
  38.3 0.1 and_bitcast_fusion.1
  38.3 0.1 and_bitcast_fusion
  38.5 0.7 copy.58
  39.2 1.4 broadcast_select_fusion.refs_10_
  40.6 4.8 %slice_bitcast_fusion.2 = (bf16[2,512,1024]{2,1,0:T(8,128)(2,1)}, bf16[2,512,1024]{2,1,0:T(8,128)(2,1)}) fusion(bf16[2,512,2,1024]{3,1,0,2:T(8,128)(2,1)} %bitcast.68), kind=kLoop, calls=%fused_computation.4 | loop fusion | bytes 8388608 | tf_op jit(solution)/shard_map/squeeze | solution.py:412
  45.4 2.5 slice_bitcast_fusion
  47.9 0.1 dynamic_slice.29
  48.0 0.1 broadcast_compare_fusion
  48.1 27.0 %collective-permute-done.3.after_ref.raw_ref = bf16[2,64,2,1024]{3,2,1,0:T(2,128)(2,1)S(1)} collective-permute-done((bf16[2,64,2,1024]{3,2,1,0:T(2,128)(2,1)S(1)}, bf16[2,64,2,1024]{3,2,1,0:T(2,128)(2,1)S(1)}, u32[]{:S(2)}, u32[]{:S(2)}) %collective-permute-start.3) | collective-permute-done | bytes 524320 | tf_op jit(solution)/shard_map/ppermute | solution.py:21
  75.1 0.8 copy-done.2
  75.9 0.1 compare_convert_fusion
  76.0 44.0 %collective-permute-done.6.zone_ref = bf16[2,64,2,1024]{3,2,1,0:T(2,128)(2,1)S(1)} collective-permute-done((bf16[2,64,2,1024]{3,2,1,0:T(2,128)(2,1)}, bf16[2,64,2,1024]{3,2,1,0:T(2,128)(2,1)S(1)}, u32[]{:S(2)}, u32[]{:S(2)}) %collective-permute-start.6) | collective-permute-done | bytes 524320 | tf_op jit(solution)/shard_map/ppermute | solution.py:21
  120.0 1.0 copy-done.3
  121.1 0.2 join_head.3
  121.3 2.5 fusion.7
  123.7 30.1 %collective-permute-done.after_ref.refs_8_ = bf16[2,8,384,128]{3,2,1,0:T(8,128)(2,1)} collective-permute-done((bf16[2,8,384,128]{3,2,1,0:T(8,128)(2,1)}, bf16[2,8,384,128]{3,2,1,0:T(8,128)(2,1)}, u32[]{:S(2)}, u32[]{:S(2)}) %collective-permute-start) | collective-permute-done | bytes 1572896 | tf_op jit(solution)/shard_map/ppermute | solution.py:21
  153.8 2.1 copy_bitcast_fusion.3
  155.9 0.1 copy-done.9
  156.1 1.6 copy-done.10
  157.7 1.6 copy-done.11
  159.2 1.6 copy-done.12
  160.8 1.5 copy-done.13
  162.3 1.4 copy-done.14
  163.7 1.6 copy-done.18
  165.3 35.5 %attention.1 = f32[2,64,512]{2,1,0:T(8,128)S(1)} custom-call(bf16[2,512,1024]{2,1,0:T(8,128)(2,1)S(1)} %bitcast.65, bf16[2,512,1024]{2,1,0:T(8,128)(2,1)S(1)} %copy-done.10, bf16[2,512,1024]{2,1,0:T(8,128)(2,1)S(1)} %copy-done.9, bf16[2,512,1024]{2,1,0:T(8,128)(2,1)S(1)} %copy-done.12, bf16[2,512,1024]{2,1,0:T(8,128)(2,1)S(1)} %copy-done.11, ...), custom_call_target="tpu_custom_call" | custom-call | flops 5234491392 | bytes 25165824 | tf_op jit(solution)/shard_map/attention/pallas_call | solution.py:320
  200.8 0.7 constant_dynamic-slice_fusion
  201.5 1.8 collective-permute-start.7
  203.3 0.1 multiply_reduce_fusion
  203.4 0.1 squeeze.60.pairs_ref
  203.5 0.2 multiply_reduce_fusion.1
  203.7 1.0 copy-done.8
  204.8 1.1 join_head.2.whole_ref
  205.8 2.7 %collective-permute-done.4.after_ref.piece_ref = bf16[384,2,1024]{2,1,0:T(2,128)(2,1)S(1)} collective-permute-done((bf16[384,2,1024]{2,1,0:T(2,128)(2,1)}, bf16[384,2,1024]{2,1,0:T(2,128)(2,1)S(1)}, u32[]{:S(2)}, u32[]{:S(2)}) %collective-permute-start.4) | collective-permute-done | bytes 1572896 | tf_op jit(solution)/shard_map/ppermute | solution.py:21
  208.5 1.2 copy-done
  209.7 0.0 collective-permute-start.5
  209.7 26.9 %collective-permute-done.1.after_ref.piece_ref = bf16[240,2,1024]{2,1,0:T(2,128)(2,1)S(1)} collective-permute-done((bf16[240,2,1024]{2,1,0:T(2,128)(2,1)}, bf16[240,2,1024]{2,1,0:T(2,128)(2,1)S(1)}, u32[]{:S(2)}, u32[]{:S(2)}) %collective-permute-start.1) | collective-permute-done | bytes 983072 | tf_op jit(solution)/shard_map/ppermute | solution.py:21
  236.6 1.0 copy-done.5
  237.6 0.7 fusion.2
  238.2 1.6 fusion.1
  239.9 2.7 %restore.4.whole_ref = bf16[2,512,2,1024]{3,2,1,0:T(2,128)(2,1)} custom-call(s32[256]{0:T(256)S(1)} %squeeze.60.pairs_ref, bf16[384,2,1024]{2,1,0:T(2,128)(2,1)S(1)} %copy-done.1, bf16[2,512,2,1024]{3,2,1,0:T(2,128)(2,1)} %join_head.2.whole_ref, bf16[80,2,1024]{2,1,0:T(2,128)(2,1)S(1)} %copy-done.15), custom_call_target="tpu_custom_call", output_to_operand_aliasing={{}: (2, {})} | custom-call | bytes 3145728 | tf_op jit(solution)/shard_map/restore/pallas_call | solution.py:187
  242.6 2.6 %restore.5.whole_ref = bf16[2,512,2,1024]{3,2,1,0:T(2,128)(2,1)} custom-call(s32[256]{0:T(256)S(1)} %squeeze.60.pairs_ref, bf16[240,2,1024]{2,1,0:T(2,128)(2,1)S(1)} %copy-done.6, bf16[2,512,2,1024]{3,2,1,0:T(2,128)(2,1)} %restore.4.whole_ref, bf16[64,2,1024]{2,1,0:T(2,128)(2,1)S(1)} %copy-done.16), custom_call_target="tpu_custom_call", output_to_operand_aliasing={{}: (2, {})} | custom-call | bytes 1966080 | tf_op jit(solution)/shard_map/restore/pallas_call | solution.py:187
  245.2 4.1 %collective-permute-done.5.piece_ref = bf16[80,2,1024]{2,1,0:T(2,128)(2,1)} collective-permute-done((bf16[80,2,1024]{2,1,0:T(2,128)(2,1)}, bf16[80,2,1024]{2,1,0:T(2,128)(2,1)}, u32[]{:S(2)}, u32[]{:S(2)}) %collective-permute-start.5) | collective-permute-done | bytes 327712 | tf_op jit(solution)/shard_map/ppermute | solution.py:21
  249.3 2.2 restore.6.whole_ref
  251.6 2.5 collective-permute-done.2.piece_ref
  254.0 2.1 restore.7
  (61 shorter events, 0.2 us)
Async XLA Ops:
  2.0 6.2 %copy-start.21 = (bf16[2,64,2,1024]{3,2,1,0:T(2,128)(2,1)}, bf16[2,64,2,1024]{3,2,1,0:T(2,128)(2,1)S(1)}, u32[]{:S(2)}) copy-start(bf16[2,64,2,1024]{3,2,1,0:T(2,128)(2,1)S(1)} %slice_bitcast_fusion.6.after_ref) | copy-start | bytes 1572868
  2.1 73.0 %collective-permute-start.3 = (bf16[2,64,2,1024]{3,2,1,0:T(2,128)(2,1)S(1)}, bf16[2,64,2,1024]{3,2,1,0:T(2,128)(2,1)S(1)}, u32[]{:S(2)}, u32[]{:S(2)}) collective-permute-start(bf16[2,64,2,1024]{3,2,1,0:T(2,128)(2,1)S(1)} %slice_bitcast_fusion.6.after_ref), channel_id=1, source_target_pairs={{16,0},{18,2},{20,4},{22,6},{24,8},{26,10},{28,12},{30,14},{0,16},... | collective-permute-start | bytes 1572872 | tf_op jit(solution)/shard_map/ppermute | solution.py:21
  11.9 108.1 %collective-permute-start.6 = (bf16[2,64,2,1024]{3,2,1,0:T(2,128)(2,1)}, bf16[2,64,2,1024]{3,2,1,0:T(2,128)(2,1)S(1)}, u32[]{:S(2)}, u32[]{:S(2)}) collective-permute-start(bf16[2,64,2,1024]{3,2,1,0:T(2,128)(2,1)} %get-tuple-element.10.after_ref), channel_id=1, source_target_pairs={{16,0},{18,2},{20,4},{22,6},{24,8},{26,10},{28,12},{30,14},{0,16},... | collective-permute-start | bytes 1572872 | tf_op jit(solution)/shard_map/ppermute | solution.py:21
  25.9 127.9 %collective-permute-start = (bf16[2,8,384,128]{3,2,1,0:T(8,128)(2,1)}, bf16[2,8,384,128]{3,2,1,0:T(8,128)(2,1)}, u32[]{:S(2)}, u32[]{:S(2)}) collective-permute-start(bf16[2,8,384,128]{3,2,1,0:T(8,128)(2,1)} %project_text.1.refs_7_), channel_id=1, source_target_pairs={{16,0},{18,2},{20,4},{22,6},{24,8},{26,10},{28,12},{30,14},{0,16},... | collective-permute-start | bytes 4718600 | tf_op jit(solution)/shard_map/ppermute | solution.py:21
  28.7 5.7 %copy-start.20 = (bf16[1,2,512,2,1024]{4,3,2,1,0:T(2,128)(2,1)S(1)}, bf16[1,2,512,2,1024]{4,3,2,1,0:T(2,128)(2,1)}, u32[]{:S(2)}) copy-start(bf16[1,2,512,2,1024]{4,3,2,1,0:T(2,128)(2,1)} %param.12) | copy-start | bytes 12582916
  34.4 3.6 %copy-start.22 = (s32[16,2]{0,1:T(2,128)S(1)}, s32[16,2]{0,1:T(2,128)}, u32[]{:S(2)}) copy-start(s32[16,2]{0,1:T(2,128)} %param.16) | copy-start | bytes 388
  40.6 4.8 %copy-start.19 = (bf16[1,2,512,2,1024]{4,2,1,3,0:T(8,128)(2,1)S(1)}, bf16[1,2,512,2,1024]{4,2,1,3,0:T(8,128)(2,1)}, u32[]{:S(2)}) copy-start(bf16[1,2,512,2,1024]{4,2,1,3,0:T(8,128)(2,1)} %copy.66) | copy-start | bytes 12582916
  45.4 2.5 copy-start.24
  75.1 0.8 copy-start.2
  75.9 132.6 %collective-permute-start.4 = (bf16[384,2,1024]{2,1,0:T(2,128)(2,1)}, bf16[384,2,1024]{2,1,0:T(2,128)(2,1)S(1)}, u32[]{:S(2)}, u32[]{:S(2)}) collective-permute-start(bf16[384,2,1024]{2,1,0:T(2,128)(2,1)} %hold.6), channel_id=1, source_target_pairs={{16,0},{18,2},{20,4},{22,6},{24,8},{26,10},{28,12},{30,14},{0,16},... | collective-permute-start | bytes 4718600 | tf_op jit(solution)/shard_map/ppermute | solution.py:21
  120.0 1.0 copy-start.3
  121.1 2.7 %copy-start.7 = (bf16[2,64,2,1024]{3,2,1,0:T(2,128)(2,1)}, bf16[2,64,2,1024]{3,2,1,0:T(2,128)(2,1)S(1)}, u32[]{:S(2)}) copy-start(bf16[2,64,2,1024]{3,2,1,0:T(2,128)(2,1)S(1)} %collective-permute-done.6.zone_ref) | copy-start | bytes 1572868
  153.8 2.2 copy-start.9
  153.8 2.2 copy-start.17
  153.8 82.8 %collective-permute-start.1 = (bf16[240,2,1024]{2,1,0:T(2,128)(2,1)}, bf16[240,2,1024]{2,1,0:T(2,128)(2,1)S(1)}, u32[]{:S(2)}, u32[]{:S(2)}) collective-permute-start(bf16[240,2,1024]{2,1,0:T(2,128)(2,1)} %hold.4), channel_id=1, source_target_pairs={{16,0},{18,2},{20,4},{22,6},{24,8},{26,10},{28,12},{30,14},{0,16},... | collective-permute-start | bytes 2949128 | tf_op jit(solution)/shard_map/ppermute | solution.py:21
  156.1 1.6 copy-start.10
  157.7 1.6 copy-start.11
  159.2 1.6 copy-start.12
  160.8 1.5 copy-start.13
  162.3 1.4 copy-start.14
  163.7 1.6 copy-start.18
  165.3 38.0 %copy-start.23 = (s32[16,2]{0,1:T(2,128)S(1)}, s32[16,2]{0,1:T(2,128)}, u32[]{:S(2)}) copy-start(s32[16,2]{0,1:T(2,128)} %param.19) | copy-start | bytes 388
  165.3 38.4 %copy-start.4 = (bf16[2,64,2,1024]{3,2,1,0:T(2,128)(2,1)S(1)}, bf16[2,64,2,1024]{3,2,1,0:T(2,128)(2,1)}, u32[]{:S(2)}) copy-start(bf16[2,64,2,1024]{3,2,1,0:T(2,128)(2,1)} %copy-done.2) | copy-start | bytes 1572868
  201.5 36.0 %collective-permute-start.7 = (f32[2,64,256]{2,1,0:T(8,128)}, f32[2,64,256]{2,1,0:T(8,128)S(1)}, u32[]{:S(2)}, u32[]{:S(2)}) collective-permute-start(f32[2,64,256]{2,1,0:T(8,128)} %constant_dynamic-slice_fusion), channel_id=1, source_target_pairs={{1,0},{0,1},{3,2},{2,3},{5,4},{4,5},{7,6},{6,7},{9,8},{8,9},{11,10... | collective-permute-start | bytes 393224 | tf_op jit(solution)/shard_map/ppermute | solution.py:21
  203.7 1.0 copy-start.8
  208.5 1.2 copy-start
  209.7 30.2 %copy-start.1 = (bf16[384,2,1024]{2,1,0:T(2,128)(2,1)S(1)}, bf16[384,2,1024]{2,1,0:T(2,128)(2,1)}, u32[]{:S(2)}) copy-start(bf16[384,2,1024]{2,1,0:T(2,128)(2,1)} %copy-done) | copy-start | bytes 4718596
  209.7 30.2 %copy-start.15 = (bf16[80,2,1024]{2,1,0:T(2,128)(2,1)S(1)}, bf16[80,2,1024]{2,1,0:T(2,128)(2,1)}, u32[]{:S(2)}) copy-start(bf16[80,2,1024]{2,1,0:T(2,128)(2,1)} %hold.7.refs_0_) | copy-start | bytes 983044
  209.7 39.7 %collective-permute-start.5 = (bf16[80,2,1024]{2,1,0:T(2,128)(2,1)}, bf16[80,2,1024]{2,1,0:T(2,128)(2,1)}, u32[]{:S(2)}, u32[]{:S(2)}) collective-permute-start(bf16[80,2,1024]{2,1,0:T(2,128)(2,1)} %hold.7.refs_0_), channel_id=1, source_target_pairs={{16,0},{18,2},{20,4},{22,6},{24,8},{26,10},{28,12},{30,14},{0,16},... | collective-permute-start | bytes 983048 | tf_op jit(solution)/shard_map/ppermute | solution.py:21
  236.6 1.0 copy-start.5
  237.5 16.5 %collective-permute-start.2 = (bf16[64,2,1024]{2,1,0:T(2,128)(2,1)}, bf16[64,2,1024]{2,1,0:T(2,128)(2,1)S(1)}, u32[]{:S(2)}, u32[]{:S(2)}) collective-permute-start(bf16[64,2,1024]{2,1,0:T(2,128)(2,1)} %hold.5.refs_0_), channel_id=1, source_target_pairs={{16,0},{18,2},{20,4},{22,6},{24,8},{26,10},{28,12},{30,14},{0,16},... | collective-permute-start | bytes 786440 | tf_op jit(solution)/shard_map/ppermute | solution.py:21
  239.9 2.7 %copy-start.6 = (bf16[240,2,1024]{2,1,0:T(2,128)(2,1)S(1)}, bf16[240,2,1024]{2,1,0:T(2,128)(2,1)}, u32[]{:S(2)}) copy-start(bf16[240,2,1024]{2,1,0:T(2,128)(2,1)} %copy-done.5) | copy-start | bytes 2949124
  239.9 2.7 %copy-start.16 = (bf16[64,2,1024]{2,1,0:T(2,128)(2,1)S(1)}, bf16[64,2,1024]{2,1,0:T(2,128)(2,1)}, u32[]{:S(2)}) copy-start(bf16[64,2,1024]{2,1,0:T(2,128)(2,1)} %hold.5.refs_0_) | copy-start | bytes 786436

commit v6 on v5

--- a/solution.py
+++ b/solution.py
@@ -385,7 +385,11 @@
         else:
             gate = arrived[index - 2]
         held.append(hold(block, gate))
-        arrived.append(from_behind(held[-1], "grp", half_groups))
+        if index < final:
+            round_about = half_groups + half_groups // 2
+            arrived.append(from_behind(from_behind(held[-1], "grp", round_about), "grp", round_about))
+        else:
+            arrived.append(from_behind(held[-1], "grp", half_groups))
 
     my_live = lax.dynamic_index_in_dim(live_counts, my_group, 0, keepdims=False)
     partner_live = lax.dynamic_index_in_dim(live_counts, partner, 0, keepdims=False)

time: 257 us -> 265 us (1.031)
  starting transfers between devices: 8.92 us -> 16.4 us
    ppermute x8 -> x9, starting transfers between devices: 8.92 us -> 16.4 us  [from_behind(): return lax.ppermute(block, axis, route)]
    ppermute x8 -> x9, waiting for transfers between devices: 137 us -> 137 us  [from_behind(): return lax.ppermute(block, axis, route)]
  transfers between devices with their start and end apart: 8 -> 9, of which waited for: 7 -> 4; matrix products, arithmetic and copies ran while one was open for 13% -> 12% of each run, Pallas kernels for 23% -> 22%
where the time goes in v6:
time: 265 us; the launch traced here: 264 us
  waiting for transfers between devices  137 us (52%)
  Pallas kernels  60.3 us (23%)
  local copies, waits for them, and re-layouts  44.5 us (17%)
  starting transfers between devices  16.4 us (6%)
  other arithmetic  4.38 us (2%)
    ppermute x9, waiting for transfers between devices, from_behind(): return lax.ppermute(block, axis, route)  137 us
    pallas_call x1, Pallas kernels, attention(): pl.pallas_call(functools.partial(attention_kernel, text_rows), grid=(slot...  35.5 us
    unnamed x53, local copies, waits for them, and re-layouts  26.8 us
    ppermute x9, starting transfers between devices, from_behind(): return lax.ppermute(block, axis, route)  16.4 us
    pallas_call x1, Pallas kernels, project_text(): pl.pallas_call(text_kernel, grid=(slots, heads), out_shape=jax.ShapeDtype...  10.1 us
    pallas_call x4, Pallas kernels, restore(): pl.pallas_call(functools.partial(restore_kernel, slot, start, stop), out_...  9.7 us
  transfers between devices with their start and end apart: 9, of which 4 were waited for; matrix products, arithmetic and copies ran while one was open for 12% of the time, Pallas kernels for 22%

profile of v6, /device:TPU:0, one launch (start us, length us, event | category | flops | bytes accessed | tf_op | source)
XLA Modules:
  0.0 263.7 jit_solution(6281506356487231189)
XLA Ops:
  0.6 1.4 slice_bitcast_fusion.6.after_ref
  2.0 0.0 copy-start.20
  2.1 4.1 %collective-permute-start.3 = (bf16[2,64,2,1024]{3,2,1,0:T(2,128)(2,1)S(1)}, bf16[2,64,2,1024]{3,2,1,0:T(2,128)(2,1)S(1)}, u32[]{:S(2)}, u32[]{:S(2)}) collective-permute-start(bf16[2,64,2,1024]{3,2,1,0:T(2,128)(2,1)S(1)} %slice_bitcast_fusion.6.after_ref), channel_id=1, source_target_pairs={{16,0},{18,2},{20,4},{22,6},{24,8},{26,10},{28,12},{30,14},{0,16},... | collective-permute-start | bytes 1572872 | tf_op jit(solution)/shard_map/ppermute | solution.py:21
  6.2 0.7 constant_dynamic-slice_fusion.4
  6.9 0.1 compare_reduce_fusion
  7.0 0.2 convert_reduce_fusion.1
  7.3 0.3 select_reduce_fusion
  7.6 0.6 squeeze.61.pairs_ref
  8.2 3.7 %arrange.1 = (bf16[2,64,2,1024]{3,2,1,0:T(2,128)(2,1)}, bf16[384,2,1024]{2,1,0:T(2,128)(2,1)}, bf16[240,2,1024]{2,1,0:T(2,128)(2,1)}, bf16[80,2,1024]{2,1,0:T(2,128)(2,1)}, bf16[64,2,1024]{2,1,0:T(2,128)(2,1)}) custom-call(s32[256]{0:T(256)} %squeeze.61.pairs_ref, bf16[1,2,512,2,1024]{4,3,2,1,0:T(2,128)(2,1)} %fresh_ref.1, bf16[2,64,2,1024]{3,2,1,0:T(2,128)(2,1)} %copy-done.20), custom_call_target="tpu_custom_call" | custom-call | bytes 8388608 | tf_op jit(solution)/shard_map/arrange/pallas_call | solution.py:117
  12.0 0.1 collective-permute-start.7
  12.1 2.2 copy.68
  14.3 1.5 slice_bitcast_fusion.4
  15.8 10.1 %project_text.1.refs_7_ = bf16[2,8,384,128]{3,2,1,0:T(8,128)(2,1)} custom-call(bf16[2,256,1024]{2,1,0:T(8,128)(2,1)} %get-tuple-element.24.k_ref, bf16[2,256,1024]{2,1,0:T(8,128)(2,1)} %get-tuple-element.23.v_ref, bf16[64,1024]{1,0:T(8,128)(2,1)} %bitcast.63, bf16[2,64,2,1024]{3,2,1,0:T(2,128)(2,1)} %get-tuple-element.10.after_ref), custom_call_target="tpu_custom_call" | custom-call | flops 67108864 | bytes 4194304 | tf_op jit(solution)/shard_map/project_text/pallas_call | solution.py:241
  25.9 2.8 %collective-permute-start = (bf16[2,8,384,128]{3,2,1,0:T(8,128)(2,1)}, bf16[2,8,384,128]{3,2,1,0:T(8,128)(2,1)}, u32[]{:S(2)}, u32[]{:S(2)}) collective-permute-start(bf16[2,8,384,128]{3,2,1,0:T(8,128)(2,1)} %project_text.1.refs_7_), channel_id=1, source_target_pairs={{16,0},{18,2},{20,4},{22,6},{24,8},{26,10},{28,12},{30,14},{0,16},... | collective-permute-start | bytes 4718600 | tf_op jit(solution)/shard_map/ppermute | solution.py:21
  28.8 0.1 fusion
  28.9 0.1 pad_add_fusion.2
  28.9 0.1 compare_reduce_fusion.1
  29.1 0.2 fusion.4
  29.3 0.1 and_bitcast_fusion
  29.4 0.1 and_bitcast_fusion.1
  29.4 5.7 %copy.67 = bf16[1,2,512,2,1024]{4,2,1,3,0:T(8,128)(2,1)} copy(bf16[1,2,512,2,1024]{4,3,2,1,0:T(2,128)(2,1)} %fresh_ref.1) | data formatting | bytes 8388608 | tf_op args[1]
  35.1 3.3 %copy.66 = bf16[1,2,512,2,1024]{4,2,1,3,0:T(8,128)(2,1)} copy(bf16[1,2,512,2,1024]{4,3,2,1,0:T(2,128)(2,1)S(1)} %copy-done.19) | data formatting | bytes 8388608 | tf_op args[2]
  38.5 36.6 %collective-permute-done.3.after_ref.raw_ref = bf16[2,64,2,1024]{3,2,1,0:T(2,128)(2,1)S(1)} collective-permute-done((bf16[2,64,2,1024]{3,2,1,0:T(2,128)(2,1)S(1)}, bf16[2,64,2,1024]{3,2,1,0:T(2,128)(2,1)S(1)}, u32[]{:S(2)}, u32[]{:S(2)}) %collective-permute-start.3) | collective-permute-done | bytes 524320 | tf_op jit(solution)/shard_map/ppermute | solution.py:21
  75.1 0.8 copy-done.2
  75.9 2.8 %collective-permute-start.4 = (bf16[384,2,1024]{2,1,0:T(2,128)(2,1)}, bf16[384,2,1024]{2,1,0:T(2,128)(2,1)}, u32[]{:S(2)}, u32[]{:S(2)}) collective-permute-start(bf16[384,2,1024]{2,1,0:T(2,128)(2,1)} %hold.6), channel_id=1, source_target_pairs={{8,0},{10,2},{12,4},{14,6},{16,8},{18,10},{20,12},{22,14},{24,16},... | collective-permute-start | bytes 4718600 | tf_op jit(solution)/shard_map/ppermute | solution.py:21
  78.7 4.8 %slice_bitcast_fusion.2 = (bf16[2,512,1024]{2,1,0:T(8,128)(2,1)}, bf16[2,512,1024]{2,1,0:T(8,128)(2,1)}) fusion(bf16[2,512,2,1024]{3,1,0,2:T(8,128)(2,1)} %bitcast.68), kind=kLoop, calls=%fused_computation.4 | loop fusion | bytes 8388608 | tf_op jit(solution)/shard_map/squeeze | solution.py:416
  83.5 2.5 slice_bitcast_fusion
  86.0 0.7 copy.58
  86.7 0.1 dynamic_slice.29
  86.8 1.3 broadcast_select_fusion.refs_10_
  88.1 0.1 broadcast_compare_fusion
  88.2 64.8 %collective-permute-done.4 = bf16[384,2,1024]{2,1,0:T(2,128)(2,1)} collective-permute-done((bf16[384,2,1024]{2,1,0:T(2,128)(2,1)}, bf16[384,2,1024]{2,1,0:T(2,128)(2,1)}, u32[]{:S(2)}, u32[]{:S(2)}) %collective-permute-start.4) | collective-permute-done | bytes 1572896 | tf_op jit(solution)/shard_map/ppermute | solution.py:21
  153.0 0.1 compare_convert_fusion
  153.1 0.2 join_head.3
  153.3 2.5 fusion.7
  155.8 2.1 collective-permute-start.1
  158.0 1.9 copy_bitcast_fusion.3
  159.9 1.6 copy-done.9
  161.5 1.6 copy-done.10
  163.1 1.6 copy-done.11
  164.7 1.5 copy-done.12
  166.1 1.4 copy-done.13
  167.6 1.6 copy-done.17
  169.1 35.5 %attention.1 = f32[2,64,512]{2,1,0:T(8,128)S(1)} custom-call(bf16[2,512,1024]{2,1,0:T(8,128)(2,1)S(1)} %bitcast.65, bf16[2,512,1024]{2,1,0:T(8,128)(2,1)S(1)} %copy-done.9, bf16[2,512,1024]{2,1,0:T(8,128)(2,1)S(1)} %copy-done.8, bf16[2,512,1024]{2,1,0:T(8,128)(2,1)S(1)} %copy-done.11, bf16[2,512,1024]{2,1,0:T(8,128)(2,1)S(1)} %copy-done.10, ...), custom_call_target="tpu_custom_call" | custom-call | flops 5234491392 | bytes 25165824 | tf_op jit(solution)/shard_map/attention/pallas_call | solution.py:320
  204.7 0.7 constant_dynamic-slice_fusion
  205.3 1.5 collective-permute-start.8
  206.8 0.1 multiply_reduce_fusion
  207.0 0.1 squeeze.60.pairs_ref
  207.1 0.2 multiply_reduce_fusion.1
  207.3 1.0 copy-done.7
  208.3 1.1 join_head.2.whole_ref
  209.4 21.6 %collective-permute-done.1.after_ref.piece_ref = bf16[240,2,1024]{2,1,0:T(2,128)(2,1)S(1)} collective-permute-done((bf16[240,2,1024]{2,1,0:T(2,128)(2,1)}, bf16[240,2,1024]{2,1,0:T(2,128)(2,1)S(1)}, u32[]{:S(2)}, u32[]{:S(2)}) %collective-permute-start.1) | collective-permute-done | bytes 983072 | tf_op jit(solution)/shard_map/ppermute | solution.py:21
  231.0 0.9 copy-done.4
  231.9 1.2 copy-done
  233.1 2.9 %collective-permute-start.6 = (bf16[80,2,1024]{2,1,0:T(2,128)(2,1)}, bf16[80,2,1024]{2,1,0:T(2,128)(2,1)S(1)}, u32[]{:S(2)}, u32[]{:S(2)}) collective-permute-start(bf16[80,2,1024]{2,1,0:T(2,128)(2,1)} %hold.7.refs_0_), channel_id=1, source_target_pairs={{16,0},{18,2},{20,4},{22,6},{24,8},{26,10},{28,12},{30,14},{0,16},... | collective-permute-start | bytes 983048 | tf_op jit(solution)/shard_map/ppermute | solution.py:21
  236.0 0.7 fusion.2
  236.7 0.7 fusion.1
  237.4 1.4 copy-done.1
  238.8 1.0 copy-done.14
  239.8 2.7 %restore.4.whole_ref = bf16[2,512,2,1024]{3,2,1,0:T(2,128)(2,1)} custom-call(s32[256]{0:T(256)S(1)} %squeeze.60.pairs_ref, bf16[384,2,1024]{2,1,0:T(2,128)(2,1)S(1)} %copy-done.1, bf16[2,512,2,1024]{3,2,1,0:T(2,128)(2,1)} %join_head.2.whole_ref, bf16[80,2,1024]{2,1,0:T(2,128)(2,1)S(1)} %copy-done.14), custom_call_target="tpu_custom_call", output_to_operand_aliasing={{}: (2, {})} | custom-call | bytes 3145728 | tf_op jit(solution)/shard_map/restore/pallas_call | solution.py:187
  242.5 2.6 restore.5.whole_ref
  245.2 14.1 %collective-permute-done.6.piece_ref = bf16[80,2,1024]{2,1,0:T(2,128)(2,1)S(1)} collective-permute-done((bf16[80,2,1024]{2,1,0:T(2,128)(2,1)}, bf16[80,2,1024]{2,1,0:T(2,128)(2,1)S(1)}, u32[]{:S(2)}, u32[]{:S(2)}) %collective-permute-start.6) | collective-permute-done | bytes 327712 | tf_op jit(solution)/shard_map/ppermute | solution.py:21
  259.3 2.2 restore.6.whole_ref
  261.5 2.2 restore.7
  (63 shorter events, 0.2 us)
Async XLA Ops:
  2.0 6.2 %copy-start.20 = (bf16[2,64,2,1024]{3,2,1,0:T(2,128)(2,1)}, bf16[2,64,2,1024]{3,2,1,0:T(2,128)(2,1)S(1)}, u32[]{:S(2)}) copy-start(bf16[2,64,2,1024]{3,2,1,0:T(2,128)(2,1)S(1)} %slice_bitcast_fusion.6.after_ref) | copy-start | bytes 1572868
  2.1 73.0 %collective-permute-start.3 = (bf16[2,64,2,1024]{3,2,1,0:T(2,128)(2,1)S(1)}, bf16[2,64,2,1024]{3,2,1,0:T(2,128)(2,1)S(1)}, u32[]{:S(2)}, u32[]{:S(2)}) collective-permute-start(bf16[2,64,2,1024]{3,2,1,0:T(2,128)(2,1)S(1)} %slice_bitcast_fusion.6.after_ref), channel_id=1, source_target_pairs={{16,0},{18,2},{20,4},{22,6},{24,8},{26,10},{28,12},{30,14},{0,16},... | collective-permute-start | bytes 1572872 | tf_op jit(solution)/shard_map/ppermute | solution.py:21
  12.0 141.1 %collective-permute-start.7 = (bf16[2,64,2,1024]{3,2,1,0:T(2,128)(2,1)}, bf16[2,64,2,1024]{3,2,1,0:T(2,128)(2,1)S(1)}, u32[]{:S(2)}, u32[]{:S(2)}) collective-permute-start(bf16[2,64,2,1024]{3,2,1,0:T(2,128)(2,1)} %get-tuple-element.10.after_ref), channel_id=1, source_target_pairs={{16,0},{18,2},{20,4},{22,6},{24,8},{26,10},{28,12},{30,14},{0,16},... | collective-permute-start | bytes 1572872 | tf_op jit(solution)/shard_map/ppermute | solution.py:21
  15.8 13.2 %copy-start.22 = (s32[16,2]{0,1:T(2,128)S(1)}, s32[16,2]{0,1:T(2,128)}, u32[]{:S(2)}) copy-start(s32[16,2]{0,1:T(2,128)} %param.16) | copy-start | bytes 388
  25.9 129.9 %collective-permute-start = (bf16[2,8,384,128]{3,2,1,0:T(8,128)(2,1)}, bf16[2,8,384,128]{3,2,1,0:T(8,128)(2,1)}, u32[]{:S(2)}, u32[]{:S(2)}) collective-permute-start(bf16[2,8,384,128]{3,2,1,0:T(8,128)(2,1)} %project_text.1.refs_7_), channel_id=1, source_target_pairs={{16,0},{18,2},{20,4},{22,6},{24,8},{26,10},{28,12},{30,14},{0,16},... | collective-permute-start | bytes 4718600 | tf_op jit(solution)/shard_map/ppermute | solution.py:21
  29.4 5.7 %copy-start.19 = (bf16[1,2,512,2,1024]{4,3,2,1,0:T(2,128)(2,1)S(1)}, bf16[1,2,512,2,1024]{4,3,2,1,0:T(2,128)(2,1)}, u32[]{:S(2)}) copy-start(bf16[1,2,512,2,1024]{4,3,2,1,0:T(2,128)(2,1)} %param.12) | copy-start | bytes 12582916
  75.1 0.8 copy-start.2
  75.9 77.1 %collective-permute-start.4 = (bf16[384,2,1024]{2,1,0:T(2,128)(2,1)}, bf16[384,2,1024]{2,1,0:T(2,128)(2,1)}, u32[]{:S(2)}, u32[]{:S(2)}) collective-permute-start(bf16[384,2,1024]{2,1,0:T(2,128)(2,1)} %hold.6), channel_id=1, source_target_pairs={{8,0},{10,2},{12,4},{14,6},{16,8},{18,10},{20,12},{22,14},{24,16},... | collective-permute-start | bytes 4718600 | tf_op jit(solution)/shard_map/ppermute | solution.py:21
  78.7 4.8 %copy-start.18 = (bf16[1,2,512,2,1024]{4,2,1,3,0:T(8,128)(2,1)S(1)}, bf16[1,2,512,2,1024]{4,2,1,3,0:T(8,128)(2,1)}, u32[]{:S(2)}) copy-start(bf16[1,2,512,2,1024]{4,2,1,3,0:T(8,128)(2,1)} %copy.66) | copy-start | bytes 12582916
  83.5 3.2 %copy-start.24 = (s32[16]{0:T(128)S(1)}, s32[16]{0:T(128)}, u32[]{:S(2)}) copy-start(s32[16]{0:T(128)} %param.18) | copy-start | bytes 196
  86.0 67.1 %copy-start.3 = (bf16[2,64,2,1024]{3,2,1,0:T(2,128)(2,1)S(1)}, bf16[2,64,2,1024]{3,2,1,0:T(2,128)(2,1)}, u32[]{:S(2)}) copy-start(bf16[2,64,2,1024]{3,2,1,0:T(2,128)(2,1)} %copy-done.2) | copy-start | bytes 1572868
  153.0 78.9 %collective-permute-start.5 = (bf16[384,2,1024]{2,1,0:T(2,128)(2,1)}, bf16[384,2,1024]{2,1,0:T(2,128)(2,1)S(1)}, u32[]{:S(2)}, u32[]{:S(2)}) collective-permute-start(bf16[384,2,1024]{2,1,0:T(2,128)(2,1)} %collective-permute-done.4), channel_id=1, source_target_pairs={{8,0},{10,2},{12,4},{14,6},{16,8},{18,10},{20,12},{22,14},{24,16},... | collective-permute-start | bytes 4718600 | tf_op jit(solution)/shard_map/ppermute | solution.py:21
  153.1 2.7 %copy-start.6 = (bf16[2,64,2,1024]{3,2,1,0:T(2,128)(2,1)}, bf16[2,64,2,1024]{3,2,1,0:T(2,128)(2,1)S(1)}, u32[]{:S(2)}) copy-start(bf16[2,64,2,1024]{3,2,1,0:T(2,128)(2,1)S(1)} %collective-permute-done.7.zone_ref) | copy-start | bytes 1572868
  155.8 4.1 %copy-start.8 = (bf16[2,512,1024]{2,1,0:T(8,128)(2,1)S(1)}, bf16[2,512,1024]{2,1,0:T(8,128)(2,1)}, u32[]{:S(2)}) copy-start(bf16[2,512,1024]{2,1,0:T(8,128)(2,1)} %get-tuple-element.21.refs_2_) | copy-start | bytes 6291460
  155.8 4.1 %copy-start.16 = (bf16[1024,64]{0,1:T(8,128)(2,1)S(1)}, bf16[1024,64]{0,1:T(8,128)(2,1)}, u32[]{:S(2)}) copy-start(bf16[1024,64]{0,1:T(8,128)(2,1)} %param.14) | copy-start | bytes 393220
  155.8 75.1 %collective-permute-start.1 = (bf16[240,2,1024]{2,1,0:T(2,128)(2,1)}, bf16[240,2,1024]{2,1,0:T(2,128)(2,1)S(1)}, u32[]{:S(2)}, u32[]{:S(2)}) collective-permute-start(bf16[240,2,1024]{2,1,0:T(2,128)(2,1)} %hold.4), channel_id=1, source_target_pairs={{16,0},{18,2},{20,4},{22,6},{24,8},{26,10},{28,12},{30,14},{0,16},... | collective-permute-start | bytes 2949128 | tf_op jit(solution)/shard_map/ppermute | solution.py:21
  159.9 1.6 copy-start.9
  161.5 1.6 copy-start.10
  163.1 1.6 copy-start.11
  164.7 1.5 copy-start.12
  166.1 1.4 copy-start.13
  167.5 1.6 copy-start.17
  169.1 37.7 %copy-start.23 = (s32[16,2]{0,1:T(2,128)S(1)}, s32[16,2]{0,1:T(2,128)}, u32[]{:S(2)}) copy-start(s32[16,2]{0,1:T(2,128)} %param.19) | copy-start | bytes 388
  205.3 30.7 %collective-permute-start.8 = (f32[2,64,256]{2,1,0:T(8,128)}, f32[2,64,256]{2,1,0:T(8,128)S(1)}, u32[]{:S(2)}, u32[]{:S(2)}) collective-permute-start(f32[2,64,256]{2,1,0:T(8,128)} %constant_dynamic-slice_fusion), channel_id=1, source_target_pairs={{1,0},{0,1},{3,2},{2,3},{5,4},{4,5},{7,6},{6,7},{9,8},{8,9},{11,10... | collective-permute-start | bytes 393224 | tf_op jit(solution)/shard_map/ppermute | solution.py:21
  207.3 1.1 copy-start.7
  209.4 27.3 %copy-start.21 = (f32[1,2,256,64]{2,3,1,0:T(8,128)S(1)}, f32[1,2,256,64]{2,3,1,0:T(8,128)}, u32[]{:S(2)}) copy-start(f32[1,2,256,64]{2,3,1,0:T(8,128)} %param.15) | copy-start | bytes 393220
  231.0 0.9 copy-start.4
  231.9 29.6 %collective-permute-start.2 = (bf16[64,2,1024]{2,1,0:T(2,128)(2,1)}, bf16[64,2,1024]{2,1,0:T(2,128)(2,1)S(1)}, u32[]{:S(2)}, u32[]{:S(2)}) collective-permute-start(bf16[64,2,1024]{2,1,0:T(2,128)(2,1)} %hold.5.refs_0_), channel_id=1, source_target_pairs={{16,0},{18,2},{20,4},{22,6},{24,8},{26,10},{28,12},{30,14},{0,16},... | collective-permute-start | bytes 786440 | tf_op jit(solution)/shard_map/ppermute | solution.py:21
  231.9 1.2 copy-start
  233.1 26.2 %collective-permute-start.6 = (bf16[80,2,1024]{2,1,0:T(2,128)(2,1)}, bf16[80,2,1024]{2,1,0:T(2,128)(2,1)S(1)}, u32[]{:S(2)}, u32[]{:S(2)}) collective-permute-start(bf16[80,2,1024]{2,1,0:T(2,128)(2,1)} %hold.7.refs_0_), channel_id=1, source_target_pairs={{16,0},{18,2},{20,4},{22,6},{24,8},{26,10},{28,12},{30,14},{0,16},... | collective-permute-start | bytes 983048 | tf_op jit(solution)/shard_map/ppermute | solution.py:21
  237.4 1.4 copy-start.1
  238.8 1.0 copy-start.14
  239.8 2.7 %copy-start.5 = (bf16[240,2,1024]{2,1,0:T(2,128)(2,1)S(1)}, bf16[240,2,1024]{2,1,0:T(2,128)(2,1)}, u32[]{:S(2)}) copy-start(bf16[240,2,1024]{2,1,0:T(2,128)(2,1)} %copy-done.4) | copy-start | bytes 2949124
  239.8 2.7 %copy-start.15 = (bf16[64,2,1024]{2,1,0:T(2,128)(2,1)S(1)}, bf16[64,2,1024]{2,1,0:T(2,128)(2,1)}, u32[]{:S(2)}) copy-start(bf16[64,2,1024]{2,1,0:T(2,128)(2,1)} %hold.5.refs_0_) | copy-start | bytes 786436

commit v7 on v5

--- a/solution.py
+++ b/solution.py
@@ -68,9 +68,10 @@
         copy.wait()
 
 
-def arrange_kernel(slots, pieces, pairs_ref, fresh_ref, after_ref, *refs):
-    zone_out, piece_outs = refs[0], refs[1 : 1 + len(pieces)]
-    pairs, zones, rests, sems = refs[1 + len(pieces) :]
+def arrange_kernel(slots, pieces, pairs_ref, fresh_ref, *refs):
+    refs = refs[slots:]
+    zone_outs, piece_outs = refs[:slots], refs[slots : slots + len(pieces)]
+    pairs, zones, rests, sems = refs[slots + len(pieces) :]
     count = zones.shape[1] - 1
     rest_rows = rests.shape[1] - 1
     copy_pairs = pltpu.make_async_copy(pairs_ref, pairs, sems.at[3 * slots + len(pieces)])
@@ -96,7 +97,7 @@
             copy.wait()
         swap_rows(pairs, slots, slot, zones.at[slot], rests.at[slot], 2 * count, 2 * count + rest_rows)
         copies_out.append(
-            pltpu.make_async_copy(zones.at[slot, :count], zone_out.at[slot], sems.at[2 * slots + slot])
+            pltpu.make_async_copy(zones.at[slot, :count], zone_outs[slot], sems.at[2 * slots + slot])
         )
         copies_out[-1].start()
         for index, (piece_slot, start, stop) in enumerate(pieces):
@@ -116,10 +117,10 @@
     count = pairs.shape[0] // (2 * slots)
     outs = pl.pallas_call(
         functools.partial(arrange_kernel, slots, pieces),
-        out_shape=[jax.ShapeDtypeStruct((slots, count) + tail, fresh_kv.dtype)]
+        out_shape=[jax.ShapeDtypeStruct((count,) + tail, fresh_kv.dtype)] * slots
         + [jax.ShapeDtypeStruct((stop - start,) + tail, fresh_kv.dtype) for _, start, stop in pieces],
-        in_specs=[pl.BlockSpec(memory_space=HBM)] * 3,
-        out_specs=[pl.BlockSpec(memory_space=HBM)] * (1 + len(pieces)),
+        in_specs=[pl.BlockSpec(memory_space=HBM)] * (2 + slots),
+        out_specs=[pl.BlockSpec(memory_space=HBM)] * (slots + len(pieces)),
         scratch_shapes=[
             pltpu.SMEM(pairs.shape, pairs.dtype),
             pltpu.VMEM((slots, count + 1) + tail, fresh_kv.dtype),
@@ -129,77 +130,97 @@
         cost_estimate=pl.CostEstimate(flops=0, bytes_accessed=4 * fresh_kv.size, transcendentals=0),
         compiler_params=pltpu.CompilerParams(vmem_limit_bytes=WIDE_LIMIT),
         name="arrange",
-    )(pairs, fresh_kv, after)
-    return outs[0], outs[1:]
-
-
-def join_kernel(raw_ref, zone_ref, out_ref, stage, sems):
-    count = raw_ref.shape[1]
-    relay(
-        [
-            (raw_ref, stage.at[0], out_ref.at[:, :count]),
-            (zone_ref, stage.at[1], out_ref.at[:, count : 2 * count]),
+    )(pairs, fresh_kv, *after)
+    return outs[:slots], outs[slots:]
+
+
+def join_kernel(places, *refs):
+    count = len(places)
+    out_ref, stage, sems = refs[count:]
+    rows = stage.shape[1]
+    targets = [out_ref.at[slot, start : start + rows] for slot, start in places]
+    inner = [pltpu.make_async_copy(refs[i], stage.at[i], sems.at[i]) for i in range(count)]
+    outer = [pltpu.make_async_copy(stage.at[i], targets[i], sems.at[count + i]) for i in range(count)]
+    for copy in inner:
+        copy.start()
+    for arrive, leave in zip(inner, outer):
+        arrive.wait()
+        leave.start()
+    for copy in outer:
+        copy.wait()
+
+
+def join_head(blocks, places, shape):
+    block = blocks[0]
+    return pl.pallas_call(
+        functools.partial(join_kernel, places),
+        out_shape=jax.ShapeDtypeStruct(shape, block.dtype),
+        in_specs=[pl.BlockSpec(memory_space=HBM)] * len(blocks),
+        out_specs=pl.BlockSpec(memory_space=HBM),
+        scratch_shapes=[
+            pltpu.VMEM((len(blocks),) + block.shape, block.dtype),
+            pltpu.SemaphoreType.DMA((2 * len(blocks),)),
         ],
-        sems,
-    )
-
-
-def join_head(raw, zone, shape):
-    return pl.pallas_call(
-        join_kernel,
-        out_shape=jax.ShapeDtypeStruct(shape, raw.dtype),
-        in_specs=[pl.BlockSpec(memory_space=HBM)] * 2,
-        out_specs=pl.BlockSpec(memory_space=HBM),
-        scratch_shapes=[pltpu.VMEM((2,) + raw.shape, raw.dtype), pltpu.SemaphoreType.DMA((2, 2))],
-        cost_estimate=pl.CostEstimate(flops=0, bytes_accessed=8 * raw.size, transcendentals=0),
+        cost_estimate=pl.CostEstimate(
+            flops=0, bytes_accessed=4 * len(blocks) * block.size, transcendentals=0
+        ),
         compiler_params=pltpu.CompilerParams(vmem_limit_bytes=VMEM_LIMIT),
         name="join_head",
-    )(raw, zone)
-
-
-def restore_kernel(slot, start, stop, pairs_ref, piece_ref, whole_ref, *refs):
-    out_ref, pairs, zone, piece, sems = refs[-5:]
-    count = zone.shape[0] - 1
-    inner = [
-        pltpu.make_async_copy(pairs_ref, pairs, sems.at[4]),
-        pltpu.make_async_copy(piece_ref, piece.at[: stop - start], sems.at[0]),
-        pltpu.make_async_copy(out_ref.at[slot, count : 2 * count], zone.at[:count], sems.at[1]),
-    ]
+    )(*blocks)
+
+
+def restore_kernel(pieces, pairs_ref, *refs):
+    number = len(pieces)
+    piece_refs = refs[:number]
+    out_ref, pairs, zones, stage, sems = refs[-5:]
+    slots = out_ref.shape[0]
+    count = zones.shape[1] - 1
+    copy_pairs = pltpu.make_async_copy(pairs_ref, pairs, sems.at[4 * number])
+    copy_pairs.start()
+    inner, outer = [], []
+    for i, (slot, start, stop) in enumerate(pieces):
+        block, head = stage.at[i, : stop - start], zones.at[i, :count]
+        head_out = out_ref.at[slot, count : 2 * count]
+        inner.append(pltpu.make_async_copy(piece_refs[i], block, sems.at[4 * i]))
+        inner.append(pltpu.make_async_copy(head_out, head, sems.at[4 * i + 1]))
+        outer.append(pltpu.make_async_copy(block, out_ref.at[slot, start:stop], sems.at[4 * i + 2]))
+        outer.append(pltpu.make_async_copy(head, head_out, sems.at[4 * i + 3]))
     for copy in inner:
         copy.start()
-    for copy in inner:
-        copy.wait()
-    swap_rows(pairs, out_ref.shape[0], slot, zone, piece, start, stop)
-    outer = [
-        pltpu.make_async_copy(piece.at[: stop - start], out_ref.at[slot, start:stop], sems.at[2]),
-        pltpu.make_async_copy(zone.at[:count], out_ref.at[slot, count : 2 * count], sems.at[3]),
-    ]
-    for copy in outer:
-        copy.start()
+    copy_pairs.wait()
+    for i, (slot, start, stop) in enumerate(pieces):
+        inner[2 * i].wait()
+        inner[2 * i + 1].wait()
+        swap_rows(pairs, slots, slot, zones.at[i], stage.at[i], start, stop)
+        outer[2 * i].start()
+        outer[2 * i + 1].start()
     for copy in outer:
         copy.wait()
 
 
-def restore(pairs, block, whole, piece, after=()):
-    slot, start, stop = piece
+def restore(pairs, blocks, whole, pieces):
     tail = whole.shape[2:]
+    number = len(pieces)
     count = pairs.shape[0] // (2 * whole.shape[0])
+    rows = max(stop - start for _, start, stop in pieces)
     return pl.pallas_call(
-        functools.partial(restore_kernel, slot, start, stop),
+        functools.partial(restore_kernel, pieces),
         out_shape=jax.ShapeDtypeStruct(whole.shape, whole.dtype),
-        in_specs=[pl.BlockSpec(memory_space=HBM)] * (3 + len(after)),
+        in_specs=[pl.BlockSpec(memory_space=HBM)] * (2 + number),
         out_specs=pl.BlockSpec(memory_space=HBM),
         scratch_shapes=[
             pltpu.SMEM(pairs.shape, pairs.dtype),
-            pltpu.VMEM((count + 1,) + tail, whole.dtype),
-            pltpu.VMEM((stop - start + 1,) + tail, whole.dtype),
-            pltpu.SemaphoreType.DMA((5,)),
+            pltpu.VMEM((number, count + 1) + tail, whole.dtype),
+            pltpu.VMEM((number, rows + 1) + tail, whole.dtype),
+            pltpu.SemaphoreType.DMA((4 * number + 1,)),
         ],
-        input_output_aliases={2: 0},
-        cost_estimate=pl.CostEstimate(flops=0, bytes_accessed=4 * block.size, transcendentals=0),
+        input_output_aliases={1 + number: 0},
+        cost_estimate=pl.CostEstimate(
+            flops=0, bytes_accessed=4 * number * blocks[0].size, transcendentals=0
+        ),
         compiler_params=pltpu.CompilerParams(vmem_limit_bytes=VMEM_LIMIT),
         name="restore",
-    )(pairs, block, whole, *after)
+    )(pairs, *blocks, whole)
 
 
 def hold_kernel(block_ref, after_ref, out_ref):
@@ -223,30 +244,31 @@
 
 
 def text_kernel(k_ref, v_ref, w_ref, after_ref, out_ref):
-    rows = k_ref.shape[1]
+    rows, width = k_ref.shape
     channels = w_ref.shape[0]
-    out_ref[0, 0, :rows, :] = k_ref[0]
-    projected = across(w_ref[...], v_ref[0]).astype(out_ref.dtype)
-    for part in range(rows // HD):
-        start = rows + part * channels
-        out_ref[0, 0, start : start + channels, :] = projected[:, part * HD : (part + 1) * HD]
+    for head in range(width // HD):
+        columns = slice(head * HD, (head + 1) * HD)
+        out_ref[head, :rows, :] = k_ref[:, columns]
+        projected = across(w_ref[:, columns], v_ref[:, columns]).astype(out_ref.dtype)
+        for part in range(rows // HD):
+            start = rows + part * channels
+            out_ref[head, start : start + channels, :] = projected[:, part * HD : (part + 1) * HD]
 
 
 def project_text(keys, values, w_t, after):
-    slots, rows, width = keys.shape
+    rows, width = keys.shape
     heads = width // HD
     channels = w_t.shape[0]
     packed = rows + channels * rows // HD
-    block = pl.BlockSpec((1, rows, HD), lambda s, h: (s, 0, h))
     return pl.pallas_call(
         text_kernel,
-        grid=(slots, heads),
-        out_shape=jax.ShapeDtypeStruct((slots, heads, packed, HD), keys.dtype),
-        in_specs=[block, block, pl.BlockSpec((channels, HD), lambda s, h: (0, h)), pl.BlockSpec(memory_space=HBM)],
-        out_specs=pl.BlockSpec((1, 1, packed, HD), lambda s, h: (s, h, 0, 0)),
+        out_shape=jax.ShapeDtypeStruct((heads, packed, HD), keys.dtype),
+        in_specs=[pl.BlockSpec(memory_space=pltpu.VMEM)] * 3 + [pl.BlockSpec(memory_space=HBM)],
+        out_specs=pl.BlockSpec(memory_space=pltpu.VMEM),
         cost_estimate=pl.CostEstimate(
-            flops=2 * slots * rows * width * channels, bytes_accessed=4 * keys.size * 2, transcendentals=0
+            flops=2 * rows * width * channels, bytes_accessed=4 * keys.size * 2, transcendentals=0
         ),
+        compiler_params=pltpu.CompilerParams(vmem_limit_bytes=VMEM_LIMIT),
         name="project_text",
     )(keys, values, w_t, after)
 
@@ -254,23 +276,23 @@
 def attention_kernel(text_rows, *refs):
     (q_ref, kf_ref, vf_ref, ks_ref, vs_ref, kh_ref, vh_ref, own_ref, other_ref, w_ref, bias_ref) = refs[:11]
     out_ref, scores_ref = refs[11], refs[12]
-    head = pl.program_id(1)
-    query = q_ref[0]
+    head = pl.program_id(0)
+    query = q_ref[...]
     w_t = w_ref[...]
     channels = w_t.shape[0]
     scale = 1.0 / math.sqrt(HD)
     pieces = []
     for k_ref, v_ref in ((kf_ref, vf_ref), (ks_ref, vs_ref), (kh_ref, vh_ref)):
-        rows = k_ref.shape[1]
+        rows = k_ref.shape[0]
         step = min(rows, 256)
         for start in range(0, rows, step):
-            pieces.append((k_ref.at[0, start : start + step], v_ref.at[0, start : start + step], step))
+            pieces.append((k_ref.at[start : start + step], v_ref.at[start : start + step], step))
     for t_ref in (own_ref, other_ref):
-        pieces.append((t_ref.at[0, 0, :text_rows], t_ref, text_rows))
+        pieces.append((t_ref.at[0, :text_rows], t_ref, text_rows))
     top = None
     at = 0
     for k_ref, _, rows in pieces:
-        scores = across(k_ref[...], query) * scale + bias_ref[0, at : at + rows]
+        scores = across(k_ref[...], query) * scale + bias_ref[at : at + rows]
         scores_ref[at : at + rows, :] = scores
         piece_top = jnp.max(scores, axis=0, keepdims=True)
         top = piece_top if top is None else jnp.maximum(top, piece_top)
@@ -289,7 +311,7 @@
             for part in range(rows // HD):
                 start = rows + part * channels
                 blended += jnp.dot(
-                    v_ref[0, 0, start : start + channels, :],
+                    v_ref[0, start : start + channels, :],
                     rounded[part * HD : (part + 1) * HD],
                     preferred_element_type=jnp.float32,
                 )
@@ -298,40 +320,40 @@
 
     @pl.when(head == 0)
     def _():
-        out_ref[0] = term
+        out_ref[...] = term
 
     @pl.when(head != 0)
     def _():
-        out_ref[0] += term
+        out_ref[...] += term
 
 
 def attention(queries, fresh_k, fresh_v, stale_k, stale_v, hot_k, hot_v, text_own, text_other, w_t, bias):
-    slots, rows, width = queries.shape
+    rows, width = queries.shape
     heads = width // HD
     channels = w_t.shape[0]
-    key_rows = bias.shape[1]
-    text_rows = (text_own.shape[2] * HD) // (HD + channels)
+    key_rows = bias.shape[0]
+    text_rows = (text_own.shape[1] * HD) // (HD + channels)
 
     def wide(array):
-        return pl.BlockSpec((1, array.shape[1], HD), lambda s, h: (s, 0, h))
-
-    packed = pl.BlockSpec((1, 1) + text_own.shape[2:], lambda s, h: (s, h, 0, 0))
-    many = slots * heads * rows * key_rows
+        return pl.BlockSpec((array.shape[0], HD), lambda h: (0, h))
+
+    packed = pl.BlockSpec((1,) + text_own.shape[1:], lambda h: (h, 0, 0))
+    many = heads * rows * key_rows
     return pl.pallas_call(
         functools.partial(attention_kernel, text_rows),
-        grid=(slots, heads),
-        out_shape=jax.ShapeDtypeStruct((slots, channels, rows), jnp.float32),
+        grid=(heads,),
+        out_shape=jax.ShapeDtypeStruct((channels, rows), jnp.float32),
         in_specs=[wide(a) for a in (queries, fresh_k, fresh_v, stale_k, stale_v, hot_k, hot_v)]
         + [
             packed,
             packed,
-            pl.BlockSpec((channels, HD), lambda s, h: (0, h)),
-            pl.BlockSpec((1, key_rows, 1), lambda s, h: (s, 0, 0)),
+            pl.BlockSpec((channels, HD), lambda h: (0, h)),
+            pl.BlockSpec((key_rows, 1), lambda h: (0, 0)),
         ],
-        out_specs=pl.BlockSpec((1, channels, rows), lambda s, h: (s, 0, 0)),
+        out_specs=pl.BlockSpec((channels, rows), lambda h: (0, 0)),
         scratch_shapes=[pltpu.VMEM((key_rows, rows), jnp.float32)],
         cost_estimate=pl.CostEstimate(
-            flops=2 * many * (HD + channels), bytes_accessed=24 * 1024 * 1024, transcendentals=many
+            flops=2 * many * (HD + channels), bytes_accessed=12 * 1024 * 1024, transcendentals=many
         ),
         compiler_params=pltpu.CompilerParams(vmem_limit_bytes=VMEM_LIMIT),
         name="attention",
@@ -358,34 +380,40 @@
     listed_count = refresh_rows.shape[2]
     hot_rows = 2 * listed_count
 
-    raw = fresh_kv[0, :, :listed_count]
-    raw_in = from_behind(raw, "grp", half_groups)
+    both = range(slots)
+
+    def pass_on(block, slot):
+        if half_groups != 8:
+            return [from_behind(block, "grp", half_groups)]
+        step = half_groups // 2 if slot % 2 == 0 else half_groups + half_groups // 2
+        first = from_behind(block, "grp", step)
+        return [first, from_behind(first, "grp", step)]
+
+    raw = [fresh_kv[0, slot, :listed_count] for slot in both]
+    raw_way = [pass_on(raw[slot], slot) for slot in both]
 
     my_list = lax.dynamic_index_in_dim(refresh_rows, my_group, 0, keepdims=False)
     partner_list = lax.dynamic_index_in_dim(refresh_rows, partner, 0, keepdims=False)
     near, far, sources = swap_pairs(jnp.stack([my_list, partner_list]))
     pairs = jnp.stack([near, far], axis=1).reshape(2, -1)
 
-    first_cut = hot_rows + (img_rows - hot_rows) * 5 // 8
-    last_cut = img_rows - listed_count
-    final = slots - 1
-    pieces = [(slot, hot_rows, img_rows) for slot in range(final)]
-    pieces += [(final, hot_rows, first_cut), (final, first_cut, last_cut), (final, last_cut, img_rows)]
-    zone, blocks = arrange(pairs[0], fresh_kv, pieces, raw)
-    zone_in = from_behind(zone, "grp", half_groups)
+    rest = img_rows - hot_rows
+    cuts = [hot_rows, hot_rows + rest // 2, img_rows - listed_count, img_rows]
+    layers = [[(slot, start, stop) for slot in both] for start, stop in zip(cuts[:-1], cuts[1:])]
+    zone, blocks = arrange(pairs[0], fresh_kv, sum(layers, []), raw)
+    zone_way = [pass_on(zone[slot], slot) for slot in both]
     w_t = w_velocity.T
-    text_own = project_text(text[:, :, 0], text[:, :, 1], w_t, zone)
-    text_in = from_behind(text_own, "grp", half_groups)
-    arrived, held = [], []
-    for index, block in enumerate(blocks):
-        if index < final:
-            gate = raw_in
-        elif index == final:
-            gate = text_in
-        else:
-            gate = arrived[index - 2]
-        held.append(hold(block, gate))
-        arrived.append(from_behind(held[-1], "grp", half_groups))
+    text_own = [project_text(text[slot, :, 0], text[slot, :, 1], w_t, zone[slot]) for slot in both]
+    text_way = [pass_on(text_own[slot], slot) for slot in both]
+    layer_way = []
+    for index in range(len(layers)):
+        ways = []
+        for slot in both:
+            gate = (text_way[slot][0], text_way[slot][-1], None)[index]
+            if gate is None:
+                gate = layer_way[index - 1][slot][0]
+            ways.append(pass_on(hold(blocks[index * slots + slot], gate), slot))
+        layer_way.append(ways)
 
     my_live = lax.dynamic_index_in_dim(live_counts, my_group, 0, keepdims=False)
     partner_live = lax.dynamic_index_in_dim(live_counts, partner, 0, keepdims=False)
@@ -405,20 +433,27 @@
         axis=1,
     )
     bias = jnp.where(live, 0.0, -jnp.inf).astype(jnp.float32)[:, :, None]
-    hot = join_head(raw_in, zone_in, (slots, hot_rows) + fresh.shape[2:])
-    partial = attention(
-        queries,
-        fresh[:, :, 0],
-        fresh[:, :, 1],
-        stale[:, :, 0],
-        stale[:, :, 1],
-        hot[:, :, 0],
-        hot[:, :, 1],
-        text_own,
-        text_in,
-        w_t,
-        bias,
-    )
+    partials = []
+    for slot in both:
+        hot = join_head(
+            [raw_way[slot][-1], zone_way[slot][-1]], [(0, 0), (0, listed_count)], (1, hot_rows) + fresh.shape[2:]
+        )
+        partials.append(
+            attention(
+                queries[slot],
+                fresh[slot, :, 0],
+                fresh[slot, :, 1],
+                stale[slot, :, 0],
+                stale[slot, :, 1],
+                hot[0, :, 0],
+                hot[0, :, 1],
+                text_own[slot],
+                text_way[slot][-1],
+                w_t,
+                bias[slot],
+            )
+        )
+    partial = jnp.stack(partials)
 
     tp_count = lax.axis_size("tp")
     tp_index = lax.axis_index("tp")
@@ -442,9 +477,13 @@
     step_size = (times[:, 1] - times[:, 0]).astype(jnp.float32) / 1000.0
     latent_next = latent[0] + step_size[:, None, None] * velocity
 
-    next_stale = join_head(raw_in, zone_in, fresh.shape)
-    for index, piece in enumerate(pieces):
-        next_stale = restore(pairs[1], arrived[index], next_stale, piece, held[index + 2 : index + 3])
+    next_stale = join_head(
+        [raw_way[slot][-1] for slot in both] + [zone_way[slot][-1] for slot in both],
+        [(slot, 0) for slot in both] + [(slot, listed_count) for slot in both],
+        fresh.shape,
+    )
+    for pieces, ways in zip(layers, layer_way):
+        next_stale = restore(pairs[1], [way[-1] for way in ways], next_stale, pieces)
     return (next_stale[None], velocity[None], latent_next[None])
 
 

time: 257 us -> 261 us (1.016)
  starting transfers between devices: 8.92 us -> 46.1 us
  local copies, waits for them, and re-layouts: 43.5 us -> 31 us
  Pallas kernels: 60.2 us -> 50.7 us
  waiting for transfers between devices: 137 us -> 128 us
    ppermute x8 -> x25, starting transfers between devices: 8.92 us -> 46.1 us  [from_behind(): return lax.ppermute(block, axis, route)]
    unnamed x53 -> x67, local copies, waits for them, and re-layouts: 25.6 us -> 14.2 us
    pallas_call x8 -> x10, Pallas kernels: 56.6 us -> 47 us  [the longest x2 36.2 us: attention(): pl.pallas_call(functools.partial(attention_kernel, text_rows), grid=(head...]
    ppermute x8 -> x25, waiting for transfers between devices: 137 us -> 128 us  [from_behind(): return lax.ppermute(block, axis, route)]
    squeeze x6 -> x11, local copies, waits for them, and re-layouts: 12.9 us -> 13.3 us  [the longest x2 3.07 us: shards(): hot[0, :, 1]]
  transfers between devices with their start and end apart: 8 -> 25, of which waited for: 7 -> 11; matrix products, arithmetic and copies ran while one was open for 13% -> 8% of each run, Pallas kernels for 23% -> 18%
where the time goes in v7:
time: 261 us; the launch traced here: 260 us
  waiting for transfers between devices  128 us (49%)
  Pallas kernels  50.7 us (19%)
  starting transfers between devices  46.1 us (18%)
  local copies, waits for them, and re-layouts  31 us (12%)
  other arithmetic  3.29 us (1%)
    ppermute x25, waiting for transfers between devices, from_behind(): return lax.ppermute(block, axis, route)  128 us
    ppermute x25, starting transfers between devices, from_behind(): return lax.ppermute(block, axis, route)  46.1 us
    pallas_call x2, Pallas kernels, attention(): pl.pallas_call(functools.partial(attention_kernel, text_rows), grid=(head...  36.2 us
    unnamed x67, local copies, waits for them, and re-layouts  14.2 us
    pallas_call x3, Pallas kernels, restore(): pl.pallas_call(functools.partial(restore_kernel, pieces), out_shape=jax.S...  7.85 us
  transfers between devices with their start and end apart: 25, of which 11 were waited for; matrix products, arithmetic and copies ran while one was open for 8% of the time, Pallas kernels for 18%

profile of v7, /device:TPU:0, one launch (start us, length us, event | category | flops | bytes accessed | tf_op | source)
XLA Modules:
  0.0 260.4 jit_solution(15736780432484130576)
XLA Ops:
  0.6 2.2 slice_bitcast_fusion.14
  2.9 5.0 %collective-permute-start.18 = (bf16[64,2,1024]{2,1,0:T(2,128)(2,1)S(1)}, bf16[64,2,1024]{2,1,0:T(2,128)(2,1)S(1)}, u32[]{:S(2)}, u32[]{:S(2)}) collective-permute-start(bf16[64,2,1024]{2,1,0:T(2,128)(2,1)S(1)} %get-tuple-element.35.refs_1_), channel_id=1, source_target_pairs={{8,0},{10,2},{12,4},{14,6},{16,8},{18,10},{20,12},{22,14},{24,16},... | collective-permute-start | bytes 786440 | tf_op jit(solution)/shard_map/ppermute | solution.py:21
  7.9 0.7 constant_dynamic-slice_fusion.3
  9.0 0.3 select_reduce_fusion
  9.3 0.6 squeeze.99.pairs_ref
  10.0 3.7 %arrange.1 = (bf16[64,2,1024]{2,1,0:T(2,128)(2,1)}, bf16[64,2,1024]{2,1,0:T(2,128)(2,1)}, bf16[192,2,1024]{2,1,0:T(2,128)(2,1)}, bf16[192,2,1024]{2,1,0:T(2,128)...) custom-call(s32[256]{0:T(256)} %squeeze.99.pairs_ref, ...), custom_call_target="tpu_custom_call" | custom-call | bytes 8388608 | tf_op jit(solution)/shard_map/arrange/pallas_call | solution.py:118
  13.7 0.5 collective-permute-start.22
  14.2 0.6 copy.75
  15.1 0.4 project_text.3.refs_7_
  15.5 0.5 collective-permute-start.5
  16.0 1.6 collective-permute-start.20
  17.6 1.2 project_text.2.refs_7_
  18.8 1.6 collective-permute-start
  21.1 1.3 copy.73
  22.5 2.2 slice_bitcast_fusion
  24.7 1.5 copy-done.23
  26.2 1.3 copy.74
  27.5 2.2 slice_bitcast_fusion.2
  29.8 3.8 %collective-permute-start.23 = (bf16[64,2,1024]{2,1,0:T(2,128)(2,1)S(1)}, bf16[64,2,1024]{2,1,0:T(2,128)(2,1)S(1)}, u32[]{:S(2)}, u32[]{:S(2)}) collective-permute-start(bf16[64,2,1024]{2,1,0:T(2,128)(2,1)S(1)} %collective-permute-done.22), channel_id=1, source_target_pairs={{8,0},{10,2},{12,4},{14,6},{16,8},{18,10},{20,12},{22,14},{24,16},... | collective-permute-start | bytes 786440 | tf_op jit(solution)/shard_map/ppermute | solution.py:21
  33.6 11.2 %collective-permute-done.20 = bf16[64,2,1024]{2,1,0:T(2,128)(2,1)} collective-permute-done((bf16[64,2,1024]{2,1,0:T(2,128)(2,1)S(1)}, bf16[64,2,1024]{2,1,0:T(2,128)(2,1)}, u32[]{:S(2)}, u32[]{:S(2)}) %collective-permute-start.20) | collective-permute-done | bytes 262176 | tf_op jit(solution)/shard_map/ppermute | solution.py:21
  44.8 1.8 collective-permute-start.19
  46.7 1.1 slice_bitcast_fusion.8
  47.9 20.4 %collective-permute-done.5.after_ref = bf16[8,384,128]{2,1,0:T(8,128)(2,1)} collective-permute-done((bf16[8,384,128]{2,1,0:T(8,128)(2,1)S(1)}, bf16[8,384,128]{2,1,0:T(8,128)(2,1)}, u32[]{:S(2)}, u32[]{:S(2)}) %collective-permute-start.5) | collective-permute-done | bytes 786464 | tf_op jit(solution)/shard_map/ppermute | solution.py:21
  68.3 1.3 copy.61.refs_10_
  69.6 0.3 copy.58.refs_10_
  70.0 2.1 collective-permute-start.21
  72.0 1.8 collective-permute-done.23.refs_3_.refs_1_
  73.8 5.6 %collective-permute-done.19.refs_1_.refs_0_ = bf16[64,2,1024]{2,1,0:T(2,128)(2,1)S(1)} collective-permute-done((bf16[64,2,1024]{2,1,0:T(2,128)(2,1)S(1)}, bf16[64,2,1024]{2,1,0:T(2,128)(2,1)S(1)}, u32[]{:S(2)}, u32[]{:S(2)}) %collective-permute-start.19) | collective-permute-done | bytes 262176 | tf_op jit(solution)/shard_map/ppermute | solution.py:21
  79.5 2.5 collective-permute-start.14
  82.0 0.7 fusion.11
  82.8 18.2 %collective-permute-done.21.refs_2_.refs_1_ = bf16[64,2,1024]{2,1,0:T(2,128)(2,1)S(1)} collective-permute-done((bf16[64,2,1024]{2,1,0:T(2,128)(2,1)}, bf16[64,2,1024]{2,1,0:T(2,128)(2,1)S(1)}, u32[]{:S(2)}, u32[]{:S(2)}) %collective-permute-start.21) | collective-permute-done | bytes 262176 | tf_op jit(solution)/shard_map/ppermute | solution.py:21
  101.0 5.5 %collective-permute-done.17.refs_0_ = bf16[64,2,1024]{2,1,0:T(2,128)(2,1)S(1)} collective-permute-done((bf16[64,2,1024]{2,1,0:T(2,128)(2,1)}, bf16[64,2,1024]{2,1,0:T(2,128)(2,1)S(1)}, u32[]{:S(2)}, u32[]{:S(2)}) %collective-permute-start.17) | collective-permute-done | bytes 262176 | tf_op jit(solution)/shard_map/ppermute | solution.py:21
  106.6 0.9 copy_bitcast_fusion.3
  107.5 1.7 fusion.12
  109.2 1.6 collective-permute-start.12
  110.8 2.3 collective-permute-start.7
  113.0 2.2 copy_bitcast_fusion.5
  115.2 25.2 %collective-permute-done.1.after_ref.refs_8_ = bf16[8,384,128]{2,1,0:T(8,128)(2,1)} collective-permute-done((bf16[8,384,128]{2,1,0:T(8,128)(2,1)}, bf16[8,384,128]{2,1,0:T(8,128)(2,1)}, u32[]{:S(2)}, u32[]{:S(2)}) %collective-permute-start.1) | collective-permute-done | bytes 786464 | tf_op jit(solution)/shard_map/ppermute | solution.py:21
  140.4 1.5 collective-permute-start.2
  141.9 16.3 %collective-permute-done.14 = bf16[192,2,1024]{2,1,0:T(2,128)(2,1)} collective-permute-done((bf16[192,2,1024]{2,1,0:T(2,128)(2,1)}, bf16[192,2,1024]{2,1,0:T(2,128)(2,1)}, u32[]{:S(2)}, u32[]{:S(2)}) %collective-permute-start.14) | collective-permute-done | bytes 786464 | tf_op jit(solution)/shard_map/ppermute | solution.py:21
  158.2 1.2 copy-done
  159.4 1.2 copy-done.5
  160.6 1.2 copy-done.6
  161.8 1.2 copy-done.7
  163.1 1.2 copy-done.8
  164.3 1.2 copy-done.9
  165.4 1.1 copy-done.11
  166.6 0.9 copy-done.20
  167.6 18.1 %attention.3 = f32[64,512]{1,0:T(8,128)S(1)} custom-call(bf16[512,1024]{1,0:T(8,128)(2,1)S(1)} %copy-done, bf16[512,1024]{1,0:T(8,128)(2,1)S(1)} %copy-done.8, bf16[512,1024]{1,0:T(8,128)(2,1)S(1)} %copy-done.7, bf16[512,1024]{1,0:T(8,128)(2,1)S(1)} %copy-done.6, bf16[512,1024]{1,0:T(8,128)(2,1)S(1)} %copy-done.5, bf16[128,1024]{1,0:T(8,128)(2,1)S(1)} %copy-done.20, ...), custom_call_target="tpu_custom_call" | custom-call | flops 2617245696 | bytes 12582912 | tf_op jit(solution)/shard_map/attention/pallas_call | solution.py:342
  185.8 18.1 %attention.2 = f32[64,512]{1,0:T(8,128)S(1)} custom-call(bf16[512,1024]{1,0:T(8,128)(2,1)S(1)} %get-tuple-element.38.refs_0_, bf16[512,1024]{1,0:T(8,128)(2,1)S(1)} %copy-done.4, bf16[512,1024]{1,0:T(8,128)(2,1)S(1)} %copy-done.3, bf16[512,1024]{1,0:T(8,128)(2,1)S(1)} %copy-done.2, bf16[512,1024]{1,0:T(8,128)(2,1)S(1)} %copy-done.1, ...), custom_call_target="tpu_custom_call" | custom-call | flops 2617245696 | bytes 12582912 | tf_op jit(solution)/shard_map/attention/pallas_call | solution.py:342
  204.0 1.6 collective-permute-start.24
  205.6 2.0 collective-permute-start.13
  207.8 2.0 collective-permute-start.3
  209.8 1.9 collective-permute-start.11
  211.7 4.2 %collective-permute-done.8 = bf16[64,2,1024]{2,1,0:T(2,128)(2,1)} collective-permute-done((bf16[64,2,1024]{2,1,0:T(2,128)(2,1)}, bf16[64,2,1024]{2,1,0:T(2,128)(2,1)}, u32[]{:S(2)}, u32[]{:S(2)}) %collective-permute-start.8) | collective-permute-done | bytes 262176 | tf_op jit(solution)/shard_map/ppermute | solution.py:21
  215.9 1.3 collective-permute-start.10
  217.3 19.2 %collective-permute-done.3 = bf16[64,2,1024]{2,1,0:T(2,128)(2,1)} collective-permute-done((bf16[64,2,1024]{2,1,0:T(2,128)(2,1)}, bf16[64,2,1024]{2,1,0:T(2,128)(2,1)}, u32[]{:S(2)}, u32[]{:S(2)}) %collective-permute-start.3) | collective-permute-done | bytes 262176 | tf_op jit(solution)/shard_map/ppermute | solution.py:21
  236.5 12.4 %collective-permute-start.9 = (bf16[64,2,1024]{2,1,0:T(2,128)(2,1)}, bf16[64,2,1024]{2,1,0:T(2,128)(2,1)S(1)}, u32[]{:S(2)}, u32[]{:S(2)}) collective-permute-start(bf16[64,2,1024]{2,1,0:T(2,128)(2,1)} %collective-permute-done.8), channel_id=1, source_target_pairs={{8,0},{10,2},{12,4},{14,6},{16,8},{18,10},{20,12},{22,14},{24,16},... | collective-permute-start | bytes 786440 | tf_op jit(solution)/shard_map/ppermute | solution.py:21
  249.2 1.1 join_head.3.refs_2_
  250.3 1.6 fusion.5
  252.0 2.7 %restore.3.refs_2_ = bf16[2,512,2,1024]{3,2,1,0:T(2,128)(2,1)} custom-call(s32[256]{0:T(256)S(1)} %squeeze.98.pairs_ref, bf16[192,2,1024]{2,1,0:T(2,128)(2,1)S(1)} %collective-permute-done.13.refs_0_, bf16[192,2,1024]{2,1,0:T(2,128)(2,1)} %collective-permute-done.15.refs_1_, bf16[2,512,2,1024]{3,2,1,0:T(2,128)(2,1)} %join_head.3.refs_2_), custom_call_target="tpu_custom_call", output_to_operand_aliasing={{}: (3, {})} | custom-call | bytes 3145728 | tf_op jit(solution)/shard_map/restore/pallas_call | solution.py:206
  254.7 2.6 restore.4.refs_2_
  257.3 0.4 collective-permute-done.9.refs_1_
  257.7 2.6 restore.5
  (116 shorter events, 2.5 us)
Async XLA Ops:
  0.6 13.6 %copy-start.25 = (bf16[1,2,256,2,1024]{4,3,2,1,0:T(2,128)(2,1)S(1)}, bf16[1,2,256,2,1024]{4,3,2,1,0:T(2,128)(2,1)}, u32[]{:S(2)}) copy-start(bf16[1,2,256,2,1024]{4,3,2,1,0:T(2,128)(2,1)} %param.13) | copy-start | bytes 6291460
  2.9 7.1 %copy-start.28 = (bf16[64,2,1024]{2,1,0:T(2,128)(2,1)}, bf16[64,2,1024]{2,1,0:T(2,128)(2,1)S(1)}, u32[]{:S(2)}) copy-start(bf16[64,2,1024]{2,1,0:T(2,128)(2,1)S(1)} %get-tuple-element.35.refs_1_) | copy-start | bytes 786436
  2.9 26.9 %collective-permute-start.18 = (bf16[64,2,1024]{2,1,0:T(2,128)(2,1)S(1)}, bf16[64,2,1024]{2,1,0:T(2,128)(2,1)S(1)}, u32[]{:S(2)}, u32[]{:S(2)}) collective-permute-start(bf16[64,2,1024]{2,1,0:T(2,128)(2,1)S(1)} %get-tuple-element.35.refs_1_), channel_id=1, source_target_pairs={{8,0},{10,2},{12,4},{14,6},{16,8},{18,10},{20,12},{22,14},{24,16},... | collective-permute-start | bytes 786440 | tf_op jit(solution)/shard_map/ppermute | solution.py:21
  13.7 1.4 copy-start.12
  13.7 1.4 copy-start.19
  13.7 16.0 %collective-permute-start.22 = (bf16[64,2,1024]{2,1,0:T(2,128)(2,1)}, bf16[64,2,1024]{2,1,0:T(2,128)(2,1)S(1)}, u32[]{:S(2)}, u32[]{:S(2)}) collective-permute-start(bf16[64,2,1024]{2,1,0:T(2,128)(2,1)} %get-tuple-element.16.after_ref), channel_id=1, source_target_pairs={{8,0},{10,2},{12,4},{14,6},{16,8},{18,10},{20,12},{22,14},{24,16},... | collective-permute-start | bytes 786440 | tf_op jit(solution)/shard_map/ppermute | solution.py:21
  14.9 1.1 copy-start.18
  14.9 5.8 %copy-start.29 = (s32[16,2]{0,1:T(2,128)S(1)}, s32[16,2]{0,1:T(2,128)}, u32[]{:S(2)}) copy-start(s32[16,2]{0,1:T(2,128)} %param.16) | copy-start | bytes 388
  14.9 6.2 %copy-start.24 = (bf16[1,2,512,2,1024]{4,3,2,1,0:T(2,128)(2,1)S(1)}, bf16[1,2,512,2,1024]{4,3,2,1,0:T(2,128)(2,1)}, u32[]{:S(2)}) copy-start(bf16[1,2,512,2,1024]{4,3,2,1,0:T(2,128)(2,1)} %param.12) | copy-start | bytes 12582916
  15.5 7.0 %copy-start.10 = (bf16[8,384,128]{2,1,0:T(8,128)(2,1)}, bf16[8,384,128]{2,1,0:T(8,128)(2,1)S(1)}, u32[]{:S(2)}) copy-start(bf16[8,384,128]{2,1,0:T(8,128)(2,1)S(1)} %project_text.3.refs_7_) | copy-start | bytes 2359300
  15.5 52.8 %collective-permute-start.5 = (bf16[8,384,128]{2,1,0:T(8,128)(2,1)S(1)}, bf16[8,384,128]{2,1,0:T(8,128)(2,1)}, u32[]{:S(2)}, u32[]{:S(2)}) collective-permute-start(bf16[8,384,128]{2,1,0:T(8,128)(2,1)S(1)} %project_text.3.refs_7_), channel_id=1, source_target_pairs={{8,0},{10,2},{12,4},{14,6},{16,8},{18,10},{20,12},{22,14},{24,16},... | collective-permute-start | bytes 2359304 | tf_op jit(solution)/shard_map/ppermute | solution.py:21
  16.0 28.8 %collective-permute-start.20 = (bf16[64,2,1024]{2,1,0:T(2,128)(2,1)S(1)}, bf16[64,2,1024]{2,1,0:T(2,128)(2,1)}, u32[]{:S(2)}, u32[]{:S(2)}) collective-permute-start(bf16[64,2,1024]{2,1,0:T(2,128)(2,1)S(1)} %copy-done.18), channel_id=1, source_target_pairs={{24,0},{26,2},{28,4},{30,6},{0,8},{2,10},{4,12},{6,14},{8,16},{10,... | collective-permute-start | bytes 786440 | tf_op jit(solution)/shard_map/ppermute | solution.py:21
  18.8 63.2 %collective-permute-start = (bf16[8,384,128]{2,1,0:T(8,128)(2,1)}, bf16[8,384,128]{2,1,0:T(8,128)(2,1)}, u32[]{:S(2)}, u32[]{:S(2)}) collective-permute-start(bf16[8,384,128]{2,1,0:T(8,128)(2,1)} %project_text.2.refs_7_), channel_id=1, source_target_pairs={{24,0},{26,2},{28,4},{30,6},{0,8},{2,10},{4,12},{6,14},{8,16},{10,... | collective-permute-start | bytes 2359304 | tf_op jit(solution)/shard_map/ppermute | solution.py:21
  22.5 3.7 %copy-start.23 = (bf16[1,2,512,2,1024]{4,3,2,1,0:T(2,128)(2,1)S(1)}, bf16[1,2,512,2,1024]{4,3,2,1,0:T(2,128)(2,1)}, u32[]{:S(2)}) copy-start(bf16[1,2,512,2,1024]{4,3,2,1,0:T(2,128)(2,1)} %fresh_ref.1) | copy-start | bytes 12582916
  27.5 2.2 copy-start.27
  27.5 19.2 %copy-start.26 = (bf16[1,2,512,1024]{3,2,1,0:T(8,128)(2,1)S(1)}, bf16[1,2,512,1024]{3,2,1,0:T(8,128)(2,1)}, u32[]{:S(2)}) copy-start(bf16[1,2,512,1024]{3,2,1,0:T(8,128)(2,1)} %param.10) | copy-start | bytes 6291460
  29.7 18.1 %copy-start.31 = (s32[16]{0:T(128)S(1)}, s32[16]{0:T(128)}, u32[]{:S(2)}) copy-start(s32[16]{0:T(128)} %param.18) | copy-start | bytes 196
  29.7 40.2 %collective-permute-start.16 = (bf16[64,2,1024]{2,1,0:T(2,128)(2,1)S(1)}, bf16[64,2,1024]{2,1,0:T(2,128)(2,1)}, u32[]{:S(2)}, u32[]{:S(2)}) collective-permute-start(bf16[64,2,1024]{2,1,0:T(2,128)(2,1)S(1)} %copy-done.27), channel_id=1, source_target_pairs={{24,0},{26,2},{28,4},{30,6},{0,8},{2,10},{4,12},{6,14},{8,16},{10,... | collective-permute-start | bytes 786440 | tf_op jit(solution)/shard_map/ppermute | solution.py:21
  29.8 44.0 %collective-permute-start.23 = (bf16[64,2,1024]{2,1,0:T(2,128)(2,1)S(1)}, bf16[64,2,1024]{2,1,0:T(2,128)(2,1)S(1)}, u32[]{:S(2)}, u32[]{:S(2)}) collective-permute-start(bf16[64,2,1024]{2,1,0:T(2,128)(2,1)S(1)} %collective-permute-done.22), channel_id=1, source_target_pairs={{8,0},{10,2},{12,4},{14,6},{16,8},{18,10},{20,12},{22,14},{24,16},... | collective-permute-start | bytes 786440 | tf_op jit(solution)/shard_map/ppermute | solution.py:21
  44.8 34.6 %collective-permute-start.19 = (bf16[64,2,1024]{2,1,0:T(2,128)(2,1)S(1)}, bf16[64,2,1024]{2,1,0:T(2,128)(2,1)S(1)}, u32[]{:S(2)}, u32[]{:S(2)}) collective-permute-start(bf16[64,2,1024]{2,1,0:T(2,128)(2,1)S(1)} %collective-permute-done.18), channel_id=1, source_target_pairs={{8,0},{10,2},{12,4},{14,6},{16,8},{18,10},{20,12},{22,14},{24,16},... | collective-permute-start | bytes 786440 | tf_op jit(solution)/shard_map/ppermute | solution.py:21
  68.3 42.5 %collective-permute-start.6 = (bf16[8,384,128]{2,1,0:T(8,128)(2,1)}, bf16[8,384,128]{2,1,0:T(8,128)(2,1)}, u32[]{:S(2)}, u32[]{:S(2)}) collective-permute-start(bf16[8,384,128]{2,1,0:T(8,128)(2,1)} %collective-permute-done.5.after_ref), channel_id=1, source_target_pairs={{8,0},{10,2},{12,4},{14,6},{16,8},{18,10},{20,12},{22,14},{24,16},... | collective-permute-start | bytes 2359304 | tf_op jit(solution)/shard_map/ppermute | solution.py:21
  70.0 31.0 %collective-permute-start.21 = (bf16[64,2,1024]{2,1,0:T(2,128)(2,1)}, bf16[64,2,1024]{2,1,0:T(2,128)(2,1)S(1)}, u32[]{:S(2)}, u32[]{:S(2)}) collective-permute-start(bf16[64,2,1024]{2,1,0:T(2,128)(2,1)} %collective-permute-done.20), channel_id=1, source_target_pairs={{24,0},{26,2},{28,4},{30,6},{0,8},{2,10},{4,12},{6,14},{8,16},{10,... | collective-permute-start | bytes 786440 | tf_op jit(solution)/shard_map/ppermute | solution.py:21
  73.8 32.7 %collective-permute-start.17 = (bf16[64,2,1024]{2,1,0:T(2,128)(2,1)}, bf16[64,2,1024]{2,1,0:T(2,128)(2,1)S(1)}, u32[]{:S(2)}, u32[]{:S(2)}) collective-permute-start(bf16[64,2,1024]{2,1,0:T(2,128)(2,1)} %collective-permute-done.16), channel_id=1, source_target_pairs={{24,0},{26,2},{28,4},{30,6},{0,8},{2,10},{4,12},{6,14},{8,16},{10,... | collective-permute-start | bytes 786440 | tf_op jit(solution)/shard_map/ppermute | solution.py:21
  79.5 78.6 %collective-permute-start.14 = (bf16[192,2,1024]{2,1,0:T(2,128)(2,1)}, bf16[192,2,1024]{2,1,0:T(2,128)(2,1)}, u32[]{:S(2)}, u32[]{:S(2)}) collective-permute-start(bf16[192,2,1024]{2,1,0:T(2,128)(2,1)} %hold.11), channel_id=1, source_target_pairs={{8,0},{10,2},{12,4},{14,6},{16,8},{18,10},{20,12},{22,14},{24,16},... | collective-permute-start | bytes 2359304 | tf_op jit(solution)/shard_map/ppermute | solution.py:21
  82.0 58.4 %collective-permute-start.1 = (bf16[8,384,128]{2,1,0:T(8,128)(2,1)}, bf16[8,384,128]{2,1,0:T(8,128)(2,1)}, u32[]{:S(2)}, u32[]{:S(2)}) collective-permute-start(bf16[8,384,128]{2,1,0:T(8,128)(2,1)} %collective-permute-done.after_ref), channel_id=1, source_target_pairs={{24,0},{26,2},{28,4},{30,6},{0,8},{2,10},{4,12},{6,14},{8,16},{10,... | collective-permute-start | bytes 2359304 | tf_op jit(solution)/shard_map/ppermute | solution.py:21
  109.2 49.0 %copy-start.13 = (bf16[1024,64]{0,1:T(8,128)(2,1)S(1)}, bf16[1024,64]{0,1:T(8,128)(2,1)}, u32[]{:S(2)}) copy-start(bf16[1024,64]{0,1:T(8,128)(2,1)} %param.14) | copy-start | bytes 393220
  109.2 96.4 %collective-permute-start.12 = (bf16[192,2,1024]{2,1,0:T(2,128)(2,1)}, bf16[192,2,1024]{2,1,0:T(2,128)(2,1)}, u32[]{:S(2)}, u32[]{:S(2)}) collective-permute-start(bf16[192,2,1024]{2,1,0:T(2,128)(2,1)} %hold.10), channel_id=1, source_target_pairs={{24,0},{26,2},{28,4},{30,6},{0,8},{2,10},{4,12},{6,14},{8,16},{10,... | collective-permute-start | bytes 2359304 | tf_op jit(solution)/shard_map/ppermute | solution.py:21
  110.8 93.1 %collective-permute-start.7 = (bf16[128,2,1024]{2,1,0:T(2,128)(2,1)}, bf16[128,2,1024]{2,1,0:T(2,128)(2,1)}, u32[]{:S(2)}, u32[]{:S(2)}) collective-permute-start(bf16[128,2,1024]{2,1,0:T(2,128)(2,1)} %hold.8), channel_id=1, source_target_pairs={{8,0},{10,2},{12,4},{14,6},{16,8},{18,10},{20,12},{22,14},{24,16},... | collective-permute-start | bytes 1572872 | tf_op jit(solution)/shard_map/ppermute | solution.py:21
  140.4 67.3 %collective-permute-start.2 = (bf16[128,2,1024]{2,1,0:T(2,128)(2,1)}, bf16[128,2,1024]{2,1,0:T(2,128)(2,1)}, u32[]{:S(2)}, u32[]{:S(2)}) collective-permute-start(bf16[128,2,1024]{2,1,0:T(2,128)(2,1)} %hold.6), channel_id=1, source_target_pairs={{24,0},{26,2},{28,4},{30,6},{0,8},{2,10},{4,12},{6,14},{8,16},{10,... | collective-permute-start | bytes 1572872 | tf_op jit(solution)/shard_map/ppermute | solution.py:21
  158.2 90.8 %collective-permute-start.15 = (bf16[192,2,1024]{2,1,0:T(2,128)(2,1)}, bf16[192,2,1024]{2,1,0:T(2,128)(2,1)}, u32[]{:S(2)}, u32[]{:S(2)}) collective-permute-start(bf16[192,2,1024]{2,1,0:T(2,128)(2,1)} %collective-permute-done.14), channel_id=1, source_target_pairs={{8,0},{10,2},{12,4},{14,6},{16,8},{18,10},{20,12},{22,14},{24,16},... | collective-permute-start | bytes 2359304 | tf_op jit(solution)/shard_map/ppermute | solution.py:21
  158.2 1.2 copy-start
  159.4 1.2 copy-start.5
  160.6 1.2 copy-start.6
  161.8 1.2 copy-start.7
  163.1 1.2 copy-start.8
  164.3 1.2 copy-start.9
  165.4 1.1 copy-start.11
  166.6 0.9 copy-start.20
  167.5 18.2 %copy-start.1 = (bf16[512,1024]{1,0:T(8,128)(2,1)S(1)}, bf16[512,1024]{1,0:T(8,128)(2,1)}, u32[]{:S(2)}) copy-start(bf16[512,1024]{1,0:T(8,128)(2,1)} %get-tuple-element.29.refs_4_) | copy-start | bytes 3145732
  167.5 18.2 %copy-start.2 = (bf16[512,1024]{1,0:T(8,128)(2,1)S(1)}, bf16[512,1024]{1,0:T(8,128)(2,1)}, u32[]{:S(2)}) copy-start(bf16[512,1024]{1,0:T(8,128)(2,1)} %get-tuple-element.30.refs_3_) | copy-start | bytes 3145732
  167.5 18.2 %copy-start.3 = (bf16[512,1024]{1,0:T(8,128)(2,1)S(1)}, bf16[512,1024]{1,0:T(8,128)(2,1)}, u32[]{:S(2)}) copy-start(bf16[512,1024]{1,0:T(8,128)(2,1)} %get-tuple-element.33.refs_2_) | copy-start | bytes 3145732
  167.5 18.2 %copy-start.4 = (bf16[512,1024]{1,0:T(8,128)(2,1)S(1)}, bf16[512,1024]{1,0:T(8,128)(2,1)}, u32[]{:S(2)}) copy-start(bf16[512,1024]{1,0:T(8,128)(2,1)} %get-tuple-element.34.refs_1_) | copy-start | bytes 3145732
  167.5 18.2 %copy-start.21 = (bf16[128,1024]{1,0:T(8,128)(2,1)S(1)}, bf16[128,1024]{1,0:T(8,128)(2,1)}, u32[]{:S(2)}) copy-start(bf16[128,1024]{1,0:T(8,128)(2,1)} %get-tuple-element.53.refs_6_) | copy-start | bytes 786436
  167.6 18.2 %copy-start.22 = (bf16[128,1024]{1,0:T(8,128)(2,1)S(1)}, bf16[128,1024]{1,0:T(8,128)(2,1)}, u32[]{:S(2)}) copy-start(bf16[128,1024]{1,0:T(8,128)(2,1)} %get-tuple-element.54.refs_5_) | copy-start | bytes 786436
  185.7 18.3 %copy-start.14 = (f32[64,512]{1,0:T(8,128)}, f32[64,512]{1,0:T(8,128)S(1)}, u32[]{:S(2)}) copy-start(f32[64,512]{1,0:T(8,128)S(1)} %attention.3) | copy-start | bytes 393220
  185.8 21.9 %copy-start.30 = (s32[16,2]{0,1:T(2,128)S(1)}, s32[16,2]{0,1:T(2,128)}, u32[]{:S(2)}) copy-start(s32[16,2]{0,1:T(2,128)} %param.19) | copy-start | bytes 388
  203.9 6.0 %copy-start.16 = (f32[64,512]{1,0:T(8,128)}, f32[64,512]{1,0:T(8,128)S(1)}, u32[]{:S(2)}) copy-start(f32[64,512]{1,0:T(8,128)S(1)} %attention.2) | copy-start | bytes 393220
  203.9 12.0 %collective-permute-start.8 = (bf16[64,2,1024]{2,1,0:T(2,128)(2,1)}, bf16[64,2,1024]{2,1,0:T(2,128)(2,1)}, u32[]{:S(2)}, u32[]{:S(2)}) collective-permute-start(bf16[64,2,1024]{2,1,0:T(2,128)(2,1)} %hold.9), channel_id=1, source_target_pairs={{8,0},{10,2},{12,4},{14,6},{16,8},{18,10},{20,12},{22,14},{24,16},... | collective-permute-start | bytes 786440 | tf_op jit(solution)/shard_map/ppermute | solution.py:21
  204.0 46.3 %copy-start.15 = (f32[64,512]{1,0:T(8,128)S(1)}, f32[64,512]{1,0:T(8,128)}, u32[]{:S(2)}) copy-start(f32[64,512]{1,0:T(8,128)} %copy-done.14) | copy-start | bytes 393220
  204.0 5.8 %collective-permute-start.24 = (f32[2,64,256]{2,1,0:T(8,128)S(1)}, f32[2,64,256]{2,1,0:T(8,128)S(1)}, u32[]{:S(2)}, u32[]{:S(2)}) collective-permute-start(f32[2,64,256]{2,1,0:T(8,128)S(1)} %fusion.1), channel_id=1, source_target_pairs={{1,0},{0,1},{3,2},{2,3},{5,4},{4,5},{7,6},{6,7},{9,8},{8,9},{11,10... | collective-permute-start | bytes 393224 | tf_op jit(solution)/shard_map/ppermute | solution.py:21
  205.6 46.4 %collective-permute-start.13 = (bf16[192,2,1024]{2,1,0:T(2,128)(2,1)}, bf16[192,2,1024]{2,1,0:T(2,128)(2,1)S(1)}, u32[]{:S(2)}, u32[]{:S(2)}) collective-permute-start(bf16[192,2,1024]{2,1,0:T(2,128)(2,1)} %collective-permute-done.12), channel_id=1, source_target_pairs={{24,0},{26,2},{28,4},{30,6},{0,8},{2,10},{4,12},{6,14},{8,16},{10,... | collective-permute-start | bytes 2359304 | tf_op jit(solution)/shard_map/ppermute | solution.py:21
  207.8 28.7 %collective-permute-start.3 = (bf16[64,2,1024]{2,1,0:T(2,128)(2,1)}, bf16[64,2,1024]{2,1,0:T(2,128)(2,1)}, u32[]{:S(2)}, u32[]{:S(2)}) collective-permute-start(bf16[64,2,1024]{2,1,0:T(2,128)(2,1)} %hold.7), channel_id=1, source_target_pairs={{24,0},{26,2},{28,4},{30,6},{0,8},{2,10},{4,12},{6,14},{8,16},{10,... | collective-permute-start | bytes 786440 | tf_op jit(solution)/shard_map/ppermute | solution.py:21
  209.8 40.5 %copy-start.17 = (f32[64,512]{1,0:T(8,128)S(1)}, f32[64,512]{1,0:T(8,128)}, u32[]{:S(2)}) copy-start(f32[64,512]{1,0:T(8,128)} %copy-done.16) | copy-start | bytes 393220
  209.8 44.8 %collective-permute-start.11 = (bf16[128,2,1024]{2,1,0:T(2,128)(2,1)}, bf16[128,2,1024]{2,1,0:T(2,128)(2,1)S(1)}, u32[]{:S(2)}, u32[]{:S(2)}) collective-permute-start(bf16[128,2,1024]{2,1,0:T(2,128)(2,1)} %collective-permute-done.7.after_ref), channel_id=1, source_target_pairs={{8,0},{10,2},{12,4},{14,6},{16,8},{18,10},{20,12},{22,14},{24,16},... | collective-permute-start | bytes 1572872 | tf_op jit(solution)/shard_map/ppermute | solution.py:21
  215.9 38.7 %collective-permute-start.10 = (bf16[128,2,1024]{2,1,0:T(2,128)(2,1)}, bf16[128,2,1024]{2,1,0:T(2,128)(2,1)S(1)}, u32[]{:S(2)}, u32[]{:S(2)}) collective-permute-start(bf16[128,2,1024]{2,1,0:T(2,128)(2,1)} %collective-permute-done.2.after_ref), channel_id=1, source_target_pairs={{24,0},{26,2},{28,4},{30,6},{0,8},{2,10},{4,12},{6,14},{8,16},{10,... | collective-permute-start | bytes 1572872 | tf_op jit(solution)/shard_map/ppermute | solution.py:21
  236.5 21.2 %collective-permute-start.9 = (bf16[64,2,1024]{2,1,0:T(2,128)(2,1)}, bf16[64,2,1024]{2,1,0:T(2,128)(2,1)S(1)}, u32[]{:S(2)}, u32[]{:S(2)}) collective-permute-start(bf16[64,2,1024]{2,1,0:T(2,128)(2,1)} %collective-permute-done.8), channel_id=1, source_target_pairs={{8,0},{10,2},{12,4},{14,6},{16,8},{18,10},{20,12},{22,14},{24,16},... | collective-permute-start | bytes 786440 | tf_op jit(solution)/shard_map/ppermute | solution.py:21
  248.9 8.8 %collective-permute-start.4 = (bf16[64,2,1024]{2,1,0:T(2,128)(2,1)}, bf16[64,2,1024]{2,1,0:T(2,128)(2,1)}, u32[]{:S(2)}, u32[]{:S(2)}) collective-permute-start(bf16[64,2,1024]{2,1,0:T(2,128)(2,1)} %collective-permute-done.3), channel_id=1, source_target_pairs={{24,0},{26,2},{28,4},{30,6},{0,8},{2,10},{4,12},{6,14},{8,16},{10,... | collective-permute-start | bytes 786440 | tf_op jit(solution)/shard_map/ppermute | solution.py:21

commit v8 on v5

--- a/solution.py
+++ b/solution.py
@@ -157,16 +157,28 @@
     )(raw, zone)
 
 
-def restore_kernel(slot, start, stop, pairs_ref, piece_ref, whole_ref, *refs):
+def restore_kernel(slot, start, stop, groups, pairs_ref, end_ref, middle_ref, whole_ref, *refs):
     out_ref, pairs, zone, piece, sems = refs[-5:]
     count = zone.shape[0] - 1
     inner = [
         pltpu.make_async_copy(pairs_ref, pairs, sems.at[4]),
-        pltpu.make_async_copy(piece_ref, piece.at[: stop - start], sems.at[0]),
         pltpu.make_async_copy(out_ref.at[slot, count : 2 * count], zone.at[:count], sems.at[1]),
     ]
     for copy in inner:
         copy.start()
+    from_end = pltpu.make_async_copy(end_ref, piece.at[: stop - start], sems.at[0])
+    from_middle = pltpu.make_async_copy(middle_ref, piece.at[: stop - start], sems.at[0])
+    middle = on_the_way(groups)
+
+    @pl.when(middle)
+    def _():
+        from_middle.start()
+
+    @pl.when(jnp.logical_not(middle))
+    def _():
+        from_end.start()
+
+    inner.append(from_end)
     for copy in inner:
         copy.wait()
     swap_rows(pairs, out_ref.shape[0], slot, zone, piece, start, stop)
@@ -180,14 +192,14 @@
         copy.wait()
 
 
-def restore(pairs, block, whole, piece, after=()):
+def restore(pairs, ways, whole, piece, groups, after=()):
     slot, start, stop = piece
     tail = whole.shape[2:]
     count = pairs.shape[0] // (2 * whole.shape[0])
     return pl.pallas_call(
-        functools.partial(restore_kernel, slot, start, stop),
+        functools.partial(restore_kernel, slot, start, stop, groups),
         out_shape=jax.ShapeDtypeStruct(whole.shape, whole.dtype),
-        in_specs=[pl.BlockSpec(memory_space=HBM)] * (3 + len(after)),
+        in_specs=[pl.BlockSpec(memory_space=HBM)] * (4 + len(after)),
         out_specs=pl.BlockSpec(memory_space=HBM),
         scratch_shapes=[
             pltpu.SMEM(pairs.shape, pairs.dtype),
@@ -195,11 +207,71 @@
             pltpu.VMEM((stop - start + 1,) + tail, whole.dtype),
             pltpu.SemaphoreType.DMA((5,)),
         ],
-        input_output_aliases={2: 0},
-        cost_estimate=pl.CostEstimate(flops=0, bytes_accessed=4 * block.size, transcendentals=0),
+        input_output_aliases={3: 0},
+        cost_estimate=pl.CostEstimate(flops=0, bytes_accessed=4 * ways[1].size, transcendentals=0),
         compiler_params=pltpu.CompilerParams(vmem_limit_bytes=VMEM_LIMIT),
         name="restore",
-    )(pairs, block, whole, *after)
+    )(pairs, ways[1], ways[2], whole, *after)
+
+
+def on_the_way(groups):
+    place = lax.axis_index("grp") // (groups // 4)
+    return jnp.logical_or(place == 1, place == 2)
+
+
+def either_kernel(groups, end_ref, middle_ref, out_ref, stage, sems):
+    middle = on_the_way(groups)
+    from_end = pltpu.make_async_copy(end_ref, stage, sems.at[0])
+    from_middle = pltpu.make_async_copy(middle_ref, stage, sems.at[0])
+
+    @pl.when(middle)
+    def _():
+        from_middle.start()
+
+    @pl.when(jnp.logical_not(middle))
+    def _():
+        from_end.start()
+
+    from_end.wait()
+    leave = pltpu.make_async_copy(stage, out_ref, sems.at[1])
+    leave.start()
+    leave.wait()
+
+
+def either(end_block, middle_block, groups):
+    return pl.pallas_call(
+        functools.partial(either_kernel, groups),
+        out_shape=jax.ShapeDtypeStruct(end_block.shape, end_block.dtype),
+        in_specs=[pl.BlockSpec(memory_space=HBM)] * 2,
+        out_specs=pl.BlockSpec(memory_space=HBM),
+        scratch_shapes=[pltpu.VMEM(end_block.shape, end_block.dtype), pltpu.SemaphoreType.DMA((2,))],
+        cost_estimate=pl.CostEstimate(flops=0, bytes_accessed=4 * end_block.size, transcendentals=0),
+        compiler_params=pltpu.CompilerParams(vmem_limit_bytes=VMEM_LIMIT),
+        name="either",
+    )(end_block, middle_block)
+
+
+def swap_along(block, groups, couples):
+    quarter = groups // 4
+    route = []
+    for one, other in couples:
+        for i in range(quarter):
+            route.append((one * quarter + i, other * quarter + i))
+            route.append((other * quarter + i, one * quarter + i))
+    return lax.ppermute(block, "grp", route)
+
+
+def pass_along(block, groups):
+    if groups != 16:
+        direct = from_behind(block, "grp", groups // 2)
+        return direct, direct, direct
+    crossed = swap_along(block, groups, [(1, 2)])
+    outer = swap_along(either(block, crossed, groups), groups, [(0, 1), (2, 3)])
+    return crossed, outer, swap_along(outer, groups, [(1, 2)])
+
+
+def arrived_block(ways, groups):
+    return ways[1] if groups != 16 else either(ways[1], ways[2], groups)
 
 
 def hold_kernel(block_ref, after_ref, out_ref):
@@ -222,14 +294,18 @@
     return lax.dot_general(a, b, (((1,), (1,)), ((), ())), preferred_element_type=jnp.float32)
 
 
-def text_kernel(k_ref, v_ref, w_ref, after_ref, out_ref):
-    rows = k_ref.shape[1]
+def text_kernel(k_ref, v_ref, w_ref, *refs):
+    out_ref = refs[-1]
+    slots, rows, width = k_ref.shape
     channels = w_ref.shape[0]
-    out_ref[0, 0, :rows, :] = k_ref[0]
-    projected = across(w_ref[...], v_ref[0]).astype(out_ref.dtype)
-    for part in range(rows // HD):
-        start = rows + part * channels
-        out_ref[0, 0, start : start + channels, :] = projected[:, part * HD : (part + 1) * HD]
+    for slot in range(slots):
+        for head in range(width // HD):
+            columns = slice(head * HD, (head + 1) * HD)
+            out_ref[slot, head, :rows, :] = k_ref[slot, :, columns]
+            projected = across(w_ref[:, columns], v_ref[slot, :, columns]).astype(out_ref.dtype)
+            for part in range(rows // HD):
+                start = rows + part * channels
+                out_ref[slot, head, start : start + channels, :] = projected[:, part * HD : (part + 1) * HD]
 
 
 def project_text(keys, values, w_t, after):
@@ -237,18 +313,18 @@
     heads = width // HD
     channels = w_t.shape[0]
     packed = rows + channels * rows // HD
-    block = pl.BlockSpec((1, rows, HD), lambda s, h: (s, 0, h))
     return pl.pallas_call(
         text_kernel,
-        grid=(slots, heads),
         out_shape=jax.ShapeDtypeStruct((slots, heads, packed, HD), keys.dtype),
-        in_specs=[block, block, pl.BlockSpec((channels, HD), lambda s, h: (0, h)), pl.BlockSpec(memory_space=HBM)],
-        out_specs=pl.BlockSpec((1, 1, packed, HD), lambda s, h: (s, h, 0, 0)),
+        in_specs=[pl.BlockSpec(memory_space=pltpu.VMEM)] * 3
+        + [pl.BlockSpec(memory_space=HBM)] * len(after),
+        out_specs=pl.BlockSpec(memory_space=pltpu.VMEM),
         cost_estimate=pl.CostEstimate(
             flops=2 * slots * rows * width * channels, bytes_accessed=4 * keys.size * 2, transcendentals=0
         ),
+        compiler_params=pltpu.CompilerParams(vmem_limit_bytes=VMEM_LIMIT),
         name="project_text",
-    )(keys, values, w_t, after)
+    )(keys, values, w_t, *after)
 
 
 def attention_kernel(text_rows, *refs):
@@ -359,7 +435,8 @@
     hot_rows = 2 * listed_count
 
     raw = fresh_kv[0, :, :listed_count]
-    raw_in = from_behind(raw, "grp", half_groups)
+    groups = 2 * half_groups
+    raw_ways = pass_along(raw, groups)
 
     my_list = lax.dynamic_index_in_dim(refresh_rows, my_group, 0, keepdims=False)
     partner_list = lax.dynamic_index_in_dim(refresh_rows, partner, 0, keepdims=False)
@@ -372,20 +449,15 @@
     pieces = [(slot, hot_rows, img_rows) for slot in range(final)]
     pieces += [(final, hot_rows, first_cut), (final, first_cut, last_cut), (final, last_cut, img_rows)]
     zone, blocks = arrange(pairs[0], fresh_kv, pieces, raw)
-    zone_in = from_behind(zone, "grp", half_groups)
+    zone_ways = pass_along(zone, groups)
     w_t = w_velocity.T
-    text_own = project_text(text[:, :, 0], text[:, :, 1], w_t, zone)
-    text_in = from_behind(text_own, "grp", half_groups)
-    arrived, held = [], []
-    for index, block in enumerate(blocks):
-        if index < final:
-            gate = raw_in
-        elif index == final:
-            gate = text_in
-        else:
-            gate = arrived[index - 2]
-        held.append(hold(block, gate))
-        arrived.append(from_behind(held[-1], "grp", half_groups))
+    text_own = project_text(text[:, :, 0], text[:, :, 1], w_t, (zone_ways[0], raw_ways[0]))
+    text_ways = pass_along(text_own, groups)
+    piece_ways, gate = [], text_ways[0]
+    for block in blocks:
+        piece_ways.append(pass_along(hold(block, gate), groups))
+        gate = piece_ways[-1][0]
+    raw_in, zone_in, text_in = (arrived_block(ways, groups) for ways in (raw_ways, zone_ways, text_ways))
 
     my_live = lax.dynamic_index_in_dim(live_counts, my_group, 0, keepdims=False)
     partner_live = lax.dynamic_index_in_dim(live_counts, partner, 0, keepdims=False)
@@ -444,7 +516,7 @@
 
     next_stale = join_head(raw_in, zone_in, fresh.shape)
     for index, piece in enumerate(pieces):
-        next_stale = restore(pairs[1], arrived[index], next_stale, piece, held[index + 2 : index + 3])
+        next_stale = restore(pairs[1], piece_ways[index], next_stale, piece, groups)
     return (next_stale[None], velocity[None], latent_next[None])
 
 

time: 257 us -> 280 us (1.089)
  starting transfers between devices: 8.92 us -> 144 us
  waiting for transfers between devices: 137 us -> 27.8 us
  local copies, waits for them, and re-layouts: 43.5 us -> 38.3 us
    ppermute x0 -> x21, starting transfers between devices: none -> 143 us  [swap_along(): return lax.ppermute(block, 'grp', route)]
    ppermute x8 -> x1, waiting for transfers between devices: 137 us -> 0.02 us  [from_behind(): return lax.ppermute(block, axis, route)]
    ppermute x0 -> x21, waiting for transfers between devices: none -> 27.8 us  [swap_along(): return lax.ppermute(block, 'grp', route)]
    ppermute x8 -> x1, starting transfers between devices: 8.92 us -> 1.56 us  [from_behind(): return lax.ppermute(block, axis, route)]
    unnamed x53 -> x71, local copies, waits for them, and re-layouts: 25.6 us -> 23.1 us
    pallas_call x5 -> x15, Pallas kernels: 19.8 us -> 21 us  [the longest x10 10.3 us: either(): pl.pallas_call(functools.partial(either_kernel, groups), out_shape=jax.Sh...]
  transfers between devices with their start and end apart: 8 -> 22, of which waited for: 7 -> 3; matrix products, arithmetic and copies ran while one was open for 13% -> 9% of each run, Pallas kernels for 23% -> 19%
where the time goes in v8:
time: 280 us; the launch traced here: 278 us
  starting transfers between devices  144 us (51%)
  Pallas kernels  60.7 us (22%)
  local copies, waits for them, and re-layouts  38.3 us (14%)
  waiting for transfers between devices  27.8 us (10%)
  other arithmetic  5.43 us (2%)
    ppermute x21, starting transfers between devices, swap_along(): return lax.ppermute(block, 'grp', route)  143 us
    pallas_call x1, Pallas kernels, attention(): pl.pallas_call(functools.partial(attention_kernel, text_rows), grid=(slot...  34.6 us
    ppermute x21, waiting for transfers between devices, swap_along(): return lax.ppermute(block, 'grp', route)  27.8 us
    unnamed x71, local copies, waits for them, and re-layouts  23.1 us
    pallas_call x10, Pallas kernels, either(): pl.pallas_call(functools.partial(either_kernel, groups), out_shape=jax.Sh...  10.3 us
    pallas_call x4, Pallas kernels, restore(): pl.pallas_call(functools.partial(restore_kernel, slot, start, stop, group...  10.1 us
  transfers between devices with their start and end apart: 22, of which 3 were waited for; matrix products, arithmetic and copies ran while one was open for 9% of the time, Pallas kernels for 19%

profile of v8, /device:TPU:0, one launch (start us, length us, event | category | flops | bytes accessed | tf_op | source)
XLA Modules:
  0.0 277.9 jit_solution(17966209159289416257)
XLA Ops:
  0.7 0.7 constant_dynamic-slice_fusion.4
  2.1 0.6 squeeze.61.pairs_ref
  2.7 2.2 slice_bitcast_fusion.6.after_ref.end_ref
  4.9 3.8 %arrange.1 = (bf16[2,64,2,1024]{3,2,1,0:T(2,128)(2,1)}, bf16[384,2,1024]{2,1,0:T(2,128)(2,1)}, bf16[240,2,1024]{2,1,0:T(2,128)(2,1)}, bf16[80,2,1024]{2,1,0:T(2,128)(2,1)}, bf16[64,2,1024]{2,1,0:T(2,128)(2,1)}) custom-call(s32[256]{0:T(256)} %squeeze.61.pairs_ref, bf16[1,2,512,2,1024]{4,3,2,1,0:T(2,128)(2,1)} %fresh_ref.1, ...), custom_call_target="tpu_custom_call" | custom-call | bytes 8388608 | tf_op jit(solution)/shard_map/arrange/pallas_call | solution.py:117
  8.8 0.7 collective-permute-start
  9.5 0.7 collective-permute-start.1
  10.2 0.6 copy.68
  11.1 0.7 copy-done.26
  12.4 0.8 collective-permute-start.2
  13.4 1.2 copy-done.3
  14.6 0.7 collective-permute-start.3
  15.7 1.4 copy-done.4
  17.1 1.3 either.18
  18.4 66.1 %collective-permute-start.19 = (bf16[2,8,384,128]{3,2,1,0:T(8,128)(2,1)}, bf16[2,8,384,128]{3,2,1,0:T(8,128)(2,1)}, u32[]{:S(2)}, u32[]{:S(2)}) collective-permute-start(bf16[2,8,384,128]{3,2,1,0:T(8,128)(2,1)} %either.18), channel_id=1, source_target_pairs={{0,8},{8,0},{2,10},{10,2},{4,12},{12,4},{6,14},{14,6},{16,24},{24,... | collective-permute-start | bytes 4718600 | tf_op jit(solution)/shard_map/ppermute | solution.py:261
  84.7 1.3 copy.58
  86.0 1.1 copy-done
  87.1 0.7 collective-permute-start.4
  87.8 2.4 broadcast_select_fusion.refs_10_
  90.2 3.7 %copy.67 = bf16[1,2,512,2,1024]{4,2,1,3,0:T(8,128)(2,1)S(1)} copy(bf16[1,2,512,2,1024]{4,3,2,1,0:T(2,128)(2,1)} %fresh_ref.1) | data formatting | bytes 8388608 | tf_op args[1]
  93.9 0.9 either.14
  94.8 31.2 %collective-permute-start.15 = (bf16[2,64,2,1024]{3,2,1,0:T(2,128)(2,1)}, bf16[2,64,2,1024]{3,2,1,0:T(2,128)(2,1)}, u32[]{:S(2)}, u32[]{:S(2)}) collective-permute-start(bf16[2,64,2,1024]{3,2,1,0:T(2,128)(2,1)} %either.14), channel_id=1, source_target_pairs={{0,8},{8,0},{2,10},{10,2},{4,12},{12,4},{6,14},{14,6},{16,24},{24,... | collective-permute-start | bytes 1572872 | tf_op jit(solution)/shard_map/ppermute | solution.py:261
  126.0 0.8 either.16
  127.0 1.3 either.13
  128.3 2.0 collective-permute-start.13
  130.3 2.4 slice_bitcast_fusion.2
  132.7 5.6 %copy.66 = bf16[1,2,512,2,1024]{4,2,1,3,0:T(8,128)(2,1)} copy(bf16[1,2,512,2,1024]{4,3,2,1,0:T(2,128)(2,1)} %param.12) | data formatting | bytes 8388608 | tf_op args[2]
  138.4 1.8 collective-permute-start.20
  140.3 0.7 collective-permute-start.16
  141.0 9.4 %collective-permute-done.17.end_ref = bf16[2,64,2,1024]{3,2,1,0:T(2,128)(2,1)} collective-permute-done((bf16[2,64,2,1024]{3,2,1,0:T(2,128)(2,1)}, bf16[2,64,2,1024]{3,2,1,0:T(2,128)(2,1)}, u32[]{:S(2)}, u32[]{:S(2)}) %collective-permute-start.17) | collective-permute-done | bytes 524320 | tf_op jit(solution)/shard_map/ppermute | solution.py:261
  150.4 0.7 collective-permute-start.18
  151.2 1.3 either.12
  152.5 3.7 %collective-permute-start.11 = (bf16[240,2,1024]{2,1,0:T(2,128)(2,1)}, bf16[240,2,1024]{2,1,0:T(2,128)(2,1)}, u32[]{:S(2)}, u32[]{:S(2)}) collective-permute-start(bf16[240,2,1024]{2,1,0:T(2,128)(2,1)} %either.12), channel_id=1, source_target_pairs={{0,8},{8,0},{2,10},{10,2},{4,12},{12,4},{6,14},{14,6},{16,24},{24,... | collective-permute-start | bytes 2949128 | tf_op jit(solution)/shard_map/ppermute | solution.py:261
  156.3 4.7 %slice_bitcast_fusion = (bf16[2,512,1024]{2,1,0:T(8,128)(2,1)}, bf16[2,512,1024]{2,1,0:T(8,128)(2,1)}) fusion(bf16[2,512,2,1024]{3,1,0,2:T(8,128)(2,1)} %bitcast.67), kind=kLoop, calls=%fused_computation.2 | loop fusion | bytes 8388608 | tf_op jit(solution)/shard_map/squeeze | solution.py:486
  161.0 1.1 either.15.raw_ref
  162.1 1.1 either.17.zone_ref
  163.4 0.8 copy-done.7
  164.2 0.7 collective-permute-start.5
  164.9 1.5 fusion.7
  166.4 17.7 %collective-permute-done.13.end_ref = bf16[384,2,1024]{2,1,0:T(2,128)(2,1)} collective-permute-done((bf16[384,2,1024]{2,1,0:T(2,128)(2,1)}, bf16[384,2,1024]{2,1,0:T(2,128)(2,1)}, u32[]{:S(2)}, u32[]{:S(2)}) %collective-permute-start.13) | collective-permute-done | bytes 1572896 | tf_op jit(solution)/shard_map/ppermute | solution.py:261
  184.1 1.8 collective-permute-start.14
  185.9 1.2 copy_bitcast_fusion.3
  187.1 0.7 copy-done.20
  187.8 0.7 collective-permute-start.6
  188.5 1.0 copy-done.21
  189.5 0.9 either.11
  190.4 24.2 %collective-permute-start.9 = (bf16[80,2,1024]{2,1,0:T(2,128)(2,1)}, bf16[80,2,1024]{2,1,0:T(2,128)(2,1)}, u32[]{:S(2)}, u32[]{:S(2)}) collective-permute-start(bf16[80,2,1024]{2,1,0:T(2,128)(2,1)} %either.11), channel_id=1, source_target_pairs={{0,8},{8,0},{2,10},{10,2},{4,12},{12,4},{6,14},{14,6},{16,24},{24,... | collective-permute-start | bytes 983048 | tf_op jit(solution)/shard_map/ppermute | solution.py:261
  214.5 1.5 either.19.refs_8_
  216.1 1.6 collective-permute-start.12
  217.8 1.6 copy-done.17
  219.3 1.6 copy-done.18
  220.9 1.5 copy-done.19
  222.4 1.6 copy-done.28
  224.0 34.6 %attention.1 = f32[2,64,512]{2,1,0:T(8,128)S(1)} custom-call(bf16[2,512,1024]{2,1,0:T(8,128)(2,1)S(1)} %bitcast.65, bf16[2,512,1024]{2,1,0:T(8,128)(2,1)S(1)} %copy-done.16, bf16[2,512,1024]{2,1,0:T(8,128)(2,1)S(1)} %copy-done.15, bf16[2,512,1024]{2,1,0:T(8,128)(2,1)S(1)} %copy-done.18, bf16[2,512,1024]{2,1,0:T(8,128)(2,1)S(1)} %copy-done.17, ...), custom_call_target="tpu_custom_call" | custom-call | flops 5234491392 | bytes 25165824 | tf_op jit(solution)/shard_map/attention/pallas_call | solution.py:396
  258.7 2.5 collective-permute-start.7
  261.2 1.6 collective-permute-start.21
  263.2 1.1 join_head.2.whole_ref
  264.2 0.7 collective-permute-start.10
  265.5 0.7 collective-permute-start.8
  266.2 0.7 fusion.2
  266.9 0.7 fusion.1
  267.6 3.0 %restore.4.whole_ref = bf16[2,512,2,1024]{3,2,1,0:T(2,128)(2,1)} custom-call(s32[256]{0:T(256)S(1)} %squeeze.60.pairs_ref, bf16[384,2,1024]{2,1,0:T(2,128)(2,1)} %collective-permute-done.13.end_ref, bf16[384,2,1024]{2,1,0:T(2,128)(2,1)} %collective-permute-done.14.middle_ref, ...), custom_call_target="tpu_custom_call", output_to_operand_aliasing={{}: (3, {})} | custom-call | bytes 3145728 | tf_op jit(solution)/shard_map/restore/pallas_call | solution.py:199
  270.7 2.7 restore.5.whole_ref
  273.3 2.3 restore.6.whole_ref
  275.6 2.2 restore.7
  (117 shorter events, 4.0 us)
Async XLA Ops:
  4.9 4.5 %copy-start.5 = (bf16[2,64,2,1024]{3,2,1,0:T(2,128)(2,1)S(1)}, bf16[2,64,2,1024]{3,2,1,0:T(2,128)(2,1)}, u32[]{:S(2)}) copy-start(bf16[2,64,2,1024]{3,2,1,0:T(2,128)(2,1)} %slice_bitcast_fusion.6.after_ref.end_ref) | copy-start | bytes 1572868
  4.9 5.2 %copy-start.29 = (bf16[1,2,256,2,1024]{4,3,2,1,0:T(2,128)(2,1)S(1)}, bf16[1,2,256,2,1024]{4,3,2,1,0:T(2,128)(2,1)}, u32[]{:S(2)}) copy-start(bf16[1,2,256,2,1024]{4,3,2,1,0:T(2,128)(2,1)} %param.13) | copy-start | bytes 6291460
  8.8 2.2 collective-permute-start
  9.5 1.6 collective-permute-start.1
  10.8 0.9 copy-start.26
  11.0 1.3 copy-start.11
  11.1 1.3 copy-start.13
  11.7 1.4 copy-start.31
  12.4 1.0 collective-permute-start.2
  13.4 1.2 copy-start.3
  14.6 71.4 %collective-permute-start.3 = (bf16[384,2,1024]{2,1,0:T(2,128)(2,1)}, bf16[384,2,1024]{2,1,0:T(2,128)(2,1)S(1)}, u32[]{:S(2)}, u32[]{:S(2)}) collective-permute-start(bf16[384,2,1024]{2,1,0:T(2,128)(2,1)} %hold.4.end_ref), channel_id=1, source_target_pairs={{8,16},{16,8},{10,18},{18,10},{12,20},{20,12},{14,22},{22,14},{9,1... | collective-permute-start | bytes 4718600 | tf_op jit(solution)/shard_map/ppermute | solution.py:261
  15.7 1.4 copy-start.4
  18.4 120.0 %collective-permute-start.19 = (bf16[2,8,384,128]{3,2,1,0:T(8,128)(2,1)}, bf16[2,8,384,128]{3,2,1,0:T(8,128)(2,1)}, u32[]{:S(2)}, u32[]{:S(2)}) collective-permute-start(bf16[2,8,384,128]{3,2,1,0:T(8,128)(2,1)} %either.18), channel_id=1, source_target_pairs={{0,8},{8,0},{2,10},{10,2},{4,12},{12,4},{6,14},{14,6},{16,24},{24,... | collective-permute-start | bytes 4718600 | tf_op jit(solution)/shard_map/ppermute | solution.py:261
  86.0 1.1 copy-start
  87.1 64.1 %collective-permute-start.4 = (bf16[240,2,1024]{2,1,0:T(2,128)(2,1)}, bf16[240,2,1024]{2,1,0:T(2,128)(2,1)S(1)}, u32[]{:S(2)}, u32[]{:S(2)}) collective-permute-start(bf16[240,2,1024]{2,1,0:T(2,128)(2,1)} %hold.5.end_ref), channel_id=1, source_target_pairs={{8,16},{16,8},{10,18},{18,10},{12,20},{20,12},{14,22},{22,14},{9,1... | collective-permute-start | bytes 2949128 | tf_op jit(solution)/shard_map/ppermute | solution.py:261
  90.2 3.7 %copy-start.6 = (bf16[2,64,2,1024]{3,2,1,0:T(2,128)(2,1)S(1)}, bf16[2,64,2,1024]{3,2,1,0:T(2,128)(2,1)}, u32[]{:S(2)}) copy-start(bf16[2,64,2,1024]{3,2,1,0:T(2,128)(2,1)} %slice_bitcast_fusion.6.after_ref.end_ref) | copy-start | bytes 1572868
  90.2 3.7 %copy-start.14 = (bf16[2,64,2,1024]{3,2,1,0:T(2,128)(2,1)S(1)}, bf16[2,64,2,1024]{3,2,1,0:T(2,128)(2,1)}, u32[]{:S(2)}) copy-start(bf16[2,64,2,1024]{3,2,1,0:T(2,128)(2,1)} %copy-done.13) | copy-start | bytes 1572868
  90.2 35.8 %copy-start.12 = (bf16[2,64,2,1024]{3,2,1,0:T(2,128)(2,1)S(1)}, bf16[2,64,2,1024]{3,2,1,0:T(2,128)(2,1)}, u32[]{:S(2)}) copy-start(bf16[2,64,2,1024]{3,2,1,0:T(2,128)(2,1)} %copy-done.11) | copy-start | bytes 1572868
  90.2 35.8 %copy-start.24 = (bf16[2,64,2,1024]{3,2,1,0:T(2,128)(2,1)S(1)}, bf16[2,64,2,1024]{3,2,1,0:T(2,128)(2,1)}, u32[]{:S(2)}) copy-start(bf16[2,64,2,1024]{3,2,1,0:T(2,128)(2,1)} %get-tuple-element.12.end_ref) | copy-start | bytes 1572868
  93.9 33.1 %copy-start.1 = (bf16[384,2,1024]{2,1,0:T(2,128)(2,1)S(1)}, bf16[384,2,1024]{2,1,0:T(2,128)(2,1)}, u32[]{:S(2)}) copy-start(bf16[384,2,1024]{2,1,0:T(2,128)(2,1)} %copy-done) | copy-start | bytes 4718596
  93.9 33.1 %copy-start.2 = (bf16[384,2,1024]{2,1,0:T(2,128)(2,1)S(1)}, bf16[384,2,1024]{2,1,0:T(2,128)(2,1)}, u32[]{:S(2)}) copy-start(bf16[384,2,1024]{2,1,0:T(2,128)(2,1)} %hold.4.end_ref) | copy-start | bytes 4718596
  94.8 45.5 %collective-permute-start.15 = (bf16[2,64,2,1024]{3,2,1,0:T(2,128)(2,1)}, bf16[2,64,2,1024]{3,2,1,0:T(2,128)(2,1)}, u32[]{:S(2)}, u32[]{:S(2)}) collective-permute-start(bf16[2,64,2,1024]{3,2,1,0:T(2,128)(2,1)} %either.14), channel_id=1, source_target_pairs={{0,8},{8,0},{2,10},{10,2},{4,12},{12,4},{6,14},{14,6},{16,24},{24,... | collective-permute-start | bytes 1572872 | tf_op jit(solution)/shard_map/ppermute | solution.py:261
  126.9 23.5 %collective-permute-start.17 = (bf16[2,64,2,1024]{3,2,1,0:T(2,128)(2,1)}, bf16[2,64,2,1024]{3,2,1,0:T(2,128)(2,1)}, u32[]{:S(2)}, u32[]{:S(2)}) collective-permute-start(bf16[2,64,2,1024]{3,2,1,0:T(2,128)(2,1)} %either.16), channel_id=1, source_target_pairs={{0,8},{8,0},{2,10},{10,2},{4,12},{12,4},{6,14},{14,6},{16,24},{24,... | collective-permute-start | bytes 1572872 | tf_op jit(solution)/shard_map/ppermute | solution.py:261
  128.3 55.9 %collective-permute-start.13 = (bf16[384,2,1024]{2,1,0:T(2,128)(2,1)}, bf16[384,2,1024]{2,1,0:T(2,128)(2,1)}, u32[]{:S(2)}, u32[]{:S(2)}) collective-permute-start(bf16[384,2,1024]{2,1,0:T(2,128)(2,1)} %either.13), channel_id=1, source_target_pairs={{0,8},{8,0},{2,10},{10,2},{4,12},{12,4},{6,14},{14,6},{16,24},{24,... | collective-permute-start | bytes 4718600 | tf_op jit(solution)/shard_map/ppermute | solution.py:261
  132.7 5.6 %copy-start.33 = (s32[16]{0:T(128)S(1)}, s32[16]{0:T(128)}, u32[]{:S(2)}) copy-start(s32[16]{0:T(128)} %param.18) | copy-start | bytes 196
  132.7 18.5 %copy-start.10 = (bf16[240,2,1024]{2,1,0:T(2,128)(2,1)S(1)}, bf16[240,2,1024]{2,1,0:T(2,128)(2,1)}, u32[]{:S(2)}) copy-start(bf16[240,2,1024]{2,1,0:T(2,128)(2,1)} %hold.5.end_ref) | copy-start | bytes 2949124
  138.4 76.1 %collective-permute-start.20 = (bf16[2,8,384,128]{3,2,1,0:T(8,128)(2,1)}, bf16[2,8,384,128]{3,2,1,0:T(8,128)(2,1)}, u32[]{:S(2)}, u32[]{:S(2)}) collective-permute-start(bf16[2,8,384,128]{3,2,1,0:T(8,128)(2,1)} %collective-permute-done.19.end_ref), channel_id=1, source_target_pairs={{8,16},{16,8},{10,18},{18,10},{12,20},{20,12},{14,22},{22,14},{9,1... | collective-permute-start | bytes 4718600 | tf_op jit(solution)/shard_map/ppermute | solution.py:261
  140.3 20.7 %collective-permute-start.16 = (bf16[2,64,2,1024]{3,2,1,0:T(2,128)(2,1)}, bf16[2,64,2,1024]{3,2,1,0:T(2,128)(2,1)S(1)}, u32[]{:S(2)}, u32[]{:S(2)}) collective-permute-start(bf16[2,64,2,1024]{3,2,1,0:T(2,128)(2,1)} %collective-permute-done.15.end_ref), channel_id=1, source_target_pairs={{8,16},{16,8},{10,18},{18,10},{12,20},{20,12},{14,22},{22,14},{9,1... | collective-permute-start | bytes 1572872 | tf_op jit(solution)/shard_map/ppermute | solution.py:261
  150.4 11.7 %collective-permute-start.18 = (bf16[2,64,2,1024]{3,2,1,0:T(2,128)(2,1)}, bf16[2,64,2,1024]{3,2,1,0:T(2,128)(2,1)S(1)}, u32[]{:S(2)}, u32[]{:S(2)}) collective-permute-start(bf16[2,64,2,1024]{3,2,1,0:T(2,128)(2,1)} %collective-permute-done.17.end_ref), channel_id=1, source_target_pairs={{8,16},{16,8},{10,18},{18,10},{12,20},{20,12},{14,22},{22,14},{9,1... | collective-permute-start | bytes 1572872 | tf_op jit(solution)/shard_map/ppermute | solution.py:261
  151.2 9.8 %copy-start.9 = (bf16[240,2,1024]{2,1,0:T(2,128)(2,1)}, bf16[240,2,1024]{2,1,0:T(2,128)(2,1)S(1)}, u32[]{:S(2)}) copy-start(bf16[240,2,1024]{2,1,0:T(2,128)(2,1)S(1)} %collective-permute-done.4.after_ref.middle_ref) | copy-start | bytes 2949124
  152.5 63.5 %collective-permute-start.11 = (bf16[240,2,1024]{2,1,0:T(2,128)(2,1)}, bf16[240,2,1024]{2,1,0:T(2,128)(2,1)}, u32[]{:S(2)}, u32[]{:S(2)}) collective-permute-start(bf16[240,2,1024]{2,1,0:T(2,128)(2,1)} %either.12), channel_id=1, source_target_pairs={{0,8},{8,0},{2,10},{10,2},{4,12},{12,4},{6,14},{14,6},{16,24},{24,... | collective-permute-start | bytes 2949128 | tf_op jit(solution)/shard_map/ppermute | solution.py:261
  163.4 0.8 copy-start.7
  164.2 22.9 %collective-permute-start.5 = (bf16[80,2,1024]{2,1,0:T(2,128)(2,1)}, bf16[80,2,1024]{2,1,0:T(2,128)(2,1)S(1)}, u32[]{:S(2)}, u32[]{:S(2)}) collective-permute-start(bf16[80,2,1024]{2,1,0:T(2,128)(2,1)} %hold.6.end_ref), channel_id=1, source_target_pairs={{8,16},{16,8},{10,18},{18,10},{12,20},{20,12},{14,22},{22,14},{9,1... | collective-permute-start | bytes 983048 | tf_op jit(solution)/shard_map/ppermute | solution.py:261
  166.4 22.1 %copy-start.22 = (bf16[80,2,1024]{2,1,0:T(2,128)(2,1)S(1)}, bf16[80,2,1024]{2,1,0:T(2,128)(2,1)}, u32[]{:S(2)}) copy-start(bf16[80,2,1024]{2,1,0:T(2,128)(2,1)} %hold.6.end_ref) | copy-start | bytes 983044
  184.1 83.5 %collective-permute-start.14 = (bf16[384,2,1024]{2,1,0:T(2,128)(2,1)}, bf16[384,2,1024]{2,1,0:T(2,128)(2,1)}, u32[]{:S(2)}, u32[]{:S(2)}) collective-permute-start(bf16[384,2,1024]{2,1,0:T(2,128)(2,1)} %collective-permute-done.13.end_ref), channel_id=1, source_target_pairs={{8,16},{16,8},{10,18},{18,10},{12,20},{20,12},{14,22},{22,14},{9,1... | collective-permute-start | bytes 4718600 | tf_op jit(solution)/shard_map/ppermute | solution.py:261
  187.1 0.7 copy-start.20
  187.8 70.7 %collective-permute-start.6 = (bf16[64,2,1024]{2,1,0:T(2,128)(2,1)}, bf16[64,2,1024]{2,1,0:T(2,128)(2,1)S(1)}, u32[]{:S(2)}, u32[]{:S(2)}) collective-permute-start(bf16[64,2,1024]{2,1,0:T(2,128)(2,1)} %hold.7.end_ref), channel_id=1, source_target_pairs={{8,16},{16,8},{10,18},{18,10},{12,20},{20,12},{14,22},{22,14},{9,1... | collective-permute-start | bytes 786440 | tf_op jit(solution)/shard_map/ppermute | solution.py:261
  188.5 1.0 copy-start.21
  189.5 28.2 %copy-start.27 = (bf16[1024,64]{0,1:T(8,128)(2,1)S(1)}, bf16[1024,64]{0,1:T(8,128)(2,1)}, u32[]{:S(2)}) copy-start(bf16[1024,64]{0,1:T(8,128)(2,1)} %param.14) | copy-start | bytes 393220
  190.4 27.4 %copy-start.15 = (bf16[2,512,1024]{2,1,0:T(8,128)(2,1)S(1)}, bf16[2,512,1024]{2,1,0:T(8,128)(2,1)}, u32[]{:S(2)}) copy-start(bf16[2,512,1024]{2,1,0:T(8,128)(2,1)} %get-tuple-element.21.refs_2_) | copy-start | bytes 6291460
  190.4 27.4 %copy-start.16 = (bf16[2,512,1024]{2,1,0:T(8,128)(2,1)S(1)}, bf16[2,512,1024]{2,1,0:T(8,128)(2,1)}, u32[]{:S(2)}) copy-start(bf16[2,512,1024]{2,1,0:T(8,128)(2,1)} %get-tuple-element.22.refs_1_) | copy-start | bytes 6291460
  190.4 27.4 %copy-start.25 = (bf16[2,128,1024]{2,1,0:T(8,128)(2,1)S(1)}, bf16[2,128,1024]{2,1,0:T(8,128)(2,1)}, u32[]{:S(2)}) copy-start(bf16[2,128,1024]{2,1,0:T(8,128)(2,1)} %get-tuple-element.32.refs_5_) | copy-start | bytes 1572868
  190.4 73.9 %collective-permute-start.9 = (bf16[80,2,1024]{2,1,0:T(2,128)(2,1)}, bf16[80,2,1024]{2,1,0:T(2,128)(2,1)}, u32[]{:S(2)}, u32[]{:S(2)}) collective-permute-start(bf16[80,2,1024]{2,1,0:T(2,128)(2,1)} %either.11), channel_id=1, source_target_pairs={{0,8},{8,0},{2,10},{10,2},{4,12},{12,4},{6,14},{14,6},{16,24},{24,... | collective-permute-start | bytes 983048 | tf_op jit(solution)/shard_map/ppermute | solution.py:261
  216.1 54.6 %collective-permute-start.12 = (bf16[240,2,1024]{2,1,0:T(2,128)(2,1)}, bf16[240,2,1024]{2,1,0:T(2,128)(2,1)}, u32[]{:S(2)}, u32[]{:S(2)}) collective-permute-start(bf16[240,2,1024]{2,1,0:T(2,128)(2,1)} %collective-permute-done.11.end_ref), channel_id=1, source_target_pairs={{8,16},{16,8},{10,18},{18,10},{12,20},{20,12},{14,22},{22,14},{9,1... | collective-permute-start | bytes 2949128 | tf_op jit(solution)/shard_map/ppermute | solution.py:261
  217.7 1.6 copy-start.17
  219.3 1.6 copy-start.18
  220.9 1.5 copy-start.19
  222.4 1.6 copy-start.28
  224.0 34.6 %copy-start.23 = (bf16[64,2,1024]{2,1,0:T(2,128)(2,1)S(1)}, bf16[64,2,1024]{2,1,0:T(2,128)(2,1)}, u32[]{:S(2)}) copy-start(bf16[64,2,1024]{2,1,0:T(2,128)(2,1)} %hold.7.end_ref) | copy-start | bytes 786436
  224.0 38.7 %copy-start.32 = (s32[16,2]{0,1:T(2,128)S(1)}, s32[16,2]{0,1:T(2,128)}, u32[]{:S(2)}) copy-start(s32[16,2]{0,1:T(2,128)} %param.19) | copy-start | bytes 388
  224.0 39.2 %copy-start.8 = (bf16[2,64,2,1024]{3,2,1,0:T(2,128)(2,1)S(1)}, bf16[2,64,2,1024]{3,2,1,0:T(2,128)(2,1)}, u32[]{:S(2)}) copy-start(bf16[2,64,2,1024]{3,2,1,0:T(2,128)(2,1)} %copy-done.7) | copy-start | bytes 1572868
  258.7 6.8 %collective-permute-start.7 = (bf16[64,2,1024]{2,1,0:T(2,128)(2,1)S(1)}, bf16[64,2,1024]{2,1,0:T(2,128)(2,1)S(1)}, u32[]{:S(2)}, u32[]{:S(2)}) collective-permute-start(bf16[64,2,1024]{2,1,0:T(2,128)(2,1)S(1)} %either.10), channel_id=1, source_target_pairs={{0,8},{8,0},{2,10},{10,2},{4,12},{12,4},{6,14},{14,6},{16,24},{24,... | collective-permute-start | bytes 786440 | tf_op jit(solution)/shard_map/ppermute | solution.py:261
  261.2 5.0 %collective-permute-start.21 = (f32[2,64,256]{2,1,0:T(8,128)S(1)}, f32[2,64,256]{2,1,0:T(8,128)S(1)}, u32[]{:S(2)}, u32[]{:S(2)}) collective-permute-start(f32[2,64,256]{2,1,0:T(8,128)S(1)} %constant_dynamic-slice_fusion), channel_id=1, source_target_pairs={{1,0},{0,1},{3,2},{2,3},{5,4},{4,5},{7,6},{6,7},{9,8},{8,9},{11,10... | collective-permute-start | bytes 393224 | tf_op jit(solution)/shard_map/ppermute | solution.py:21
  263.1 3.7 %copy-start.30 = (f32[1,2,256,64]{2,3,1,0:T(8,128)S(1)}, f32[1,2,256,64]{2,3,1,0:T(8,128)}, u32[]{:S(2)}) copy-start(f32[1,2,256,64]{2,3,1,0:T(8,128)} %param.15) | copy-start | bytes 393220
  264.2 9.1 %collective-permute-start.10 = (bf16[80,2,1024]{2,1,0:T(2,128)(2,1)}, bf16[80,2,1024]{2,1,0:T(2,128)(2,1)S(1)}, u32[]{:S(2)}, u32[]{:S(2)}) collective-permute-start(bf16[80,2,1024]{2,1,0:T(2,128)(2,1)} %collective-permute-done.9.end_ref), channel_id=1, source_target_pairs={{8,16},{16,8},{10,18},{18,10},{12,20},{20,12},{14,22},{22,14},{9,1... | collective-permute-start | bytes 983048 | tf_op jit(solution)/shard_map/ppermute | solution.py:261
  265.5 10.1 %collective-permute-start.8 = (bf16[64,2,1024]{2,1,0:T(2,128)(2,1)S(1)}, bf16[64,2,1024]{2,1,0:T(2,128)(2,1)S(1)}, u32[]{:S(2)}, u32[]{:S(2)}) collective-permute-start(bf16[64,2,1024]{2,1,0:T(2,128)(2,1)S(1)} %collective-permute-done.7.end_ref), channel_id=1, source_target_pairs={{8,16},{16,8},{10,18},{18,10},{12,20},{20,12},{14,22},{22,14},{9,1... | collective-permute-start | bytes 786440 | tf_op jit(solution)/shard_map/ppermute | solution.py:261

commit v9 on v8

--- a/solution.py
+++ b/solution.py
@@ -211,7 +211,7 @@
         cost_estimate=pl.CostEstimate(flops=0, bytes_accessed=4 * ways[1].size, transcendentals=0),
         compiler_params=pltpu.CompilerParams(vmem_limit_bytes=VMEM_LIMIT),
         name="restore",
-    )(pairs, ways[1], ways[2], whole, *after)
+    )(pairs, *ways, whole, *after)
 
 
 def on_the_way(groups):
@@ -261,17 +261,17 @@
     return lax.ppermute(block, "grp", route)
 
 
-def pass_along(block, groups):
+def pass_direct(block, groups):
+    direct = from_behind(block, "grp", groups // 2)
+    return direct, direct
+
+
+def pass_around(block, groups):
     if groups != 16:
-        direct = from_behind(block, "grp", groups // 2)
-        return direct, direct, direct
-    crossed = swap_along(block, groups, [(1, 2)])
-    outer = swap_along(either(block, crossed, groups), groups, [(0, 1), (2, 3)])
-    return crossed, outer, swap_along(outer, groups, [(1, 2)])
-
-
-def arrived_block(ways, groups):
-    return ways[1] if groups != 16 else either(ways[1], ways[2], groups)
+        return pass_direct(block, groups)
+    crossed = swap_along(block, groups, [(0, 3)])
+    outer = swap_along(either(crossed, block, groups), groups, [(0, 1), (2, 3)])
+    return swap_along(outer, groups, [(0, 3)]), outer
 
 
 def hold_kernel(block_ref, after_ref, out_ref):
@@ -436,28 +436,22 @@
 
     raw = fresh_kv[0, :, :listed_count]
     groups = 2 * half_groups
-    raw_ways = pass_along(raw, groups)
+    raw_in = from_behind(raw, "grp", half_groups)
 
     my_list = lax.dynamic_index_in_dim(refresh_rows, my_group, 0, keepdims=False)
     partner_list = lax.dynamic_index_in_dim(refresh_rows, partner, 0, keepdims=False)
     near, far, sources = swap_pairs(jnp.stack([my_list, partner_list]))
     pairs = jnp.stack([near, far], axis=1).reshape(2, -1)
 
-    first_cut = hot_rows + (img_rows - hot_rows) * 5 // 8
-    last_cut = img_rows - listed_count
     final = slots - 1
-    pieces = [(slot, hot_rows, img_rows) for slot in range(final)]
-    pieces += [(final, hot_rows, first_cut), (final, first_cut, last_cut), (final, last_cut, img_rows)]
+    pieces = [(slot, hot_rows, img_rows) for slot in range(slots)]
     zone, blocks = arrange(pairs[0], fresh_kv, pieces, raw)
-    zone_ways = pass_along(zone, groups)
+    zone_in = from_behind(zone, "grp", half_groups)
     w_t = w_velocity.T
-    text_own = project_text(text[:, :, 0], text[:, :, 1], w_t, (zone_ways[0], raw_ways[0]))
-    text_ways = pass_along(text_own, groups)
-    piece_ways, gate = [], text_ways[0]
-    for block in blocks:
-        piece_ways.append(pass_along(hold(block, gate), groups))
-        gate = piece_ways[-1][0]
-    raw_in, zone_in, text_in = (arrived_block(ways, groups) for ways in (raw_ways, zone_ways, text_ways))
+    text_own = project_text(text[:, :, 0], text[:, :, 1], w_t, (zone,))
+    text_in = from_behind(text_own, "grp", half_groups)
+    piece_ways = [pass_direct(hold(block, text_in), groups) for block in blocks[:final]]
+    piece_ways.append(pass_around(blocks[final], groups))
 
     my_live = lax.dynamic_index_in_dim(live_counts, my_group, 0, keepdims=False)
     partner_live = lax.dynamic_index_in_dim(live_counts, partner, 0, keepdims=False)
@@ -515,7 +509,7 @@
     latent_next = latent[0] + step_size[:, None, None] * velocity
 
     next_stale = join_head(raw_in, zone_in, fresh.shape)
-    for index, piece in enumerate(pieces):
+    for index, piece in reversed(list(enumerate(pieces))):
         next_stale = restore(pairs[1], piece_ways[index], next_stale, piece, groups)
     return (next_stale[None], velocity[None], latent_next[None])
 

time: 280 us -> 260 us (0.929)
  starting transfers between devices: 144 us -> 15.9 us
  waiting for transfers between devices: 27.8 us -> 150 us
  Pallas kernels: 60.7 us -> 49.4 us
    ppermute x21 -> x3, starting transfers between devices: 143 us -> 7.16 us  [swap_along(): return lax.ppermute(block, 'grp', route)]
    ppermute x21 -> x3, waiting for transfers between devices: 27.8 us -> 93.3 us  [swap_along(): return lax.ppermute(block, 'grp', route)]
    ppermute x1 -> x5, waiting for transfers between devices: 0.02 us -> 56.7 us  [from_behind(): return lax.ppermute(block, axis, route)]
    pallas_call x10 -> x1, Pallas kernels: 10.3 us -> 2.6 us  [either(): pl.pallas_call(functools.partial(either_kernel, groups), out_shape=jax.Sh...]
    ppermute x1 -> x5, starting transfers between devices: 1.56 us -> 8.71 us  [from_behind(): return lax.ppermute(block, axis, route)]
    pallas_call x4 -> x2, Pallas kernels: 10.1 us -> 5.55 us  [restore(): pl.pallas_call(functools.partial(restore_kernel, slot, start, stop, group...]
    unnamed x71 -> x37, local copies, waits for them, and re-layouts: 23.1 us -> 21.8 us
  transfers between devices with their start and end apart: 22 -> 8, of which waited for: 3 -> 7; matrix products, arithmetic and copies ran while one was open for 9% -> 12% of each run, Pallas kernels for 19% -> 18%
where the time goes in v9:
time: 260 us
  waiting for transfers between devices  150 us (58%)
  Pallas kernels  49.4 us (19%)
  local copies, waits for them, and re-layouts  38.1 us (15%)
  starting transfers between devices  15.9 us (6%)
  other arithmetic  5.41 us (2%)
    ppermute x3, waiting for transfers between devices, swap_along(): return lax.ppermute(block, 'grp', route)  93.3 us
    ppermute x5, waiting for transfers between devices, from_behind(): return lax.ppermute(block, axis, route)  56.7 us
    pallas_call x1, Pallas kernels, attention(): pl.pallas_call(functools.partial(attention_kernel, text_rows), grid=(slot...  35.5 us
    unnamed x37, local copies, waits for them, and re-layouts  21.8 us
    ppermute x5, starting transfers between devices, from_behind(): return lax.ppermute(block, axis, route)  8.71 us
    ppermute x3, starting transfers between devices, swap_along(): return lax.ppermute(block, 'grp', route)  7.16 us
    pallas_call x2, Pallas kernels, restore(): pl.pallas_call(functools.partial(restore_kernel, slot, start, stop, group...  5.55 us
  transfers between devices with their start and end apart: 8, of which 7 were waited for; matrix products, arithmetic and copies ran while one was open for 12% of the time, Pallas kernels for 18%

profile of v9, /device:TPU:0, one launch (start us, length us, event | category | flops | bytes accessed | tf_op | source)
XLA Modules:
  0.0 259.7 jit_solution(2089347925931859837)
XLA Ops:
  0.6 1.4 slice_bitcast_fusion.6.after_ref
  2.0 0.0 copy-start.11
  2.1 4.1 %collective-permute-start.5 = (bf16[2,64,2,1024]{3,2,1,0:T(2,128)(2,1)S(1)}, bf16[2,64,2,1024]{3,2,1,0:T(2,128)(2,1)S(1)}, u32[]{:S(2)}, u32[]{:S(2)}) collective-permute-start(bf16[2,64,2,1024]{3,2,1,0:T(2,128)(2,1)S(1)} %slice_bitcast_fusion.6.after_ref), channel_id=1, source_target_pairs={{16,0},{18,2},{20,4},{22,6},{24,8},{26,10},{28,12},{30,14},{0,16},... | collective-permute-start | bytes 1572872 | tf_op jit(solution)/shard_map/ppermute | solution.py:21
  6.2 0.7 constant_dynamic-slice_fusion.4
  6.9 0.1 compare_reduce_fusion
  7.0 0.2 convert_reduce_fusion.1
  7.3 0.3 select_reduce_fusion
  7.6 0.6 squeeze.59.pairs_ref
  8.2 3.9 %arrange.1 = (bf16[2,64,2,1024]{3,2,1,0:T(2,128)(2,1)}, bf16[384,2,1024]{2,1,0:T(2,128)(2,1)}, bf16[384,2,1024]{2,1,0:T(2,128)(2,1)}) custom-call(s32[256]{0:T(256)} %squeeze.59.pairs_ref, bf16[1,2,512,2,1024]{4,3,2,1,0:T(2,128)(2,1)} %fresh_ref.1, bf16[2,64,2,1024]{3,2,1,0:T(2,128)(2,1)} %copy-done.11), custom_call_target="tpu_custom_call" | custom-call | bytes 8388608 | tf_op jit(solution)/shard_map/arrange/pallas_call | solution.py:117
  12.2 0.1 collective-permute-start.6
  12.3 0.6 copy.63
  12.9 0.0 copy-start.8
  13.0 0.2 slice_bitcast_fusion.4
  13.1 0.8 copy-done.7
  14.0 0.0 copy-done.8
  14.0 0.6 project_text.1.refs_7_
  14.6 2.9 %collective-permute-start = (bf16[2,8,384,128]{3,2,1,0:T(8,128)(2,1)S(1)}, bf16[2,8,384,128]{3,2,1,0:T(8,128)(2,1)}, u32[]{:S(2)}, u32[]{:S(2)}) collective-permute-start(bf16[2,8,384,128]{3,2,1,0:T(8,128)(2,1)S(1)} %project_text.1.refs_7_), channel_id=1, source_target_pairs={{16,0},{18,2},{20,4},{22,6},{24,8},{26,10},{28,12},{30,14},{0,16},... | collective-permute-start | bytes 4718600 | tf_op jit(solution)/shard_map/ppermute | solution.py:21
  17.5 3.2 %collective-permute-start.2 = (bf16[384,2,1024]{2,1,0:T(2,128)(2,1)}, bf16[384,2,1024]{2,1,0:T(2,128)(2,1)}, u32[]{:S(2)}, u32[]{:S(2)}) collective-permute-start(bf16[384,2,1024]{2,1,0:T(2,128)(2,1)} %get-tuple-element.8.middle_ref), channel_id=1, source_target_pairs={{0,24},{24,0},{2,26},{26,2},{4,28},{28,4},{6,30},{30,6},{1,25},{25... | collective-permute-start | bytes 4718600 | tf_op jit(solution)/shard_map/ppermute | solution.py:261
  20.8 0.1 pad_add_fusion.2
  20.9 0.1 compare_reduce_fusion.1
  21.0 5.5 %copy.62 = bf16[1,2,512,2,1024]{4,2,1,3,0:T(8,128)(2,1)} copy(bf16[1,2,512,2,1024]{4,3,2,1,0:T(2,128)(2,1)} %fresh_ref.1) | data formatting | bytes 8388608 | tf_op args[1]
  26.6 5.5 %copy.61 = bf16[1,2,512,2,1024]{4,2,1,3,0:T(8,128)(2,1)} copy(bf16[1,2,512,2,1024]{4,3,2,1,0:T(2,128)(2,1)} %param.12) | data formatting | bytes 8388608 | tf_op args[2]
  32.1 0.1 dynamic_slice.29
  32.1 0.2 fusion.4
  32.4 0.1 fusion
  32.5 0.1 and_bitcast_fusion.1
  32.6 0.1 broadcast_compare_fusion
  32.6 0.1 and_bitcast_fusion
  32.7 4.8 %slice_bitcast_fusion.2 = (bf16[2,512,1024]{2,1,0:T(8,128)(2,1)}, bf16[2,512,1024]{2,1,0:T(8,128)(2,1)}) fusion(bf16[2,512,2,1024]{3,1,0,2:T(8,128)(2,1)} %bitcast.67), kind=kLoop, calls=%fused_computation.4 | loop fusion | bytes 8388608 | tf_op jit(solution)/shard_map/squeeze | solution.py:478
  37.5 2.5 slice_bitcast_fusion
  40.0 58.0 %collective-permute-done.2.end_ref = bf16[384,2,1024]{2,1,0:T(2,128)(2,1)} collective-permute-done((bf16[384,2,1024]{2,1,0:T(2,128)(2,1)}, bf16[384,2,1024]{2,1,0:T(2,128)(2,1)}, u32[]{:S(2)}, u32[]{:S(2)}) %collective-permute-start.2) | collective-permute-done | bytes 1572896 | tf_op jit(solution)/shard_map/ppermute | solution.py:261
  98.0 2.6 either.1
  100.6 0.1 collective-permute-start.3
  100.7 0.1 compare_convert_fusion
  100.8 1.3 copy.53
  102.1 2.4 broadcast_select_fusion.refs_10_
  104.5 4.4 %collective-permute-done.5.raw_ref = bf16[2,64,2,1024]{3,2,1,0:T(2,128)(2,1)S(1)} collective-permute-done((bf16[2,64,2,1024]{3,2,1,0:T(2,128)(2,1)S(1)}, bf16[2,64,2,1024]{3,2,1,0:T(2,128)(2,1)S(1)}, u32[]{:S(2)}, u32[]{:S(2)}) %collective-permute-start.5) | collective-permute-done | bytes 524320 | tf_op jit(solution)/shard_map/ppermute | solution.py:21
  108.9 11.2 %collective-permute-done.6.zone_ref = bf16[2,64,2,1024]{3,2,1,0:T(2,128)(2,1)S(1)} collective-permute-done((bf16[2,64,2,1024]{3,2,1,0:T(2,128)(2,1)}, bf16[2,64,2,1024]{3,2,1,0:T(2,128)(2,1)S(1)}, u32[]{:S(2)}, u32[]{:S(2)}) %collective-permute-start.6) | collective-permute-done | bytes 524320 | tf_op jit(solution)/shard_map/ppermute | solution.py:21
  120.1 0.2 join_head.3
  120.3 2.5 fusion.7
  122.8 30.3 %collective-permute-done.after_ref.refs_8_ = bf16[2,8,384,128]{3,2,1,0:T(8,128)(2,1)} collective-permute-done((bf16[2,8,384,128]{3,2,1,0:T(8,128)(2,1)S(1)}, bf16[2,8,384,128]{3,2,1,0:T(8,128)(2,1)}, u32[]{:S(2)}, u32[]{:S(2)}) %collective-permute-start) | collective-permute-done | bytes 1572896 | tf_op jit(solution)/shard_map/ppermute | solution.py:21
  153.1 0.0 collective-permute-start.1
  153.1 35.3 %collective-permute-done.3.middle_ref = bf16[384,2,1024]{2,1,0:T(2,128)(2,1)} collective-permute-done((bf16[384,2,1024]{2,1,0:T(2,128)(2,1)}, bf16[384,2,1024]{2,1,0:T(2,128)(2,1)}, u32[]{:S(2)}, u32[]{:S(2)}) %collective-permute-start.3) | collective-permute-done | bytes 1572896 | tf_op jit(solution)/shard_map/ppermute | solution.py:261
  188.4 3.8 %collective-permute-start.4 = (bf16[384,2,1024]{2,1,0:T(2,128)(2,1)}, bf16[384,2,1024]{2,1,0:T(2,128)(2,1)}, u32[]{:S(2)}, u32[]{:S(2)}) collective-permute-start(bf16[384,2,1024]{2,1,0:T(2,128)(2,1)} %collective-permute-done.3.middle_ref), channel_id=1, source_target_pairs={{0,24},{24,0},{2,26},{26,2},{4,28},{28,4},{6,30},{30,6},{1,25},{25... | collective-permute-start | bytes 4718600 | tf_op jit(solution)/shard_map/ppermute | solution.py:261
  192.3 1.9 copy_bitcast_fusion.3
  194.2 1.6 copy-done.1
  195.8 1.6 copy-done.2
  197.4 1.6 copy-done.3
  199.0 1.5 copy-done.4
  200.4 1.4 copy-done.6
  201.8 1.6 copy-done.9
  203.4 35.5 %attention.1 = f32[2,64,512]{2,1,0:T(8,128)S(1)} custom-call(bf16[2,512,1024]{2,1,0:T(8,128)(2,1)S(1)} %bitcast.65, bf16[2,512,1024]{2,1,0:T(8,128)(2,1)S(1)} %copy-done.1, bf16[2,512,1024]{2,1,0:T(8,128)(2,1)S(1)} %copy-done, bf16[2,512,1024]{2,1,0:T(8,128)(2,1)S(1)} %copy-done.3, bf16[2,512,1024]{2,1,0:T(8,128)(2,1)S(1)} %copy-done.2, ...), custom_call_target="tpu_custom_call" | custom-call | flops 5234491392 | bytes 25165824 | tf_op jit(solution)/shard_map/attention/pallas_call | solution.py:396
  238.9 1.6 collective-permute-start.7
  240.5 0.1 multiply_reduce_fusion
  240.6 0.1 squeeze.58.pairs_ref
  240.7 0.2 multiply_reduce_fusion.1
  240.9 0.0 copy-start.13
  240.9 1.1 join_head.2.whole_ref
  242.0 2.1 collective-permute-done.7
  244.1 0.7 fusion.2
  244.8 0.7 fusion.1
  245.5 3.1 %restore.2.whole_ref = bf16[2,512,2,1024]{3,2,1,0:T(2,128)(2,1)} custom-call(s32[256]{0:T(256)S(1)} %squeeze.58.pairs_ref, bf16[384,2,1024]{2,1,0:T(2,128)(2,1)} %collective-permute-done.4.end_ref, bf16[384,2,1024]{2,1,0:T(2,128)(2,1)} %collective-permute-done.3.middle_ref, bf16[2,512,2,1024]{3,2,1,0:T(2,128)(2,1)} %join_head.2.whole_ref), custom_call_target="tpu_custom_call", output_to_operand_aliasing={{}: (3, {})} | custom-call | bytes 3145728 | tf_op jit(solution)/shard_map/restore/pallas_call | solution.py:199
  248.6 8.6 %collective-permute-done.1.end_ref.middle_ref = bf16[384,2,1024]{2,1,0:T(2,128)(2,1)S(1)} collective-permute-done((bf16[384,2,1024]{2,1,0:T(2,128)(2,1)}, bf16[384,2,1024]{2,1,0:T(2,128)(2,1)S(1)}, u32[]{:S(2)}, u32[]{:S(2)}) %collective-permute-start.1) | collective-permute-done | bytes 1572896 | tf_op jit(solution)/shard_map/ppermute | solution.py:21
  257.2 2.5 restore.3
  (41 shorter events, 0.2 us)
Async XLA Ops:
  2.0 6.2 %copy-start.11 = (bf16[2,64,2,1024]{3,2,1,0:T(2,128)(2,1)}, bf16[2,64,2,1024]{3,2,1,0:T(2,128)(2,1)S(1)}, u32[]{:S(2)}) copy-start(bf16[2,64,2,1024]{3,2,1,0:T(2,128)(2,1)S(1)} %slice_bitcast_fusion.6.after_ref) | copy-start | bytes 1572868
  2.1 106.8 %collective-permute-start.5 = (bf16[2,64,2,1024]{3,2,1,0:T(2,128)(2,1)S(1)}, bf16[2,64,2,1024]{3,2,1,0:T(2,128)(2,1)S(1)}, u32[]{:S(2)}, u32[]{:S(2)}) collective-permute-start(bf16[2,64,2,1024]{3,2,1,0:T(2,128)(2,1)S(1)} %slice_bitcast_fusion.6.after_ref), channel_id=1, source_target_pairs={{16,0},{18,2},{20,4},{22,6},{24,8},{26,10},{28,12},{30,14},{0,16},... | collective-permute-start | bytes 1572872 | tf_op jit(solution)/shard_map/ppermute | solution.py:21
  8.2 4.1 %copy-start.12 = (bf16[1,2,256,2,1024]{4,3,2,1,0:T(2,128)(2,1)S(1)}, bf16[1,2,256,2,1024]{4,3,2,1,0:T(2,128)(2,1)}, u32[]{:S(2)}) copy-start(bf16[1,2,256,2,1024]{4,3,2,1,0:T(2,128)(2,1)} %param.13) | copy-start | bytes 6291460
  12.2 108.0 %collective-permute-start.6 = (bf16[2,64,2,1024]{3,2,1,0:T(2,128)(2,1)}, bf16[2,64,2,1024]{3,2,1,0:T(2,128)(2,1)S(1)}, u32[]{:S(2)}, u32[]{:S(2)}) collective-permute-start(bf16[2,64,2,1024]{3,2,1,0:T(2,128)(2,1)} %get-tuple-element.7.refs_0_), channel_id=1, source_target_pairs={{16,0},{18,2},{20,4},{22,6},{24,8},{26,10},{28,12},{30,14},{0,16},... | collective-permute-start | bytes 1572872 | tf_op jit(solution)/shard_map/ppermute | solution.py:21
  12.9 1.0 copy-start.7
  12.9 1.1 copy-start.8
  14.6 11.9 %copy-start.5 = (bf16[2,8,384,128]{3,2,1,0:T(8,128)(2,1)}, bf16[2,8,384,128]{3,2,1,0:T(8,128)(2,1)S(1)}, u32[]{:S(2)}) copy-start(bf16[2,8,384,128]{3,2,1,0:T(8,128)(2,1)S(1)} %project_text.1.refs_7_) | copy-start | bytes 4718596
  14.6 138.5 %collective-permute-start = (bf16[2,8,384,128]{3,2,1,0:T(8,128)(2,1)S(1)}, bf16[2,8,384,128]{3,2,1,0:T(8,128)(2,1)}, u32[]{:S(2)}, u32[]{:S(2)}) collective-permute-start(bf16[2,8,384,128]{3,2,1,0:T(8,128)(2,1)S(1)} %project_text.1.refs_7_), channel_id=1, source_target_pairs={{16,0},{18,2},{20,4},{22,6},{24,8},{26,10},{28,12},{30,14},{0,16},... | collective-permute-start | bytes 4718600 | tf_op jit(solution)/shard_map/ppermute | solution.py:21
  17.5 80.5 %collective-permute-start.2 = (bf16[384,2,1024]{2,1,0:T(2,128)(2,1)}, bf16[384,2,1024]{2,1,0:T(2,128)(2,1)}, u32[]{:S(2)}, u32[]{:S(2)}) collective-permute-start(bf16[384,2,1024]{2,1,0:T(2,128)(2,1)} %get-tuple-element.8.middle_ref), channel_id=1, source_target_pairs={{0,24},{24,0},{2,26},{26,2},{4,28},{28,4},{6,30},{30,6},{1,25},{25... | collective-permute-start | bytes 4718600 | tf_op jit(solution)/shard_map/ppermute | solution.py:261
  26.5 5.5 %copy-start.16 = (s32[16]{0:T(128)S(1)}, s32[16]{0:T(128)}, u32[]{:S(2)}) copy-start(s32[16]{0:T(128)} %param.18) | copy-start | bytes 196
  26.5 5.6 %copy-start.14 = (s32[16,2]{0,1:T(2,128)S(1)}, s32[16,2]{0,1:T(2,128)}, u32[]{:S(2)}) copy-start(s32[16,2]{0,1:T(2,128)} %param.16) | copy-start | bytes 388
  32.7 4.8 %copy-start.10 = (bf16[1,2,512,2,1024]{4,2,1,3,0:T(8,128)(2,1)S(1)}, bf16[1,2,512,2,1024]{4,2,1,3,0:T(8,128)(2,1)}, u32[]{:S(2)}) copy-start(bf16[1,2,512,2,1024]{4,2,1,3,0:T(8,128)(2,1)} %copy.61) | copy-start | bytes 12582916
  100.6 87.8 %collective-permute-start.3 = (bf16[384,2,1024]{2,1,0:T(2,128)(2,1)}, bf16[384,2,1024]{2,1,0:T(2,128)(2,1)}, u32[]{:S(2)}, u32[]{:S(2)}) collective-permute-start(bf16[384,2,1024]{2,1,0:T(2,128)(2,1)} %either.1), channel_id=1, source_target_pairs={{0,8},{8,0},{2,10},{10,2},{4,12},{12,4},{6,14},{14,6},{16,24},{24,... | collective-permute-start | bytes 4718600 | tf_op jit(solution)/shard_map/ppermute | solution.py:261
  153.1 41.1 %copy-start = (bf16[2,512,1024]{2,1,0:T(8,128)(2,1)S(1)}, bf16[2,512,1024]{2,1,0:T(8,128)(2,1)}, u32[]{:S(2)}) copy-start(bf16[2,512,1024]{2,1,0:T(8,128)(2,1)} %get-tuple-element.17.refs_2_) | copy-start | bytes 6291460
  153.1 104.1 %collective-permute-start.1 = (bf16[384,2,1024]{2,1,0:T(2,128)(2,1)}, bf16[384,2,1024]{2,1,0:T(2,128)(2,1)S(1)}, u32[]{:S(2)}, u32[]{:S(2)}) collective-permute-start(bf16[384,2,1024]{2,1,0:T(2,128)(2,1)} %hold.1), channel_id=1, source_target_pairs={{16,0},{18,2},{20,4},{22,6},{24,8},{26,10},{28,12},{30,14},{0,16},... | collective-permute-start | bytes 4718600 | tf_op jit(solution)/shard_map/ppermute | solution.py:21
  188.4 57.1 %collective-permute-start.4 = (bf16[384,2,1024]{2,1,0:T(2,128)(2,1)}, bf16[384,2,1024]{2,1,0:T(2,128)(2,1)}, u32[]{:S(2)}, u32[]{:S(2)}) collective-permute-start(bf16[384,2,1024]{2,1,0:T(2,128)(2,1)} %collective-permute-done.3.middle_ref), channel_id=1, source_target_pairs={{0,24},{24,0},{2,26},{26,2},{4,28},{28,4},{6,30},{30,6},{1,25},{25... | collective-permute-start | bytes 4718600 | tf_op jit(solution)/shard_map/ppermute | solution.py:261
  194.2 1.6 copy-start.1
  195.8 1.6 copy-start.2
  197.4 1.6 copy-start.3
  199.0 1.5 copy-start.4
  200.4 1.4 copy-start.6
  201.8 1.6 copy-start.9
  203.4 37.1 %copy-start.15 = (s32[16,2]{0,1:T(2,128)S(1)}, s32[16,2]{0,1:T(2,128)}, u32[]{:S(2)}) copy-start(s32[16,2]{0,1:T(2,128)} %param.19) | copy-start | bytes 388
  238.9 5.2 %collective-permute-start.7 = (f32[2,64,256]{2,1,0:T(8,128)S(1)}, f32[2,64,256]{2,1,0:T(8,128)S(1)}, u32[]{:S(2)}, u32[]{:S(2)}) collective-permute-start(f32[2,64,256]{2,1,0:T(8,128)S(1)} %constant_dynamic-slice_fusion), channel_id=1, source_target_pairs={{1,0},{0,1},{3,2},{2,3},{5,4},{4,5},{7,6},{6,7},{9,8},{8,9},{11,10... | collective-permute-start | bytes 393224 | tf_op jit(solution)/shard_map/ppermute | solution.py:21
  240.9 3.9 %copy-start.13 = (f32[1,2,256,64]{2,3,1,0:T(8,128)S(1)}, f32[1,2,256,64]{2,3,1,0:T(8,128)}, u32[]{:S(2)}) copy-start(f32[1,2,256,64]{2,3,1,0:T(8,128)} %param.15) | copy-start | bytes 393220

commit v10 on v7

--- a/solution.py
+++ b/solution.py
@@ -382,15 +382,11 @@
 
     both = range(slots)
 
-    def pass_on(block, slot):
-        if half_groups != 8:
-            return [from_behind(block, "grp", half_groups)]
-        step = half_groups // 2 if slot % 2 == 0 else half_groups + half_groups // 2
-        first = from_behind(block, "grp", step)
-        return [first, from_behind(first, "grp", step)]
+    def pass_on(block):
+        return [from_behind(block, "grp", half_groups)]
 
     raw = [fresh_kv[0, slot, :listed_count] for slot in both]
-    raw_way = [pass_on(raw[slot], slot) for slot in both]
+    raw_way = [pass_on(raw[slot]) for slot in both]
 
     my_list = lax.dynamic_index_in_dim(refresh_rows, my_group, 0, keepdims=False)
     partner_list = lax.dynamic_index_in_dim(refresh_rows, partner, 0, keepdims=False)
@@ -398,21 +394,19 @@
     pairs = jnp.stack([near, far], axis=1).reshape(2, -1)
 
     rest = img_rows - hot_rows
-    cuts = [hot_rows, hot_rows + rest // 2, img_rows - listed_count, img_rows]
+    cuts = [hot_rows, hot_rows + rest // 2, img_rows]
     layers = [[(slot, start, stop) for slot in both] for start, stop in zip(cuts[:-1], cuts[1:])]
     zone, blocks = arrange(pairs[0], fresh_kv, sum(layers, []), raw)
-    zone_way = [pass_on(zone[slot], slot) for slot in both]
+    zone_way = [pass_on(zone[slot]) for slot in both]
     w_t = w_velocity.T
     text_own = [project_text(text[slot, :, 0], text[slot, :, 1], w_t, zone[slot]) for slot in both]
-    text_way = [pass_on(text_own[slot], slot) for slot in both]
+    text_way = [pass_on(text_own[slot]) for slot in both]
     layer_way = []
     for index in range(len(layers)):
         ways = []
         for slot in both:
-            gate = (text_way[slot][0], text_way[slot][-1], None)[index]
-            if gate is None:
-                gate = layer_way[index - 1][slot][0]
-            ways.append(pass_on(hold(blocks[index * slots + slot], gate), slot))
+            gate = (raw_way, text_way)[index][slot][0]
+            ways.append(pass_on(hold(blocks[index * slots + slot], gate)))
         layer_way.append(ways)
 
     my_live = lax.dynamic_index_in_dim(live_counts, my_group, 0, keepdims=False)

time: 261 us -> 259 us (level)
  starting transfers between devices: 46.1 us -> 14.9 us
  waiting for transfers between devices: 128 us -> 151 us
  local copies, waits for them, and re-layouts: 31 us -> 36.2 us
    ppermute x25 -> x11, starting transfers between devices: 46.1 us -> 14.9 us  [from_behind(): return lax.ppermute(block, axis, route)]
    ppermute x25 -> x11, waiting for transfers between devices: 128 us -> 151 us  [from_behind(): return lax.ppermute(block, axis, route)]
    unnamed x67, local copies, waits for them, and re-layouts: 14.2 us -> 19.9 us
    pallas_call x3 -> x2, Pallas kernels: 7.85 us -> 5.7 us  [restore(): pl.pallas_call(functools.partial(restore_kernel, pieces), out_shape=jax.S...]
  transfers between devices with their start and end apart: 25 -> 11, of which waited for: 11 -> 7; matrix products, arithmetic and copies ran while one was open for 8% -> 10% of each run, Pallas kernels for 18% -> 18%
where the time goes in v10:
time: 259 us; the launch traced here: 258 us
  waiting for transfers between devices  151 us (58%)
  Pallas kernels  49.7 us (19%)
  local copies, waits for them, and re-layouts  36.2 us (14%)
  starting transfers between devices  14.9 us (6%)
  other arithmetic  4.79 us (2%)
    ppermute x11, waiting for transfers between devices, from_behind(): return lax.ppermute(block, axis, route)  151 us
    pallas_call x2, Pallas kernels, attention(): pl.pallas_call(functools.partial(attention_kernel, text_rows), grid=(head...  36.5 us
    unnamed x67, local copies, waits for them, and re-layouts  19.9 us
    ppermute x11, starting transfers between devices, from_behind(): return lax.ppermute(block, axis, route)  14.9 us
    pallas_call x2, Pallas kernels, restore(): pl.pallas_call(functools.partial(restore_kernel, pieces), out_shape=jax.S...  5.7 us
  transfers between devices with their start and end apart: 11, of which 7 were waited for; matrix products, arithmetic and copies ran while one was open for 10% of the time, Pallas kernels for 18%

profile of v10, /device:TPU:0, one launch (start us, length us, event | category | flops | bytes accessed | tf_op | source)
XLA Modules:
  0.0 258.2 jit_solution(6492598548655791606)
XLA Ops:
  0.6 2.4 slice_bitcast_fusion.14
  3.0 4.0 %collective-permute-start.6 = (bf16[64,2,1024]{2,1,0:T(2,128)(2,1)}, bf16[64,2,1024]{2,1,0:T(2,128)(2,1)S(1)}, u32[]{:S(2)}, u32[]{:S(2)}) collective-permute-start(bf16[64,2,1024]{2,1,0:T(2,128)(2,1)} %get-tuple-element.31.refs_1_), channel_id=1, source_target_pairs={{16,0},{18,2},{20,4},{22,6},{24,8},{26,10},{28,12},{30,14},{0,16},... | collective-permute-start | bytes 786440 | tf_op jit(solution)/shard_map/ppermute | solution.py:21
  7.1 0.7 constant_dynamic-slice_fusion.3
  7.8 0.1 compare_reduce_fusion
  7.9 0.2 convert_reduce_fusion.1
  8.2 0.3 select_reduce_fusion
  8.5 0.6 pad_add_fusion
  9.1 0.6 squeeze.98.pairs_ref
  9.7 3.7 %arrange.1 = (bf16[64,2,1024]{2,1,0:T(2,128)(2,1)}, bf16[64,2,1024]{2,1,0:T(2,128)(2,1)}, bf16[192,2,1024]{2,1,0:T(2,128)(2,1)}, bf16[192,2,1024]{2,1,0:T(2,128)...) custom-call(s32[256]{0:T(256)} %squeeze.98.pairs_ref, bf16[1,2,512,2,1024]{4,3,2,1,0:T(2,128)(2,1)} %fresh_ref.1, ...), custom_call_target="tpu_custom_call" | custom-call | bytes 8388608 | tf_op jit(solution)/shard_map/arrange/pallas_call | solution.py:118
  13.5 3.0 %collective-permute-start.9 = (bf16[64,2,1024]{2,1,0:T(2,128)(2,1)}, bf16[64,2,1024]{2,1,0:T(2,128)(2,1)S(1)}, u32[]{:S(2)}, u32[]{:S(2)}) collective-permute-start(bf16[64,2,1024]{2,1,0:T(2,128)(2,1)} %get-tuple-element.12.after_ref), channel_id=1, source_target_pairs={{16,0},{18,2},{20,4},{22,6},{24,8},{26,10},{28,12},{30,14},{0,16},... | collective-permute-start | bytes 786440 | tf_op jit(solution)/shard_map/ppermute | solution.py:21
  16.4 0.6 copy.72
  17.1 0.2 slice_bitcast_fusion.10
  17.3 1.2 project_text.3.refs_7_
  18.6 2.9 %collective-permute-start.8 = (bf16[64,2,1024]{2,1,0:T(2,128)(2,1)S(1)}, bf16[64,2,1024]{2,1,0:T(2,128)(2,1)S(1)}, u32[]{:S(2)}, u32[]{:S(2)}) collective-permute-start(bf16[64,2,1024]{2,1,0:T(2,128)(2,1)S(1)} %copy-done.17), channel_id=1, source_target_pairs={{16,0},{18,2},{20,4},{22,6},{24,8},{26,10},{28,12},{30,14},{0,16},... | collective-permute-start | bytes 786440 | tf_op jit(solution)/shard_map/ppermute | solution.py:21
  21.4 3.3 %copy.71 = bf16[1,2,512,2,1024]{4,2,3,1,0:T(8,128)(2,1)} copy(bf16[1,2,512,2,1024]{4,3,2,1,0:T(2,128)(2,1)S(1)} %copy-done.21) | data formatting | bytes 8388608 | tf_op args[1]
  24.8 0.1 fusion
  25.0 0.1 compare_reduce_fusion.1
  25.1 0.2 fusion.7
  25.5 0.4 copy-done.28
  25.9 3.5 %copy.70 = bf16[1,2,512,2,1024]{4,2,3,1,0:T(8,128)(2,1)S(1)} copy(bf16[1,2,512,2,1024]{4,3,2,1,0:T(2,128)(2,1)} %param.12) | data formatting | bytes 8388608 | tf_op args[2]
  29.4 2.2 slice_bitcast_fusion
  31.6 1.5 copy-done.22
  33.1 2.1 slice_bitcast_fusion.2
  35.3 0.8 copy-done.24
  36.1 1.1 slice_bitcast_fusion.8
  37.2 0.7 dynamic_slice.29
  37.9 0.6 compare_convert_fusion
  38.6 0.6 iota_add_fusion
  39.2 1.2 copy.58.refs_10_
  40.4 1.3 copy.55.refs_10_
  41.7 1.2 project_text.2.refs_7_
  42.9 0.8 broadcast_compare_fusion
  43.7 21.3 %collective-permute-done.9.refs_3_.refs_1_ = bf16[64,2,1024]{2,1,0:T(2,128)(2,1)S(1)} collective-permute-done((bf16[64,2,1024]{2,1,0:T(2,128)(2,1)}, bf16[64,2,1024]{2,1,0:T(2,128)(2,1)S(1)}, u32[]{:S(2)}, u32[]{:S(2)}) %collective-permute-start.9) | collective-permute-done | bytes 262176 | tf_op jit(solution)/shard_map/ppermute | solution.py:21
  65.0 0.1 join_head.5
  65.1 1.5 fusion.11
  66.6 0.7 copy-done.2
  67.3 2.9 %collective-permute-start.5 = (bf16[192,2,1024]{2,1,0:T(2,128)(2,1)}, bf16[192,2,1024]{2,1,0:T(2,128)(2,1)}, u32[]{:S(2)}, u32[]{:S(2)}) collective-permute-start(bf16[192,2,1024]{2,1,0:T(2,128)(2,1)} %hold.6), channel_id=1, source_target_pairs={{16,0},{18,2},{20,4},{22,6},{24,8},{26,10},{28,12},{30,14},{0,16},... | collective-permute-start | bytes 2359304 | tf_op jit(solution)/shard_map/ppermute | solution.py:21
  70.3 67.7 %collective-permute-done.8.refs_2_.refs_1_ = bf16[64,2,1024]{2,1,0:T(2,128)(2,1)S(1)} collective-permute-done((bf16[64,2,1024]{2,1,0:T(2,128)(2,1)S(1)}, bf16[64,2,1024]{2,1,0:T(2,128)(2,1)S(1)}, u32[]{:S(2)}, u32[]{:S(2)}) %collective-permute-start.8) | collective-permute-done | bytes 262176 | tf_op jit(solution)/shard_map/ppermute | solution.py:21
  138.0 0.9 copy-done.3
  138.9 0.1 join_head.4
  139.1 1.0 copy_bitcast_fusion.3
  140.0 0.7 fusion.12
  140.8 0.2 copy_bitcast_fusion.5
  141.0 30.8 %collective-permute-done.after_ref.refs_8_ = bf16[8,384,128]{2,1,0:T(8,128)(2,1)} collective-permute-done((bf16[8,384,128]{2,1,0:T(8,128)(2,1)}, bf16[8,384,128]{2,1,0:T(8,128)(2,1)}, u32[]{:S(2)}, u32[]{:S(2)}) %collective-permute-start) | collective-permute-done | bytes 786464 | tf_op jit(solution)/shard_map/ppermute | solution.py:21
  171.8 1.2 copy-done.10
  173.0 1.2 copy-done.11
  174.3 1.2 copy-done.12
  175.5 1.2 copy-done.13
  176.7 1.2 copy-done.15
  177.9 0.9 copy-done.19
  178.8 0.9 copy-done.20
  179.8 18.2 %attention.3 = f32[64,512]{1,0:T(8,128)S(1)} custom-call(bf16[512,1024]{1,0:T(8,128)(2,1)S(1)} %copy-done.5, bf16[512,1024]{1,0:T(8,128)(2,1)S(1)} %copy-done.13, bf16[512,1024]{1,0:T(8,128)(2,1)S(1)} %copy-done.12, bf16[512,1024]{1,0:T(8,128)(2,1)S(1)} %copy-done.11, bf16[512,1024]{1,0:T(8,128)(2,1)S(1)} %copy-done.10, bf16[128,1024]{1,0:T(8,128)(2,1)S(1)} %copy-done.20, ...), custom_call_target="tpu_custom_call" | custom-call | flops 2617245696 | bytes 12582912 | tf_op jit(solution)/shard_map/attention/pallas_call | solution.py:342
  198.1 18.3 %attention.2 = f32[64,512]{1,0:T(8,128)S(1)} custom-call(bf16[512,1024]{1,0:T(8,128)(2,1)S(1)} %get-tuple-element.34.refs_0_, bf16[512,1024]{1,0:T(8,128)(2,1)S(1)} %copy-done.9, bf16[512,1024]{1,0:T(8,128)(2,1)S(1)} %copy-done.8, bf16[512,1024]{1,0:T(8,128)(2,1)S(1)} %copy-done.7, bf16[512,1024]{1,0:T(8,128)(2,1)S(1)} %copy-done.6, ...), custom_call_target="tpu_custom_call" | custom-call | flops 2617245696 | bytes 12582912 | tf_op jit(solution)/shard_map/attention/pallas_call | solution.py:342
  216.5 1.9 collective-permute-start.10
  218.4 0.1 multiply_reduce_fusion
  218.6 0.2 multiply_reduce_fusion.1
  218.8 1.1 join_head.3.refs_2_
  219.9 1.6 collective-permute-done.10
  221.5 0.7 fusion.5
  222.2 0.1 collective-permute-done.7.refs_1_
  222.4 2.8 %restore.2.refs_2_ = bf16[2,512,2,1024]{3,2,1,0:T(2,128)(2,1)} custom-call(s32[256]{0:T(256)S(1)} %squeeze.97.pairs_ref, bf16[192,2,1024]{2,1,0:T(2,128)(2,1)} %collective-permute-done.5.refs_0_, bf16[192,2,1024]{2,1,0:T(2,128)(2,1)} %collective-permute-done.7.refs_1_, bf16[2,512,2,1024]{3,2,1,0:T(2,128)(2,1)} %join_head.3.refs_2_), custom_call_target="tpu_custom_call", output_to_operand_aliasing={{}: (3, {})} | custom-call | bytes 3145728 | tf_op jit(solution)/shard_map/restore/pallas_call | solution.py:206
  225.2 14.0 %collective-permute-done.3.refs_1_ = bf16[192,2,1024]{2,1,0:T(2,128)(2,1)} collective-permute-done((bf16[192,2,1024]{2,1,0:T(2,128)(2,1)}, bf16[192,2,1024]{2,1,0:T(2,128)(2,1)}, u32[]{:S(2)}, u32[]{:S(2)}) %collective-permute-start.3) | collective-permute-done | bytes 786464 | tf_op jit(solution)/shard_map/ppermute | solution.py:21
  239.2 16.0 %collective-permute-done.1.refs_0_ = bf16[192,2,1024]{2,1,0:T(2,128)(2,1)} collective-permute-done((bf16[192,2,1024]{2,1,0:T(2,128)(2,1)}, bf16[192,2,1024]{2,1,0:T(2,128)(2,1)}, u32[]{:S(2)}, u32[]{:S(2)}) %collective-permute-start.1) | collective-permute-done | bytes 786464 | tf_op jit(solution)/shard_map/ppermute | solution.py:21
  255.2 2.8 %restore.3 = bf16[2,512,2,1024]{3,2,1,0:T(2,128)(2,1)} custom-call(s32[256]{0:T(256)S(1)} %squeeze.97.pairs_ref, bf16[192,2,1024]{2,1,0:T(2,128)(2,1)} %collective-permute-done.1.refs_0_, bf16[192,2,1024]{2,1,0:T(2,128)(2,1)} %collective-permute-done.3.refs_1_, bf16[2,512,2,1024]{3,2,1,0:T(2,128)(2,1)} %restore.2.refs_2_), custom_call_target="tpu_custom_call", output_to_operand_aliasing={{}: (3, {})} | custom-call | bytes 3145728 | tf_op jit(solution)/shard_map/restore/pallas_call | solution.py:206
  (85 shorter events, 0.8 us)
Async XLA Ops:
  0.6 15.8 %copy-start.23 = (bf16[1,2,256,2,1024]{4,3,2,1,0:T(2,128)(2,1)S(1)}, bf16[1,2,256,2,1024]{4,3,2,1,0:T(2,128)(2,1)}, u32[]{:S(2)}) copy-start(bf16[1,2,256,2,1024]{4,3,2,1,0:T(2,128)(2,1)} %param.13) | copy-start | bytes 6291460
  3.0 61.9 %collective-permute-start.6 = (bf16[64,2,1024]{2,1,0:T(2,128)(2,1)}, bf16[64,2,1024]{2,1,0:T(2,128)(2,1)S(1)}, u32[]{:S(2)}, u32[]{:S(2)}) collective-permute-start(bf16[64,2,1024]{2,1,0:T(2,128)(2,1)} %get-tuple-element.31.refs_1_), channel_id=1, source_target_pairs={{16,0},{18,2},{20,4},{22,6},{24,8},{26,10},{28,12},{30,14},{0,16},... | collective-permute-start | bytes 786440 | tf_op jit(solution)/shard_map/ppermute | solution.py:21
  7.0 59.6 %collective-permute-start.4 = (bf16[64,2,1024]{2,1,0:T(2,128)(2,1)}, bf16[64,2,1024]{2,1,0:T(2,128)(2,1)S(1)}, u32[]{:S(2)}, u32[]{:S(2)}) collective-permute-start(bf16[64,2,1024]{2,1,0:T(2,128)(2,1)} %get-tuple-element.32.refs_0_), channel_id=1, source_target_pairs={{16,0},{18,2},{20,4},{22,6},{24,8},{26,10},{28,12},{30,14},{0,16},... | collective-permute-start | bytes 786440 | tf_op jit(solution)/shard_map/ppermute | solution.py:21
  13.4 3.8 %copy-start.16 = (bf16[1024,64]{0,1:T(8,128)(2,1)S(1)}, bf16[1024,64]{0,1:T(8,128)(2,1)}, u32[]{:S(2)}) copy-start(bf16[1024,64]{0,1:T(8,128)(2,1)} %param.14) | copy-start | bytes 393220
  13.4 3.8 %copy-start.18 = (bf16[64,2,1024]{2,1,0:T(2,128)(2,1)S(1)}, bf16[64,2,1024]{2,1,0:T(2,128)(2,1)}, u32[]{:S(2)}) copy-start(bf16[64,2,1024]{2,1,0:T(2,128)(2,1)} %get-tuple-element.12.after_ref) | copy-start | bytes 786436
  13.5 51.5 %collective-permute-start.9 = (bf16[64,2,1024]{2,1,0:T(2,128)(2,1)}, bf16[64,2,1024]{2,1,0:T(2,128)(2,1)S(1)}, u32[]{:S(2)}, u32[]{:S(2)}) collective-permute-start(bf16[64,2,1024]{2,1,0:T(2,128)(2,1)} %get-tuple-element.12.after_ref), channel_id=1, source_target_pairs={{16,0},{18,2},{20,4},{22,6},{24,8},{26,10},{28,12},{30,14},{0,16},... | collective-permute-start | bytes 786440 | tf_op jit(solution)/shard_map/ppermute | solution.py:21
  17.1 1.5 copy-start.17
  17.1 4.3 %copy-start.21 = (bf16[1,2,512,2,1024]{4,3,2,1,0:T(2,128)(2,1)S(1)}, bf16[1,2,512,2,1024]{4,3,2,1,0:T(2,128)(2,1)}, u32[]{:S(2)}) copy-start(bf16[1,2,512,2,1024]{4,3,2,1,0:T(2,128)(2,1)} %fresh_ref.1) | copy-start | bytes 12582916
  18.5 122.4 %collective-permute-start.2 = (bf16[8,384,128]{2,1,0:T(8,128)(2,1)}, bf16[8,384,128]{2,1,0:T(8,128)(2,1)}, u32[]{:S(2)}, u32[]{:S(2)}) collective-permute-start(bf16[8,384,128]{2,1,0:T(8,128)(2,1)} %project_text.3.refs_7_), channel_id=1, source_target_pairs={{16,0},{18,2},{20,4},{22,6},{24,8},{26,10},{28,12},{30,14},{0,16},... | collective-permute-start | bytes 2359304 | tf_op jit(solution)/shard_map/ppermute | solution.py:21
  18.6 6.5 %copy-start.29 = (s32[16,2]{0,1:T(2,128)S(1)}, s32[16,2]{0,1:T(2,128)}, u32[]{:S(2)}) copy-start(s32[16,2]{0,1:T(2,128)} %param.16) | copy-start | bytes 388
  18.6 119.4 %collective-permute-start.8 = (bf16[64,2,1024]{2,1,0:T(2,128)(2,1)S(1)}, bf16[64,2,1024]{2,1,0:T(2,128)(2,1)S(1)}, u32[]{:S(2)}, u32[]{:S(2)}) collective-permute-start(bf16[64,2,1024]{2,1,0:T(2,128)(2,1)S(1)} %copy-done.17), channel_id=1, source_target_pairs={{16,0},{18,2},{20,4},{22,6},{24,8},{26,10},{28,12},{30,14},{0,16},... | collective-permute-start | bytes 786440 | tf_op jit(solution)/shard_map/ppermute | solution.py:21
  25.3 0.6 copy-start.28
  29.4 3.7 %copy-start.22 = (bf16[1,2,512,2,1024]{4,2,3,1,0:T(8,128)(2,1)S(1)}, bf16[1,2,512,2,1024]{4,2,3,1,0:T(8,128)(2,1)}, u32[]{:S(2)}) copy-start(bf16[1,2,512,2,1024]{4,2,3,1,0:T(8,128)(2,1)} %copy.71) | copy-start | bytes 12582916
  33.1 2.9 %copy-start.24 = (bf16[1,2,512,1024]{3,2,1,0:T(8,128)(2,1)S(1)}, bf16[1,2,512,1024]{3,2,1,0:T(8,128)(2,1)}, u32[]{:S(2)}) copy-start(bf16[1,2,512,1024]{3,2,1,0:T(8,128)(2,1)} %param.10) | copy-start | bytes 6291460
  65.0 106.8 %collective-permute-start = (bf16[8,384,128]{2,1,0:T(8,128)(2,1)}, bf16[8,384,128]{2,1,0:T(8,128)(2,1)}, u32[]{:S(2)}, u32[]{:S(2)}) collective-permute-start(bf16[8,384,128]{2,1,0:T(8,128)(2,1)} %project_text.2.refs_7_), channel_id=1, source_target_pairs={{16,0},{18,2},{20,4},{22,6},{24,8},{26,10},{28,12},{30,14},{0,16},... | collective-permute-start | bytes 2359304 | tf_op jit(solution)/shard_map/ppermute | solution.py:21
  65.0 5.3 %copy-start = (bf16[64,2,1024]{2,1,0:T(2,128)(2,1)}, bf16[64,2,1024]{2,1,0:T(2,128)(2,1)S(1)}, u32[]{:S(2)}) copy-start(bf16[64,2,1024]{2,1,0:T(2,128)(2,1)S(1)} %collective-permute-done.6.after_ref.refs_1_.refs_0_) | copy-start | bytes 786436
  66.6 72.5 %copy-start.25 = (bf16[1,128,1,1024]{3,2,1,0:T(2,128)(2,1)S(1)}, bf16[1,128,1,1024]{3,2,1,0:T(2,128)(2,1)}, u32[]{:S(2)}) copy-start(bf16[1,128,1,1024]{3,2,1,0:T(2,128)(2,1)} %get-tuple-element.40) | copy-start | bytes 786436
  66.6 0.7 copy-start.2
  67.3 154.9 %collective-permute-start.5 = (bf16[192,2,1024]{2,1,0:T(2,128)(2,1)}, bf16[192,2,1024]{2,1,0:T(2,128)(2,1)}, u32[]{:S(2)}, u32[]{:S(2)}) collective-permute-start(bf16[192,2,1024]{2,1,0:T(2,128)(2,1)} %hold.6), channel_id=1, source_target_pairs={{16,0},{18,2},{20,4},{22,6},{24,8},{26,10},{28,12},{30,14},{0,16},... | collective-permute-start | bytes 2359304 | tf_op jit(solution)/shard_map/ppermute | solution.py:21
  70.2 152.1 %collective-permute-start.7 = (bf16[192,2,1024]{2,1,0:T(2,128)(2,1)}, bf16[192,2,1024]{2,1,0:T(2,128)(2,1)}, u32[]{:S(2)}, u32[]{:S(2)}) collective-permute-start(bf16[192,2,1024]{2,1,0:T(2,128)(2,1)} %hold.7), channel_id=1, source_target_pairs={{16,0},{18,2},{20,4},{22,6},{24,8},{26,10},{28,12},{30,14},{0,16},... | collective-permute-start | bytes 2359304 | tf_op jit(solution)/shard_map/ppermute | solution.py:21
  138.0 1.0 copy-start.3
  140.0 31.8 %copy-start.5 = (bf16[512,1024]{1,0:T(8,128)(2,1)S(1)}, bf16[512,1024]{1,0:T(8,128)(2,1)}, u32[]{:S(2)}) copy-start(bf16[512,1024]{1,0:T(8,128)(2,1)} %get-tuple-element.33.refs_0_) | copy-start | bytes 3145732
  140.9 98.3 %collective-permute-start.3 = (bf16[192,2,1024]{2,1,0:T(2,128)(2,1)}, bf16[192,2,1024]{2,1,0:T(2,128)(2,1)}, u32[]{:S(2)}, u32[]{:S(2)}) collective-permute-start(bf16[192,2,1024]{2,1,0:T(2,128)(2,1)} %hold.5), channel_id=1, source_target_pairs={{16,0},{18,2},{20,4},{22,6},{24,8},{26,10},{28,12},{30,14},{0,16},... | collective-permute-start | bytes 2359304 | tf_op jit(solution)/shard_map/ppermute | solution.py:21
  171.8 83.4 %collective-permute-start.1 = (bf16[192,2,1024]{2,1,0:T(2,128)(2,1)}, bf16[192,2,1024]{2,1,0:T(2,128)(2,1)}, u32[]{:S(2)}, u32[]{:S(2)}) collective-permute-start(bf16[192,2,1024]{2,1,0:T(2,128)(2,1)} %hold.4), channel_id=1, source_target_pairs={{16,0},{18,2},{20,4},{22,6},{24,8},{26,10},{28,12},{30,14},{0,16},... | collective-permute-start | bytes 2359304 | tf_op jit(solution)/shard_map/ppermute | solution.py:21
  171.8 1.2 copy-start.10
  173.0 1.2 copy-start.11
  174.3 1.2 copy-start.12
  175.5 1.2 copy-start.13
  176.7 1.2 copy-start.15
  177.9 0.9 copy-start.19
  178.8 0.9 copy-start.20
  179.8 18.3 %copy-start.6 = (bf16[512,1024]{1,0:T(8,128)(2,1)S(1)}, bf16[512,1024]{1,0:T(8,128)(2,1)}, u32[]{:S(2)}) copy-start(bf16[512,1024]{1,0:T(8,128)(2,1)} %get-tuple-element.25.refs_4_) | copy-start | bytes 3145732
  179.8 18.3 %copy-start.7 = (bf16[512,1024]{1,0:T(8,128)(2,1)S(1)}, bf16[512,1024]{1,0:T(8,128)(2,1)}, u32[]{:S(2)}) copy-start(bf16[512,1024]{1,0:T(8,128)(2,1)} %get-tuple-element.26.refs_3_) | copy-start | bytes 3145732
  179.8 18.3 %copy-start.8 = (bf16[512,1024]{1,0:T(8,128)(2,1)S(1)}, bf16[512,1024]{1,0:T(8,128)(2,1)}, u32[]{:S(2)}) copy-start(bf16[512,1024]{1,0:T(8,128)(2,1)} %get-tuple-element.29.refs_2_) | copy-start | bytes 3145732
  179.8 18.3 %copy-start.9 = (bf16[512,1024]{1,0:T(8,128)(2,1)S(1)}, bf16[512,1024]{1,0:T(8,128)(2,1)}, u32[]{:S(2)}) copy-start(bf16[512,1024]{1,0:T(8,128)(2,1)} %get-tuple-element.30.refs_1_) | copy-start | bytes 3145732
  179.8 18.3 %copy-start.14 = (f32[1664,1]{1,0:T(8,128)S(1)}, f32[1664,1]{1,0:T(8,128)}, u32[]{:S(2)}) copy-start(f32[1664,1]{1,0:T(8,128)} %copy.55.refs_10_) | copy-start | bytes 19972
  198.1 20.3 %copy-start.30 = (s32[16,2]{0,1:T(2,128)S(1)}, s32[16,2]{0,1:T(2,128)}, u32[]{:S(2)}) copy-start(s32[16,2]{0,1:T(2,128)} %param.19) | copy-start | bytes 388
  198.1 20.3 %copy-start.31 = (s32[2,16]{1,0:T(2,128)S(1)}, s32[2,16]{1,0:T(2,128)}, u32[]{:S(2)}) copy-start(s32[2,16]{1,0:T(2,128)} %compare_convert_fusion) | copy-start | bytes 388
  198.1 20.4 %copy-start.27 = (s32[1,2,2,64]{3,2,0,1:T(2,128)S(1)}, s32[1,2,2,64]{3,2,0,1:T(2,128)}, u32[]{:S(2)}) copy-start(s32[1,2,2,64]{3,2,0,1:T(2,128)} %get-tuple-element.48) | copy-start | bytes 3076
  198.1 20.7 %copy-start.1 = (bf16[64,2,1024]{2,1,0:T(2,128)(2,1)S(1)}, bf16[64,2,1024]{2,1,0:T(2,128)(2,1)}, u32[]{:S(2)}) copy-start(bf16[64,2,1024]{2,1,0:T(2,128)(2,1)} %copy-done) | copy-start | bytes 786436
  198.1 20.7 %copy-start.4 = (bf16[64,2,1024]{2,1,0:T(2,128)(2,1)S(1)}, bf16[64,2,1024]{2,1,0:T(2,128)(2,1)}, u32[]{:S(2)}) copy-start(bf16[64,2,1024]{2,1,0:T(2,128)(2,1)} %copy-done.2) | copy-start | bytes 786436
  216.4 5.1 %copy-start.26 = (f32[1,2,256,64]{2,3,1,0:T(8,128)S(1)}, f32[1,2,256,64]{2,3,1,0:T(8,128)}, u32[]{:S(2)}) copy-start(f32[1,2,256,64]{2,3,1,0:T(8,128)} %param.15) | copy-start | bytes 393220
  216.5 5.0 %collective-permute-start.10 = (f32[2,64,256]{2,1,0:T(8,128)S(1)}, f32[2,64,256]{2,1,0:T(8,128)S(1)}, u32[]{:S(2)}, u32[]{:S(2)}) collective-permute-start(f32[2,64,256]{2,1,0:T(8,128)S(1)} %fusion.1), channel_id=1, source_target_pairs={{1,0},{0,1},{3,2},{2,3},{5,4},{4,5},{7,6},{6,7},{9,8},{8,9},{11,10... | collective-permute-start | bytes 393224 | tf_op jit(solution)/shard_map/ppermute | solution.py:21

commit v11 on v5

--- a/solution.py
+++ b/solution.py
@@ -21,13 +21,13 @@
     return lax.ppermute(block, axis, route)
 
 
-def swap_pairs(lists):
+def swap_pairs(lists, first):
     count = lists.shape[2]
-    zone = count + jnp.arange(count, dtype=jnp.int32)
+    zone = first + jnp.arange(count, dtype=jnp.int32)
     order = jnp.arange(count, dtype=jnp.int32)
     earlier = order[:, None] >= order[None, :]
     free = jnp.logical_not(jnp.any(lists[..., :, None] == zone, axis=2))
-    outside = lists >= 2 * count
+    outside = lists >= first + count
     free_rank = jnp.sum((earlier & free[..., None, :]).astype(jnp.int32), axis=3)
     outside_rank = jnp.sum((earlier & outside[..., None, :]).astype(jnp.int32), axis=3)
     match = (
@@ -73,6 +73,7 @@
     pairs, zones, rests, sems = refs[1 + len(pieces) :]
     count = zones.shape[1] - 1
     rest_rows = rests.shape[1] - 1
+    below = fresh_ref.shape[2] - rest_rows
     copy_pairs = pltpu.make_async_copy(pairs_ref, pairs, sems.at[3 * slots + len(pieces)])
     copy_pairs.start()
     copies_in = []
@@ -80,10 +81,10 @@
         copies_in.append(
             (
                 pltpu.make_async_copy(
-                    fresh_ref.at[0, slot, count : 2 * count], zones.at[slot, :count], sems.at[slot]
+                    fresh_ref.at[0, slot, below - count : below], zones.at[slot, :count], sems.at[slot]
                 ),
                 pltpu.make_async_copy(
-                    fresh_ref.at[0, slot, 2 * count :], rests.at[slot, :rest_rows], sems.at[slots + slot]
+                    fresh_ref.at[0, slot, below:], rests.at[slot, :rest_rows], sems.at[slots + slot]
                 ),
             )
         )
@@ -94,14 +95,14 @@
     for slot in range(slots):
         for copy in copies_in[slot]:
             copy.wait()
-        swap_rows(pairs, slots, slot, zones.at[slot], rests.at[slot], 2 * count, 2 * count + rest_rows)
+        swap_rows(pairs, slots, slot, zones.at[slot], rests.at[slot], below, below + rest_rows)
         copies_out.append(
             pltpu.make_async_copy(zones.at[slot, :count], zone_out.at[slot], sems.at[2 * slots + slot])
         )
         copies_out[-1].start()
         for index, (piece_slot, start, stop) in enumerate(pieces):
             if piece_slot == slot:
-                source = rests.at[slot, start - 2 * count : stop - 2 * count]
+                source = rests.at[slot, start - below : stop - below]
                 copies_out.append(
                     pltpu.make_async_copy(source, piece_outs[index], sems.at[3 * slots + index])
                 )
@@ -110,7 +111,7 @@
         copy.wait()
 
 
-def arrange(pairs, fresh_kv, pieces, after):
+def arrange(pairs, fresh_kv, pieces, below, after):
     slots, rows = fresh_kv.shape[1:3]
     tail = fresh_kv.shape[3:]
     count = pairs.shape[0] // (2 * slots)
@@ -123,7 +124,7 @@
         scratch_shapes=[
             pltpu.SMEM(pairs.shape, pairs.dtype),
             pltpu.VMEM((slots, count + 1) + tail, fresh_kv.dtype),
-            pltpu.VMEM((slots, rows - 2 * count + 1) + tail, fresh_kv.dtype),
+            pltpu.VMEM((slots, rows - below + 1) + tail, fresh_kv.dtype),
             pltpu.SemaphoreType.DMA((3 * slots + len(pieces) + 1,)),
         ],
         cost_estimate=pl.CostEstimate(flops=0, bytes_accessed=4 * fresh_kv.size, transcendentals=0),
@@ -133,15 +134,23 @@
     return outs[0], outs[1:]
 
 
-def join_kernel(raw_ref, zone_ref, out_ref, stage, sems):
-    count = raw_ref.shape[1]
-    relay(
-        [
-            (raw_ref, stage.at[0], out_ref.at[:, :count]),
-            (zone_ref, stage.at[1], out_ref.at[:, count : 2 * count]),
-        ],
-        sems,
-    )
+def join_kernel(raw_ref, zone_ref, out_ref, raw, zone, sems):
+    first, count = raw.shape[1], zone.shape[1]
+    inner = [
+        pltpu.make_async_copy(raw_ref, raw, sems.at[0]),
+        pltpu.make_async_copy(zone_ref, zone, sems.at[1]),
+    ]
+    outer = [
+        pltpu.make_async_copy(raw, out_ref.at[:, :first], sems.at[2]),
+        pltpu.make_async_copy(zone, out_ref.at[:, first : first + count], sems.at[3]),
+    ]
+    for copy in inner:
+        copy.start()
+    for arrive, leave in zip(inner, outer):
+        arrive.wait()
+        leave.start()
+    for copy in outer:
+        copy.wait()
 
 
 def join_head(raw, zone, shape):
@@ -150,20 +159,24 @@
         out_shape=jax.ShapeDtypeStruct(shape, raw.dtype),
         in_specs=[pl.BlockSpec(memory_space=HBM)] * 2,
         out_specs=pl.BlockSpec(memory_space=HBM),
-        scratch_shapes=[pltpu.VMEM((2,) + raw.shape, raw.dtype), pltpu.SemaphoreType.DMA((2, 2))],
-        cost_estimate=pl.CostEstimate(flops=0, bytes_accessed=8 * raw.size, transcendentals=0),
+        scratch_shapes=[
+            pltpu.VMEM(raw.shape, raw.dtype),
+            pltpu.VMEM(zone.shape, raw.dtype),
+            pltpu.SemaphoreType.DMA((4,)),
+        ],
+        cost_estimate=pl.CostEstimate(flops=0, bytes_accessed=8 * zone.size, transcendentals=0),
         compiler_params=pltpu.CompilerParams(vmem_limit_bytes=VMEM_LIMIT),
         name="join_head",
     )(raw, zone)
 
 
-def restore_kernel(slot, start, stop, pairs_ref, piece_ref, whole_ref, *refs):
+def restore_kernel(slot, start, stop, first, pairs_ref, piece_ref, whole_ref, *refs):
     out_ref, pairs, zone, piece, sems = refs[-5:]
     count = zone.shape[0] - 1
     inner = [
         pltpu.make_async_copy(pairs_ref, pairs, sems.at[4]),
         pltpu.make_async_copy(piece_ref, piece.at[: stop - start], sems.at[0]),
-        pltpu.make_async_copy(out_ref.at[slot, count : 2 * count], zone.at[:count], sems.at[1]),
+        pltpu.make_async_copy(out_ref.at[slot, first : first + count], zone.at[:count], sems.at[1]),
     ]
     for copy in inner:
         copy.start()
@@ -172,7 +185,7 @@
     swap_rows(pairs, out_ref.shape[0], slot, zone, piece, start, stop)
     outer = [
         pltpu.make_async_copy(piece.at[: stop - start], out_ref.at[slot, start:stop], sems.at[2]),
-        pltpu.make_async_copy(zone.at[:count], out_ref.at[slot, count : 2 * count], sems.at[3]),
+        pltpu.make_async_copy(zone.at[:count], out_ref.at[slot, first : first + count], sems.at[3]),
     ]
     for copy in outer:
         copy.start()
@@ -180,12 +193,12 @@
         copy.wait()
 
 
-def restore(pairs, block, whole, piece, after=()):
+def restore(pairs, block, whole, piece, first, after=()):
     slot, start, stop = piece
     tail = whole.shape[2:]
     count = pairs.shape[0] // (2 * whole.shape[0])
     return pl.pallas_call(
-        functools.partial(restore_kernel, slot, start, stop),
+        functools.partial(restore_kernel, slot, start, stop, first),
         out_shape=jax.ShapeDtypeStruct(whole.shape, whole.dtype),
         in_specs=[pl.BlockSpec(memory_space=HBM)] * (3 + len(after)),
         out_specs=pl.BlockSpec(memory_space=HBM),
@@ -356,14 +369,15 @@
     queries, fresh, stale, text = queries[0], fresh_kv[0], stale_kv[0], text_kv[0]
     slots, img_rows = queries.shape[:2]
     listed_count = refresh_rows.shape[2]
-    hot_rows = 2 * listed_count
-
-    raw = fresh_kv[0, :, :listed_count]
+    first = listed_count // 2
+    hot_rows = first + listed_count
+
+    raw = fresh_kv[0, :, :first]
     raw_in = from_behind(raw, "grp", half_groups)
 
     my_list = lax.dynamic_index_in_dim(refresh_rows, my_group, 0, keepdims=False)
     partner_list = lax.dynamic_index_in_dim(refresh_rows, partner, 0, keepdims=False)
-    near, far, sources = swap_pairs(jnp.stack([my_list, partner_list]))
+    near, far, sources = swap_pairs(jnp.stack([my_list, partner_list]), first)
     pairs = jnp.stack([near, far], axis=1).reshape(2, -1)
 
     first_cut = hot_rows + (img_rows - hot_rows) * 5 // 8
@@ -371,7 +385,7 @@
     final = slots - 1
     pieces = [(slot, hot_rows, img_rows) for slot in range(final)]
     pieces += [(final, hot_rows, first_cut), (final, first_cut, last_cut), (final, last_cut, img_rows)]
-    zone, blocks = arrange(pairs[0], fresh_kv, pieces, raw)
+    zone, blocks = arrange(pairs[0], fresh_kv, pieces, hot_rows, raw)
     zone_in = from_behind(zone, "grp", half_groups)
     w_t = w_velocity.T
     text_own = project_text(text[:, :, 0], text[:, :, 1], w_t, zone)
@@ -391,7 +405,7 @@
     partner_live = lax.dynamic_index_in_dim(live_counts, partner, 0, keepdims=False)
     row_ids = jnp.arange(img_rows, dtype=jnp.int32)
     hot_source = jnp.concatenate(
-        [jnp.broadcast_to(row_ids[:listed_count], partner_list.shape), sources[1]], axis=1
+        [jnp.broadcast_to(row_ids[:first], (slots, first)), sources[1]], axis=1
     )
     stale_listed = jnp.any(partner_list[:, :, None] == row_ids, axis=1)
     hot_listed = jnp.any(partner_list[:, :, None] == hot_source[:, None, :], axis=1)
@@ -444,7 +458,7 @@
 
     next_stale = join_head(raw_in, zone_in, fresh.shape)
     for index, piece in enumerate(pieces):
-        next_stale = restore(pairs[1], arrived[index], next_stale, piece, held[index + 2 : index + 3])
+        next_stale = restore(pairs[1], arrived[index], next_stale, piece, first, held[index + 2 : index + 3])
     return (next_stale[None], velocity[None], latent_next[None])
 
 

time: 257 us -> 257 us (level)
  other arithmetic: 5.37 us -> 9.91 us
    unnamed x53 -> x57, local copies, waits for them, and re-layouts: 25.6 us -> 23.5 us
  transfers between devices with their start and end apart: 8 -> 8, of which waited for: 7 -> 7; matrix products, arithmetic and copies ran while one was open for 13% -> 14% of each run, Pallas kernels for 23% -> 22%
where the time goes in v11:
time: 257 us; the launch traced here: 256 us
  waiting for transfers between devices  135 us (53%)
  Pallas kernels  59.1 us (23%)
  local copies, waits for them, and re-layouts  41.9 us (16%)
  other arithmetic  9.91 us (4%)
  starting transfers between devices  8.93 us (3%)
    ppermute x8, waiting for transfers between devices, from_behind(): return lax.ppermute(block, axis, route)  135 us
    pallas_call x1, Pallas kernels, attention(): pl.pallas_call(functools.partial(attention_kernel, text_rows), grid=(slot...  34.1 us
    unnamed x57, local copies, waits for them, and re-layouts  23.5 us
    pallas_call x1, Pallas kernels, project_text(): pl.pallas_call(text_kernel, grid=(slots, heads), out_shape=jax.ShapeDtype...  10.1 us
    pallas_call x4, Pallas kernels, restore(): pl.pallas_call(functools.partial(restore_kernel, slot, start, stop, first...  9.79 us
    ppermute x8, starting transfers between devices, from_behind(): return lax.ppermute(block, axis, route)  8.93 us
  transfers between devices with their start and end apart: 8, of which 7 were waited for; matrix products, arithmetic and copies ran while one was open for 14% of the time, Pallas kernels for 22%

profile of v11, /device:TPU:0, one launch (start us, length us, event | category | flops | bytes accessed | tf_op | source)
XLA Modules:
  0.0 255.9 jit_solution(2172362403771458753)
XLA Ops:
  0.6 1.1 slice_bitcast_fusion.6.after_ref
  1.8 4.1 %collective-permute-start.3 = (bf16[2,32,2,1024]{3,2,1,0:T(2,128)(2,1)S(1)}, bf16[2,32,2,1024]{3,2,1,0:T(2,128)(2,1)S(1)}, u32[]{:S(2)}, u32[]{:S(2)}) collective-permute-start(bf16[2,32,2,1024]{3,2,1,0:T(2,128)(2,1)S(1)} %slice_bitcast_fusion.6.after_ref), channel_id=1, source_target_pairs={{16,0},{18,2},{20,4},{22,6},{24,8},{26,10},{28,12},{30,14},{0,16},... | collective-permute-start | bytes 786440 | tf_op jit(solution)/shard_map/ppermute | solution.py:21
  5.9 0.7 constant_dynamic-slice_fusion.4
  6.6 0.1 compare_reduce_fusion
  6.8 0.2 convert_reduce_fusion.1
  7.0 0.3 select_reduce_fusion
  7.3 0.6 pad_add_fusion
  7.9 0.6 squeeze.61.pairs_ref
  8.5 4.0 %arrange.1 = (bf16[2,64,2,1024]{3,2,1,0:T(2,128)(2,1)}, bf16[416,2,1024]{2,1,0:T(2,128)(2,1)}, bf16[260,2,1024]{2,1,0:T(2,128)(2,1)}, bf16[92,2,1024]{2,1,0:T(2,128)(2,1)}, bf16[64,2,1024]{2,1,0:T(2,128)(2,1)}) custom-call(s32[256]{0:T(256)} %squeeze.61.pairs_ref, bf16[1,2,512,2,1024]{4,3,2,1,0:T(2,128)(2,1)} %fresh_ref.1, bf16[2,32,2,1024]{3,2,1,0:T(2,128)(2,1)} %copy-done.22), custom_call_target="tpu_custom_call" | custom-call | bytes 8388608 | tf_op jit(solution)/shard_map/arrange/pallas_call | solution.py:118
  12.5 0.1 collective-permute-start.6
  12.6 0.6 copy.68
  13.2 1.5 slice_bitcast_fusion.4
  14.7 10.1 %project_text.1.refs_7_ = bf16[2,8,384,128]{3,2,1,0:T(8,128)(2,1)} custom-call(bf16[2,256,1024]{2,1,0:T(8,128)(2,1)} %get-tuple-element.24.k_ref, bf16[2,256,1024]{2,1,0:T(8,128)(2,1)} %get-tuple-element.23.v_ref, bf16[64,1024]{1,0:T(8,128)(2,1)} %bitcast.63, bf16[2,64,2,1024]{3,2,1,0:T(2,128)(2,1)} %get-tuple-element.10.after_ref), custom_call_target="tpu_custom_call" | custom-call | flops 67108864 | bytes 4194304 | tf_op jit(solution)/shard_map/project_text/pallas_call | solution.py:254
  24.8 2.9 %collective-permute-start = (bf16[2,8,384,128]{3,2,1,0:T(8,128)(2,1)}, bf16[2,8,384,128]{3,2,1,0:T(8,128)(2,1)}, u32[]{:S(2)}, u32[]{:S(2)}) collective-permute-start(bf16[2,8,384,128]{3,2,1,0:T(8,128)(2,1)} %project_text.1.refs_7_), channel_id=1, source_target_pairs={{16,0},{18,2},{20,4},{22,6},{24,8},{26,10},{28,12},{30,14},{0,16},... | collective-permute-start | bytes 4718600 | tf_op jit(solution)/shard_map/ppermute | solution.py:21
  27.7 5.5 %copy.67 = bf16[1,2,512,2,1024]{4,2,1,3,0:T(8,128)(2,1)} copy(bf16[1,2,512,2,1024]{4,3,2,1,0:T(2,128)(2,1)} %fresh_ref.1) | data formatting | bytes 8388608 | tf_op args[1]
  33.3 3.3 %copy.66 = bf16[1,2,512,2,1024]{4,2,1,3,0:T(8,128)(2,1)} copy(bf16[1,2,512,2,1024]{4,3,2,1,0:T(2,128)(2,1)S(1)} %copy-done.20) | data formatting | bytes 8388608 | tf_op args[2]
  36.5 0.1 fusion
  36.7 0.2 fusion.5
  36.9 0.1 pad_add_fusion.2
  37.0 0.1 compare_reduce_fusion.1
  37.1 0.1 and_bitcast_fusion.1
  37.2 0.1 and_bitcast_fusion
  37.3 0.1 concatenate.56
  37.4 0.7 copy.58
  38.1 1.3 broadcast_select_fusion.refs_10_
  39.4 4.8 %slice_bitcast_fusion.2 = (bf16[2,512,1024]{2,1,0:T(8,128)(2,1)}, bf16[2,512,1024]{2,1,0:T(8,128)(2,1)}) fusion(bf16[2,512,2,1024]{3,1,0,2:T(8,128)(2,1)} %bitcast.68), kind=kLoop, calls=%fused_computation.4 | loop fusion | bytes 8388608 | tf_op jit(solution)/shard_map/squeeze | solution.py:426
  44.2 2.5 slice_bitcast_fusion
  46.8 0.6 compare_convert_fusion
  47.4 16.1 %collective-permute-done.3.after_ref.raw_ref = bf16[2,32,2,1024]{3,2,1,0:T(2,128)(2,1)S(1)} collective-permute-done((bf16[2,32,2,1024]{3,2,1,0:T(2,128)(2,1)S(1)}, bf16[2,32,2,1024]{3,2,1,0:T(2,128)(2,1)S(1)}, u32[]{:S(2)}, u32[]{:S(2)}) %collective-permute-start.3) | collective-permute-done | bytes 262176 | tf_op jit(solution)/shard_map/ppermute | solution.py:21
  63.6 0.7 copy-done.4
  64.3 0.6 broadcast_compare_fusion
  64.9 9.9 %collective-permute-done.6.zone_ref = bf16[2,64,2,1024]{3,2,1,0:T(2,128)(2,1)S(1)} collective-permute-done((bf16[2,64,2,1024]{3,2,1,0:T(2,128)(2,1)}, bf16[2,64,2,1024]{3,2,1,0:T(2,128)(2,1)S(1)}, u32[]{:S(2)}, u32[]{:S(2)}) %collective-permute-start.6) | collective-permute-done | bytes 524320 | tf_op jit(solution)/shard_map/ppermute | solution.py:21
  74.8 0.9 copy-done.5
  75.8 0.1 join_head.3
  75.9 2.2 fusion.7
  78.2 67.0 %collective-permute-done.after_ref.refs_8_ = bf16[2,8,384,128]{3,2,1,0:T(8,128)(2,1)} collective-permute-done((bf16[2,8,384,128]{3,2,1,0:T(8,128)(2,1)}, bf16[2,8,384,128]{3,2,1,0:T(8,128)(2,1)}, u32[]{:S(2)}, u32[]{:S(2)}) %collective-permute-start) | collective-permute-done | bytes 1572896 | tf_op jit(solution)/shard_map/ppermute | solution.py:21
  145.1 1.8 copy_bitcast_fusion.3
  146.9 0.3 copy-done.7
  147.2 1.6 copy-done.8
  148.8 1.6 copy-done.9
  150.4 1.6 copy-done.10
  152.0 1.4 copy-done.11
  153.4 1.4 copy-done.12
  154.8 1.6 copy-done.18
  156.4 34.1 %attention.1 = f32[2,64,512]{2,1,0:T(8,128)S(1)} custom-call(bf16[2,512,1024]{2,1,0:T(8,128)(2,1)S(1)} %bitcast.65, bf16[2,512,1024]{2,1,0:T(8,128)(2,1)S(1)} %copy-done.8, bf16[2,512,1024]{2,1,0:T(8,128)(2,1)S(1)} %copy-done.7, bf16[2,512,1024]{2,1,0:T(8,128)(2,1)S(1)} %copy-done.10, bf16[2,512,1024]{2,1,0:T(8,128)(2,1)S(1)} %copy-done.9, ...), custom_call_target="tpu_custom_call" | custom-call | flops 5133828096 | bytes 25165824 | tf_op jit(solution)/shard_map/attention/pallas_call | solution.py:333
  190.6 0.7 copy-done.15
  191.3 0.7 constant_dynamic-slice_fusion
  191.9 1.8 collective-permute-start.7
  193.8 0.7 multiply_reduce_fusion
  194.5 1.3 squeeze.60.pairs_ref
  195.8 1.5 multiply_reduce_fusion.1
  197.3 1.0 join_head.2.whole_ref
  198.3 6.1 %collective-permute-done.4.after_ref.piece_ref = bf16[416,2,1024]{2,1,0:T(2,128)(2,1)S(1)} collective-permute-done((bf16[416,2,1024]{2,1,0:T(2,128)(2,1)}, bf16[416,2,1024]{2,1,0:T(2,128)(2,1)S(1)}, u32[]{:S(2)}, u32[]{:S(2)}) %collective-permute-start.4) | collective-permute-done | bytes 1703968 | tf_op jit(solution)/shard_map/ppermute | solution.py:21
  204.4 1.2 copy-done
  205.6 29.7 %collective-permute-done.1.after_ref.piece_ref = bf16[260,2,1024]{2,1,0:T(2,128)(2,1)S(1)} collective-permute-done((bf16[260,2,1024]{2,1,0:T(2,128)(2,1)}, bf16[260,2,1024]{2,1,0:T(2,128)(2,1)S(1)}, u32[]{:S(2)}, u32[]{:S(2)}) %collective-permute-start.1) | collective-permute-done | bytes 1064992 | tf_op jit(solution)/shard_map/ppermute | solution.py:21
  235.3 1.0 copy-done.2
  236.2 1.6 fusion.2
  237.9 1.8 fusion.1
  239.7 2.9 %restore.4.whole_ref = bf16[2,512,2,1024]{3,2,1,0:T(2,128)(2,1)} custom-call(s32[256]{0:T(256)S(1)} %copy-done.17, bf16[416,2,1024]{2,1,0:T(2,128)(2,1)S(1)} %copy-done.1, bf16[2,512,2,1024]{3,2,1,0:T(2,128)(2,1)} %join_head.2.whole_ref, bf16[92,2,1024]{2,1,0:T(2,128)(2,1)S(1)} %copy-done.13), custom_call_target="tpu_custom_call", output_to_operand_aliasing={{}: (2, {})} | custom-call | bytes 3407872 | tf_op jit(solution)/shard_map/restore/pallas_call | solution.py:200
  242.6 2.4 restore.5.whole_ref
  245.1 3.9 %collective-permute-done.5.piece_ref = bf16[92,2,1024]{2,1,0:T(2,128)(2,1)S(1)} collective-permute-done((bf16[92,2,1024]{2,1,0:T(2,128)(2,1)}, bf16[92,2,1024]{2,1,0:T(2,128)(2,1)S(1)}, u32[]{:S(2)}, u32[]{:S(2)}) %collective-permute-start.5) | collective-permute-done | bytes 376864 | tf_op jit(solution)/shard_map/ppermute | solution.py:21
  249.0 2.3 restore.6.whole_ref
  251.3 2.5 collective-permute-done.2.piece_ref
  253.7 2.1 restore.7
  (64 shorter events, 0.2 us)
Async XLA Ops:
  1.8 6.8 %copy-start.22 = (bf16[2,32,2,1024]{3,2,1,0:T(2,128)(2,1)}, bf16[2,32,2,1024]{3,2,1,0:T(2,128)(2,1)S(1)}, u32[]{:S(2)}) copy-start(bf16[2,32,2,1024]{3,2,1,0:T(2,128)(2,1)S(1)} %slice_bitcast_fusion.6.after_ref) | copy-start | bytes 786436
  1.8 61.8 %collective-permute-start.3 = (bf16[2,32,2,1024]{3,2,1,0:T(2,128)(2,1)S(1)}, bf16[2,32,2,1024]{3,2,1,0:T(2,128)(2,1)S(1)}, u32[]{:S(2)}, u32[]{:S(2)}) collective-permute-start(bf16[2,32,2,1024]{3,2,1,0:T(2,128)(2,1)S(1)} %slice_bitcast_fusion.6.after_ref), channel_id=1, source_target_pairs={{16,0},{18,2},{20,4},{22,6},{24,8},{26,10},{28,12},{30,14},{0,16},... | collective-permute-start | bytes 786440 | tf_op jit(solution)/shard_map/ppermute | solution.py:21
  8.5 4.1 %copy-start.21 = (bf16[1,2,256,2,1024]{4,3,2,1,0:T(2,128)(2,1)S(1)}, bf16[1,2,256,2,1024]{4,3,2,1,0:T(2,128)(2,1)}, u32[]{:S(2)}) copy-start(bf16[1,2,256,2,1024]{4,3,2,1,0:T(2,128)(2,1)} %param.13) | copy-start | bytes 6291460
  12.5 62.3 %collective-permute-start.6 = (bf16[2,64,2,1024]{3,2,1,0:T(2,128)(2,1)}, bf16[2,64,2,1024]{3,2,1,0:T(2,128)(2,1)S(1)}, u32[]{:S(2)}, u32[]{:S(2)}) collective-permute-start(bf16[2,64,2,1024]{3,2,1,0:T(2,128)(2,1)} %get-tuple-element.10.after_ref), channel_id=1, source_target_pairs={{16,0},{18,2},{20,4},{22,6},{24,8},{26,10},{28,12},{30,14},{0,16},... | collective-permute-start | bytes 1572872 | tf_op jit(solution)/shard_map/ppermute | solution.py:21
  24.8 8.4 %copy-start.20 = (bf16[1,2,512,2,1024]{4,3,2,1,0:T(2,128)(2,1)S(1)}, bf16[1,2,512,2,1024]{4,3,2,1,0:T(2,128)(2,1)}, u32[]{:S(2)}) copy-start(bf16[1,2,512,2,1024]{4,3,2,1,0:T(2,128)(2,1)} %param.12) | copy-start | bytes 12582916
  24.8 120.3 %collective-permute-start = (bf16[2,8,384,128]{3,2,1,0:T(8,128)(2,1)}, bf16[2,8,384,128]{3,2,1,0:T(8,128)(2,1)}, u32[]{:S(2)}, u32[]{:S(2)}) collective-permute-start(bf16[2,8,384,128]{3,2,1,0:T(8,128)(2,1)} %project_text.1.refs_7_), channel_id=1, source_target_pairs={{16,0},{18,2},{20,4},{22,6},{24,8},{26,10},{28,12},{30,14},{0,16},... | collective-permute-start | bytes 4718600 | tf_op jit(solution)/shard_map/ppermute | solution.py:21
  33.3 3.4 %copy-start.23 = (s32[16,2]{0,1:T(2,128)S(1)}, s32[16,2]{0,1:T(2,128)}, u32[]{:S(2)}) copy-start(s32[16,2]{0,1:T(2,128)} %param.16) | copy-start | bytes 388
  39.4 4.8 %copy-start.19 = (bf16[1,2,512,2,1024]{4,2,1,3,0:T(8,128)(2,1)S(1)}, bf16[1,2,512,2,1024]{4,2,1,3,0:T(8,128)(2,1)}, u32[]{:S(2)}) copy-start(bf16[1,2,512,2,1024]{4,2,1,3,0:T(8,128)(2,1)} %copy.66) | copy-start | bytes 12582916
  44.2 2.5 copy-start.26
  63.6 0.7 copy-start.4
  64.3 140.1 %collective-permute-start.4 = (bf16[416,2,1024]{2,1,0:T(2,128)(2,1)}, bf16[416,2,1024]{2,1,0:T(2,128)(2,1)S(1)}, u32[]{:S(2)}, u32[]{:S(2)}) collective-permute-start(bf16[416,2,1024]{2,1,0:T(2,128)(2,1)} %hold.6), channel_id=1, source_target_pairs={{16,0},{18,2},{20,4},{22,6},{24,8},{26,10},{28,12},{30,14},{0,16},... | collective-permute-start | bytes 5111816 | tf_op jit(solution)/shard_map/ppermute | solution.py:21
  74.8 1.0 copy-start.5
  145.1 2.1 copy-start.7
  145.1 2.1 copy-start.16
  145.1 90.1 %collective-permute-start.1 = (bf16[260,2,1024]{2,1,0:T(2,128)(2,1)}, bf16[260,2,1024]{2,1,0:T(2,128)(2,1)S(1)}, u32[]{:S(2)}, u32[]{:S(2)}) collective-permute-start(bf16[260,2,1024]{2,1,0:T(2,128)(2,1)} %hold.4), channel_id=1, source_target_pairs={{16,0},{18,2},{20,4},{22,6},{24,8},{26,10},{28,12},{30,14},{0,16},... | collective-permute-start | bytes 3194888 | tf_op jit(solution)/shard_map/ppermute | solution.py:21
  147.2 1.6 copy-start.8
  148.8 1.6 copy-start.9
  150.4 1.6 copy-start.10
  152.0 1.4 copy-start.11
  153.4 1.4 copy-start.12
  154.8 1.6 copy-start.18
  156.4 37.3 %copy-start.24 = (s32[16,2]{0,1:T(2,128)S(1)}, s32[16,2]{0,1:T(2,128)}, u32[]{:S(2)}) copy-start(s32[16,2]{0,1:T(2,128)} %param.19) | copy-start | bytes 388
  156.4 37.3 %copy-start.25 = (s32[2,16]{1,0:T(2,128)S(1)}, s32[2,16]{1,0:T(2,128)}, u32[]{:S(2)}) copy-start(s32[2,16]{1,0:T(2,128)} %compare_convert_fusion) | copy-start | bytes 388
  156.4 40.9 %copy-start.6 = (bf16[2,32,2,1024]{3,2,1,0:T(2,128)(2,1)S(1)}, bf16[2,32,2,1024]{3,2,1,0:T(2,128)(2,1)}, u32[]{:S(2)}) copy-start(bf16[2,32,2,1024]{3,2,1,0:T(2,128)(2,1)} %copy-done.4) | copy-start | bytes 786436
  190.6 0.7 copy-start.15
  191.9 44.3 %collective-permute-start.7 = (f32[2,64,256]{2,1,0:T(8,128)}, f32[2,64,256]{2,1,0:T(8,128)}, u32[]{:S(2)}, u32[]{:S(2)}) collective-permute-start(f32[2,64,256]{2,1,0:T(8,128)} %constant_dynamic-slice_fusion), channel_id=1, source_target_pairs={{1,0},{0,1},{3,2},{2,3},{5,4},{4,5},{7,6},{6,7},{9,8},{8,9},{11,10... | collective-permute-start | bytes 393224 | tf_op jit(solution)/shard_map/ppermute | solution.py:21
  204.4 1.2 copy-start
  205.6 34.1 %copy-start.1 = (bf16[416,2,1024]{2,1,0:T(2,128)(2,1)S(1)}, bf16[416,2,1024]{2,1,0:T(2,128)(2,1)}, u32[]{:S(2)}) copy-start(bf16[416,2,1024]{2,1,0:T(2,128)(2,1)} %copy-done) | copy-start | bytes 5111812
  205.6 34.1 %copy-start.13 = (bf16[92,2,1024]{2,1,0:T(2,128)(2,1)S(1)}, bf16[92,2,1024]{2,1,0:T(2,128)(2,1)}, u32[]{:S(2)}) copy-start(bf16[92,2,1024]{2,1,0:T(2,128)(2,1)} %hold.7.refs_0_) | copy-start | bytes 1130500
  205.6 34.1 %copy-start.17 = (s32[256]{0:T(256)S(1)}, s32[256]{0:T(256)}, u32[]{:S(2)}) copy-start(s32[256]{0:T(256)} %squeeze.60.pairs_ref) | copy-start | bytes 3076
  205.6 43.4 %collective-permute-start.5 = (bf16[92,2,1024]{2,1,0:T(2,128)(2,1)}, bf16[92,2,1024]{2,1,0:T(2,128)(2,1)S(1)}, u32[]{:S(2)}, u32[]{:S(2)}) collective-permute-start(bf16[92,2,1024]{2,1,0:T(2,128)(2,1)} %hold.7.refs_0_), channel_id=1, source_target_pairs={{16,0},{18,2},{20,4},{22,6},{24,8},{26,10},{28,12},{30,14},{0,16},... | collective-permute-start | bytes 1130504 | tf_op jit(solution)/shard_map/ppermute | solution.py:21
  235.3 1.0 copy-start.2
  236.2 17.5 %collective-permute-start.2 = (bf16[64,2,1024]{2,1,0:T(2,128)(2,1)}, bf16[64,2,1024]{2,1,0:T(2,128)(2,1)S(1)}, u32[]{:S(2)}, u32[]{:S(2)}) collective-permute-start(bf16[64,2,1024]{2,1,0:T(2,128)(2,1)} %hold.5.refs_0_), channel_id=1, source_target_pairs={{16,0},{18,2},{20,4},{22,6},{24,8},{26,10},{28,12},{30,14},{0,16},... | collective-permute-start | bytes 786440 | tf_op jit(solution)/shard_map/ppermute | solution.py:21
  239.7 2.9 %copy-start.3 = (bf16[260,2,1024]{2,1,0:T(2,128)(2,1)S(1)}, bf16[260,2,1024]{2,1,0:T(2,128)(2,1)}, u32[]{:S(2)}) copy-start(bf16[260,2,1024]{2,1,0:T(2,128)(2,1)} %copy-done.2) | copy-start | bytes 3194884
  239.7 2.9 %copy-start.14 = (bf16[64,2,1024]{2,1,0:T(2,128)(2,1)S(1)}, bf16[64,2,1024]{2,1,0:T(2,128)(2,1)}, u32[]{:S(2)}) copy-start(bf16[64,2,1024]{2,1,0:T(2,128)(2,1)} %hold.5.refs_0_) | copy-start | bytes 786436

commit v12 on v11

--- a/solution.py
+++ b/solution.py
@@ -171,7 +171,7 @@
 
 
 def restore_kernel(slot, start, stop, first, pairs_ref, piece_ref, whole_ref, *refs):
-    out_ref, pairs, zone, piece, sems = refs[-5:]
+    out_ref, zone_out, pairs, zone, piece, sems = refs[-6:]
     count = zone.shape[0] - 1
     inner = [
         pltpu.make_async_copy(pairs_ref, pairs, sems.at[4]),
@@ -186,6 +186,7 @@
     outer = [
         pltpu.make_async_copy(piece.at[: stop - start], out_ref.at[slot, start:stop], sems.at[2]),
         pltpu.make_async_copy(zone.at[:count], out_ref.at[slot, first : first + count], sems.at[3]),
+        pltpu.make_async_copy(zone.at[:count], zone_out, sems.at[5]),
     ]
     for copy in outer:
         copy.start()
@@ -199,20 +200,68 @@
     count = pairs.shape[0] // (2 * whole.shape[0])
     return pl.pallas_call(
         functools.partial(restore_kernel, slot, start, stop, first),
+        out_shape=[
+            jax.ShapeDtypeStruct(whole.shape, whole.dtype),
+            jax.ShapeDtypeStruct((count,) + tail, whole.dtype),
+        ],
+        in_specs=[pl.BlockSpec(memory_space=HBM)] * (3 + len(after)),
+        out_specs=[pl.BlockSpec(memory_space=HBM)] * 2,
+        scratch_shapes=[
+            pltpu.SMEM(pairs.shape, pairs.dtype),
+            pltpu.VMEM((count + 1,) + tail, whole.dtype),
+            pltpu.VMEM((stop - start + 1,) + tail, whole.dtype),
+            pltpu.SemaphoreType.DMA((6,)),
+        ],
+        input_output_aliases={2: 0},
+        cost_estimate=pl.CostEstimate(flops=0, bytes_accessed=4 * block.size, transcendentals=0),
+        compiler_params=pltpu.CompilerParams(vmem_limit_bytes=VMEM_LIMIT),
+        name="restore",
+    )(pairs, block, whole, *after)
+
+
+def finish_kernel(slot, start, stop, first, pairs_ref, piece_ref, zone_ref, whole_ref, out_ref, pairs, zone, piece, sems):
+    count, rows = zone.shape[0] - 1, stop - start
+    copy_pairs = pltpu.make_async_copy(pairs_ref, pairs, sems.at[0])
+    copy_pairs.start()
+    zone[:count] = zone_ref[...]
+    piece[:rows] = piece_ref[...]
+    copy_pairs.wait()
+    swap_rows(pairs, out_ref.shape[0], slot, zone, piece, start, stop)
+    outer = [
+        pltpu.make_async_copy(piece.at[:rows], out_ref.at[slot, start:stop], sems.at[1]),
+        pltpu.make_async_copy(zone.at[:count], out_ref.at[slot, first : first + count], sems.at[2]),
+    ]
+    for copy in outer:
+        copy.start()
+    for copy in outer:
+        copy.wait()
+
+
+def finish(pairs, block, zone, whole, piece, first):
+    slot, start, stop = piece
+    tail = whole.shape[2:]
+    count = zone.shape[0]
+    return pl.pallas_call(
+        functools.partial(finish_kernel, slot, start, stop, first),
         out_shape=jax.ShapeDtypeStruct(whole.shape, whole.dtype),
-        in_specs=[pl.BlockSpec(memory_space=HBM)] * (3 + len(after)),
+        in_specs=[
+            pl.BlockSpec(memory_space=HBM),
+            pl.BlockSpec(memory_space=pltpu.VMEM),
+            pl.BlockSpec(memory_space=pltpu.VMEM),
+            pl.BlockSpec(memory_space=HBM),
+        ],
         out_specs=pl.BlockSpec(memory_space=HBM),
         scratch_shapes=[
             pltpu.SMEM(pairs.shape, pairs.dtype),
             pltpu.VMEM((count + 1,) + tail, whole.dtype),
             pltpu.VMEM((stop - start + 1,) + tail, whole.dtype),
-            pltpu.SemaphoreType.DMA((5,)),
-        ],
-        input_output_aliases={2: 0},
+            pltpu.SemaphoreType.DMA((3,)),
+        ],
+        input_output_aliases={3: 0},
         cost_estimate=pl.CostEstimate(flops=0, bytes_accessed=4 * block.size, transcendentals=0),
         compiler_params=pltpu.CompilerParams(vmem_limit_bytes=VMEM_LIMIT),
-        name="restore",
-    )(pairs, block, whole, *after)
+        name="finish",
+    )(pairs, block, zone, whole)
 
 
 def hold_kernel(block_ref, after_ref, out_ref):
@@ -457,8 +506,11 @@
     latent_next = latent[0] + step_size[:, None, None] * velocity
 
     next_stale = join_head(raw_in, zone_in, fresh.shape)
-    for index, piece in enumerate(pieces):
-        next_stale = restore(pairs[1], arrived[index], next_stale, piece, first, held[index + 2 : index + 3])
+    for index, piece in enumerate(pieces[:-1]):
+        next_stale, zone_now = restore(
+            pairs[1], arrived[index], next_stale, piece, first, held[index + 2 : index + 3]
+        )
+    next_stale = finish(pairs[1], arrived[-1], zone_now, next_stale, pieces[-1], first)
     return (next_stale[None], velocity[None], latent_next[None])
 
 

time: 257 us -> 257 us (level)
    pallas_call x4 -> x3, Pallas kernels: 9.79 us -> 7.82 us  [restore(): pl.pallas_call(functools.partial(restore_kernel, slot, start, stop, first...]
where the time goes in v12:
time: 257 us; the launch traced here: 255 us
  waiting for transfers between devices  135 us (53%)
  Pallas kernels  58.8 us (23%)
  local copies, waits for them, and re-layouts  41.9 us (16%)
  other arithmetic  10 us (4%)
  starting transfers between devices  8.93 us (3%)
    ppermute x8, waiting for transfers between devices, from_behind(): return lax.ppermute(block, axis, route)  135 us
    pallas_call x1, Pallas kernels, attention(): pl.pallas_call(functools.partial(attention_kernel, text_rows), grid=(slot...  34.1 us
    unnamed x57, local copies, waits for them, and re-layouts  23.5 us
    pallas_call x1, Pallas kernels, project_text(): pl.pallas_call(text_kernel, grid=(slots, heads), out_shape=jax.ShapeDtype...  10.1 us
    ppermute x8, starting transfers between devices, from_behind(): return lax.ppermute(block, axis, route)  8.93 us
    pallas_call x3, Pallas kernels, restore(): pl.pallas_call(functools.partial(restore_kernel, slot, start, stop, first...  7.82 us
  transfers between devices with their start and end apart: 8, of which 7 were waited for; matrix products, arithmetic and copies ran while one was open for 14% of the time, Pallas kernels for 22%

profile of v12, /device:TPU:0, one launch (start us, length us, event | category | flops | bytes accessed | tf_op | source)
XLA Modules:
  0.0 255.5 jit_solution(13972505862607754662)
XLA Ops:
  0.6 1.1 slice_bitcast_fusion.6.after_ref
  1.8 4.1 %collective-permute-start.3 = (bf16[2,32,2,1024]{3,2,1,0:T(2,128)(2,1)S(1)}, bf16[2,32,2,1024]{3,2,1,0:T(2,128)(2,1)S(1)}, u32[]{:S(2)}, u32[]{:S(2)}) collective-permute-start(bf16[2,32,2,1024]{3,2,1,0:T(2,128)(2,1)S(1)} %slice_bitcast_fusion.6.after_ref), channel_id=1, source_target_pairs={{16,0},{18,2},{20,4},{22,6},{24,8},{26,10},{28,12},{30,14},{0,16},... | collective-permute-start | bytes 786440 | tf_op jit(solution)/shard_map/ppermute | solution.py:21
  5.9 0.7 constant_dynamic-slice_fusion.4
  6.6 0.1 compare_reduce_fusion
  6.8 0.2 convert_reduce_fusion.1
  7.0 0.3 select_reduce_fusion
  7.3 0.6 pad_add_fusion
  7.9 0.6 squeeze.61.pairs_ref
  8.5 4.0 %arrange.1 = (bf16[2,64,2,1024]{3,2,1,0:T(2,128)(2,1)}, bf16[416,2,1024]{2,1,0:T(2,128)(2,1)}, bf16[260,2,1024]{2,1,0:T(2,128)(2,1)}, bf16[92,2,1024]{2,1,0:T(2,128)(2,1)}, bf16[64,2,1024]{2,1,0:T(2,128)(2,1)}) custom-call(s32[256]{0:T(256)} %squeeze.61.pairs_ref, bf16[1,2,512,2,1024]{4,3,2,1,0:T(2,128)(2,1)} %fresh_ref.1, bf16[2,32,2,1024]{3,2,1,0:T(2,128)(2,1)} %copy-done.22), custom_call_target="tpu_custom_call" | custom-call | bytes 8388608 | tf_op jit(solution)/shard_map/arrange/pallas_call | solution.py:118
  12.5 0.1 collective-permute-start.6
  12.6 0.6 copy.68
  13.2 1.5 slice_bitcast_fusion.4
  14.7 10.1 %project_text.1.refs_7_ = bf16[2,8,384,128]{3,2,1,0:T(8,128)(2,1)} custom-call(bf16[2,256,1024]{2,1,0:T(8,128)(2,1)} %get-tuple-element.32.k_ref, bf16[2,256,1024]{2,1,0:T(8,128)(2,1)} %get-tuple-element.31.v_ref, bf16[64,1024]{1,0:T(8,128)(2,1)} %bitcast.63, bf16[2,64,2,1024]{3,2,1,0:T(2,128)(2,1)} %get-tuple-element.14.after_ref), custom_call_target="tpu_custom_call" | custom-call | flops 67108864 | bytes 4194304 | tf_op jit(solution)/shard_map/project_text/pallas_call | solution.py:303
  24.8 2.9 %collective-permute-start = (bf16[2,8,384,128]{3,2,1,0:T(8,128)(2,1)}, bf16[2,8,384,128]{3,2,1,0:T(8,128)(2,1)}, u32[]{:S(2)}, u32[]{:S(2)}) collective-permute-start(bf16[2,8,384,128]{3,2,1,0:T(8,128)(2,1)} %project_text.1.refs_7_), channel_id=1, source_target_pairs={{16,0},{18,2},{20,4},{22,6},{24,8},{26,10},{28,12},{30,14},{0,16},... | collective-permute-start | bytes 4718600 | tf_op jit(solution)/shard_map/ppermute | solution.py:21
  27.7 5.5 %copy.67 = bf16[1,2,512,2,1024]{4,2,1,3,0:T(8,128)(2,1)} copy(bf16[1,2,512,2,1024]{4,3,2,1,0:T(2,128)(2,1)} %fresh_ref.1) | data formatting | bytes 8388608 | tf_op args[1]
  33.2 3.3 %copy.66 = bf16[1,2,512,2,1024]{4,2,1,3,0:T(8,128)(2,1)} copy(bf16[1,2,512,2,1024]{4,3,2,1,0:T(2,128)(2,1)S(1)} %copy-done.20) | data formatting | bytes 8388608 | tf_op args[2]
  36.5 0.1 fusion
  36.6 0.2 fusion.5
  36.9 0.1 pad_add_fusion.2
  37.0 0.1 compare_reduce_fusion.1
  37.1 0.1 and_bitcast_fusion.1
  37.1 0.1 and_bitcast_fusion
  37.2 0.1 concatenate.56
  37.3 0.7 copy.58
  38.0 1.3 broadcast_select_fusion.refs_10_
  39.4 4.8 %slice_bitcast_fusion.2 = (bf16[2,512,1024]{2,1,0:T(8,128)(2,1)}, bf16[2,512,1024]{2,1,0:T(8,128)(2,1)}) fusion(bf16[2,512,2,1024]{3,1,0,2:T(8,128)(2,1)} %bitcast.68), kind=kLoop, calls=%fused_computation.4 | loop fusion | bytes 8388608 | tf_op jit(solution)/shard_map/squeeze | solution.py:475
  44.2 2.5 slice_bitcast_fusion
  46.8 0.7 compare_convert_fusion
  47.4 16.1 %collective-permute-done.3.after_ref.raw_ref = bf16[2,32,2,1024]{3,2,1,0:T(2,128)(2,1)S(1)} collective-permute-done((bf16[2,32,2,1024]{3,2,1,0:T(2,128)(2,1)S(1)}, bf16[2,32,2,1024]{3,2,1,0:T(2,128)(2,1)S(1)}, u32[]{:S(2)}, u32[]{:S(2)}) %collective-permute-start.3) | collective-permute-done | bytes 262176 | tf_op jit(solution)/shard_map/ppermute | solution.py:21
  63.6 0.7 copy-done.4
  64.3 0.7 broadcast_compare_fusion
  64.9 9.9 %collective-permute-done.6.zone_ref = bf16[2,64,2,1024]{3,2,1,0:T(2,128)(2,1)S(1)} collective-permute-done((bf16[2,64,2,1024]{3,2,1,0:T(2,128)(2,1)}, bf16[2,64,2,1024]{3,2,1,0:T(2,128)(2,1)S(1)}, u32[]{:S(2)}, u32[]{:S(2)}) %collective-permute-start.6) | collective-permute-done | bytes 524320 | tf_op jit(solution)/shard_map/ppermute | solution.py:21
  74.8 0.9 copy-done.5
  75.8 0.1 join_head.3
  75.9 2.2 fusion.7
  78.2 67.0 %collective-permute-done.after_ref.refs_8_ = bf16[2,8,384,128]{3,2,1,0:T(8,128)(2,1)} collective-permute-done((bf16[2,8,384,128]{3,2,1,0:T(8,128)(2,1)}, bf16[2,8,384,128]{3,2,1,0:T(8,128)(2,1)}, u32[]{:S(2)}, u32[]{:S(2)}) %collective-permute-start) | collective-permute-done | bytes 1572896 | tf_op jit(solution)/shard_map/ppermute | solution.py:21
  145.1 1.8 copy_bitcast_fusion.3
  146.9 0.3 copy-done.7
  147.2 1.6 copy-done.8
  148.8 1.6 copy-done.9
  150.4 1.6 copy-done.10
  152.0 1.4 copy-done.11
  153.4 1.4 copy-done.12
  154.8 1.6 copy-done.18
  156.4 34.1 %attention.1 = f32[2,64,512]{2,1,0:T(8,128)S(1)} custom-call(bf16[2,512,1024]{2,1,0:T(8,128)(2,1)S(1)} %bitcast.65, bf16[2,512,1024]{2,1,0:T(8,128)(2,1)S(1)} %copy-done.8, bf16[2,512,1024]{2,1,0:T(8,128)(2,1)S(1)} %copy-done.7, bf16[2,512,1024]{2,1,0:T(8,128)(2,1)S(1)} %copy-done.10, bf16[2,512,1024]{2,1,0:T(8,128)(2,1)S(1)} %copy-done.9, ...), custom_call_target="tpu_custom_call" | custom-call | flops 5133828096 | bytes 25165824 | tf_op jit(solution)/shard_map/attention/pallas_call | solution.py:382
  190.6 0.7 copy-done.15
  191.3 0.7 constant_dynamic-slice_fusion
  191.9 1.8 collective-permute-start.7
  193.8 0.7 multiply_reduce_fusion
  194.5 1.4 squeeze.60.pairs_ref
  195.8 1.5 multiply_reduce_fusion.1
  197.3 1.0 join_head.2.whole_ref
  198.3 6.0 %collective-permute-done.4.after_ref.piece_ref = bf16[416,2,1024]{2,1,0:T(2,128)(2,1)S(1)} collective-permute-done((bf16[416,2,1024]{2,1,0:T(2,128)(2,1)}, bf16[416,2,1024]{2,1,0:T(2,128)(2,1)S(1)}, u32[]{:S(2)}, u32[]{:S(2)}) %collective-permute-start.4) | collective-permute-done | bytes 1703968 | tf_op jit(solution)/shard_map/ppermute | solution.py:21
  204.4 1.2 copy-done
  205.6 29.7 %collective-permute-done.1.after_ref.piece_ref = bf16[260,2,1024]{2,1,0:T(2,128)(2,1)S(1)} collective-permute-done((bf16[260,2,1024]{2,1,0:T(2,128)(2,1)}, bf16[260,2,1024]{2,1,0:T(2,128)(2,1)S(1)}, u32[]{:S(2)}, u32[]{:S(2)}) %collective-permute-start.1) | collective-permute-done | bytes 1064992 | tf_op jit(solution)/shard_map/ppermute | solution.py:21
  235.3 1.0 copy-done.2
  236.3 1.6 fusion.2
  237.9 1.8 fusion.1
  239.7 3.0 %restore.3 = (bf16[2,512,2,1024]{3,2,1,0:T(2,128)(2,1)}, bf16[64,2,1024]{2,1,0:T(2,128)(2,1)}) custom-call(s32[256]{0:T(256)S(1)} %copy-done.17, bf16[416,2,1024]{2,1,0:T(2,128)(2,1)S(1)} %copy-done.1, bf16[2,512,2,1024]{3,2,1,0:T(2,128)(2,1)} %join_head.2.whole_ref, bf16[92,2,1024]{2,1,0:T(2,128)(2,1)S(1)} %copy-done.13), custom_call_target="tpu_custom_call", output_to_operand_aliasing={{0}: (2, {})} | custom-call | bytes 3407872 | tf_op jit(solution)/shard_map/restore/pallas_call | solution.py:201
  242.7 2.5 restore.4
  245.2 3.7 %collective-permute-done.5.piece_ref = bf16[92,2,1024]{2,1,0:T(2,128)(2,1)S(1)} collective-permute-done((bf16[92,2,1024]{2,1,0:T(2,128)(2,1)}, bf16[92,2,1024]{2,1,0:T(2,128)(2,1)S(1)}, u32[]{:S(2)}, u32[]{:S(2)}) %collective-permute-start.5) | collective-permute-done | bytes 376864 | tf_op jit(solution)/shard_map/ppermute | solution.py:21
  249.0 2.3 restore.5
  251.3 2.5 collective-permute-done.2.piece_ref
  253.7 1.7 finish.1
  (64 shorter events, 0.2 us)
Async XLA Ops:
  1.8 6.8 %copy-start.22 = (bf16[2,32,2,1024]{3,2,1,0:T(2,128)(2,1)}, bf16[2,32,2,1024]{3,2,1,0:T(2,128)(2,1)S(1)}, u32[]{:S(2)}) copy-start(bf16[2,32,2,1024]{3,2,1,0:T(2,128)(2,1)S(1)} %slice_bitcast_fusion.6.after_ref) | copy-start | bytes 786436
  1.8 61.8 %collective-permute-start.3 = (bf16[2,32,2,1024]{3,2,1,0:T(2,128)(2,1)S(1)}, bf16[2,32,2,1024]{3,2,1,0:T(2,128)(2,1)S(1)}, u32[]{:S(2)}, u32[]{:S(2)}) collective-permute-start(bf16[2,32,2,1024]{3,2,1,0:T(2,128)(2,1)S(1)} %slice_bitcast_fusion.6.after_ref), channel_id=1, source_target_pairs={{16,0},{18,2},{20,4},{22,6},{24,8},{26,10},{28,12},{30,14},{0,16},... | collective-permute-start | bytes 786440 | tf_op jit(solution)/shard_map/ppermute | solution.py:21
  8.5 4.1 %copy-start.21 = (bf16[1,2,256,2,1024]{4,3,2,1,0:T(2,128)(2,1)S(1)}, bf16[1,2,256,2,1024]{4,3,2,1,0:T(2,128)(2,1)}, u32[]{:S(2)}) copy-start(bf16[1,2,256,2,1024]{4,3,2,1,0:T(2,128)(2,1)} %param.13) | copy-start | bytes 6291460
  12.5 62.3 %collective-permute-start.6 = (bf16[2,64,2,1024]{3,2,1,0:T(2,128)(2,1)}, bf16[2,64,2,1024]{3,2,1,0:T(2,128)(2,1)S(1)}, u32[]{:S(2)}, u32[]{:S(2)}) collective-permute-start(bf16[2,64,2,1024]{3,2,1,0:T(2,128)(2,1)} %get-tuple-element.14.after_ref), channel_id=1, source_target_pairs={{16,0},{18,2},{20,4},{22,6},{24,8},{26,10},{28,12},{30,14},{0,16},... | collective-permute-start | bytes 1572872 | tf_op jit(solution)/shard_map/ppermute | solution.py:21
  24.8 8.4 %copy-start.20 = (bf16[1,2,512,2,1024]{4,3,2,1,0:T(2,128)(2,1)S(1)}, bf16[1,2,512,2,1024]{4,3,2,1,0:T(2,128)(2,1)}, u32[]{:S(2)}) copy-start(bf16[1,2,512,2,1024]{4,3,2,1,0:T(2,128)(2,1)} %param.12) | copy-start | bytes 12582916
  24.8 120.4 %collective-permute-start = (bf16[2,8,384,128]{3,2,1,0:T(8,128)(2,1)}, bf16[2,8,384,128]{3,2,1,0:T(8,128)(2,1)}, u32[]{:S(2)}, u32[]{:S(2)}) collective-permute-start(bf16[2,8,384,128]{3,2,1,0:T(8,128)(2,1)} %project_text.1.refs_7_), channel_id=1, source_target_pairs={{16,0},{18,2},{20,4},{22,6},{24,8},{26,10},{28,12},{30,14},{0,16},... | collective-permute-start | bytes 4718600 | tf_op jit(solution)/shard_map/ppermute | solution.py:21
  33.2 3.4 %copy-start.23 = (s32[16,2]{0,1:T(2,128)S(1)}, s32[16,2]{0,1:T(2,128)}, u32[]{:S(2)}) copy-start(s32[16,2]{0,1:T(2,128)} %param.16) | copy-start | bytes 388
  39.4 4.8 %copy-start.19 = (bf16[1,2,512,2,1024]{4,2,1,3,0:T(8,128)(2,1)S(1)}, bf16[1,2,512,2,1024]{4,2,1,3,0:T(8,128)(2,1)}, u32[]{:S(2)}) copy-start(bf16[1,2,512,2,1024]{4,2,1,3,0:T(8,128)(2,1)} %copy.66) | copy-start | bytes 12582916
  44.2 2.5 copy-start.26
  63.6 0.7 copy-start.4
  64.3 140.1 %collective-permute-start.4 = (bf16[416,2,1024]{2,1,0:T(2,128)(2,1)}, bf16[416,2,1024]{2,1,0:T(2,128)(2,1)S(1)}, u32[]{:S(2)}, u32[]{:S(2)}) collective-permute-start(bf16[416,2,1024]{2,1,0:T(2,128)(2,1)} %hold.6), channel_id=1, source_target_pairs={{16,0},{18,2},{20,4},{22,6},{24,8},{26,10},{28,12},{30,14},{0,16},... | collective-permute-start | bytes 5111816 | tf_op jit(solution)/shard_map/ppermute | solution.py:21
  74.8 1.0 copy-start.5
  145.1 2.1 copy-start.7
  145.1 2.1 copy-start.16
  145.1 90.1 %collective-permute-start.1 = (bf16[260,2,1024]{2,1,0:T(2,128)(2,1)}, bf16[260,2,1024]{2,1,0:T(2,128)(2,1)S(1)}, u32[]{:S(2)}, u32[]{:S(2)}) collective-permute-start(bf16[260,2,1024]{2,1,0:T(2,128)(2,1)} %hold.4), channel_id=1, source_target_pairs={{16,0},{18,2},{20,4},{22,6},{24,8},{26,10},{28,12},{30,14},{0,16},... | collective-permute-start | bytes 3194888 | tf_op jit(solution)/shard_map/ppermute | solution.py:21
  147.2 1.6 copy-start.8
  148.8 1.6 copy-start.9
  150.4 1.6 copy-start.10
  152.0 1.4 copy-start.11
  153.4 1.4 copy-start.12
  154.8 1.6 copy-start.18
  156.4 37.3 %copy-start.24 = (s32[16,2]{0,1:T(2,128)S(1)}, s32[16,2]{0,1:T(2,128)}, u32[]{:S(2)}) copy-start(s32[16,2]{0,1:T(2,128)} %param.19) | copy-start | bytes 388
  156.4 37.3 %copy-start.25 = (s32[2,16]{1,0:T(2,128)S(1)}, s32[2,16]{1,0:T(2,128)}, u32[]{:S(2)}) copy-start(s32[2,16]{1,0:T(2,128)} %compare_convert_fusion) | copy-start | bytes 388
  156.4 40.9 %copy-start.6 = (bf16[2,32,2,1024]{3,2,1,0:T(2,128)(2,1)S(1)}, bf16[2,32,2,1024]{3,2,1,0:T(2,128)(2,1)}, u32[]{:S(2)}) copy-start(bf16[2,32,2,1024]{3,2,1,0:T(2,128)(2,1)} %copy-done.4) | copy-start | bytes 786436
  190.6 0.7 copy-start.15
  191.9 44.3 %collective-permute-start.7 = (f32[2,64,256]{2,1,0:T(8,128)}, f32[2,64,256]{2,1,0:T(8,128)}, u32[]{:S(2)}, u32[]{:S(2)}) collective-permute-start(f32[2,64,256]{2,1,0:T(8,128)} %constant_dynamic-slice_fusion), channel_id=1, source_target_pairs={{1,0},{0,1},{3,2},{2,3},{5,4},{4,5},{7,6},{6,7},{9,8},{8,9},{11,10... | collective-permute-start | bytes 393224 | tf_op jit(solution)/shard_map/ppermute | solution.py:21
  204.4 1.2 copy-start
  205.6 34.1 %copy-start.1 = (bf16[416,2,1024]{2,1,0:T(2,128)(2,1)S(1)}, bf16[416,2,1024]{2,1,0:T(2,128)(2,1)}, u32[]{:S(2)}) copy-start(bf16[416,2,1024]{2,1,0:T(2,128)(2,1)} %copy-done) | copy-start | bytes 5111812
  205.6 34.1 %copy-start.13 = (bf16[92,2,1024]{2,1,0:T(2,128)(2,1)S(1)}, bf16[92,2,1024]{2,1,0:T(2,128)(2,1)}, u32[]{:S(2)}) copy-start(bf16[92,2,1024]{2,1,0:T(2,128)(2,1)} %hold.7.refs_0_) | copy-start | bytes 1130500
  205.6 34.1 %copy-start.17 = (s32[256]{0:T(256)S(1)}, s32[256]{0:T(256)}, u32[]{:S(2)}) copy-start(s32[256]{0:T(256)} %squeeze.60.pairs_ref) | copy-start | bytes 3076
  205.6 43.4 %collective-permute-start.5 = (bf16[92,2,1024]{2,1,0:T(2,128)(2,1)}, bf16[92,2,1024]{2,1,0:T(2,128)(2,1)S(1)}, u32[]{:S(2)}, u32[]{:S(2)}) collective-permute-start(bf16[92,2,1024]{2,1,0:T(2,128)(2,1)} %hold.7.refs_0_), channel_id=1, source_target_pairs={{16,0},{18,2},{20,4},{22,6},{24,8},{26,10},{28,12},{30,14},{0,16},... | collective-permute-start | bytes 1130504 | tf_op jit(solution)/shard_map/ppermute | solution.py:21
  235.3 1.0 copy-start.2
  236.2 17.5 %collective-permute-start.2 = (bf16[64,2,1024]{2,1,0:T(2,128)(2,1)}, bf16[64,2,1024]{2,1,0:T(2,128)(2,1)S(1)}, u32[]{:S(2)}, u32[]{:S(2)}) collective-permute-start(bf16[64,2,1024]{2,1,0:T(2,128)(2,1)} %hold.5.refs_0_), channel_id=1, source_target_pairs={{16,0},{18,2},{20,4},{22,6},{24,8},{26,10},{28,12},{30,14},{0,16},... | collective-permute-start | bytes 786440 | tf_op jit(solution)/shard_map/ppermute | solution.py:21
  239.7 3.0 %copy-start.3 = (bf16[260,2,1024]{2,1,0:T(2,128)(2,1)S(1)}, bf16[260,2,1024]{2,1,0:T(2,128)(2,1)}, u32[]{:S(2)}) copy-start(bf16[260,2,1024]{2,1,0:T(2,128)(2,1)} %copy-done.2) | copy-start | bytes 3194884
  239.7 3.0 %copy-start.14 = (bf16[64,2,1024]{2,1,0:T(2,128)(2,1)S(1)}, bf16[64,2,1024]{2,1,0:T(2,128)(2,1)}, u32[]{:S(2)}) copy-start(bf16[64,2,1024]{2,1,0:T(2,128)(2,1)} %hold.5.refs_0_) | copy-start | bytes 786436
